TPU v7x, 32 devices: a whole 2x2x4 slice. The times are simulated.
32 devices in a mesh: section: 2 (over core), row: 4 (over z), col: 4 (over y, x).
Axes of the slice: x: 2, y: 2, z: 4, core: 2. Of those that a mesh axis runs over, the one named last changes fastest.
Arguments:
- block_input: bfloat16 [4, 1600, 2048], P(None, 'col', 'row'), may hold values from -6 to 6
- out_cotangent: bfloat16 [4, 1600, 2048], P(None, 'col', 'row'), may hold values from -6 to 6
- group_order: int32 [8], replicated, may hold values from 0 to 7, each once
- first_gain: float32 [2, 1600], P('section', 'col'), may hold values from 0.1 to 1.9
- first_bias: float32 [2, 1600], P('section', 'col'), may hold values from -4 to 4
- query_weight: bfloat16 [2, 1600, 1600], P('section', 'row', 'col'), may hold values from -0.15625 to 0.15625
- key_weight: bfloat16 [2, 1600, 1600], P('section', 'row', 'col'), may hold values from -0.15625 to 0.15625
- value_weight: bfloat16 [2, 1600, 1600], P('section', 'row', 'col'), may hold values from -0.15625 to 0.15625
- query_bias: float32 [2, 1600], P('section', 'col'), may hold values from -4 to 4
- value_bias: float32 [2, 1600], P('section', 'col'), may hold values from -4 to 4
- out_weight: bfloat16 [2, 1600, 1600], P('section', 'col', 'row'), may hold values from -1.25 to 1.25
- out_bias: float32 [2, 1600], P('section', 'col'), may hold values from -4 to 4
- second_gain: float32 [2, 1600], P('section', 'col'), may hold values from 0.1 to 1.9
- second_bias: float32 [2, 1600], P('section', 'col'), may hold values from -4 to 4
- up_weight: bfloat16 [2, 1600, 6400], P('section', 'row', 'col'), may hold values from -0.15625 to 0.15625
- up_bias: float32 [2, 6400], P('section', 'col'), may hold values from -4 to 4
- down_weight: bfloat16 [2, 1600, 6400], P('section', 'row', 'col'), may hold values from -0.078125 to 0.078125
- down_bias: float32 [2, 1600], P('section', 'col'), may hold values from -4 to 4
Outputs:
- boundary: float32 [2, 4, 1600, 2048], P('section', None, 'col', 'row')
- first_gain_gradient: float32 [2, 1600], P('section', 'col')
- first_bias_gradient: float32 [2, 1600], P('section', 'col')
- query_weight_gradient: float32 [2, 1600, 1600], P('section', 'row', 'col')
- key_weight_gradient: float32 [2, 1600, 1600], P('section', 'row', 'col')
- value_weight_gradient: float32 [2, 1600, 1600], P('section', 'row', 'col')
- query_bias_gradient: float32 [2, 1600], P('section', 'col')
- value_bias_gradient: float32 [2, 1600], P('section', 'col')
- out_weight_gradient: float32 [2, 1600, 1600], P('section', 'col', 'row')
- out_bias_gradient: float32 [2, 1600], P('section', 'col')
- second_gain_gradient: float32 [2, 1600], P('section', 'col')
- second_bias_gradient: float32 [2, 1600], P('section', 'col')
- up_weight_gradient: float32 [2, 1600, 6400], P('section', 'row', 'col')
- up_bias_gradient: float32 [2, 6400], P('section', 'col')
- down_weight_gradient: float32 [2, 1600, 6400], P('section', 'row', 'col')
- down_bias_gradient: float32 [2, 1600], P('section', 'col')
Inputs may be any that keep to these rules, and one draw needn't show every extreme that they name: `group_order`: a permutation of 0 to 7, the same for every sequence.
All inputs are finite; a program needn't handle non-finite values.
Results may differ from a plain program's by a relative error of at most 0.015.
Values may be sent and summed in bfloat16 or wider, within the bound.
No kernel may reach another device: no remote copies, remote signals or barrier semaphores. Data moves between devices by JAX's collectives and lax.ppermute only.
A program may use at most 448 MiB of HBM per device.

v0:
```python
import math

import jax
import jax.numpy as jnp
from jax import lax
from jax.sharding import PartitionSpec as P

H = 25
HD = 64
L = 512


epsilon = 1e-05
tanh_scale = math.sqrt(2.0 / math.pi)
cubic_weight = 0.044715


def shifted(value, axis, steps):
    count = lax.axis_size(axis)
    initial, last = (max(0, -steps), min(count, count - steps))
    return lax.ppermute(value, axis, [(source, source + steps) for source in range(initial, last)])


def gelu_value(inputs):
    inner = tanh_scale * (inputs + cubic_weight * inputs * inputs * inputs)
    return 0.5 * inputs * (1.0 + jnp.tanh(inner))


def gelu_slope(inputs):
    inner = tanh_scale * (inputs + cubic_weight * inputs * inputs * inputs)
    tangent = jnp.tanh(inner)
    return 0.5 * (1.0 + tangent) + 0.5 * inputs * (1.0 - tangent * tangent) * tanh_scale * (
        1.0 + 3.0 * cubic_weight * inputs * inputs
    )


def matmul(left, right):
    return jnp.dot(left, right, preferred_element_type=jnp.float32)


def left_inner(left, right):
    return lax.dot_general(
        left, right, (((0,), (0,)), ((), ())), preferred_element_type=jnp.float32
    )


def right_inner(left, right):
    return lax.dot_general(
        left, right, (((1,), (1,)), ((), ())), preferred_element_type=jnp.float32
    )


def gather_width(columns):
    return lax.all_gather(columns, "col", axis=1, tiled=True)


def reduce_width(partial_value):
    return lax.psum_scatter(partial_value, "col", scatter_dimension=1, tiled=True)


def row_pair(first_sum, second_sum):
    return lax.psum((first_sum, second_sum), "col")


def to_heads(columns):
    return lax.all_to_all(columns, "col", split_axis=0, concat_axis=1, tiled=True)


def to_columns(heads):
    return lax.all_to_all(heads, "col", split_axis=1, concat_axis=0, tiled=True)


def send_forward(values):
    return shifted(values, "section", 1)


def send_backward(values):
    return shifted(values, "section", -1)


def reduce_matrices(row_terms, col_terms):
    row_sums = (
        lax.psum_scatter(row_terms[0], "row", scatter_dimension=0, tiled=True),
        lax.psum_scatter(row_terms[1], "row", scatter_dimension=0, tiled=True),
        lax.psum_scatter(row_terms[2], "row", scatter_dimension=0, tiled=True),
        lax.psum_scatter(row_terms[3], "row", scatter_dimension=0, tiled=True),
        lax.psum_scatter(row_terms[4], "row", scatter_dimension=0, tiled=True),
    )
    col_sums = (lax.psum_scatter(col_terms[0], "row", scatter_dimension=1, tiled=True),)
    return (tuple(row_sums), tuple(col_sums))


def positions(group_order, first_row, row_count):
    blocks = group_order.shape[0]
    group_rows = L // blocks
    rows_here = first_row + jnp.arange(row_count, dtype=jnp.int32)
    within = rows_here % L
    block_match = (within // group_rows)[:, None] == jnp.arange(blocks, dtype=jnp.int32)[None, :]
    group_start = jnp.sum(jnp.where(block_match, group_order[None, :], 0), axis=1)
    return (group_start * group_rows + within % group_rows, rows_here // L)


def norm_forward(stream, gain, offset):
    feature_count = stream.shape[1] * lax.axis_size("col")
    row_total, squares = row_pair(jnp.sum(stream, axis=1), jnp.sum(stream * stream, axis=1))
    row_mean = row_total / feature_count
    row_scale = lax.rsqrt(squares / feature_count - row_mean * row_mean + epsilon)
    normed = (stream - row_mean[:, None]) * row_scale[:, None]
    return ((normed * gain + offset).astype(jnp.bfloat16), row_mean, row_scale)


def norm_backward(incoming, stream, row_mean, row_scale, gain):
    feature_count = stream.shape[1] * lax.axis_size("col")
    normed = (stream - row_mean[:, None]) * row_scale[:, None]
    scaled = incoming * gain
    row_total, cross = row_pair(jnp.sum(scaled, axis=1), jnp.sum(scaled * normed, axis=1))
    outgoing = row_scale[:, None] * (
        scaled - row_total[:, None] / feature_count - normed * cross[:, None] / feature_count
    )
    return (outgoing, jnp.sum(incoming * normed, axis=0), jnp.sum(incoming, axis=0))


def split_heads(values):
    return values.reshape(values.shape[0], H, HD)


def attention_scores(query_heads, key_rows, allowed):
    logits = jnp.einsum(
        "qhd,khd->hqk",
        split_heads(query_heads),
        split_heads(key_rows),
        preferred_element_type=jnp.float32,
    ) * HD ** (-0.5)
    return jnp.where(allowed[None], logits, -jnp.inf)


def layer_forward(stream, weights, smalls, allowed):
    query_full, key_full, value_full, up_full, down_full, out_full = weights
    (
        gain_one,
        bias_one,
        query_shift,
        value_shift,
        out_shift,
        gain_two,
        bias_two,
        up_shift,
        down_shift,
    ) = smalls
    normed_one, mean_one, scale_one = norm_forward(stream, gain_one, bias_one)
    inputs_one = gather_width(normed_one)
    queries = (matmul(inputs_one, query_full) + query_shift).astype(jnp.bfloat16)
    key_cols = matmul(inputs_one, key_full).astype(jnp.bfloat16)
    value_cols = (matmul(inputs_one, value_full) + value_shift).astype(jnp.bfloat16)
    query_heads = to_heads(queries)
    key_rows, value_rows = (
        lax.all_gather(key_cols, "col", axis=1, tiled=True),
        lax.all_gather(value_cols, "col", axis=1, tiled=True),
    )
    scores = attention_scores(query_heads, key_rows, allowed)
    row_peak = jnp.max(scores, axis=2, keepdims=True)
    log_total = row_peak + jnp.log(jnp.sum(jnp.exp(scores - row_peak), axis=2, keepdims=True))
    softmax_half = jnp.exp(scores - log_total).astype(jnp.bfloat16)
    attended = jnp.einsum(
        "hqk,khd->qhd", softmax_half, split_heads(value_rows), preferred_element_type=jnp.float32
    )
    attended = attended.astype(jnp.bfloat16).reshape(query_heads.shape)
    attended_cols = to_columns(attended)
    middle = stream + reduce_width(matmul(attended_cols, out_full)) + out_shift
    normed_two, mean_two, scale_two = norm_forward(middle, gain_two, bias_two)
    inputs_two = gather_width(normed_two)
    hidden_pre = matmul(inputs_two, up_full) + up_shift
    hidden = gelu_value(hidden_pre).astype(jnp.bfloat16)
    result = middle + reduce_width(right_inner(hidden, down_full)) + down_shift
    saved = (
        stream,
        mean_one,
        scale_one,
        inputs_one,
        query_heads,
        key_rows,
        value_rows,
        log_total,
        attended_cols,
        middle,
        mean_two,
        scale_two,
        inputs_two,
        hidden_pre,
        hidden,
    )
    return (result, saved)


def layer_backward(upstream, saved, weights, smalls, allowed):
    query_full, key_full, value_full, up_full, down_full, out_full = weights
    (
        gain_one,
        bias_one,
        query_shift,
        value_shift,
        out_shift,
        gain_two,
        bias_two,
        up_shift,
        down_shift,
    ) = smalls
    (
        stream,
        mean_one,
        scale_one,
        inputs_one,
        query_heads,
        key_rows,
        value_rows,
        log_total,
        attended_cols,
        middle,
        mean_two,
        scale_two,
        inputs_two,
        hidden_pre,
        hidden,
    ) = saved
    upstream_half = upstream.astype(jnp.bfloat16)
    upstream_full = gather_width(upstream_half)
    down_grad = left_inner(upstream_full, hidden)
    down_shift_grad = jnp.sum(upstream, axis=0)
    hidden_grad = matmul(upstream_full, down_full) * gelu_slope(hidden_pre)
    hidden_half = hidden_grad.astype(jnp.bfloat16)
    up_shift_grad = jnp.sum(hidden_grad, axis=0)
    up_grad = left_inner(inputs_two, hidden_half)
    normed_two_grad = reduce_width(right_inner(hidden_half, up_full))
    middle_part, gain_two_grad, bias_two_grad = norm_backward(
        normed_two_grad, middle, mean_two, scale_two, gain_two
    )
    middle_grad = upstream + middle_part
    middle_half = middle_grad.astype(jnp.bfloat16)
    middle_full = gather_width(middle_half)
    out_shift_grad = jnp.sum(middle_grad, axis=0)
    out_grad = left_inner(attended_cols, middle_full)
    attended_grad = to_heads(right_inner(middle_full, out_full).astype(jnp.bfloat16))
    scores = attention_scores(query_heads, key_rows, allowed)
    softmax_weights = jnp.exp(scores - log_total)
    softmax_half = softmax_weights.astype(jnp.bfloat16)
    grad_heads = split_heads(attended_grad)
    value_part = jnp.einsum(
        "hqk,qhd->khd", softmax_half, grad_heads, preferred_element_type=jnp.float32
    ).reshape(key_rows.shape)
    probs_grad = jnp.einsum(
        "qhd,khd->hqk", grad_heads, split_heads(value_rows), preferred_element_type=jnp.float32
    )
    row_dot = jnp.sum(softmax_weights * probs_grad, axis=2, keepdims=True)
    scores_grad = (softmax_weights * (probs_grad - row_dot) * HD ** (-0.5)).astype(jnp.bfloat16)
    query_grad_heads = jnp.einsum(
        "hqk,khd->qhd", scores_grad, split_heads(key_rows), preferred_element_type=jnp.float32
    )
    query_grad_heads = query_grad_heads.astype(jnp.bfloat16).reshape(query_heads.shape)
    key_part = jnp.einsum(
        "hqk,qhd->khd", scores_grad, split_heads(query_heads), preferred_element_type=jnp.float32
    ).reshape(key_rows.shape)
    key_sums, value_sums = (
        lax.psum_scatter(key_part, "col", scatter_dimension=1, tiled=True),
        lax.psum_scatter(value_part, "col", scatter_dimension=1, tiled=True),
    )
    query_cols = to_columns(query_grad_heads)
    key_half = key_sums.astype(jnp.bfloat16)
    value_half = value_sums.astype(jnp.bfloat16)
    query_shift_grad = jnp.sum(query_cols.astype(jnp.float32), axis=0)
    value_shift_grad = jnp.sum(value_sums, axis=0)
    query_grad = left_inner(inputs_one, query_cols)
    key_grad = left_inner(inputs_one, key_half)
    value_grad = left_inner(inputs_one, value_half)
    normed_one_grad = reduce_width(
        right_inner(query_cols, query_full)
        + right_inner(key_half, key_full)
        + right_inner(value_half, value_full)
    )
    stream_part, gain_one_grad, bias_one_grad = norm_backward(
        normed_one_grad, stream, mean_one, scale_one, gain_one
    )
    stream_grad = middle_grad + stream_part
    row_terms = (query_grad, key_grad, value_grad, up_grad, down_grad)
    col_terms = (out_grad,)
    small_terms = (
        gain_one_grad,
        bias_one_grad,
        query_shift_grad,
        value_shift_grad,
        out_shift_grad,
        gain_two_grad,
        bias_two_grad,
        up_shift_grad,
        down_shift_grad,
    )
    return (stream_grad, row_terms, col_terms, small_terms)


def on_device(
    block_input,
    out_cotangent,
    group_order,
    first_gain,
    first_bias,
    query_weight,
    key_weight,
    value_weight,
    query_bias,
    value_bias,
    out_weight,
    out_bias,
    second_gain,
    second_bias,
    up_weight,
    up_bias,
    down_weight,
    down_bias,
):
    section_index = lax.axis_index("section")
    col_index = lax.axis_index("col")
    batches = block_input.shape[0]
    width_here = block_input.shape[1]
    local_rows = block_input.shape[2]
    query_rows = local_rows // lax.axis_size("col")
    key_position, key_sequence = positions(group_order, 0, local_rows)
    query_position, query_sequence = positions(group_order, col_index * query_rows, query_rows)
    allowed = (query_sequence[:, None] == key_sequence[None, :]) & (
        key_position[None, :] <= query_position[:, None]
    )
    row_blocks = (
        lax.all_gather(query_weight[0], "row", axis=0, tiled=True),
        lax.all_gather(key_weight[0], "row", axis=0, tiled=True),
        lax.all_gather(value_weight[0], "row", axis=0, tiled=True),
        lax.all_gather(up_weight[0], "row", axis=0, tiled=True),
        lax.all_gather(down_weight[0], "row", axis=0, tiled=True),
    )
    col_blocks = (lax.all_gather(out_weight[0], "row", axis=1, tiled=True),)
    weights = (
        row_blocks[0],
        row_blocks[1],
        row_blocks[2],
        row_blocks[3],
        row_blocks[4],
        col_blocks[0],
    )
    smalls = (
        first_gain[0],
        first_bias[0],
        query_bias[0],
        value_bias[0],
        out_bias[0],
        second_gain[0],
        second_bias[0],
        up_bias[0],
        down_bias[0],
    )
    saved_list = []
    outputs = []
    received = jnp.zeros((local_rows, width_here), jnp.float32)
    for moment in range(batches + 1):
        if moment > 0:
            received = send_forward(outputs[-1])
        fresh_rows = block_input[min(moment, batches - 1)].T.astype(jnp.float32)
        stream = jnp.where(section_index == 0, fresh_rows, received)
        result, saved = layer_forward(stream, weights, smalls, allowed)
        outputs.append(result)
        saved_list.append(saved)
    stacked = jax.tree.map(lambda *pieces: jnp.stack(pieces), *saved_list)
    row_totals = tuple(
        (
            jnp.zeros(matrix.shape[1:], jnp.float32)
            for matrix in (query_weight, key_weight, value_weight, up_weight, down_weight)
        )
    )
    col_totals = tuple((jnp.zeros(matrix.shape[1:], jnp.float32) for matrix in (out_weight,)))
    small_totals = tuple((jnp.zeros(vector.shape, jnp.float32) for vector in smalls))
    returned = []
    incoming = jnp.zeros((local_rows, width_here), jnp.float32)
    for moment in range(batches + 1):
        if moment > 0:
            incoming = send_backward(returned[-1])
        batch_index = moment - 1 + section_index
        active = (batch_index >= 0) & (batch_index < batches)
        cotangent_cols = lax.dynamic_index_in_dim(
            out_cotangent, jnp.clip(batch_index, 0, batches - 1), 0, keepdims=False
        )
        upstream = jnp.where(section_index == 1, cotangent_cols.T.astype(jnp.float32), incoming)
        upstream = jnp.where(active, upstream, 0.0)
        slot_index = jnp.clip(moment - 1 + 2 * section_index, 0, batches)
        saved = jax.tree.map(
            lambda stacked_piece: lax.dynamic_index_in_dim(
                stacked_piece, slot_index, 0, keepdims=False
            ),
            stacked,
        )
        stream_grad, row_terms, col_terms, small_terms = layer_backward(
            upstream, saved, weights, smalls, allowed
        )
        returned.append(stream_grad)
        row_sums, col_sums = reduce_matrices(row_terms, col_terms)
        row_totals = tuple(
            (total_piece + term_piece for total_piece, term_piece in zip(row_totals, row_sums))
        )
        col_totals = tuple(
            (total_piece + term_piece for total_piece, term_piece in zip(col_totals, col_sums))
        )
        small_totals = tuple(
            (total_piece + term_piece for total_piece, term_piece in zip(small_totals, small_terms))
        )
    small_sums = lax.psum(
        (
            small_totals[0],
            small_totals[1],
            small_totals[2],
            small_totals[3],
            small_totals[4],
            small_totals[5],
            small_totals[6],
            small_totals[7],
            small_totals[8],
        ),
        "row",
    )
    boundary_rows = jnp.where(section_index == 0, jnp.stack(returned[1:]), jnp.stack(outputs[1:]))
    boundary = jnp.swapaxes(boundary_rows, 1, 2)[None]
    return (
        boundary,
        small_sums[0][None],
        small_sums[1][None],
        row_totals[0][None],
        row_totals[1][None],
        row_totals[2][None],
        small_sums[2][None],
        small_sums[3][None],
        col_totals[0][None],
        small_sums[4][None],
        small_sums[5][None],
        small_sums[6][None],
        row_totals[3][None],
        small_sums[7][None],
        row_totals[4][None],
        small_sums[8][None],
    )


def solution(mesh):
    in_specs = (
        P(None, "col", "row"),
        P(None, "col", "row"),
        P(),
        P("section", "col"),
        P("section", "col"),
        P("section", "row", "col"),
        P("section", "row", "col"),
        P("section", "row", "col"),
        P("section", "col"),
        P("section", "col"),
        P("section", "col", "row"),
        P("section", "col"),
        P("section", "col"),
        P("section", "col"),
        P("section", "row", "col"),
        P("section", "col"),
        P("section", "row", "col"),
        P("section", "col"),
    )
    out_specs = (
        P("section", None, "col", "row"),
        P("section", "col"),
        P("section", "col"),
        P("section", "row", "col"),
        P("section", "row", "col"),
        P("section", "row", "col"),
        P("section", "col"),
        P("section", "col"),
        P("section", "col", "row"),
        P("section", "col"),
        P("section", "col"),
        P("section", "col"),
        P("section", "row", "col"),
        P("section", "col"),
        P("section", "row", "col"),
        P("section", "col"),
    )
    return jax.shard_map(
        on_device, mesh=mesh, in_specs=in_specs, out_specs=out_specs, check_vma=False
    )
```

profile of v0, /device:TPU:0, one launch (start us, length us, event | category | flops | bytes accessed | tf_op | source)
XLA Modules:
  0.0 4222.1 jit_solution(16577218946394282587)
XLA Ops:
  50.5 32.8 all-gather.43.cloned.1.call-done
  87.1 35.9 all-gather.103.cloned.1.call-done
  128.6 33.0 all-gather.105.cloned.1.call-done
  200.1 28.3 all-gather.45.cloned.1.call-done
  237.8 58.4 %all-gather.109.cloned.1.call-done = bf16[1,400,1600]{1,0,2:T(2,128)(2,1)} async-done(((bf16[1,400,400]{1,0,2:T(2,128)(2,1)}), bf16[1,400,1600]{1,0,2:T(2,128)(2,1)}) %all-gather.109.cloned.1.call-update) | async-done | bytes 1280016 | tf_op jit(solution)/shard_map/all_gather | solution.py:337
  308.3 43.0 %reduce-scatter.39.cloned.1.call-done = f32[512,400]{0,1:T(8,128)} async-done(((f32[512,1600]{0,1:T(8,128)}), f32[512,400]{0,1:T(8,128)}) %reduce-scatter.39.cloned.1.call-update) | async-done | bytes 819216 | tf_op jit(solution)/shard_map/reduce_scatter | solution.py:58
  365.3 87.1 %all-gather.111.cloned.1.call-done = bf16[1,1600,1600]{2,1,0:T(8,128)(2,1)} async-done(((bf16[1,400,1600]{2,1,0:T(8,128)(2,1)}), bf16[1,1600,1600]{2,1,0:T(8,128)(2,1)}) %all-gather.111.cloned.1.call-update) | async-done | bytes 5120016 | tf_op jit(solution)/shard_map/all_gather | solution.py:334
  452.3 32.2 all-gather.49.cloned.1.call-done
  493.4 92.1 %all-gather.113.cloned.1.call-done = bf16[1,1600,1600]{2,1,0:T(8,128)(2,1)} async-done(((bf16[1,400,1600]{2,1,0:T(8,128)(2,1)}), bf16[1,1600,1600]{2,1,0:T(8,128)(2,1)}) %all-gather.113.cloned.1.call-update) | async-done | bytes 5120016 | tf_op jit(solution)/shard_map/all_gather | solution.py:335
  594.1 43.5 %reduce-scatter.41.cloned.1.call-done = f32[512,400]{0,1:T(8,128)} async-done(((f32[512,1600]{0,1:T(8,128)}), f32[512,400]{0,1:T(8,128)}) %reduce-scatter.41.cloned.1.call-update) | async-done | bytes 819216 | tf_op jit(solution)/shard_map/reduce_scatter | solution.py:58
  655.0 31.6 all-gather.51.cloned.1.call-done
  731.4 28.2 all-gather.53.cloned.1.call-done
  778.7 44.3 %reduce-scatter.43.cloned.1.call-done = f32[512,400]{0,1:T(8,128)} async-done(((f32[512,1600]{0,1:T(8,128)}), f32[512,400]{0,1:T(8,128)}) %reduce-scatter.43.cloned.1.call-update) | async-done | bytes 819216 | tf_op jit(solution)/shard_map/reduce_scatter | solution.py:58
  837.5 31.6 all-gather.57.cloned.1.call-done
  886.6 45.0 %reduce-scatter.45.cloned.1.call-done = f32[512,400]{0,1:T(8,128)} async-done(((f32[512,1600]{0,1:T(8,128)}), f32[512,400]{0,1:T(8,128)}) %reduce-scatter.45.cloned.1.call-update) | async-done | bytes 819216 | tf_op jit(solution)/shard_map/reduce_scatter | solution.py:58
  951.6 31.6 all-gather.59.cloned.1.call-done
  1028.0 28.4 all-gather.61.cloned.1.call-done
  1075.5 44.3 %reduce-scatter.47.cloned.1.call-done = f32[512,400]{0,1:T(8,128)} async-done(((f32[512,1600]{0,1:T(8,128)}), f32[512,400]{0,1:T(8,128)}) %reduce-scatter.47.cloned.1.call-update) | async-done | bytes 819216 | tf_op jit(solution)/shard_map/reduce_scatter | solution.py:58
  1134.7 31.2 all-gather.65.cloned.1.call-done
  1183.1 45.2 %reduce-scatter.49.cloned.1.call-done = f32[512,400]{0,1:T(8,128)} async-done(((f32[512,1600]{0,1:T(8,128)}), f32[512,400]{0,1:T(8,128)}) %reduce-scatter.49.cloned.1.call-update) | async-done | bytes 819216 | tf_op jit(solution)/shard_map/reduce_scatter | solution.py:58
  1247.8 31.6 all-gather.67.cloned.1.call-done
  1324.2 28.2 all-gather.69.cloned.1.call-done
  1371.4 44.3 %reduce-scatter.51.cloned.1.call-done = f32[512,400]{0,1:T(8,128)} async-done(((f32[512,1600]{0,1:T(8,128)}), f32[512,400]{0,1:T(8,128)}) %reduce-scatter.51.cloned.1.call-update) | async-done | bytes 819216 | tf_op jit(solution)/shard_map/reduce_scatter | solution.py:58
  1430.3 31.6 all-gather.73.cloned.1.call-done
  1479.4 45.0 %reduce-scatter.53.cloned.1.call-done = f32[512,400]{0,1:T(8,128)} async-done(((f32[512,1600]{0,1:T(8,128)}), f32[512,400]{0,1:T(8,128)}) %reduce-scatter.53.cloned.1.call-update) | async-done | bytes 819216 | tf_op jit(solution)/shard_map/reduce_scatter | solution.py:58
  1543.8 31.6 all-gather.75.cloned.1.call-done
  1620.2 28.2 all-gather.77.cloned.1.call-done
  1667.5 44.3 %reduce-scatter.55.cloned.1.call-done = f32[512,400]{0,1:T(8,128)} async-done(((f32[512,1600]{0,1:T(8,128)}), f32[512,400]{0,1:T(8,128)}) %reduce-scatter.55.cloned.1.call-update) | async-done | bytes 819216 | tf_op jit(solution)/shard_map/reduce_scatter | solution.py:58
  1729.3 28.6 all-gather.83.cloned.1.call-done
  1825.9 29.5 reduce-scatter.57.cloned.1.call-done
  1922.6 28.9 fusion.67
  1958.3 28.3 fusion.549
  2009.1 39.7 reduce-scatter.61.cloned.1.call-done
  2055.7 43.9 %reduce-scatter.63.cloned.1.call-done = f32[512,400]{0,1:T(8,128)} async-done(((f32[512,1600]{0,1:T(8,128)}), f32[512,400]{0,1:T(8,128)}) %reduce-scatter.63.cloned.1.call-update) | async-done | bytes 819216 | tf_op jit(solution)/shard_map/reduce_scatter | solution.py:58
  2120.8 31.1 all-gather.87.cloned.1.call-done
  2170.3 45.2 %reduce-scatter.65.cloned.1.call-done = f32[512,400]{0,1:T(8,128)} async-done(((f32[512,1600]{0,1:T(8,128)}), f32[512,400]{0,1:T(8,128)}) %reduce-scatter.65.cloned.1.call-update) | async-done | bytes 819216 | tf_op jit(solution)/shard_map/reduce_scatter | solution.py:58
  2231.2 31.6 all-gather.89.cloned.1.call-done
  2283.0 28.8 fusion.74
  2318.5 28.4 fusion.546
  2369.6 39.9 reduce-scatter.69.cloned.1.call-done
  2415.0 45.2 %reduce-scatter.71.cloned.1.call-done = f32[512,400]{0,1:T(8,128)} async-done(((f32[512,1600]{0,1:T(8,128)}), f32[512,400]{0,1:T(8,128)}) %reduce-scatter.71.cloned.1.call-update) | async-done | bytes 819216 | tf_op jit(solution)/shard_map/reduce_scatter | solution.py:58
  2481.0 31.6 all-gather.91.cloned.1.call-done
  2531.1 45.2 %reduce-scatter.73.cloned.1.call-done = f32[512,400]{0,1:T(8,128)} async-done(((f32[512,1600]{0,1:T(8,128)}), f32[512,400]{0,1:T(8,128)}) %reduce-scatter.73.cloned.1.call-update) | async-done | bytes 819216 | tf_op jit(solution)/shard_map/reduce_scatter | solution.py:58
  2592.4 31.6 all-gather.93.cloned.1.call-done
  2644.2 28.8 fusion.81
  2679.6 28.3 fusion.543
  2730.7 40.0 reduce-scatter.77.cloned.1.call-done
  2776.3 45.2 %reduce-scatter.79.cloned.1.call-done = f32[512,400]{0,1:T(8,128)} async-done(((f32[512,1600]{0,1:T(8,128)}), f32[512,400]{0,1:T(8,128)}) %reduce-scatter.79.cloned.1.call-update) | async-done | bytes 819216 | tf_op jit(solution)/shard_map/reduce_scatter | solution.py:58
  2842.4 31.5 all-gather.95.cloned.1.call-done
  2892.3 45.2 %reduce-scatter.81.cloned.1.call-done = f32[512,400]{0,1:T(8,128)} async-done(((f32[512,1600]{0,1:T(8,128)}), f32[512,400]{0,1:T(8,128)}) %reduce-scatter.81.cloned.1.call-update) | async-done | bytes 819216 | tf_op jit(solution)/shard_map/reduce_scatter | solution.py:58
  2953.4 31.6 all-gather.97.cloned.1.call-done
  3005.2 28.8 fusion.88
  3040.7 28.3 fusion.540
  3091.8 39.8 reduce-scatter.85.cloned.1.call-done
  3137.1 45.2 %reduce-scatter.87.cloned.1.call-done = f32[512,400]{0,1:T(8,128)} async-done(((f32[512,1600]{0,1:T(8,128)}), f32[512,400]{0,1:T(8,128)}) %reduce-scatter.87.cloned.1.call-update) | async-done | bytes 819216 | tf_op jit(solution)/shard_map/reduce_scatter | solution.py:58
  3203.1 31.5 all-gather.99.cloned.1.call-done
  3253.0 45.2 %reduce-scatter.89.cloned.1.call-done = f32[512,400]{0,1:T(8,128)} async-done(((f32[512,1600]{0,1:T(8,128)}), f32[512,400]{0,1:T(8,128)}) %reduce-scatter.89.cloned.1.call-update) | async-done | bytes 819216 | tf_op jit(solution)/shard_map/reduce_scatter | solution.py:58
  3314.1 31.6 all-gather.101.cloned.1.call-done
  3366.0 28.9 fusion.95
  3452.9 28.4 fusion.537
  3715.0 184.1 %reduce-scatter.105.cloned.1.call-done = f32[400,1600]{1,0:T(8,128)} async-done(((f32[1600,1600]{1,0:T(8,128)}), f32[400,1600]{1,0:T(8,128)}) %reduce-scatter.105.cloned.1.call-update) | async-done | bytes 2560016 | tf_op jit(solution)/shard_map/reduce_scatter | solution.py:86
  3899.1 184.8 %reduce-scatter.107.cloned.1.call-done = f32[400,1600]{1,0:T(8,128)} async-done(((f32[1600,1600]{1,0:T(8,128)}), f32[400,1600]{1,0:T(8,128)}) %reduce-scatter.107.cloned.1.call-update) | async-done | bytes 2560016 | tf_op jit(solution)/shard_map/reduce_scatter | solution.py:87
  4084.0 66.3 %reduce-scatter.101.cloned.1.call-done = f32[400,400]{1,0:T(8,128)} async-done(((f32[1600,400]{1,0:T(8,128)}), f32[400,400]{1,0:T(8,128)}) %reduce-scatter.101.cloned.1.call-update) | async-done | bytes 640016 | tf_op jit(solution)/shard_map/reduce_scatter | solution.py:84
  4150.2 65.2 %reduce-scatter.103.cloned.1.call-done = f32[400,400]{1,0:T(8,128)} async-done(((f32[1600,400]{1,0:T(8,128)}), f32[400,400]{1,0:T(8,128)}) %reduce-scatter.103.cloned.1.call-update) | async-done | bytes 640016 | tf_op jit(solution)/shard_map/reduce_scatter | solution.py:85
  (923 shorter events, 1456.8 us)
Async XLA Ops:
  7.9 75.4 %all-gather.43.cloned.1.call-start = ((), (), s32[]{:S(2)}) async-start(), calls=%async_computation.56 | async-start | bytes 2048000 | tf_op jit(solution)/shard_map/all_gather | solution.py:54
  24.2 98.9 %all-gather.103.cloned.1.call-start = ((), (), s32[]{:S(2)}) async-start(), calls=%async_computation.116 | async-start | bytes 2048000 | tf_op jit(solution)/shard_map/all_gather | solution.py:333
  24.9 136.6 %all-gather.105.cloned.1.call-start = ((), (), s32[]{:S(2)}) async-start(), calls=%async_computation.117 | async-start | bytes 2048000 | tf_op jit(solution)/shard_map/all_gather | solution.py:331
  25.5 169.1 %all-gather.47.cloned.1.call-start = ((), (), s32[]{:S(2)}) async-start(), calls=%async_computation.58 | async-start | bytes 2048000 | tf_op jit(solution)/shard_map/all_gather | solution.py:157
  87.1 141.3 %all-gather.45.cloned.1.call-start = ((), (), s32[]{:S(2)}) async-start(), calls=%async_computation.57 | async-start | bytes 2048000 | tf_op jit(solution)/shard_map/all_gather | solution.py:158
  126.3 170.0 %all-gather.109.cloned.1.call-start = ((), (), s32[]{:S(2)}) async-start(), calls=%async_computation.119 | async-start | bytes 4096000 | tf_op jit(solution)/shard_map/all_gather | solution.py:337
  237.8 113.5 %reduce-scatter.39.cloned.1.call-start = ((), (), s32[]{:S(2)}) async-start(), calls=%async_computation.59 | async-start | bytes 4096000 | tf_op jit(solution)/shard_map/reduce_scatter | solution.py:58
  307.5 144.8 %all-gather.111.cloned.1.call-start = ((), (), s32[]{:S(2)}) async-start(), calls=%async_computation.120 | async-start | bytes 6656000 | tf_op jit(solution)/shard_map/all_gather | solution.py:334
  308.2 176.3 %all-gather.49.cloned.1.call-start = ((), (), s32[]{:S(2)}) async-start(), calls=%async_computation.60 | async-start | bytes 2048000 | tf_op jit(solution)/shard_map/all_gather | solution.py:54
  364.0 221.5 %all-gather.113.cloned.1.call-start = ((), (), s32[]{:S(2)}) async-start(), calls=%async_computation.121 | async-start | bytes 6656000 | tf_op jit(solution)/shard_map/all_gather | solution.py:335
  364.7 272.9 %reduce-scatter.41.cloned.1.call-start = ((), (), s32[]{:S(2)}) async-start(), calls=%async_computation.61 | async-start | bytes 4096000 | tf_op jit(solution)/shard_map/reduce_scatter | solution.py:58
  594.0 92.5 %all-gather.51.cloned.1.call-start = ((), (), s32[]{:S(2)}) async-start(), calls=%async_computation.62 | async-start | bytes 2048000 | tf_op jit(solution)/shard_map/all_gather | solution.py:54
  654.9 70.9 %all-gather.55.cloned.1.call-start = ((), (), s32[]{:S(2)}) async-start(), calls=%async_computation.64 | async-start | bytes 2048000 | tf_op jit(solution)/shard_map/all_gather | solution.py:157
  693.5 129.5 %reduce-scatter.43.cloned.1.call-start = ((), (), s32[]{:S(2)}) async-start(), calls=%async_computation.65 | async-start | bytes 4096000 | tf_op jit(solution)/shard_map/reduce_scatter | solution.py:58
  778.6 90.5 %all-gather.57.cloned.1.call-start = ((), (), s32[]{:S(2)}) async-start(), calls=%async_computation.66 | async-start | bytes 2048000 | tf_op jit(solution)/shard_map/all_gather | solution.py:54
  837.5 94.0 %reduce-scatter.45.cloned.1.call-start = ((), (), s32[]{:S(2)}) async-start(), calls=%async_computation.67 | async-start | bytes 4096000 | tf_op jit(solution)/shard_map/reduce_scatter | solution.py:58
  886.3 96.9 %all-gather.59.cloned.1.call-start = ((), (), s32[]{:S(2)}) async-start(), calls=%async_computation.68 | async-start | bytes 2048000 | tf_op jit(solution)/shard_map/all_gather | solution.py:54
  951.6 70.8 %all-gather.63.cloned.1.call-start = ((), (), s32[]{:S(2)}) async-start(), calls=%async_computation.70 | async-start | bytes 2048000 | tf_op jit(solution)/shard_map/all_gather | solution.py:157
  990.1 129.7 %reduce-scatter.47.cloned.1.call-start = ((), (), s32[]{:S(2)}) async-start(), calls=%async_computation.71 | async-start | bytes 4096000 | tf_op jit(solution)/shard_map/reduce_scatter | solution.py:58
  1075.4 90.5 %all-gather.65.cloned.1.call-start = ((), (), s32[]{:S(2)}) async-start(), calls=%async_computation.72 | async-start | bytes 2048000 | tf_op jit(solution)/shard_map/all_gather | solution.py:54
  1134.3 94.0 %reduce-scatter.49.cloned.1.call-start = ((), (), s32[]{:S(2)}) async-start(), calls=%async_computation.73 | async-start | bytes 4096000 | tf_op jit(solution)/shard_map/reduce_scatter | solution.py:58
  1183.0 96.3 %all-gather.67.cloned.1.call-start = ((), (), s32[]{:S(2)}) async-start(), calls=%async_computation.74 | async-start | bytes 2048000 | tf_op jit(solution)/shard_map/all_gather | solution.py:54
  1286.2 129.5 %reduce-scatter.51.cloned.1.call-start = ((), (), s32[]{:S(2)}) async-start(), calls=%async_computation.77 | async-start | bytes 4096000 | tf_op jit(solution)/shard_map/reduce_scatter | solution.py:58
  1371.4 90.5 %all-gather.73.cloned.1.call-start = ((), (), s32[]{:S(2)}) async-start(), calls=%async_computation.78 | async-start | bytes 2048000 | tf_op jit(solution)/shard_map/all_gather | solution.py:54
  1430.2 94.1 %reduce-scatter.53.cloned.1.call-start = ((), (), s32[]{:S(2)}) async-start(), calls=%async_computation.79 | async-start | bytes 4096000 | tf_op jit(solution)/shard_map/reduce_scatter | solution.py:58
  1479.1 96.3 %all-gather.75.cloned.1.call-start = ((), (), s32[]{:S(2)}) async-start(), calls=%async_computation.80 | async-start | bytes 2048000 | tf_op jit(solution)/shard_map/all_gather | solution.py:54
  1582.2 129.6 %reduce-scatter.55.cloned.1.call-start = ((), (), s32[]{:S(2)}) async-start(), calls=%async_computation.83 | async-start | bytes 4096000 | tf_op jit(solution)/shard_map/reduce_scatter | solution.py:58
  1667.4 90.5 %all-gather.83.cloned.1.call-start = ((), (), s32[]{:S(2)}) async-start(), calls=%async_computation.85 | async-start | bytes 2048000 | tf_op jit(solution)/shard_map/all_gather | solution.py:54
  1728.9 126.4 %reduce-scatter.57.cloned.1.call-start = ((), (), s32[]{:S(2)}) async-start(), calls=%async_computation.86 | async-start | bytes 4096000 | tf_op jit(solution)/shard_map/reduce_scatter | solution.py:58
  1810.1 92.3 %all-gather.85.cloned.1.call-start = ((), (), s32[]{:S(2)}) async-start(), calls=%async_computation.87 | async-start | bytes 2048000 | tf_op jit(solution)/shard_map/all_gather | solution.py:54
  1910.1 94.0 %reduce-scatter.59.cloned.1.call-start = ((), (), s32[]{:S(2)}) async-start(), calls=%async_computation.88 | async-start | bytes 4096000 | tf_op jit(solution)/shard_map/reduce_scatter | solution.py:263
  1951.5 97.3 %reduce-scatter.61.cloned.1.call-start = ((), (), s32[]{:S(2)}) async-start(), calls=%async_computation.89 | async-start | bytes 4096000 | tf_op jit(solution)/shard_map/reduce_scatter | solution.py:264
  1958.0 141.5 %reduce-scatter.63.cloned.1.call-start = ((), (), s32[]{:S(2)}) async-start(), calls=%async_computation.90 | async-start | bytes 4096000 | tf_op jit(solution)/shard_map/reduce_scatter | solution.py:58
  2054.3 97.6 %all-gather.87.cloned.1.call-start = ((), (), s32[]{:S(2)}) async-start(), calls=%async_computation.91 | async-start | bytes 2048000 | tf_op jit(solution)/shard_map/all_gather | solution.py:54
  2120.3 95.2 %reduce-scatter.65.cloned.1.call-start = ((), (), s32[]{:S(2)}) async-start(), calls=%async_computation.92 | async-start | bytes 4096000 | tf_op jit(solution)/shard_map/reduce_scatter | solution.py:58
  2170.2 92.6 %all-gather.89.cloned.1.call-start = ((), (), s32[]{:S(2)}) async-start(), calls=%async_computation.93 | async-start | bytes 2048000 | tf_op jit(solution)/shard_map/all_gather | solution.py:54
  2270.5 94.1 %reduce-scatter.67.cloned.1.call-start = ((), (), s32[]{:S(2)}) async-start(), calls=%async_computation.94 | async-start | bytes 4096000 | tf_op jit(solution)/shard_map/reduce_scatter | solution.py:263
  2311.9 97.6 %reduce-scatter.69.cloned.1.call-start = ((), (), s32[]{:S(2)}) async-start(), calls=%async_computation.95 | async-start | bytes 4096000 | tf_op jit(solution)/shard_map/reduce_scatter | solution.py:264
  2318.4 141.8 %reduce-scatter.71.cloned.1.call-start = ((), (), s32[]{:S(2)}) async-start(), calls=%async_computation.96 | async-start | bytes 4096000 | tf_op jit(solution)/shard_map/reduce_scatter | solution.py:58
  2415.0 97.6 %all-gather.91.cloned.1.call-start = ((), (), s32[]{:S(2)}) async-start(), calls=%async_computation.97 | async-start | bytes 2048000 | tf_op jit(solution)/shard_map/all_gather | solution.py:54
  2481.0 95.3 %reduce-scatter.73.cloned.1.call-start = ((), (), s32[]{:S(2)}) async-start(), calls=%async_computation.98 | async-start | bytes 4096000 | tf_op jit(solution)/shard_map/reduce_scatter | solution.py:58
  2531.0 93.0 %all-gather.93.cloned.1.call-start = ((), (), s32[]{:S(2)}) async-start(), calls=%async_computation.99 | async-start | bytes 2048000 | tf_op jit(solution)/shard_map/all_gather | solution.py:54
  2631.7 94.0 %reduce-scatter.75.cloned.1.call-start = ((), (), s32[]{:S(2)}) async-start(), calls=%async_computation.100 | async-start | bytes 4096000 | tf_op jit(solution)/shard_map/reduce_scatter | solution.py:263
  2673.1 97.7 %reduce-scatter.77.cloned.1.call-start = ((), (), s32[]{:S(2)}) async-start(), calls=%async_computation.101 | async-start | bytes 4096000 | tf_op jit(solution)/shard_map/reduce_scatter | solution.py:264
  2679.6 141.9 %reduce-scatter.79.cloned.1.call-start = ((), (), s32[]{:S(2)}) async-start(), calls=%async_computation.102 | async-start | bytes 4096000 | tf_op jit(solution)/shard_map/reduce_scatter | solution.py:58
  2776.3 97.7 %all-gather.95.cloned.1.call-start = ((), (), s32[]{:S(2)}) async-start(), calls=%async_computation.103 | async-start | bytes 2048000 | tf_op jit(solution)/shard_map/all_gather | solution.py:54
  2842.3 95.1 %reduce-scatter.81.cloned.1.call-start = ((), (), s32[]{:S(2)}) async-start(), calls=%async_computation.104 | async-start | bytes 4096000 | tf_op jit(solution)/shard_map/reduce_scatter | solution.py:58
  2892.2 92.8 %all-gather.97.cloned.1.call-start = ((), (), s32[]{:S(2)}) async-start(), calls=%async_computation.105 | async-start | bytes 2048000 | tf_op jit(solution)/shard_map/all_gather | solution.py:54
  2992.7 94.1 %reduce-scatter.83.cloned.1.call-start = ((), (), s32[]{:S(2)}) async-start(), calls=%async_computation.106 | async-start | bytes 4096000 | tf_op jit(solution)/shard_map/reduce_scatter | solution.py:263
  3034.1 97.5 %reduce-scatter.85.cloned.1.call-start = ((), (), s32[]{:S(2)}) async-start(), calls=%async_computation.107 | async-start | bytes 4096000 | tf_op jit(solution)/shard_map/reduce_scatter | solution.py:264
  3040.6 141.7 %reduce-scatter.87.cloned.1.call-start = ((), (), s32[]{:S(2)}) async-start(), calls=%async_computation.108 | async-start | bytes 4096000 | tf_op jit(solution)/shard_map/reduce_scatter | solution.py:58
  3137.1 97.6 %all-gather.99.cloned.1.call-start = ((), (), s32[]{:S(2)}) async-start(), calls=%async_computation.109 | async-start | bytes 2048000 | tf_op jit(solution)/shard_map/all_gather | solution.py:54
  3203.1 95.1 %reduce-scatter.89.cloned.1.call-start = ((), (), s32[]{:S(2)}) async-start(), calls=%async_computation.110 | async-start | bytes 4096000 | tf_op jit(solution)/shard_map/reduce_scatter | solution.py:58
  3253.0 92.8 %all-gather.101.cloned.1.call-start = ((), (), s32[]{:S(2)}) async-start(), calls=%async_computation.111 | async-start | bytes 2048000 | tf_op jit(solution)/shard_map/all_gather | solution.py:54
  3353.4 142.2 %reduce-scatter.91.cloned.1.call-start = ((), (), s32[]{:S(2)}) async-start(), calls=%async_computation.112 | async-start | bytes 4096000 | tf_op jit(solution)/shard_map/reduce_scatter | solution.py:263
  3394.9 105.9 %reduce-scatter.93.cloned.1.call-start = ((), (), s32[]{:S(2)}) async-start(), calls=%async_computation.113 | async-start | bytes 4096000 | tf_op jit(solution)/shard_map/reduce_scatter | solution.py:264
  3401.5 252.9 %reduce-scatter.97.cloned.1.call-start = ((), (), s32[]{:S(2)}) async-start(), calls=%async_computation.115 | async-start | bytes 4096000 | tf_op jit(solution)/shard_map/reduce_scatter | solution.py:58
  3410.2 258.5 %reduce-scatter.109.cloned.1.call-start = ((), (), s32[]{:S(2)}) async-start(), calls=%async_computation.127 | async-start | bytes 4096000
  3452.9 218.4 %reduce-scatter.95.cloned.1.call-start = ((), (), s32[]{:S(2)}) async-start(), calls=%async_computation.114 | async-start | bytes 4096000 | tf_op jit(solution)/shard_map/reduce_scatter | solution.py:58
  3505.8 209.2 %reduce-scatter.99.cloned.1.call-start = ((), (), s32[]{:S(2)}) async-start(), calls=%async_computation.122 | async-start | bytes 4096000 | tf_op jit(solution)/shard_map/reduce_scatter | solution.py:83
  3523.2 375.9 %reduce-scatter.105.cloned.1.call-start = ((), (), s32[]{:S(2)}) async-start(), calls=%async_computation.125 | async-start | bytes 13312000 | tf_op jit(solution)/shard_map/reduce_scatter | solution.py:86
  3575.2 508.8 %reduce-scatter.107.cloned.1.call-start = ((), (), s32[]{:S(2)}) async-start(), calls=%async_computation.126 | async-start | bytes 13312000 | tf_op jit(solution)/shard_map/reduce_scatter | solution.py:87
  3630.4 519.8 %reduce-scatter.101.cloned.1.call-start = ((), (), s32[]{:S(2)}) async-start(), calls=%async_computation.123 | async-start | bytes 4096000 | tf_op jit(solution)/shard_map/reduce_scatter | solution.py:84
  3642.4 573.0 %reduce-scatter.103.cloned.1.call-start = ((), (), s32[]{:S(2)}) async-start(), calls=%async_computation.124 | async-start | bytes 4096000 | tf_op jit(solution)/shard_map/reduce_scatter | solution.py:85
  (215 other events, 2664.9 us)
Sparse Core Ops, SparseCore 0:
  9.6 40.8 all-gather.106
  84.9 38.1 all-gather.102
  124.5 37.0 all-gather.104
  196.9 31.5 all-gather.44
  230.6 65.6 all-gather.108
  307.6 43.6 reduce-scatter.38
  352.9 99.3 all-gather.110
  486.1 99.3 all-gather.112
  594.1 43.4 reduce-scatter.40
  655.0 31.4 all-gather.50
  689.9 35.8 all-gather.54
  728.0 31.5 all-gather.52
  778.7 44.2 reduce-scatter.42
  837.6 31.4 all-gather.56
  886.4 45.0 reduce-scatter.44
  951.7 31.4 all-gather.58
  986.5 35.8 all-gather.62
  1024.8 31.5 all-gather.60
  1075.5 44.1 reduce-scatter.46
  1134.4 31.4 all-gather.64
  1183.2 45.0 reduce-scatter.48
  1247.8 31.4 all-gather.66
  1282.6 35.8 all-gather.70
  1320.8 31.5 all-gather.68
  1371.5 44.1 reduce-scatter.50
  1430.4 31.4 all-gather.72
  1479.2 45.0 reduce-scatter.52
  1543.9 31.4 all-gather.74
  1578.6 35.8 all-gather.78
  1616.8 31.5 all-gather.76
  1667.6 44.2 reduce-scatter.54
  1726.5 31.4 all-gather.82
  1760.2 31.5 all-gather.80
  1810.2 45.0 reduce-scatter.56
  1870.9 31.4 all-gather.84
  1951.6 49.0 reduce-scatter.58
  2003.7 45.0 reduce-scatter.60
  2054.4 45.0 reduce-scatter.62
  2170.4 45.0 reduce-scatter.64
  2231.4 31.4 all-gather.88
  2312.0 49.0 reduce-scatter.66
  2364.0 45.4 reduce-scatter.68
  2415.1 45.0 reduce-scatter.70
  2481.1 31.4 all-gather.90
  2531.1 45.0 reduce-scatter.72
  2592.6 31.4 all-gather.92
  2673.2 49.0 reduce-scatter.74
  2725.3 45.4 reduce-scatter.76
  2776.4 45.0 reduce-scatter.78
  2892.3 45.0 reduce-scatter.80
  3034.2 49.1 reduce-scatter.82
  3086.2 45.3 reduce-scatter.84
  3137.2 45.0 reduce-scatter.86
  3253.1 45.0 reduce-scatter.88
  3395.0 45.0 reduce-scatter.90
  3443.0 45.1 reduce-scatter.92
  3491.2 44.9 reduce-scatter.96
  3538.4 62.2 reduce-scatter.108
  3603.6 45.1 reduce-scatter.94
  3651.7 63.2 reduce-scatter.98
  3718.0 181.0 reduce-scatter.104
  3901.9 182.0 reduce-scatter.106
  4086.9 63.3 reduce-scatter.100
  4153.0 62.3 reduce-scatter.102
  (8 shorter events, 247.8 us)
where the time goes:
time: 4240 us; the launch traced here: 4220 us
  waiting for transfers between devices  2650 us (62%)
  matrix products  846 us (20%)
  blocking collectives  369 us (9%)
  local copies, waits for them, and re-layouts  147 us (3%)
  other arithmetic  145 us (3%)
  starting transfers between devices  47 us (1%)
    reduce_scatter x20, waiting for transfers between devices, reduce_width(): lax.psum_scatter(partial_value, 'col', scatter_dimension=1, tiled=True)  788 us
    all_gather x20, waiting for transfers between devices, gather_width(): return lax.all_gather(columns, 'col', axis=1, tiled=True)  603 us
    reduce_scatter x1, waiting for transfers between devices, reduce_matrices(): lax.psum_scatter(row_terms[4], 'row', scatter_dimension=0, tiled=True)  185 us
    reduce_scatter x1, waiting for transfers between devices, reduce_matrices(): lax.psum_scatter(row_terms[3], 'row', scatter_dimension=0, tiled=True)  184 us
    psum x20, blocking collectives, row_pair(): return lax.psum((first_sum, second_sum), 'col')  181 us
    reduce_scatter x5, waiting for transfers between devices, layer_backward(): lax.psum_scatter(value_part, 'col', scatter_dimension=1, tiled=True)  159 us
    dot_general x30, matrix products, right_inner(): lax.dot_general(left, right, (((1,), (1,)), ((), ())), preferred_element_...  156 us
    dot_general x30, matrix products, matmul(): return jnp.dot(left, right, preferred_element_type=jnp.float32)  151 us
  transfers between devices with their start and end apart: 87, of which 77 were waited for; matrix products, arithmetic and copies ran while one was open for 14% of the time, Pallas kernels for 0%

commit v1 on v0

v1 whole, which is shorter than its diff:
```python
import functools
import math

import jax
import jax.numpy as jnp
from jax import lax
from jax.experimental import pallas as pl
from jax.experimental.pallas import tpu as pltpu
from jax.sharding import PartitionSpec as P

H = 25
HD = 64
L = 512
BF = jnp.bfloat16
F32 = jnp.float32

epsilon = 1e-05
tanh_scale = math.sqrt(2.0 / math.pi)
cubic_weight = 0.044715
score_scale = HD ** (-0.5)


def xor_step(value, axis, step):
    count = lax.axis_size(axis)
    return lax.ppermute(value, axis, [(i, i ^ step) for i in range(count)])


def gather_tokens(rows):
    count = lax.axis_size("col")
    return jnp.concatenate([rows] + [xor_step(rows, "col", j) for j in range(1, count)])


def scatter_terms(partial_rows):
    count = lax.axis_size("col")
    here = partial_rows.shape[0] // count
    terms = [partial_rows[:here]]
    for j in range(1, count):
        terms.append(xor_step(partial_rows[j * here : (j + 1) * here], "col", j))
    return terms


def total(terms):
    result = terms[0].astype(F32)
    for term in terms[1:]:
        result = result + term.astype(F32)
    return result


def swap_section(value):
    return xor_step(value, "section", 1)


def xor_order(stack, index):
    count = stack.shape[0]
    return jnp.stack(
        [lax.dynamic_index_in_dim(stack, index ^ t, 0, keepdims=False) for t in range(count)]
    )


def head_share():
    count = lax.axis_size("col")
    return H // count, (H // count + 1) * HD


def head_shift(col_index):
    count = lax.axis_size("col")
    return jnp.where(col_index == 0, 0, HD - (HD // count) * col_index)


def align_heads(columns, col_index):
    count = lax.axis_size("col")
    per, wide = head_share()
    lead = columns.shape[:-1]
    after = lax.ppermute(columns[..., :HD], "col", [(i + 1, i) for i in range(count - 1)])
    own = columns.shape[-1]
    pad = max(0, wide + HD - own - HD)
    extended = jnp.concatenate([columns, after, jnp.zeros(lead + (pad,), columns.dtype)], axis=-1)
    moved = lax.dynamic_slice_in_dim(
        extended, head_shift(col_index), wide, axis=extended.ndim - 1
    )
    limit = jnp.where(col_index == 0, wide, per * HD)
    return jnp.where(jnp.arange(wide) < limit, moved, jnp.zeros((), moved.dtype))


def unalign_heads(columns, width, col_index):
    count = lax.axis_size("col")
    per, wide = head_share()
    shift = head_shift(col_index)
    after_shift = HD - (HD // count) * (col_index + 1)
    begin = width - shift
    padded = jnp.concatenate(
        [columns, jnp.zeros(columns.shape[:-1] + (HD,), columns.dtype)], axis=-1
    )
    tail = lax.dynamic_slice_in_dim(padded, begin, HD, axis=columns.ndim - 1)
    before = lax.ppermute(tail, "col", [(i, i + 1) for i in range(count - 1)])
    joined = jnp.concatenate([before, columns], axis=-1)
    rest = lax.dynamic_slice_in_dim(
        jnp.concatenate(
            [joined, jnp.zeros(columns.shape[:-1] + (HD,), columns.dtype)], axis=-1
        ),
        HD - shift,
        width,
        axis=columns.ndim - 1,
    )
    front = lax.dynamic_slice_in_dim(
        jnp.concatenate(
            [before, jnp.zeros(columns.shape[:-1] + (width - HD,), columns.dtype)], axis=-1
        ),
        0,
        width,
        axis=columns.ndim - 1,
    )
    return jnp.where(jnp.arange(width) < shift, front, rest)


def contract(left, right, left_dim, right_dim):
    return lax.dot_general(
        left, right, (((left_dim,), (right_dim,)), ((), ())), preferred_element_type=F32
    )


def attention_kernel(heads, chunk, qkv_ref, mask_ref, out_ref, lse_ref):
    rows = qkv_ref.shape[0]
    wide = heads * HD
    for head in range(heads):
        low = head * HD
        key = qkv_ref[:, wide + low : wide + low + HD]
        value = qkv_ref[:, 2 * wide + low : 2 * wide + low + HD]
        for start in range(0, rows, chunk):
            part = pl.ds(start, chunk)
            query = qkv_ref[part, low : low + HD] * jnp.asarray(score_scale, BF)
            scores = contract(key, query, 1, 1) + mask_ref[:, part]
            peak = jnp.max(scores, axis=0, keepdims=True)
            weights = jnp.exp(scores - peak)
            mass = jnp.sum(weights, axis=0, keepdims=True)
            lse_ref[head : head + 1, part] = peak + jnp.log(mass)
            mixed = contract(value, weights.astype(BF), 0, 0) / mass
            out_ref[part, low : low + HD] = mixed.T.astype(BF)


def attention_forward(qkv, mask):
    rows, three = qkv.shape
    wide = three // 3
    heads = wide // HD
    return pl.pallas_call(
        functools.partial(attention_kernel, heads, 256),
        out_shape=(
            jax.ShapeDtypeStruct((rows, wide), BF),
            jax.ShapeDtypeStruct((heads, rows), F32),
        ),
        compiler_params=pltpu.CompilerParams(vmem_limit_bytes=40 * 1024 * 1024),
        cost_estimate=pl.CostEstimate(
            flops=4 * rows * rows * wide, bytes_accessed=8 * rows * wide, transcendentals=rows * rows * heads
        ),
    )(qkv, mask)


def attention_grad_kernel(heads, chunk, qkv_ref, up_ref, lse_ref, mask_ref, grad_ref, sum_ref):
    rows = qkv_ref.shape[0]
    wide = heads * HD
    for head in range(heads):
        low = head * HD
        key = qkv_ref[:, wide + low : wide + low + HD]
        value = qkv_ref[:, 2 * wide + low : 2 * wide + low + HD]
        key_grad = jnp.zeros((rows, HD), F32)
        value_grad = jnp.zeros((rows, HD), F32)
        query_sum = jnp.zeros((1, HD), F32)
        for start in range(0, rows, chunk):
            part = pl.ds(start, chunk)
            query = qkv_ref[part, low : low + HD] * jnp.asarray(score_scale, BF)
            up = up_ref[part, low : low + HD]
            scores = contract(key, query, 1, 1) + mask_ref[:, part]
            weights = jnp.exp(scores - lse_ref[head : head + 1, part])
            value_grad = value_grad + contract(weights.astype(BF), up, 1, 0)
            slope = contract(value, up, 1, 1)
            delta = jnp.sum(weights * slope, axis=0, keepdims=True)
            scores_grad = (weights * (slope - delta)).astype(BF)
            key_grad = key_grad + contract(scores_grad, query, 1, 0)
            query_grad = (contract(key, scores_grad, 0, 0) * score_scale).T.astype(BF)
            grad_ref[part, low : low + HD] = query_grad
            query_sum = query_sum + jnp.sum(query_grad.astype(F32), axis=0, keepdims=True)
        grad_ref[:, wide + low : wide + low + HD] = key_grad.astype(BF)
        grad_ref[:, 2 * wide + low : 2 * wide + low + HD] = value_grad.astype(BF)
        sum_ref[0:1, low : low + HD] = query_sum
        sum_ref[1:2, low : low + HD] = jnp.sum(value_grad, axis=0, keepdims=True)


def attention_backward(qkv, up, lse, mask):
    rows, three = qkv.shape
    wide = three // 3
    heads = wide // HD
    return pl.pallas_call(
        functools.partial(attention_grad_kernel, heads, 256),
        out_shape=(
            jax.ShapeDtypeStruct((rows, three), BF),
            jax.ShapeDtypeStruct((2, wide), F32),
        ),
        compiler_params=pltpu.CompilerParams(vmem_limit_bytes=40 * 1024 * 1024),
        cost_estimate=pl.CostEstimate(
            flops=10 * rows * rows * wide, bytes_accessed=16 * rows * wide, transcendentals=rows * rows * heads
        ),
    )(qkv, up, lse, mask)


def row_stats(stream):
    mean = jnp.mean(stream, axis=1, keepdims=True)
    scale = lax.rsqrt(jnp.mean(stream * stream, axis=1, keepdims=True) - mean * mean + epsilon)
    return mean, scale


def norm(stream, gain, offset):
    mean, scale = row_stats(stream)
    return (((stream - mean) * scale) * gain + offset).astype(BF)


def norm_backward(incoming, stream, gain):
    mean, scale = row_stats(stream)
    normed = (stream - mean) * scale
    scaled = incoming * gain
    outgoing = scale * (
        scaled
        - jnp.mean(scaled, axis=1, keepdims=True)
        - normed * jnp.mean(scaled * normed, axis=1, keepdims=True)
    )
    return outgoing, jnp.sum(incoming * normed, axis=0), jnp.sum(incoming, axis=0)


def matmul(left, right):
    return contract(left, right, 1, 0)


def gelu_both(inputs):
    inner = tanh_scale * (inputs + cubic_weight * inputs * inputs * inputs)
    tangent = jnp.tanh(inner)
    value = 0.5 * inputs * (1.0 + tangent)
    slope = 0.5 * (1.0 + tangent) + 0.5 * inputs * (1.0 - tangent * tangent) * tanh_scale * (
        1.0 + 3.0 * cubic_weight * inputs * inputs
    )
    return value.astype(BF), slope.astype(BF)


def on_device(
    block_input,
    out_cotangent,
    group_order,
    first_gain,
    first_bias,
    query_weight,
    key_weight,
    value_weight,
    query_bias,
    value_bias,
    out_weight,
    out_bias,
    second_gain,
    second_bias,
    up_weight,
    up_bias,
    down_weight,
    down_bias,
):
    section = lax.axis_index("section")
    col = lax.axis_index("col")
    cols = lax.axis_size("col")
    batches, width, rows = block_input.shape
    own = rows // cols
    mine = batches // 2
    per, wide = head_share()
    features = width * cols

    def halves(pack):
        half = pack.shape[0] // 2
        keep = lax.dynamic_slice_in_dim(pack, section * half, half, 0)
        send = lax.dynamic_slice_in_dim(pack, (1 - section) * half, half, 0)
        got = swap_section(send)
        return jnp.where(section == 0, keep, got), jnp.where(section == 0, got, keep)

    def gather_rows(half):
        return lax.all_gather(half, ("row", "section"), axis=0, tiled=True)

    heads_pack = align_heads(
        jnp.stack([query_weight[0], key_weight[0], value_weight[0], out_weight[0].T]), col
    )
    heads_pack = jnp.concatenate([heads_pack[i] for i in range(4)], axis=1)
    heads_halves = halves(heads_pack)
    wide_halves = halves(jnp.concatenate([up_weight[0], down_weight[0]], axis=1))
    hidden_width = up_weight.shape[2]

    small_wide = jnp.stack(
        [first_gain[0], first_bias[0], out_bias[0], second_gain[0], second_bias[0], down_bias[0]]
    )
    small_wide = xor_order(
        jnp.stack([small_wide] + [xor_step(small_wide, "col", j) for j in range(1, cols)]), col
    )
    small_wide = jnp.swapaxes(small_wide, 0, 1).reshape(6, features)
    small_heads = align_heads(jnp.stack([query_bias[0], value_bias[0]]), col).reshape(-1)
    small_own = jnp.concatenate([small_wide.reshape(-1), small_heads, up_bias[0]])
    small_other = swap_section(small_own)
    small_layers = (
        jnp.where(section == 0, small_own, small_other),
        jnp.where(section == 0, small_other, small_own),
    )

    def smalls_of(layer):
        flat = small_layers[layer]
        vectors = flat[: 6 * features].reshape(6, features)
        query_shift = flat[6 * features : 6 * features + wide]
        value_shift = flat[6 * features + wide : 6 * features + 2 * wide]
        qkv_shift = jnp.concatenate([query_shift, jnp.zeros((wide,), F32), value_shift])
        return vectors, qkv_shift, flat[6 * features + 2 * wide :]

    smalls = [smalls_of(0), smalls_of(1)]

    def gather_features(values):
        local = lax.dynamic_slice_in_dim(values, section * mine, mine, 0)
        stack = xor_order(
            jnp.stack([local] + [xor_step(local, "col", j) for j in range(1, cols)]), col
        )
        whole = []
        for batch in range(mine):
            plane = stack[:, batch].reshape(features, rows)
            whole.append(xor_order(plane.T.reshape(cols, own, features), col).reshape(rows, features))
        return whole

    inputs = gather_features(block_input)
    cotangents = gather_features(out_cotangent)

    blocks = group_order.shape[0]
    group_rows = L // blocks
    places = jnp.arange(rows, dtype=jnp.int32)
    places = ((places // own) ^ col) * own + places % own
    within = places % L
    match = (within // group_rows)[:, None] == jnp.arange(blocks, dtype=jnp.int32)[None, :]
    position = (
        jnp.sum(jnp.where(match, group_order[None, :], 0), axis=1) * group_rows
        + within % group_rows
    )
    sequence = places // L
    allowed = (sequence[:, None] == sequence[None, :]) & (position[:, None] <= position[None, :])
    mask = jnp.where(allowed, 0.0, -jnp.inf).astype(F32)

    weights = []
    saved = [[None] * mine, [None] * mine]
    streams = [item[:own].astype(F32) for item in inputs]
    finals = []
    for layer in range(2):
        vectors, qkv_shift, up_shift = smalls[layer]
        gain_one, bias_one, out_shift, gain_two, bias_two, down_shift = [vectors[i] for i in range(6)]
        heads_full = gather_rows(heads_halves[layer])
        wide_full = gather_rows(wide_halves[layer])
        qkv_full = heads_full[:, : 3 * wide]
        out_full = heads_full[:, 3 * wide :]
        up_full = wide_full[:, :hidden_width]
        down_full = wide_full[:, hidden_width:]
        weights.append((qkv_full, out_full, up_full, down_full))
        for batch in range(mine):
            stream = streams[batch]
            if layer == 0:
                inputs_one = norm(inputs[batch].astype(F32), gain_one, bias_one)
            else:
                inputs_one = gather_tokens(norm(stream, gain_one, bias_one))
            qkv = (matmul(inputs_one, qkv_full) + qkv_shift).astype(BF)
            attended, lse = attention_forward(qkv, mask)
            out_terms = scatter_terms(contract(attended, out_full, 1, 1).astype(BF))
            middle = stream + total(out_terms) + out_shift
            inputs_two = gather_tokens(norm(middle, gain_two, bias_two))
            hidden, slope = gelu_both(matmul(inputs_two, up_full) + up_shift)
            if layer == 0:
                down_terms = scatter_terms(contract(hidden, down_full, 1, 1).astype(BF))
                streams[batch] = middle + total(down_terms) + down_shift
            else:
                part = contract(down_full, hidden, 1, 1)
                base = (middle + down_shift).T
                part = jnp.concatenate([part[:, :own] + base, part[:, own:]], axis=1).astype(BF)
                part = part.reshape(features, cols, own)
                part = jnp.stack(
                    [
                        lax.dynamic_index_in_dim(part, col ^ t, 1, keepdims=False)
                        for t in range(cols)
                    ],
                    axis=1,
                ).reshape(cols, width, rows)
                terms = [
                    lax.dynamic_index_in_dim(part, col, 0, keepdims=False)
                ] + [
                    xor_step(
                        lax.dynamic_index_in_dim(part, col ^ j, 0, keepdims=False), "col", j
                    )
                    for j in range(1, cols)
                ]
                finals.append(total(terms))
            saved[layer][batch] = (
                stream, inputs_one, qkv, attended, lse, middle, inputs_two, hidden, slope,
            )

    def scatter_rows(grad):
        return lax.psum_scatter(grad, ("row", "section"), scatter_dimension=0, tiled=True)

    reduced = [None, None]
    wide_sums = [None, None]
    narrow_sums = [None, None]
    upstream_full = cotangents
    upstream_own = [item[:own].astype(F32) for item in cotangents]
    for layer in (1, 0):
        vectors = smalls[layer][0]
        gain_one, gain_two = vectors[0], vectors[3]
        qkv_full, out_full, up_full, down_full = weights[layer]
        halves_of = [[] for _ in range(4)]
        hidden_grads = []
        middle_grads = []
        qkv_grads = []
        sums = []
        head_sums = []
        up_sums = []
        next_own = []
        for batch in range(mine):
            stream, inputs_one, qkv, attended, lse, middle, inputs_two, hidden, slope = saved[
                layer
            ][batch]
            hidden_grad = matmul(upstream_full[batch], down_full) * slope.astype(F32)
            up_sums.append(jnp.sum(hidden_grad, axis=0))
            hidden_half = hidden_grad.astype(BF)
            hidden_grads.append(hidden_half)
            incoming = total(scatter_terms(contract(hidden_half, up_full, 1, 1).astype(BF)))
            middle_part, gain_two_grad, bias_two_grad = norm_backward(incoming, middle, gain_two)
            middle_grad = upstream_own[batch] + middle_part
            middle_full = gather_tokens(middle_grad.astype(BF))
            middle_grads.append(middle_full)
            attended_grad = matmul(middle_full, out_full).astype(BF)
            qkv_grad, head_sum = attention_backward(qkv, attended_grad, lse, mask)
            qkv_grads.append(qkv_grad)
            head_sums.append(head_sum.reshape(-1))
            incoming = total(scatter_terms(contract(qkv_grad, qkv_full, 1, 1).astype(BF)))
            stream_part, gain_one_grad, bias_one_grad = norm_backward(incoming, stream, gain_one)
            stream_grad = middle_grad + stream_part
            next_own.append(stream_grad)
            sums.append(
                jnp.stack(
                    [
                        gain_one_grad,
                        bias_one_grad,
                        jnp.sum(middle_grad, axis=0),
                        gain_two_grad,
                        bias_two_grad,
                        jnp.sum(upstream_own[batch], axis=0),
                    ]
                )
            )
        both = [[saved[layer][batch][i] for batch in range(mine)] for i in (1, 3, 6, 7)]
        join = lambda pieces: jnp.concatenate(pieces, axis=0)
        down_grad = contract(join(upstream_full), join(both[3]), 0, 0).astype(BF)
        up_grad = contract(join(both[2]), join(hidden_grads), 0, 0).astype(BF)
        out_grad = contract(join(middle_grads), join(both[1]), 0, 0).astype(BF)
        qkv_weight_grad = contract(join(both[0]), join(qkv_grads), 0, 0).astype(BF)
        reduced[layer] = (
            scatter_rows(down_grad),
            scatter_rows(up_grad),
            scatter_rows(jnp.concatenate([qkv_weight_grad, out_grad], axis=1)),
        )
        wide_sums[layer] = sum(sums[1:], sums[0])
        narrow_sums[layer] = jnp.concatenate(
            [sum(head_sums[1:], head_sums[0]), sum(up_sums[1:], up_sums[0])]
        )
        upstream_own = next_own
        if layer == 1:
            upstream_full = [gather_tokens(item.astype(BF)) for item in next_own]

    wide_both = jnp.stack(wide_sums).reshape(2, 6, cols, width)
    wide_here = lax.dynamic_index_in_dim(wide_both, col, 2, keepdims=False)
    for j in range(1, cols):
        wide_here = wide_here + xor_step(
            lax.dynamic_index_in_dim(wide_both, col ^ j, 2, keepdims=False), "col", j
        )
    small_sums = jnp.concatenate([wide_here.reshape(2, -1), jnp.stack(narrow_sums)], axis=1)
    small_own = lax.dynamic_index_in_dim(small_sums, section, 0, keepdims=False)
    small_own = small_own + swap_section(
        lax.dynamic_index_in_dim(small_sums, 1 - section, 0, keepdims=False)
    )
    step = 1
    while step < lax.axis_size("row"):
        small_own = small_own + xor_step(small_own, "row", step)
        step *= 2
    small_out = small_own[: 6 * width].reshape(6, width)
    head_out = unalign_heads(
        small_own[6 * width : 6 * width + 2 * wide].reshape(2, wide), width, col
    )
    up_bias_grad = small_own[6 * width + 2 * wide :]

    def settle(first, second):
        got = swap_section(jnp.where(section == 0, second, first))
        keep = jnp.where(section == 0, first, second)
        low = jnp.where(section == 0, keep, got)
        high = jnp.where(section == 0, got, keep)
        return jnp.concatenate([low, high], axis=0)

    down_out = settle(reduced[0][0], reduced[1][0]).astype(F32)
    up_out = settle(reduced[0][1], reduced[1][1]).astype(F32)
    heads_out = settle(reduced[0][2], reduced[1][2])
    heads_out = unalign_heads(
        jnp.stack([heads_out[:, i * wide : (i + 1) * wide] for i in range(4)]), width, col
    ).astype(F32)

    outputs = jnp.stack(finals)
    grads = jnp.stack(upstream_own).astype(BF)
    grads = lax.all_to_all(
        jnp.swapaxes(grads, 1, 2), "col", split_axis=1, concat_axis=2, tiled=True
    ).astype(F32)
    got = swap_section(jnp.where(section == 0, outputs, grads))
    keep = jnp.where(section == 0, grads, outputs)
    boundary = jnp.concatenate(
        [jnp.where(section == 0, keep, got), jnp.where(section == 0, got, keep)], axis=0
    )

    return (
        boundary[None],
        small_out[0][None],
        small_out[1][None],
        heads_out[0][None],
        heads_out[1][None],
        heads_out[2][None],
        head_out[0][None],
        head_out[1][None],
        heads_out[3].T[None],
        small_out[2][None],
        small_out[3][None],
        small_out[4][None],
        up_out[None],
        up_bias_grad[None],
        down_out[None],
        small_out[5][None],
    )


def solution(mesh):
    vector = P("section", "col")
    matrix = P("section", "row", "col")
    turned = P("section", "col", "row")
    plane = P(None, "col", "row")
    in_specs = (
        plane, plane, P(), vector, vector, matrix, matrix, matrix, vector, vector,
        turned, vector, vector, vector, matrix, vector, matrix, vector,
    )
    out_specs = (
        P("section", None, "col", "row"), vector, vector, matrix, matrix, matrix, vector, vector,
        turned, vector, vector, vector, matrix, vector, matrix, vector,
    )
    return jax.shard_map(
        on_device, mesh=mesh, in_specs=in_specs, out_specs=out_specs, check_vma=False
    )
```

time: 4240 us -> 1100 us (0.26)
  waiting for transfers between devices: 2650 us -> 290 us
  matrix products: 846 us -> 218 us
  blocking collectives: 369 us -> 0 us
  starting transfers between devices: 47 us -> 151 us
  local copies, waits for them, and re-layouts: 147 us -> 216 us
  Pallas kernels: 0 us -> 57.3 us
    reduce_scatter x35 -> x2, waiting for transfers between devices: 1450 us -> 0.04 us  [scatter_rows(): lax.psum_scatter(grad, ('row', 'section'), scatter_dimension=0, tiled=True)]
    all_gather x36 -> x4, waiting for transfers between devices: 1160 us -> 0.04 us  [gather_rows(): return lax.all_gather(half, ('row', 'section'), axis=0, tiled=True)]
    dot_general x125 -> x40, matrix products: 846 us -> 218 us  [contract(): lax.dot_general(left, right, (((left_dim,), (right_dim,)), ((), ())), pre...]
    ppermute x8 -> x110, waiting for transfers between devices: 20.6 us -> 290 us  [the longest x106 270 us: xor_step(): return lax.ppermute(value, axis, [(i, i ^ step) for i in range(count)])]
    psum x21 -> x0, blocking collectives: 205 us -> none  [the longest x20 181 us: row_pair(): return lax.psum((first_sum, second_sum), 'col')]
    all_to_all x13 -> x0, blocking collectives: 164 us -> none  [the longest x9 109 us: to_columns(): return lax.all_to_all(heads, 'col', split_axis=1, concat_axis=0, tiled=True)]
    ppermute x8 -> x110, starting transfers between devices: 12.4 us -> 146 us  [the longest x106 137 us: xor_step(): return lax.ppermute(value, axis, [(i, i ^ step) for i in range(count)])]
    pallas_call x0 -> x8, Pallas kernels: none -> 57.3 us  [the longest x4 32.4 us: attention_backward(): pl.pallas_call(functools.partial(attention_grad_kernel, heads, 256), out_...]
  transfers between devices with their start and end apart: 87 -> 121, of which waited for: 77 -> 50; matrix products, arithmetic and copies ran while one was open for 14% -> 49% of each run, Pallas kernels for 0% -> 5%
where the time goes in v1:
time: 1100 us; the launch traced here: 1090 us
  waiting for transfers between devices  290 us (26%)
  matrix products  218 us (20%)
  local copies, waits for them, and re-layouts  216 us (20%)
  starting transfers between devices  151 us (14%)
  other arithmetic  137 us (12%)
  Pallas kernels  57.3 us (5%)
  between operations  17.4 us (2%)
    ppermute x106, waiting for transfers between devices, xor_step(): return lax.ppermute(value, axis, [(i, i ^ step) for i in range(count)])  270 us
    dot_general x40, matrix products, contract(): lax.dot_general(left, right, (((left_dim,), (right_dim,)), ((), ())), pre...  218 us
    ppermute x106, starting transfers between devices, xor_step(): return lax.ppermute(value, axis, [(i, i ^ step) for i in range(count)])  137 us
    unnamed x458, local copies, waits for them, and re-layouts  91 us
    pallas_call x4, Pallas kernels, attention_backward(): pl.pallas_call(functools.partial(attention_grad_kernel, heads, 256), out_...  32.4 us
    pallas_call x4, Pallas kernels, attention_forward(): pl.pallas_call(functools.partial(attention_kernel, heads, 256), out_shape...  24.9 us
  transfers between devices with their start and end apart: 121, of which 50 were waited for; matrix products, arithmetic and copies ran while one was open for 49% of the time, Pallas kernels for 5%

profile of v1, /device:TPU:0, one launch (start us, length us, event | category | flops | bytes accessed | tf_op | source)
XLA Modules:
  0.0 1086.7 jit_solution(16359260168310077458)
XLA Ops:
  11.0 12.9 %collective-permute-done.11 = bf16[4,400,64]{2,1,0:T(8,128)(2,1)S(1)} collective-permute-done((bf16[4,400,64]{2,1,0:T(8,128)(2,1)S(1)}, bf16[4,400,64]{2,1,0:T(8,128)(2,1)S(1)}, u32[]{:S(2)}, u32[]{:S(2)}) %collective-permute-start.11) | collective-permute-done | bytes 204832 | tf_op jit(solution)/shard_map/ppermute | solution.py:74
  62.2 10.4 collective-permute-done.4
  77.2 15.0 %collective-permute-done.5 = bf16[2,400,512]{2,1,0:T(8,128)(2,1)} collective-permute-done((bf16[2,400,512]{2,1,0:T(8,128)(2,1)}, bf16[2,400,512]{2,1,0:T(8,128)(2,1)}, u32[]{:S(2)}, u32[]{:S(2)}) %collective-permute-start.5) | collective-permute-done | bytes 819232 | tf_op jit(solution)/shard_map/ppermute | solution.py:25
  125.6 4.7 copy.199
  132.3 5.2 fusion.41
  137.5 5.9 fusion.106.qkv_ref
  143.4 6.1 shard_map.297
  158.4 6.6 shard_map.301
  173.5 8.0 collective-permute-done.53
  181.5 7.3 collective-permute-done.55
  201.6 6.6 collective-permute-done.16
  210.7 42.8 %collective-permute-done.17 = bf16[128,1600]{0,1:T(8,128)(2,1)S(1)} collective-permute-done((bf16[128,1600]{0,1:T(8,128)(2,1)S(1)}, bf16[128,1600]{0,1:T(8,128)(2,1)S(1)}, u32[]{:S(2)}, u32[]{:S(2)}) %collective-permute-start.17) | collective-permute-done | bytes 409632 | tf_op jit(solution)/shard_map/ppermute | solution.py:25
  269.9 8.7 multiply_convert_fusion.2
  285.7 6.8 multiply_convert_fusion.3
  307.6 6.7 collective-permute-done.22
  331.5 16.7 %collective-permute-done.24 = bf16[128,1600]{0,1:T(8,128)(2,1)S(1)} collective-permute-done((bf16[128,1600]{0,1:T(8,128)(2,1)S(1)}, bf16[128,1600]{0,1:T(8,128)(2,1)S(1)}, u32[]{:S(2)}, u32[]{:S(2)}) %collective-permute-start.24) | collective-permute-done | bytes 409632 | tf_op jit(solution)/shard_map/ppermute | solution.py:25
  355.7 6.0 fusion.107.qkv_ref
  361.7 6.1 shard_map.298
  378.5 6.1 shard_map.302
  432.8 8.4 collective-permute-done.30
  449.8 8.3 multiply_convert_fusion.1
  458.2 7.8 fusion.393
  474.3 6.6 multiply_convert_fusion
  480.9 7.9 fusion.392
  497.9 11.0 %convolution_convert_fusion = bf16[1600,1600]{1,0:T(8,128)(2,1)} fusion(bf16[512,1600]{1,0:T(8,128)(2,1)S(1)} %bitcast.292, bf16[512,1600]{1,0:T(8,128)(2,1)S(1)} %bitcast.294, bf16[512,1600]{0,1:T(8,128)(2,1)} %get-tuple-element.437, bf16[512,1600]{0,1:T(8,128)(2,1)} %get-tuple-element.439), kind=kOutput, calls=%fused_computation | convolution fusion | flops 5258547200 | bytes 11673600 | tf_op jit(solution)/shard_map/dot_general | solution.py:117
  521.3 9.2 collective-permute-done.35
  543.2 8.0 shard_map.299
  551.2 6.0 convolution_convert_fusion.13
  569.2 7.9 shard_map.303
  577.2 5.8 convolution_convert_fusion.11
  586.9 6.0 collective-permute-done.77
  592.9 6.6 collective-permute-done.79
  608.0 9.6 collective-permute-done.41
  628.1 6.3 collective-permute-done.81
  635.5 7.8 convolution_convert_fusion.1
  648.9 10.3 convolution_convert_fusion.2
  662.5 11.1 %fusion.391 = (f32[1600]{0:T(1024)S(1)}, bf16[512,1600]{0,1:T(8,128)(2,1)S(1)}) fusion(f32[512,1600]{0,1:T(8,128)} %get-tuple-element.432, bf16[1600,3200]{1,0:T(8,128)(2,1)} %all-gather.7.cloned.1.call-done, bf16[128,1600]{0,1:T(8,128)(2,1)} %copy-done.102, bf16[128,1600]{0,1:T(8,128)(2,1)} %copy-done.103, bf16[128,1600]{0,1:T(8,128)(2,1)} %copy-done.104, ...), kind=kOutput, calls=%fused_computation.732 | convolution fusion | flops 2646014464 | bytes 11884800 | tf_op jit(solution)/shard_map/dot_general | solution.py:117
  673.6 10.4 fusion.390
  685.3 7.8 convolution_convert_fusion.3
  700.2 5.3 fusion.2
  705.7 5.3 fusion
  725.7 6.7 constant_dynamic-slice_fusion.10
  732.4 4.7 pad_maximum_fusion.11
  746.8 4.7 constant_dynamic-slice_fusion.14
  757.8 5.4 convolution_convert_fusion.4
  766.2 9.4 copy.222
  776.8 5.8 pad_maximum_fusion.9
  796.4 5.4 collective-permute-done.92
  801.8 8.9 collective-permute-done.94
  817.6 6.3 fusion.119
  828.9 5.7 fusion.116
  842.5 6.8 collective-permute-done.83
  849.3 8.8 collective-permute-done.85
  866.9 9.3 collective-permute-done.47
  886.9 8.2 shard_map.300
  901.4 8.4 shard_map.304
  915.6 5.3 convolution_convert_fusion.5
  925.4 9.6 copy.220
  939.3 5.1 convolution_convert_fusion.12
  950.3 5.1 convolution_convert_fusion.10
  981.4 7.7 copy.208
  1012.8 20.3 %collective-permute-start.103 = (f32[4896]{0:T(1024)S(1)}, f32[4896]{0:T(1024)S(1)}, u32[]{:S(2)}, u32[]{:S(2)}) collective-permute-start(f32[4896]{0:T(1024)S(1)} %add.937), channel_id=1, source_target_pairs={{0,4},{4,0},{8,12},{12,8},{1,5},{5,1},{9,13},{13,9},{2,6},{6,2},{1... | collective-permute-start | bytes 58760 | tf_op jit(solution)/shard_map/ppermute | solution.py:25
  1035.0 4.7 collective-permute-done.104
  1068.1 7.1 collective-permute-done.106
  (941 shorter events, 537.5 us)
Async XLA Ops:
  7.2 130.3 %all-gather.5.cloned.1.call-start = ((), (), s32[]{:S(2)}) async-start(), calls=%async_computation.7 | async-start | bytes 6451200 | tf_op jit(solution)/shard_map/all_gather | solution.py:279
  36.9 233.0 %all-gather.7.cloned.1.call-start = ((), (), s32[]{:S(2)}) async-start(), calls=%async_computation.8 | async-start | bytes 11520000 | tf_op jit(solution)/shard_map/all_gather | solution.py:279
  44.1 311.6 %all-gather.9.cloned.1.call-start = ((), (), s32[]{:S(2)}) async-start(), calls=%async_computation.9 | async-start | bytes 6451200 | tf_op jit(solution)/shard_map/all_gather | solution.py:279
  50.7 21.9 %collective-permute-start.4 = (bf16[2,400,512]{2,1,0:T(8,128)(2,1)}, bf16[2,400,512]{2,1,0:T(8,128)(2,1)}, u32[]{:S(2)}, u32[]{:S(2)}) collective-permute-start(bf16[2,400,512]{2,1,0:T(8,128)(2,1)} %constant_dynamic-slice_fusion.40), channel_id=1, source_target_pairs={{0,2},{1,3},{2,0},{3,1},{4,6},{5,7},{6,4},{7,5},{8,10},{9,11},{10,... | collective-permute-start | bytes 2457608 | tf_op jit(solution)/shard_map/ppermute | solution.py:25
  55.0 394.8 %all-gather.11.cloned.1.call-start = ((), (), s32[]{:S(2)}) async-start(), calls=%async_computation.10 | async-start | bytes 11520000 | tf_op jit(solution)/shard_map/all_gather | solution.py:279
  55.7 21.6 %collective-permute-start.3 = (bf16[2,400,512]{2,1,0:T(8,128)(2,1)}, bf16[2,400,512]{2,1,0:T(8,128)(2,1)}, u32[]{:S(2)}, u32[]{:S(2)}) collective-permute-start(bf16[2,400,512]{2,1,0:T(8,128)(2,1)} %constant_dynamic-slice_fusion.40), channel_id=1, source_target_pairs={{0,1},{1,0},{2,3},{3,2},{4,5},{5,4},{6,7},{7,6},{8,9},{9,8},{10,11... | collective-permute-start | bytes 2457608 | tf_op jit(solution)/shard_map/ppermute | solution.py:25
  57.0 35.2 %collective-permute-start.5 = (bf16[2,400,512]{2,1,0:T(8,128)(2,1)}, bf16[2,400,512]{2,1,0:T(8,128)(2,1)}, u32[]{:S(2)}, u32[]{:S(2)}) collective-permute-start(bf16[2,400,512]{2,1,0:T(8,128)(2,1)} %constant_dynamic-slice_fusion.40), channel_id=1, source_target_pairs={{0,3},{1,2},{2,1},{3,0},{4,7},{5,6},{6,5},{7,4},{8,11},{9,10},{10,... | collective-permute-start | bytes 2457608 | tf_op jit(solution)/shard_map/ppermute | solution.py:25
  151.9 18.9 %collective-permute-start.13 = (bf16[128,1600]{0,1:T(8,128)(2,1)S(1)}, bf16[128,1600]{0,1:T(8,128)(2,1)S(1)}, u32[]{:S(2)}, u32[]{:S(2)}) collective-permute-start(bf16[128,1600]{0,1:T(8,128)(2,1)S(1)} %get-tuple-element.327), channel_id=1, source_target_pairs={{0,1},{1,0},{2,3},{3,2},{4,5},{5,4},{6,7},{7,6},{8,9},{9,8},{10,11... | collective-permute-start | bytes 1228808 | tf_op jit(solution)/shard_map/ppermute | solution.py:25
  152.3 21.2 %collective-permute-start.15 = (bf16[128,1600]{0,1:T(8,128)(2,1)}, bf16[128,1600]{0,1:T(8,128)(2,1)S(1)}, u32[]{:S(2)}, u32[]{:S(2)}) collective-permute-start(bf16[128,1600]{0,1:T(8,128)(2,1)} %get-tuple-element.328), channel_id=1, source_target_pairs={{0,3},{1,2},{2,1},{3,0},{4,7},{5,6},{6,5},{7,4},{8,11},{9,10},{10,... | collective-permute-start | bytes 1228808 | tf_op jit(solution)/shard_map/ppermute | solution.py:25
  155.2 18.3 %collective-permute-start.14 = (bf16[128,1600]{0,1:T(8,128)(2,1)}, bf16[128,1600]{0,1:T(8,128)(2,1)S(1)}, u32[]{:S(2)}, u32[]{:S(2)}) collective-permute-start(bf16[128,1600]{0,1:T(8,128)(2,1)} %get-tuple-element.329), channel_id=1, source_target_pairs={{0,2},{1,3},{2,0},{3,1},{4,6},{5,7},{6,4},{7,5},{8,10},{9,11},{10,... | collective-permute-start | bytes 1228808 | tf_op jit(solution)/shard_map/ppermute | solution.py:25
  168.4 20.4 %collective-permute-start.55 = (bf16[128,1600]{0,1:T(8,128)(2,1)}, bf16[128,1600]{0,1:T(8,128)(2,1)}, u32[]{:S(2)}, u32[]{:S(2)}) collective-permute-start(bf16[128,1600]{0,1:T(8,128)(2,1)} %get-tuple-element.310), channel_id=1, source_target_pairs={{0,3},{1,2},{2,1},{3,0},{4,7},{5,6},{6,5},{7,4},{8,11},{9,10},{10,... | collective-permute-start | bytes 1228808 | tf_op jit(solution)/shard_map/ppermute | solution.py:25
  170.9 19.4 %collective-permute-start.54 = (bf16[128,1600]{0,1:T(8,128)(2,1)}, bf16[128,1600]{0,1:T(8,128)(2,1)}, u32[]{:S(2)}, u32[]{:S(2)}) collective-permute-start(bf16[128,1600]{0,1:T(8,128)(2,1)} %get-tuple-element.311), channel_id=1, source_target_pairs={{0,2},{1,3},{2,0},{3,1},{4,6},{5,7},{6,4},{7,5},{8,10},{9,11},{10,... | collective-permute-start | bytes 1228808 | tf_op jit(solution)/shard_map/ppermute | solution.py:25
  171.2 877.0 %reduce-scatter.29.cloned.1.call-start = ((), (), s32[]{:S(2)}) async-start(), calls=%async_computation.16 | async-start | bytes 5990400
  197.4 62.5 %collective-permute-start.1 = (bf16[2,400,512]{2,1,0:T(8,128)(2,1)}, bf16[2,400,512]{2,1,0:T(8,128)(2,1)}, u32[]{:S(2)}, u32[]{:S(2)}) collective-permute-start(bf16[2,400,512]{2,1,0:T(8,128)(2,1)} %constant_dynamic-slice_fusion.46), channel_id=1, source_target_pairs={{0,2},{1,3},{2,0},{3,1},{4,6},{5,7},{6,4},{7,5},{8,10},{9,11},{10,... | collective-permute-start | bytes 2457608 | tf_op jit(solution)/shard_map/ppermute | solution.py:25
  197.9 62.9 %collective-permute-start = (bf16[2,400,512]{2,1,0:T(8,128)(2,1)}, bf16[2,400,512]{2,1,0:T(8,128)(2,1)}, u32[]{:S(2)}, u32[]{:S(2)}) collective-permute-start(bf16[2,400,512]{2,1,0:T(8,128)(2,1)} %constant_dynamic-slice_fusion.46), channel_id=1, source_target_pairs={{0,1},{1,0},{2,3},{3,2},{4,5},{5,4},{6,7},{7,6},{8,9},{9,8},{10,11... | collective-permute-start | bytes 2457608 | tf_op jit(solution)/shard_map/ppermute | solution.py:25
  199.3 61.4 %collective-permute-start.2 = (bf16[2,400,512]{2,1,0:T(8,128)(2,1)}, bf16[2,400,512]{2,1,0:T(8,128)(2,1)}, u32[]{:S(2)}, u32[]{:S(2)}) collective-permute-start(bf16[2,400,512]{2,1,0:T(8,128)(2,1)} %constant_dynamic-slice_fusion.46), channel_id=1, source_target_pairs={{0,3},{1,2},{2,1},{3,0},{4,7},{5,6},{6,5},{7,4},{8,11},{9,10},{10,... | collective-permute-start | bytes 2457608 | tf_op jit(solution)/shard_map/ppermute | solution.py:25
  201.1 52.4 %collective-permute-start.17 = (bf16[128,1600]{0,1:T(8,128)(2,1)S(1)}, bf16[128,1600]{0,1:T(8,128)(2,1)S(1)}, u32[]{:S(2)}, u32[]{:S(2)}) collective-permute-start(bf16[128,1600]{0,1:T(8,128)(2,1)S(1)} %get-tuple-element.187), channel_id=1, source_target_pairs={{0,2},{1,3},{2,0},{3,1},{4,6},{5,7},{6,4},{7,5},{8,10},{9,11},{10,... | collective-permute-start | bytes 1228808 | tf_op jit(solution)/shard_map/ppermute | solution.py:25
  208.2 46.1 %collective-permute-start.18 = (bf16[128,1600]{0,1:T(8,128)(2,1)S(1)}, bf16[128,1600]{0,1:T(8,128)(2,1)S(1)}, u32[]{:S(2)}, u32[]{:S(2)}) collective-permute-start(bf16[128,1600]{0,1:T(8,128)(2,1)S(1)} %get-tuple-element.187), channel_id=1, source_target_pairs={{0,3},{1,2},{2,1},{3,0},{4,7},{5,6},{6,5},{7,4},{8,11},{9,10},{10,... | collective-permute-start | bytes 1228808 | tf_op jit(solution)/shard_map/ppermute | solution.py:25
  282.2 16.2 %collective-permute-start.59 = (bf16[128,1600]{0,1:T(8,128)(2,1)S(1)}, bf16[128,1600]{0,1:T(8,128)(2,1)S(1)}, u32[]{:S(2)}, u32[]{:S(2)}) collective-permute-start(bf16[128,1600]{0,1:T(8,128)(2,1)S(1)} %get-tuple-element.306), channel_id=1, source_target_pairs={{0,1},{1,0},{2,3},{3,2},{4,5},{5,4},{6,7},{7,6},{8,9},{9,8},{10,11... | collective-permute-start | bytes 1228808 | tf_op jit(solution)/shard_map/ppermute | solution.py:25
  283.3 19.9 %collective-permute-start.61 = (bf16[128,1600]{0,1:T(8,128)(2,1)S(1)}, bf16[128,1600]{0,1:T(8,128)(2,1)S(1)}, u32[]{:S(2)}, u32[]{:S(2)}) collective-permute-start(bf16[128,1600]{0,1:T(8,128)(2,1)S(1)} %get-tuple-element.307), channel_id=1, source_target_pairs={{0,3},{1,2},{2,1},{3,0},{4,7},{5,6},{6,5},{7,4},{8,11},{9,10},{10,... | collective-permute-start | bytes 1228808 | tf_op jit(solution)/shard_map/ppermute | solution.py:25
  284.1 20.5 %collective-permute-start.60 = (bf16[128,1600]{0,1:T(8,128)(2,1)S(1)}, bf16[128,1600]{0,1:T(8,128)(2,1)S(1)}, u32[]{:S(2)}, u32[]{:S(2)}) collective-permute-start(bf16[128,1600]{0,1:T(8,128)(2,1)S(1)} %get-tuple-element.308), channel_id=1, source_target_pairs={{0,2},{1,3},{2,0},{3,1},{4,6},{5,7},{6,4},{7,5},{8,10},{9,11},{10,... | collective-permute-start | bytes 1228808 | tf_op jit(solution)/shard_map/ppermute | solution.py:25
  297.5 16.8 %collective-permute-start.22 = (bf16[128,1600]{0,1:T(8,128)(2,1)S(1)}, bf16[128,1600]{0,1:T(8,128)(2,1)S(1)}, u32[]{:S(2)}, u32[]{:S(2)}) collective-permute-start(bf16[128,1600]{0,1:T(8,128)(2,1)S(1)} %get-tuple-element.325), channel_id=1, source_target_pairs={{0,3},{1,2},{2,1},{3,0},{4,7},{5,6},{6,5},{7,4},{8,11},{9,10},{10,... | collective-permute-start | bytes 1228808 | tf_op jit(solution)/shard_map/ppermute | solution.py:25
  326.7 22.3 %collective-permute-start.25 = (bf16[128,1600]{0,1:T(8,128)(2,1)S(1)}, bf16[128,1600]{0,1:T(8,128)(2,1)S(1)}, u32[]{:S(2)}, u32[]{:S(2)}) collective-permute-start(bf16[128,1600]{0,1:T(8,128)(2,1)S(1)} %get-tuple-element.201), channel_id=1, source_target_pairs={{0,3},{1,2},{2,1},{3,0},{4,7},{5,6},{6,5},{7,4},{8,11},{9,10},{10,... | collective-permute-start | bytes 1228808 | tf_op jit(solution)/shard_map/ppermute | solution.py:25
  329.4 18.8 %collective-permute-start.24 = (bf16[128,1600]{0,1:T(8,128)(2,1)S(1)}, bf16[128,1600]{0,1:T(8,128)(2,1)S(1)}, u32[]{:S(2)}, u32[]{:S(2)}) collective-permute-start(bf16[128,1600]{0,1:T(8,128)(2,1)S(1)} %get-tuple-element.201), channel_id=1, source_target_pairs={{0,2},{1,3},{2,0},{3,1},{4,6},{5,7},{6,4},{7,5},{8,10},{9,11},{10,... | collective-permute-start | bytes 1228808 | tf_op jit(solution)/shard_map/ppermute | solution.py:25
  352.0 21.2 %collective-permute-start.64 = (bf16[128,1600]{0,1:T(8,128)(2,1)}, bf16[128,1600]{0,1:T(8,128)(2,1)S(1)}, u32[]{:S(2)}, u32[]{:S(2)}) collective-permute-start(bf16[128,1600]{0,1:T(8,128)(2,1)} %get-tuple-element.199), channel_id=1, source_target_pairs={{0,3},{1,2},{2,1},{3,0},{4,7},{5,6},{6,5},{7,4},{8,11},{9,10},{10,... | collective-permute-start | bytes 1228808 | tf_op jit(solution)/shard_map/ppermute | solution.py:25
  355.2 18.8 %collective-permute-start.63 = (bf16[128,1600]{0,1:T(8,128)(2,1)}, bf16[128,1600]{0,1:T(8,128)(2,1)}, u32[]{:S(2)}, u32[]{:S(2)}) collective-permute-start(bf16[128,1600]{0,1:T(8,128)(2,1)} %get-tuple-element.199), channel_id=1, source_target_pairs={{0,2},{1,3},{2,0},{3,1},{4,6},{5,7},{6,4},{7,5},{8,10},{9,11},{10,... | collective-permute-start | bytes 1228808 | tf_op jit(solution)/shard_map/ppermute | solution.py:25
  355.2 18.8 %collective-permute-start.62 = (bf16[128,1600]{0,1:T(8,128)(2,1)}, bf16[128,1600]{0,1:T(8,128)(2,1)}, u32[]{:S(2)}, u32[]{:S(2)}) collective-permute-start(bf16[128,1600]{0,1:T(8,128)(2,1)} %get-tuple-element.199), channel_id=1, source_target_pairs={{0,1},{1,0},{2,3},{3,2},{4,5},{5,4},{6,7},{7,6},{8,9},{9,8},{10,11... | collective-permute-start | bytes 1228808 | tf_op jit(solution)/shard_map/ppermute | solution.py:25
  370.3 19.3 %collective-permute-start.26 = (bf16[128,1600]{0,1:T(8,128)(2,1)S(1)}, bf16[128,1600]{0,1:T(8,128)(2,1)S(1)}, u32[]{:S(2)}, u32[]{:S(2)}) collective-permute-start(bf16[128,1600]{0,1:T(8,128)(2,1)S(1)} %get-tuple-element.321), channel_id=1, source_target_pairs={{0,1},{1,0},{2,3},{3,2},{4,5},{5,4},{6,7},{7,6},{8,9},{9,8},{10,11... | collective-permute-start | bytes 1228808 | tf_op jit(solution)/shard_map/ppermute | solution.py:25
  371.7 40.6 %collective-permute-start.28 = (bf16[128,1600]{0,1:T(8,128)(2,1)}, bf16[128,1600]{0,1:T(8,128)(2,1)}, u32[]{:S(2)}, u32[]{:S(2)}) collective-permute-start(bf16[128,1600]{0,1:T(8,128)(2,1)} %get-tuple-element.322), channel_id=1, source_target_pairs={{0,3},{1,2},{2,1},{3,0},{4,7},{5,6},{6,5},{7,4},{8,11},{9,10},{10,... | collective-permute-start | bytes 1228808 | tf_op jit(solution)/shard_map/ppermute | solution.py:25
  373.2 39.1 %collective-permute-start.27 = (bf16[128,1600]{0,1:T(8,128)(2,1)}, bf16[128,1600]{0,1:T(8,128)(2,1)}, u32[]{:S(2)}, u32[]{:S(2)}) collective-permute-start(bf16[128,1600]{0,1:T(8,128)(2,1)} %get-tuple-element.323), channel_id=1, source_target_pairs={{0,2},{1,3},{2,0},{3,1},{4,6},{5,7},{6,4},{7,5},{8,10},{9,11},{10,... | collective-permute-start | bytes 1228808 | tf_op jit(solution)/shard_map/ppermute | solution.py:25
  386.8 25.5 %collective-permute-start.65 = (bf16[128,1600]{0,1:T(8,128)(2,1)}, bf16[128,1600]{0,1:T(8,128)(2,1)}, u32[]{:S(2)}, u32[]{:S(2)}) collective-permute-start(bf16[128,1600]{0,1:T(8,128)(2,1)} %get-tuple-element.303), channel_id=1, source_target_pairs={{0,1},{1,0},{2,3},{3,2},{4,5},{5,4},{6,7},{7,6},{8,9},{9,8},{10,11... | collective-permute-start | bytes 1228808 | tf_op jit(solution)/shard_map/ppermute | solution.py:25
  388.5 23.9 %collective-permute-start.67 = (bf16[128,1600]{0,1:T(8,128)(2,1)}, bf16[128,1600]{0,1:T(8,128)(2,1)}, u32[]{:S(2)}, u32[]{:S(2)}) collective-permute-start(bf16[128,1600]{0,1:T(8,128)(2,1)} %get-tuple-element.304), channel_id=1, source_target_pairs={{0,3},{1,2},{2,1},{3,0},{4,7},{5,6},{6,5},{7,4},{8,11},{9,10},{10,... | collective-permute-start | bytes 1228808 | tf_op jit(solution)/shard_map/ppermute | solution.py:25
  389.6 22.8 %collective-permute-start.66 = (bf16[128,1600]{0,1:T(8,128)(2,1)}, bf16[128,1600]{0,1:T(8,128)(2,1)}, u32[]{:S(2)}, u32[]{:S(2)}) collective-permute-start(bf16[128,1600]{0,1:T(8,128)(2,1)} %get-tuple-element.305), channel_id=1, source_target_pairs={{0,2},{1,3},{2,0},{3,1},{4,6},{5,7},{6,4},{7,5},{8,10},{9,11},{10,... | collective-permute-start | bytes 1228808 | tf_op jit(solution)/shard_map/ppermute | solution.py:25
  425.7 16.4 %collective-permute-start.31 = (bf16[128,1600]{0,1:T(8,128)(2,1)}, bf16[128,1600]{0,1:T(8,128)(2,1)S(1)}, u32[]{:S(2)}, u32[]{:S(2)}) collective-permute-start(bf16[128,1600]{0,1:T(8,128)(2,1)} %get-tuple-element.191), channel_id=1, source_target_pairs={{0,3},{1,2},{2,1},{3,0},{4,7},{5,6},{6,5},{7,4},{8,11},{9,10},{10,... | collective-permute-start | bytes 1228808 | tf_op jit(solution)/shard_map/ppermute | solution.py:25
  446.3 26.9 %collective-permute-start.70 = (bf16[128,1600]{0,1:T(8,128)(2,1)}, bf16[128,1600]{0,1:T(8,128)(2,1)}, u32[]{:S(2)}, u32[]{:S(2)}) collective-permute-start(bf16[128,1600]{0,1:T(8,128)(2,1)} %get-tuple-element.189), channel_id=1, source_target_pairs={{0,3},{1,2},{2,1},{3,0},{4,7},{5,6},{6,5},{7,4},{8,11},{9,10},{10,... | collective-permute-start | bytes 1228808 | tf_op jit(solution)/shard_map/ppermute | solution.py:25
  447.6 26.6 %collective-permute-start.69 = (bf16[128,1600]{0,1:T(8,128)(2,1)}, bf16[128,1600]{0,1:T(8,128)(2,1)}, u32[]{:S(2)}, u32[]{:S(2)}) collective-permute-start(bf16[128,1600]{0,1:T(8,128)(2,1)} %get-tuple-element.189), channel_id=1, source_target_pairs={{0,2},{1,3},{2,0},{3,1},{4,6},{5,7},{6,4},{7,5},{8,10},{9,11},{10,... | collective-permute-start | bytes 1228808 | tf_op jit(solution)/shard_map/ppermute | solution.py:25
  447.6 26.6 %collective-permute-start.68 = (bf16[128,1600]{0,1:T(8,128)(2,1)}, bf16[128,1600]{0,1:T(8,128)(2,1)}, u32[]{:S(2)}, u32[]{:S(2)}) collective-permute-start(bf16[128,1600]{0,1:T(8,128)(2,1)} %get-tuple-element.189), channel_id=1, source_target_pairs={{0,1},{1,0},{2,3},{3,2},{4,5},{5,4},{6,7},{7,6},{8,9},{9,8},{10,11... | collective-permute-start | bytes 1228808 | tf_op jit(solution)/shard_map/ppermute | solution.py:25
  470.8 26.1 %collective-permute-start.32 = (bf16[128,1600]{0,1:T(8,128)(2,1)S(1)}, bf16[128,1600]{0,1:T(8,128)(2,1)}, u32[]{:S(2)}, u32[]{:S(2)}) collective-permute-start(bf16[128,1600]{0,1:T(8,128)(2,1)S(1)} %get-tuple-element.318), channel_id=1, source_target_pairs={{0,1},{1,0},{2,3},{3,2},{4,5},{5,4},{6,7},{7,6},{8,9},{9,8},{10,11... | collective-permute-start | bytes 1228808 | tf_op jit(solution)/shard_map/ppermute | solution.py:25
  470.8 38.4 %collective-permute-start.34 = (bf16[128,1600]{0,1:T(8,128)(2,1)}, bf16[128,1600]{0,1:T(8,128)(2,1)}, u32[]{:S(2)}, u32[]{:S(2)}) collective-permute-start(bf16[128,1600]{0,1:T(8,128)(2,1)} %get-tuple-element.319), channel_id=1, source_target_pairs={{0,3},{1,2},{2,1},{3,0},{4,7},{5,6},{6,5},{7,4},{8,11},{9,10},{10,... | collective-permute-start | bytes 1228808 | tf_op jit(solution)/shard_map/ppermute | solution.py:25
  473.2 36.0 %collective-permute-start.33 = (bf16[128,1600]{0,1:T(8,128)(2,1)}, bf16[128,1600]{0,1:T(8,128)(2,1)}, u32[]{:S(2)}, u32[]{:S(2)}) collective-permute-start(bf16[128,1600]{0,1:T(8,128)(2,1)} %get-tuple-element.320), channel_id=1, source_target_pairs={{0,2},{1,3},{2,0},{3,1},{4,6},{5,7},{6,4},{7,5},{8,10},{9,11},{10,... | collective-permute-start | bytes 1228808 | tf_op jit(solution)/shard_map/ppermute | solution.py:25
  508.9 539.3 %reduce-scatter.27.cloned.1.call-start = ((), (), s32[]{:S(2)}) async-start(), calls=%async_computation.15 | async-start | bytes 5990400
  532.9 27.8 %collective-permute-start.76 = (bf16[128,1600]{0,1:T(8,128)(2,1)}, bf16[128,1600]{0,1:T(8,128)(2,1)}, u32[]{:S(2)}, u32[]{:S(2)}) collective-permute-start(bf16[128,1600]{0,1:T(8,128)(2,1)} %get-tuple-element.203), channel_id=1, source_target_pairs={{0,3},{1,2},{2,1},{3,0},{4,7},{5,6},{6,5},{7,4},{8,11},{9,10},{10,... | collective-permute-start | bytes 1228808 | tf_op jit(solution)/shard_map/ppermute | solution.py:25
  534.9 27.1 %collective-permute-start.75 = (bf16[128,1600]{0,1:T(8,128)(2,1)}, bf16[128,1600]{0,1:T(8,128)(2,1)}, u32[]{:S(2)}, u32[]{:S(2)}) collective-permute-start(bf16[128,1600]{0,1:T(8,128)(2,1)} %get-tuple-element.203), channel_id=1, source_target_pairs={{0,2},{1,3},{2,0},{3,1},{4,6},{5,7},{6,4},{7,5},{8,10},{9,11},{10,... | collective-permute-start | bytes 1228808 | tf_op jit(solution)/shard_map/ppermute | solution.py:25
  536.4 25.5 %collective-permute-start.74 = (bf16[128,1600]{0,1:T(8,128)(2,1)}, bf16[128,1600]{0,1:T(8,128)(2,1)}, u32[]{:S(2)}, u32[]{:S(2)}) collective-permute-start(bf16[128,1600]{0,1:T(8,128)(2,1)} %get-tuple-element.203), channel_id=1, source_target_pairs={{0,1},{1,0},{2,3},{3,2},{4,5},{5,4},{6,7},{7,6},{8,9},{9,8},{10,11... | collective-permute-start | bytes 1228808 | tf_op jit(solution)/shard_map/ppermute | solution.py:25
  558.5 27.0 %collective-permute-start.38 = (bf16[128,1600]{0,1:T(8,128)(2,1)}, bf16[128,1600]{0,1:T(8,128)(2,1)}, u32[]{:S(2)}, u32[]{:S(2)}) collective-permute-start(bf16[128,1600]{0,1:T(8,128)(2,1)} %get-tuple-element.315), channel_id=1, source_target_pairs={{0,1},{1,0},{2,3},{3,2},{4,5},{5,4},{6,7},{7,6},{8,9},{9,8},{10,11... | collective-permute-start | bytes 1228808 | tf_op jit(solution)/shard_map/ppermute | solution.py:25
  560.5 26.4 %collective-permute-start.40 = (bf16[128,1600]{0,1:T(8,128)(2,1)}, bf16[128,1600]{0,1:T(8,128)(2,1)}, u32[]{:S(2)}, u32[]{:S(2)}) collective-permute-start(bf16[128,1600]{0,1:T(8,128)(2,1)} %get-tuple-element.316), channel_id=1, source_target_pairs={{0,3},{1,2},{2,1},{3,0},{4,7},{5,6},{6,5},{7,4},{8,11},{9,10},{10,... | collective-permute-start | bytes 1228808 | tf_op jit(solution)/shard_map/ppermute | solution.py:25
  560.7 26.2 %collective-permute-start.39 = (bf16[128,1600]{0,1:T(8,128)(2,1)}, bf16[128,1600]{0,1:T(8,128)(2,1)}, u32[]{:S(2)}, u32[]{:S(2)}) collective-permute-start(bf16[128,1600]{0,1:T(8,128)(2,1)} %get-tuple-element.317), channel_id=1, source_target_pairs={{0,2},{1,3},{2,0},{3,1},{4,6},{5,7},{6,4},{7,5},{8,10},{9,11},{10,... | collective-permute-start | bytes 1228808 | tf_op jit(solution)/shard_map/ppermute | solution.py:25
  643.4 410.2 %reduce-scatter.25.cloned.1.call-start = ((), (), s32[]{:S(2)}) async-start(), calls=%async_computation.14 | async-start | bytes 5990400
  659.2 394.4 %reduce-scatter.23.cloned.1.call-start = ((), (), s32[]{:S(2)}) async-start(), calls=%async_computation.13 | async-start | bytes 5990400
  693.1 364.2 %reduce-scatter.21.cloned.1.call-start = ((), (), s32[]{:S(2)}) async-start(), calls=%async_computation.12 | async-start | bytes 6451200 | tf_op jit(solution)/shard_map/reduce_scatter | solution.py:397
  743.3 47.9 %collective-permute-start.95 = (bf16[400,512]{1,0:T(8,128)(2,1)}, bf16[400,512]{1,0:T(8,128)(2,1)}, u32[]{:S(2)}, u32[]{:S(2)}) collective-permute-start(bf16[400,512]{1,0:T(8,128)(2,1)} %get-tuple-element.281), channel_id=1, source_target_pairs={{0,1},{1,0},{2,3},{3,2},{4,5},{5,4},{6,7},{7,6},{8,9},{9,8},{10,11... | collective-permute-start | bytes 1228808 | tf_op jit(solution)/shard_map/ppermute | solution.py:25
  743.3 50.6 %collective-permute-start.97 = (bf16[400,512]{1,0:T(8,128)(2,1)}, bf16[400,512]{1,0:T(8,128)(2,1)}, u32[]{:S(2)}, u32[]{:S(2)}) collective-permute-start(bf16[400,512]{1,0:T(8,128)(2,1)} %get-tuple-element.282), channel_id=1, source_target_pairs={{0,3},{1,2},{2,1},{3,0},{4,7},{5,6},{6,5},{7,4},{8,11},{9,10},{10,... | collective-permute-start | bytes 1228808 | tf_op jit(solution)/shard_map/ppermute | solution.py:25
  745.3 48.6 %collective-permute-start.96 = (bf16[400,512]{1,0:T(8,128)(2,1)S(1)}, bf16[400,512]{1,0:T(8,128)(2,1)}, u32[]{:S(2)}, u32[]{:S(2)}) collective-permute-start(bf16[400,512]{1,0:T(8,128)(2,1)S(1)} %get-tuple-element.283), channel_id=1, source_target_pairs={{0,2},{1,3},{2,0},{3,1},{4,6},{5,7},{6,4},{7,5},{8,10},{9,11},{10,... | collective-permute-start | bytes 1228808 | tf_op jit(solution)/shard_map/ppermute | solution.py:25
  775.7 281.7 %reduce-scatter.19.cloned.1.call-start = ((), (), s32[]{:S(2)}) async-start(), calls=%async_computation.11 | async-start | bytes 6451200 | tf_op jit(solution)/shard_map/reduce_scatter | solution.py:397
  789.4 21.4 %collective-permute-start.94 = (bf16[400,512]{1,0:T(8,128)(2,1)}, bf16[400,512]{1,0:T(8,128)(2,1)}, u32[]{:S(2)}, u32[]{:S(2)}) collective-permute-start(bf16[400,512]{1,0:T(8,128)(2,1)} %get-tuple-element.275), channel_id=1, source_target_pairs={{0,3},{1,2},{2,1},{3,0},{4,7},{5,6},{6,5},{7,4},{8,11},{9,10},{10,... | collective-permute-start | bytes 1228808 | tf_op jit(solution)/shard_map/ppermute | solution.py:25
  791.2 23.4 %collective-permute-start.93 = (bf16[400,512]{1,0:T(8,128)(2,1)}, bf16[400,512]{1,0:T(8,128)(2,1)}, u32[]{:S(2)}, u32[]{:S(2)}) collective-permute-start(bf16[400,512]{1,0:T(8,128)(2,1)} %get-tuple-element.276), channel_id=1, source_target_pairs={{0,2},{1,3},{2,0},{3,1},{4,6},{5,7},{6,4},{7,5},{8,10},{9,11},{10,... | collective-permute-start | bytes 1228808 | tf_op jit(solution)/shard_map/ppermute | solution.py:25
  825.3 17.2 %collective-permute-start.46 = (bf16[128,1600]{0,1:T(8,128)(2,1)}, bf16[128,1600]{0,1:T(8,128)(2,1)}, u32[]{:S(2)}, u32[]{:S(2)}) collective-permute-start(bf16[128,1600]{0,1:T(8,128)(2,1)} %get-tuple-element.313), channel_id=1, source_target_pairs={{0,3},{1,2},{2,1},{3,0},{4,7},{5,6},{6,5},{7,4},{8,11},{9,10},{10,... | collective-permute-start | bytes 1228808 | tf_op jit(solution)/shard_map/ppermute | solution.py:25
  836.2 21.9 %collective-permute-start.85 = (bf16[128,1600]{0,1:T(8,128)(2,1)}, bf16[128,1600]{0,1:T(8,128)(2,1)}, u32[]{:S(2)}, u32[]{:S(2)}) collective-permute-start(bf16[128,1600]{0,1:T(8,128)(2,1)} %get-tuple-element.295), channel_id=1, source_target_pairs={{0,3},{1,2},{2,1},{3,0},{4,7},{5,6},{6,5},{7,4},{8,11},{9,10},{10,... | collective-permute-start | bytes 1228808 | tf_op jit(solution)/shard_map/ppermute | solution.py:25
  839.0 19.1 %collective-permute-start.84 = (bf16[128,1600]{0,1:T(8,128)(2,1)}, bf16[128,1600]{0,1:T(8,128)(2,1)}, u32[]{:S(2)}, u32[]{:S(2)}) collective-permute-start(bf16[128,1600]{0,1:T(8,128)(2,1)} %get-tuple-element.296), channel_id=1, source_target_pairs={{0,2},{1,3},{2,0},{3,1},{4,6},{5,7},{6,4},{7,5},{8,10},{9,11},{10,... | collective-permute-start | bytes 1228808 | tf_op jit(solution)/shard_map/ppermute | solution.py:25
  878.3 17.9 %collective-permute-start.88 = (bf16[128,1600]{0,1:T(8,128)(2,1)S(1)}, bf16[128,1600]{0,1:T(8,128)(2,1)S(1)}, u32[]{:S(2)}, u32[]{:S(2)}) collective-permute-start(bf16[128,1600]{0,1:T(8,128)(2,1)S(1)} %get-tuple-element.193), channel_id=1, source_target_pairs={{0,3},{1,2},{2,1},{3,0},{4,7},{5,6},{6,5},{7,4},{8,11},{9,10},{10,... | collective-permute-start | bytes 1228808 | tf_op jit(solution)/shard_map/ppermute | solution.py:25
  948.7 17.5 %collective-permute-start.51 = (bf16[128,1600]{0,1:T(8,128)(2,1)}, bf16[128,1600]{0,1:T(8,128)(2,1)S(1)}, u32[]{:S(2)}, u32[]{:S(2)}) collective-permute-start(bf16[128,1600]{0,1:T(8,128)(2,1)} %get-tuple-element.290), channel_id=1, source_target_pairs={{0,2},{1,3},{2,0},{3,1},{4,6},{5,7},{6,4},{7,5},{8,10},{9,11},{10,... | collective-permute-start | bytes 1228808 | tf_op jit(solution)/shard_map/ppermute | solution.py:25
  958.6 16.5 %collective-permute-start.90 = (bf16[128,1600]{0,1:T(8,128)(2,1)}, bf16[128,1600]{0,1:T(8,128)(2,1)}, u32[]{:S(2)}, u32[]{:S(2)}) collective-permute-start(bf16[128,1600]{0,1:T(8,128)(2,1)} %get-tuple-element.293), channel_id=1, source_target_pairs={{0,2},{1,3},{2,0},{3,1},{4,6},{5,7},{6,4},{7,5},{8,10},{9,11},{10,... | collective-permute-start | bytes 1228808 | tf_op jit(solution)/shard_map/ppermute | solution.py:25
  1009.3 35.1 %collective-permute-start.98 = (f32[2,400,512]{2,1,0:T(8,128)}, f32[2,400,512]{2,1,0:T(8,128)}, u32[]{:S(2)}, u32[]{:S(2)}) collective-permute-start(f32[2,400,512]{2,1,0:T(8,128)} %fusion.239), channel_id=1, source_target_pairs={{0,16},{16,0},{1,17},{17,1},{2,18},{18,2},{3,19},{19,3},{4,20},{20... | collective-permute-start | bytes 4915208 | tf_op jit(solution)/shard_map/ppermute | solution.py:25
  1012.8 22.1 %collective-permute-start.103 = (f32[4896]{0:T(1024)S(1)}, f32[4896]{0:T(1024)S(1)}, u32[]{:S(2)}, u32[]{:S(2)}) collective-permute-start(f32[4896]{0:T(1024)S(1)} %add.937), channel_id=1, source_target_pairs={{0,4},{4,0},{8,12},{12,8},{1,5},{5,1},{9,13},{13,9},{2,6},{6,2},{1... | collective-permute-start | bytes 58760 | tf_op jit(solution)/shard_map/ppermute | solution.py:25
  (251 other events, 3126.2 us)
Sparse Core Ops, SparseCore 0:
  37.0 61.5 all-gather.4
  100.2 96.0 all-gather.6
  198.6 58.5 all-gather.8
  258.6 96.0 all-gather.10
  509.0 70.6 reduce-scatter.28
  643.5 83.4 reduce-scatter.26
  729.4 60.0 reduce-scatter.24
  791.8 60.0 reduce-scatter.22
  854.2 63.7 reduce-scatter.20
  935.2 86.5 reduce-scatter.18

commit v2 on v1

v2 whole, which is shorter than its diff:
```python
import functools
import math

import jax
import jax.numpy as jnp
from jax import lax
from jax.experimental import pallas as pl
from jax.experimental.pallas import tpu as pltpu
from jax.sharding import PartitionSpec as P

H = 25
HD = 64
L = 512
BF = jnp.bfloat16
F32 = jnp.float32

epsilon = 1e-05
tanh_scale = math.sqrt(2.0 / math.pi)
cubic_weight = 0.044715
score_scale = HD ** (-0.5)


def xor_step(value, axis, step):
    count = lax.axis_size(axis)
    return lax.ppermute(value, axis, [(i, i ^ step) for i in range(count)])


class Link:
    def move(self, parts):
        return [xor_step(part, "col", j + 1) for j, part in enumerate(parts)]

    def spread(self, rows):
        return [rows] + self.move([rows] * (lax.axis_size("col") - 1))

    def exchange(self, parts):
        return [parts[0]] + self.move(list(parts[1:]))


def after(values, *tokens):
    return lax.optimization_barrier((values, tokens))[0]


def swap_section(value):
    return xor_step(value, "section", 1)


def xor_order(stack, index):
    count = stack.shape[0]
    return jnp.stack(
        [lax.dynamic_index_in_dim(stack, index ^ t, 0, keepdims=False) for t in range(count)]
    )


def head_share():
    count = lax.axis_size("col")
    return H // count, (H // count + 1) * HD


def head_shift(col_index):
    count = lax.axis_size("col")
    return jnp.where(col_index == 0, 0, HD - (HD // count) * col_index)


def align_heads(columns, col_index):
    count = lax.axis_size("col")
    per, wide = head_share()
    lead = columns.shape[:-1]
    after = lax.ppermute(columns[..., :HD], "col", [(i + 1, i) for i in range(count - 1)])
    own = columns.shape[-1]
    pad = max(0, wide + HD - own - HD)
    extended = jnp.concatenate([columns, after, jnp.zeros(lead + (pad,), columns.dtype)], axis=-1)
    moved = lax.dynamic_slice_in_dim(
        extended, head_shift(col_index), wide, axis=extended.ndim - 1
    )
    limit = jnp.where(col_index == 0, wide, per * HD)
    return jnp.where(jnp.arange(wide) < limit, moved, jnp.zeros((), moved.dtype))


def unalign_heads(columns, width, col_index):
    count = lax.axis_size("col")
    per, wide = head_share()
    shift = head_shift(col_index)
    begin = width - shift
    padded = jnp.concatenate(
        [columns, jnp.zeros(columns.shape[:-1] + (HD,), columns.dtype)], axis=-1
    )
    tail = lax.dynamic_slice_in_dim(padded, begin, HD, axis=columns.ndim - 1)
    before = lax.ppermute(tail, "col", [(i, i + 1) for i in range(count - 1)])
    joined = jnp.concatenate([before, columns], axis=-1)
    rest = lax.dynamic_slice_in_dim(
        jnp.concatenate(
            [joined, jnp.zeros(columns.shape[:-1] + (HD,), columns.dtype)], axis=-1
        ),
        HD - shift,
        width,
        axis=columns.ndim - 1,
    )
    front = lax.dynamic_slice_in_dim(
        jnp.concatenate(
            [before, jnp.zeros(columns.shape[:-1] + (width - HD,), columns.dtype)], axis=-1
        ),
        0,
        width,
        axis=columns.ndim - 1,
    )
    return jnp.where(jnp.arange(width) < shift, front, rest)


def contract(left, right, left_dim, right_dim):
    return lax.dot_general(
        left, right, (((left_dim,), (right_dim,)), ((), ())), preferred_element_type=F32
    )


def call(kernel, outs, args, scratch=(), flops=0, exps=0, anywhere=()):
    nbytes = sum(math.prod(x.shape) * x.dtype.itemsize for x in list(args) + list(outs))
    return pl.pallas_call(
        kernel,
        out_shape=tuple(outs),
        in_specs=[
            pl.BlockSpec(memory_space=pl.ANY if i in anywhere else pltpu.VMEM)
            for i in range(len(args))
        ],
        out_specs=tuple(pl.BlockSpec(memory_space=pltpu.VMEM) for _ in outs),
        scratch_shapes=list(scratch),
        compiler_params=pltpu.CompilerParams(vmem_limit_bytes=44 * 1024 * 1024),
        cost_estimate=pl.CostEstimate(flops=int(flops * WEIGHT), bytes_accessed=0, transcendentals=0),
    )(*args)


def shape(dims, kind):
    return jax.ShapeDtypeStruct(dims, kind)


class Matrix:
    def __init__(self, array, first, stride, block, count):
        self.array, self.first, self.stride = array, first, stride
        self.block, self.count = block, count

    @property
    def dims(self):
        return (self.block * self.count, self.array.shape[1])

    def copies(self, source, target, sems):
        return [
            pltpu.make_async_copy(
                source.at[pl.ds(self.first + self.stride * i, self.block), :],
                target.at[pl.ds(self.block * i, self.block), :],
                sems.at[i],
            )
            for i in range(self.count)
        ]

    def scratch(self):
        return [pltpu.VMEM(self.dims, BF), pltpu.SemaphoreType.DMA((self.count,))]


def fetch(matrices, sources, held):
    waits = []
    for matrix, source, (target, sems) in zip(matrices, sources, held):
        copies = matrix.copies(source, target, sems)
        for copy in copies:
            copy.start()
        waits.append(copies)
    return waits


def finish(copies):
    for copy in copies:
        copy.wait()


def stack_pieces(pieces, whole):
    begin = 0
    for piece in pieces:
        whole[begin : begin + piece.shape[0], :] = piece[...]
        begin += piece.shape[0]


def store_parts(parts, begin, value):
    here = parts[0].shape[0]
    for i in range(value.shape[0] // here):
        parts[begin // here + i][...] = value[i * here : (i + 1) * here].astype(BF)


CHUNK = 256
WEIGHT = 4


def heads_forward(pieces, first, second, bias, mask, heads, parts):
    rows = mask.shape[0]
    features = pieces[0].shape[1]
    wide = heads * HD
    count = len(pieces)

    def kernel(*refs):
        piece_refs, refs = refs[:count], refs[count:]
        first_hbm, second_hbm, bias_ref, mask_ref, qkv_ref, out_ref, lse_ref = refs[:7]
        part_refs, refs = refs[7 : 7 + parts], refs[7 + parts :]
        whole, first_ref, first_sem, second_ref, second_sem = refs
        waits = fetch(
            (first, second),
            (first_hbm, second_hbm),
            ((first_ref, first_sem), (second_ref, second_sem)),
        )
        stack_pieces(piece_refs, whole)
        finish(waits[0])
        for begin in range(0, rows, CHUNK):
            some = slice(begin, begin + CHUNK)
            value = contract(whole[some, :], first_ref[...], 1, 0) + bias_ref[:, : 2 * wide]
            qkv_ref[some, : 2 * wide] = value.astype(BF)
        finish(waits[1])
        for begin in range(0, rows, CHUNK):
            some = slice(begin, begin + CHUNK)
            value = contract(whole[some, :], second_ref[:, :wide], 1, 0) + bias_ref[:, 2 * wide :]
            qkv_ref[some, 2 * wide :] = value.astype(BF)
        for head in range(heads):
            low = head * HD
            key = qkv_ref[:, wide + low : wide + low + HD]
            value = qkv_ref[:, 2 * wide + low : 2 * wide + low + HD]
            for begin in range(0, rows, CHUNK):
                part = pl.ds(begin, CHUNK)
                query = qkv_ref[part, low : low + HD] * jnp.asarray(score_scale, BF)
                scores = contract(key, query, 1, 1) + mask_ref[:, part]
                peak = jnp.max(scores, axis=0, keepdims=True)
                weights = jnp.exp(scores - peak)
                mass = jnp.sum(weights, axis=0, keepdims=True)
                lse_ref[head : head + 1, part] = peak + jnp.log(mass)
                mixed = contract(value, weights.astype(BF), 0, 0) / mass
                out_ref[part, low : low + HD] = mixed.T.astype(BF)
        for begin in range(0, rows, CHUNK):
            some = slice(begin, begin + CHUNK)
            store_parts(part_refs, begin, contract(out_ref[some, :], second_ref[:, wide:], 1, 1))

    here = rows // parts
    result = call(
        kernel,
        [shape((rows, 3 * wide), BF), shape((rows, wide), BF), shape((heads, rows), F32)]
        + [shape((here, features), BF)] * parts,
        list(pieces) + [first.array, second.array, bias, mask],
        [pltpu.VMEM((rows, features), BF)] + first.scratch() + second.scratch(),
        flops=8 * rows * features * wide + 16 * rows * rows * wide,
        exps=rows * rows * heads,
        anywhere=(count, count + 1),
    )
    return result[0], result[1], result[2], result[3:]


def heads_backward(pieces, first, second, qkv, lse, mask, heads, parts):
    rows = mask.shape[0]
    features = pieces[0].shape[1]
    wide = heads * HD
    count = len(pieces)

    def kernel(*refs):
        piece_refs, refs = refs[:count], refs[count:]
        first_hbm, second_hbm, qkv_ref, lse_ref, mask_ref, grad_ref, sum_ref = refs[:7]
        part_refs, refs = refs[7 : 7 + parts], refs[7 + parts :]
        whole, up_ref, first_ref, first_sem, second_ref, second_sem = refs
        waits = fetch(
            (second, first),
            (second_hbm, first_hbm),
            ((second_ref, second_sem), (first_ref, first_sem)),
        )
        stack_pieces(piece_refs, whole)
        finish(waits[0])
        for begin in range(0, rows, CHUNK):
            some = slice(begin, begin + CHUNK)
            up_ref[some, :] = contract(whole[some, :], second_ref[:, wide:], 1, 0).astype(BF)
        for head in range(heads):
            low = head * HD
            key = qkv_ref[:, wide + low : wide + low + HD]
            value = qkv_ref[:, 2 * wide + low : 2 * wide + low + HD]
            key_grad = jnp.zeros((rows, HD), F32)
            value_grad = jnp.zeros((rows, HD), F32)
            query_sum = jnp.zeros((1, HD), F32)
            for begin in range(0, rows, CHUNK):
                part = pl.ds(begin, CHUNK)
                query = qkv_ref[part, low : low + HD] * jnp.asarray(score_scale, BF)
                up = up_ref[part, low : low + HD]
                scores = contract(key, query, 1, 1) + mask_ref[:, part]
                weights = jnp.exp(scores - lse_ref[head : head + 1, part])
                value_grad = value_grad + contract(weights.astype(BF), up, 1, 0)
                slope = contract(value, up, 1, 1)
                delta = jnp.sum(weights * slope, axis=0, keepdims=True)
                scores_grad = (weights * (slope - delta)).astype(BF)
                key_grad = key_grad + contract(scores_grad, query, 1, 0)
                query_grad = (contract(key, scores_grad, 0, 0) * score_scale).T.astype(BF)
                grad_ref[part, low : low + HD] = query_grad
                query_sum = query_sum + jnp.sum(query_grad.astype(F32), axis=0, keepdims=True)
            grad_ref[:, wide + low : wide + low + HD] = key_grad.astype(BF)
            grad_ref[:, 2 * wide + low : 2 * wide + low + HD] = value_grad.astype(BF)
            sum_ref[0:1, low : low + HD] = query_sum
            sum_ref[1:2, low : low + HD] = jnp.sum(value_grad, axis=0, keepdims=True)
        finish(waits[1])
        for begin in range(0, rows, CHUNK):
            some = slice(begin, begin + CHUNK)
            value = contract(grad_ref[some, : 2 * wide], first_ref[...], 1, 1)
            value = value + contract(grad_ref[some, 2 * wide :], second_ref[:, :wide], 1, 1)
            store_parts(part_refs, begin, value)

    here = rows // parts
    result = call(
        kernel,
        [shape((rows, 3 * wide), BF), shape((2, wide), F32)]
        + [shape((here, features), BF)] * parts,
        list(pieces) + [first.array, second.array, qkv, lse, mask],
        [pltpu.VMEM((rows, features), BF), pltpu.VMEM((rows, wide), BF)]
        + first.scratch()
        + second.scratch(),
        flops=8 * rows * features * wide + 40 * rows * rows * wide,
        exps=rows * rows * heads,
        anywhere=(count, count + 1),
    )
    return result[0], result[1], result[2:]


def gelu_both(inputs):
    inner = tanh_scale * (inputs + cubic_weight * inputs * inputs * inputs)
    tangent = jnp.tanh(inner)
    value = 0.5 * inputs * (1.0 + tangent)
    slope = 0.5 * (1.0 + tangent) + 0.5 * inputs * (1.0 - tangent * tangent) * tanh_scale * (
        1.0 + 3.0 * cubic_weight * inputs * inputs
    )
    return value.astype(BF), slope.astype(BF)


def feed_forward(pieces, up, down, bias, parts):
    rows = sum(piece.shape[0] for piece in pieces)
    features = pieces[0].shape[1]
    hidden = up.dims[1]
    count = len(pieces)

    def kernel(*refs):
        piece_refs, refs = refs[:count], refs[count:]
        up_hbm, down_hbm, bias_ref, hidden_ref, slope_ref = refs[:5]
        part_refs, refs = refs[5 : 5 + parts], refs[5 + parts :]
        whole, up_ref, up_sem, down_ref, down_sem = refs
        waits = fetch(
            (up, down), (up_hbm, down_hbm), ((up_ref, up_sem), (down_ref, down_sem))
        )
        stack_pieces(piece_refs, whole)
        finish(waits[0])
        for begin in range(0, rows, CHUNK):
            some = slice(begin, begin + CHUNK)
            value, slope = gelu_both(contract(whole[some, :], up_ref[...], 1, 0) + bias_ref[...])
            hidden_ref[some, :] = value
            slope_ref[some, :] = slope
        finish(waits[1])
        for begin in range(0, rows, CHUNK):
            some = slice(begin, begin + CHUNK)
            store_parts(part_refs, begin, contract(hidden_ref[some, :], down_ref[...], 1, 1))

    here = rows // parts
    result = call(
        kernel,
        [shape((rows, hidden), BF)] * 2 + [shape((here, features), BF)] * parts,
        list(pieces) + [up.array, down.array, bias],
        [pltpu.VMEM((rows, features), BF)] + up.scratch() + down.scratch(),
        flops=4 * rows * features * hidden,
        exps=rows * hidden,
        anywhere=(count, count + 1),
    )
    return result[0], result[1], result[2:]


def feed_backward(pieces, up, down, slope, parts):
    rows = sum(piece.shape[0] for piece in pieces)
    features = pieces[0].shape[1]
    hidden = up.dims[1]
    count = len(pieces)

    def kernel(*refs):
        piece_refs, refs = refs[:count], refs[count:]
        up_hbm, down_hbm, slope_ref, grad_ref, sum_ref = refs[:5]
        part_refs, refs = refs[5 : 5 + parts], refs[5 + parts :]
        whole, up_ref, up_sem, down_ref, down_sem = refs
        waits = fetch(
            (down, up), (down_hbm, up_hbm), ((down_ref, down_sem), (up_ref, up_sem))
        )
        stack_pieces(piece_refs, whole)
        finish(waits[0])
        for begin in range(0, rows, CHUNK):
            some = slice(begin, begin + CHUNK)
            value = contract(whole[some, :], down_ref[...], 1, 0) * slope_ref[some, :].astype(F32)
            grad_ref[some, :] = value.astype(BF)
            add = jnp.sum(value, axis=0, keepdims=True)
            sum_ref[...] = add if begin == 0 else sum_ref[...] + add
        finish(waits[1])
        for begin in range(0, rows, CHUNK):
            some = slice(begin, begin + CHUNK)
            store_parts(part_refs, begin, contract(grad_ref[some, :], up_ref[...], 1, 1))

    here = rows // parts
    result = call(
        kernel,
        [shape((rows, hidden), BF), shape((1, hidden), F32)]
        + [shape((here, features), BF)] * parts,
        list(pieces) + [up.array, down.array, slope],
        [pltpu.VMEM((rows, features), BF)] + up.scratch() + down.scratch(),
        flops=4 * rows * features * hidden,
        anywhere=(count, count + 1),
    )
    return result[0], result[1], result[2:]


def weight_grad(jobs):
    args = []
    for lefts, rights in jobs:
        args += list(lefts) + list(rights)
    features = jobs[0][0][0].shape[1]
    rows = sum(right.shape[0] for right in jobs[0][1])
    widths = [rights[0].shape[1] for _, rights in jobs]
    chunk = features // 4

    def kernel(*refs):
        refs = list(refs)
        turned, joined = refs[-2], refs[-1]
        out_ref = refs[len(args)]
        at = 0
        column = 0
        for (lefts, rights), width in zip(jobs, widths):
            begin = 0
            for _ in lefts:
                left = refs[at]
                at += 1
                turned[:, begin : begin + left.shape[0]] = left[...].T
                begin += left.shape[0]
            begin = 0
            for _ in rights:
                right = refs[at]
                at += 1
                joined[begin : begin + right.shape[0], :width] = right[...]
                begin += right.shape[0]

            for i in range(4):
                some = slice(i * chunk, (i + 1) * chunk)
                value = contract(turned[some, :], joined[:, :width], 1, 0)
                out_ref[some, column : column + width] = value.astype(BF)
            column += width

    return call(
        kernel,
        [shape((features, sum(widths)), BF)],
        args,
        [pltpu.VMEM((features, rows), BF), pltpu.VMEM((rows, max(widths)), BF)],
        flops=2 * rows * features * sum(widths),
    )[0]


def row_stats(stream):
    mean = jnp.mean(stream, axis=1, keepdims=True)
    scale = lax.rsqrt(jnp.mean(stream * stream, axis=1, keepdims=True) - mean * mean + epsilon)
    return mean, scale


def norm(stream, gain, offset):
    mean, scale = row_stats(stream)
    return (((stream - mean) * scale) * gain + offset).astype(BF)


def sum_refs(refs):
    value = refs[0][...].astype(F32)
    for ref in refs[1:]:
        value = value + ref[...].astype(F32)
    return value


def turn_blocks(blocks, gain, offset):
    cols = len(blocks)
    width, rows = blocks[0].shape
    own = rows // cols
    normed = gain is not None
    vectors = [gain, offset] if normed else []

    def kernel(*refs):
        block_refs, refs = refs[:cols], refs[cols:]
        vector_refs, refs = refs[: len(vectors)], refs[len(vectors) :]
        out_ref, own_ref, held = refs[0], refs[1], refs[-1]
        whole = refs[2] if normed else out_ref
        here = lax.axis_index("col")
        for j in range(cols):
            held[j] = block_refs[j][...]
        for t in range(cols):
            plane = held[here ^ t].T
            for i in range(cols):
                start = pl.multiple_of((here ^ i) * own, own)
                whole[pl.ds(start, own), t * width : (t + 1) * width] = plane[
                    i * own : (i + 1) * own
                ]
        own_ref[...] = whole[:own, :].astype(F32)
        if normed:
            for begin in range(0, rows, own):
                some = slice(begin, begin + own)
                value = whole[some, :].astype(F32)
                out_ref[some, :] = norm(value, vector_refs[0][...], vector_refs[1][...])

    full = (rows, width * cols)
    scratch = [pltpu.VMEM(full, BF)] if normed else []
    return call(
        kernel,
        [shape(full, BF), shape((own, full[1]), F32)],
        list(blocks) + vectors,
        scratch + [pltpu.VMEM((cols, width, rows), BF)],
    )


def add_and_norm(terms, stream, shift, gain, offset):
    count = len(terms)

    def kernel(*refs):
        stream_ref, shift_ref, gain_ref, offset_ref, sum_ref, norm_ref = refs[count:]
        value = stream_ref[...] + sum_refs(refs[:count]) + shift_ref[...]
        sum_ref[...] = value
        norm_ref[...] = norm(value, gain_ref[...], offset_ref[...])

    return call(
        kernel,
        [shape(stream.shape, F32), shape(stream.shape, BF)],
        list(terms) + [stream, shift, gain, offset],
    )


def add_and_turn(terms, stream, shift):
    count = len(terms)

    def kernel(*refs):
        stream_ref, shift_ref, out_ref = refs[count:]
        value = stream_ref[...] + sum_refs(refs[:count]) + shift_ref[...]
        out_ref[...] = value.T.astype(BF)

    return call(kernel, [shape(stream.shape[::-1], BF)], list(terms) + [stream, shift])[0]


def norm_backward(terms, stream, base, gain, turn, weight):
    count = len(terms)

    def kernel(*refs):
        stream_ref, base_ref, gain_ref, out_ref, half_ref, sum_ref = refs[count:]
        incoming = sum_refs(refs[:count])
        value = stream_ref[...]
        mean, scale = row_stats(value)
        normed = (value - mean) * scale
        scaled = incoming * gain_ref[...]
        outgoing = base_ref[...] + scale * (
            scaled
            - jnp.mean(scaled, axis=1, keepdims=True)
            - normed * jnp.mean(scaled * normed, axis=1, keepdims=True)
        )
        out_ref[...] = outgoing
        half_ref[...] = outgoing.T.astype(BF) if turn else outgoing.astype(BF)
        sum_ref[0:1, :] = jnp.sum(incoming * normed, axis=0, keepdims=True)
        sum_ref[1:2, :] = jnp.sum(incoming, axis=0, keepdims=True)
        sum_ref[2:3, :] = jnp.sum(outgoing, axis=0, keepdims=True)

    dims = stream.shape
    return call(
        kernel,
        [shape(dims, F32), shape(dims[::-1] if turn else dims, BF), shape((3, dims[1]), F32)],
        list(terms) + [stream, base, gain],
        flops=weight,
    )


def on_device(
    block_input,
    out_cotangent,
    group_order,
    first_gain,
    first_bias,
    query_weight,
    key_weight,
    value_weight,
    query_bias,
    value_bias,
    out_weight,
    out_bias,
    second_gain,
    second_bias,
    up_weight,
    up_bias,
    down_weight,
    down_bias,
):
    section = lax.axis_index("section")
    col = lax.axis_index("col")
    cols = lax.axis_size("col")
    batches, width, rows = block_input.shape
    own = rows // cols
    mine = batches // 2
    per, wide = head_share()
    heads = wide // HD
    features = width * cols
    is_first = section == 0

    def pairs(one, two):
        keep = jnp.where(is_first, one, two)
        got = swap_section(jnp.where(is_first, two, one))
        return jnp.where(is_first, keep, got), jnp.where(is_first, got, keep)

    def gather_pair(own_part):
        full = lax.all_gather(own_part, ("row", "section"), axis=0, tiled=True)
        block = own_part.shape[0]
        count = full.shape[0] // (2 * block)
        if block % 16 == 0:
            return (
                Matrix(full, 0, 2 * block, block, count),
                Matrix(full, block, 2 * block, block, count),
            )
        full = full.reshape(count, 2, block, -1)
        one = full[:, 0].reshape(count * block, -1)
        two = full[:, 1].reshape(count * block, -1)
        return Matrix(one, 0, 0, count * block, 1), Matrix(two, 0, 0, count * block, 1)

    heads_pack = align_heads(
        jnp.stack([query_weight[0], key_weight[0], value_weight[0], out_weight[0].T]), col
    )
    heads_parts = pairs(
        jnp.concatenate([heads_pack[0], heads_pack[1]], axis=1),
        jnp.concatenate([heads_pack[2], heads_pack[3]], axis=1),
    )

    small_wide = jnp.stack(
        [first_gain[0], first_bias[0], out_bias[0], second_gain[0], second_bias[0], down_bias[0]]
    )
    small_wide = xor_order(
        jnp.stack([small_wide] + [xor_step(small_wide, "col", j) for j in range(1, cols)]), col
    )
    small_wide = jnp.swapaxes(small_wide, 0, 1).reshape(6, features)
    small_heads = align_heads(jnp.stack([query_bias[0], value_bias[0]]), col).reshape(-1)
    small_own = jnp.concatenate([small_wide.reshape(-1), small_heads, up_bias[0]])
    small_other = swap_section(small_own)
    small_layers = (
        jnp.where(is_first, small_own, small_other),
        jnp.where(is_first, small_other, small_own),
    )

    def smalls_of(layer):
        flat = small_layers[layer]
        vectors = flat[: 6 * features].reshape(6, features)
        query_shift = flat[6 * features : 6 * features + wide]
        value_shift = flat[6 * features + wide : 6 * features + 2 * wide]
        qkv_shift = jnp.concatenate([query_shift, jnp.zeros((wide,), F32), value_shift])
        vectors = [vectors[i : i + 1] for i in range(6)]
        return vectors, qkv_shift[None], flat[6 * features + 2 * wide :][None]

    smalls = [smalls_of(0), smalls_of(1)]

    link = Link()
    input_own = lax.dynamic_slice_in_dim(block_input, section * mine, mine, 0)
    cotangent_own = lax.dynamic_slice_in_dim(out_cotangent, section * mine, mine, 0)
    early = link.spread(input_own[0])
    late_own = jnp.concatenate([input_own[1:], cotangent_own], axis=0)
    late = link.spread(after(late_own, small_layers, early))

    wide_parts = pairs(*after((up_weight[0], down_weight[0]), early))

    blocks = group_order.shape[0]
    group_rows = L // blocks
    places = jnp.arange(rows, dtype=jnp.int32)
    places = ((places // own) ^ col) * own + places % own
    within = places % L
    match = (within // group_rows)[:, None] == jnp.arange(blocks, dtype=jnp.int32)[None, :]
    position = (
        jnp.sum(jnp.where(match, group_order[None, :], 0), axis=1) * group_rows
        + within % group_rows
    )
    sequence = places // L
    allowed = (sequence[:, None] == sequence[None, :]) & (position[:, None] <= position[None, :])
    mask = jnp.where(allowed, 0.0, -jnp.inf).astype(F32)

    everyone = range(mine)
    weights = [gather_pair(heads_parts[0]) + gather_pair(wide_parts[0])]
    weights.append(gather_pair(heads_parts[1]) + gather_pair(wide_parts[1]))
    saved = [[None] * mine, [None] * mine]
    turned_input = turn_blocks(early, smalls[0][0][0], smalls[0][0][1])
    streams = [turned_input[1]]
    pieces = [[turned_input[0]]]
    for layer in range(2):
        vectors, qkv_shift, up_shift = smalls[layer]
        gain_one, bias_one, out_shift, gain_two, bias_two, down_shift = vectors
        first, second, up, down = weights[layer]
        begun = []
        for batch in everyone:
            qkv, attended, lse, parts = heads_forward(
                pieces[batch], first, second, qkv_shift, mask, heads, cols
            )
            begun.append((qkv, attended, lse, link.exchange(parts)))
            if layer == 0 and batch == 0:
                late = after(late, lse)
                for i in range(1, mine):
                    turned_input = turn_blocks(
                        [item[i - 1] for item in late], smalls[0][0][0], smalls[0][0][1]
                    )
                    streams.append(turned_input[1])
                    pieces.append([turned_input[0]])
                cotangents = [
                    turn_blocks([item[mine - 1 + i] for item in late], None, None)
                    for i in range(mine)
                ]
        middles = []
        for batch in everyone:
            middle, normed = add_and_norm(
                begun[batch][3], streams[batch], out_shift, gain_two, bias_two
            )
            middles.append((middle, link.spread(normed)))
        terms = []
        for batch in everyone:
            middle, twos = middles[batch]
            hidden, slope, parts = feed_forward(twos, up, down, up_shift, cols)
            saved[layer][batch] = (
                streams[batch], pieces[batch], *begun[batch][:3], middle, twos, hidden, slope,
            )
            terms.append(link.exchange(parts))
        if layer == 0:
            streams, pieces = [], []
            for batch in everyone:
                stream, normed = add_and_norm(
                    terms[batch], middles[batch][0], down_shift, smalls[1][0][0], smalls[1][0][1]
                )
                streams.append(stream)
                pieces.append(link.spread(normed))
        else:
            last_terms = terms
            finals = [
                add_and_turn(terms[batch], middles[batch][0], down_shift) for batch in everyone
            ]

    def to_features(pair):
        blocks_out = jnp.stack([item.reshape(cols, width, own) for item in pair], axis=1)
        blocks_in = lax.all_to_all(blocks_out, "col", split_axis=0, concat_axis=0, tiled=True)
        return blocks_in.transpose(1, 2, 0, 3).reshape(len(pair), width, rows)

    def scatter_rows(grad):
        return lax.psum_scatter(grad, ("row", "section"), scatter_dimension=0, tiled=True)

    reduced = [None, None]
    wide_sums = [None, None]
    narrow_sums = [None, None]
    ups = [[item[0]] for item in cotangents]
    bases = [item[1] for item in cotangents]
    base_sum = sum(jnp.sum(base, axis=0, keepdims=True) for base in bases)
    results = []
    turned = []
    for layer in (1, 0):
        vectors = smalls[layer][0]
        gain_one, gain_two = vectors[0], vectors[3]
        first, second, up, down = weights[layer]
        mids = []
        hidden_grads = []
        qkv_grads = []
        sums = []
        head_sums = []
        up_sums = []
        next_bases = []
        next_ups = []
        down_job = (ups[0] + ups[1], [saved[layer][batch][7] for batch in everyone])
        if layer == 1:
            down_grad = weight_grad([down_job])
            down_sum = scatter_rows(down_grad)
        terms = []
        for batch in everyone:
            slope = saved[layer][batch][8]
            slope = after(slope, down_grad if layer == 1 else first_sum)
            if layer == 1 and batch == mine - 1:
                slope = after(slope, last_terms)
            hidden_grad, hidden_sum, parts = feed_backward(ups[batch], up, down, slope, cols)
            hidden_grads.append(hidden_grad)
            up_sums.append(hidden_sum[0])
            terms.append(link.exchange(parts))
        up_job = (saved[layer][0][6] + saved[layer][1][6], hidden_grads)
        if layer == 1:
            up_grad = weight_grad([up_job])
            up_sum = scatter_rows(up_grad)
        else:
            wide_grad = weight_grad([down_job, up_job])
            wide_sum = scatter_rows(wide_grad)
        middle_grads = []
        seconds = []
        for batch in everyone:
            middle = saved[layer][batch][5]
            if layer == 1:
                middle = after(middle, up_grad)
            middle_grad, half, second_sums = norm_backward(
                terms[batch], middle, bases[batch], gain_two, False, layer * 15000000000
            )
            middle_grads.append(middle_grad)
            seconds.append(second_sums)
            mids.append(link.spread(half))
        terms = []
        for batch in everyone:
            qkv, lse = saved[layer][batch][2], saved[layer][batch][4]
            if layer == 0:
                lse = after(lse, wide_grad, reduced[1][2])
            qkv_grad, head_sum, parts = heads_backward(
                mids[batch], first, second, qkv, lse, mask, heads, cols
            )
            qkv_grads.append(qkv_grad)
            head_sums.append(head_sum.reshape(-1))
            terms.append(link.exchange(parts))
        heads_grad = weight_grad(
            [
                (saved[layer][0][1] + saved[layer][1][1], qkv_grads),
                (mids[0] + mids[1], [saved[layer][batch][3] for batch in everyone]),
            ]
        )
        for batch in everyone:
            stream = after(saved[layer][batch][0], heads_grad)
            stream_grad, half, first_sums = norm_backward(
                terms[batch], stream, middle_grads[batch], gain_one, layer == 0, layer * 15000000000
            )
            second_sums = seconds[batch]
            next_bases.append(stream_grad)
            if layer == 1:
                next_ups.append(link.spread(half))
            else:
                turned.append(half)
            sums.append((first_sums, second_sums))
        if layer == 1:
            wide_sum = jnp.concatenate([down_sum, up_sum], axis=1)
        first_sum = (down_sum, up_sum) if layer == 1 else None
        if layer == 0:
            heads_grad = after(heads_grad, wide_sum, turned)
        reduced[layer] = (wide_sum, up_sum, scatter_rows(heads_grad))
        first_sums = sums[0][0] + sums[1][0]
        second_sums = sums[0][1] + sums[1][1]
        wide_sums[layer] = jnp.concatenate(
            [first_sums[:2], second_sums[2:3], second_sums[:2], base_sum], axis=0
        )
        base_sum = first_sums[2:3]
        narrow_sums[layer] = jnp.concatenate(
            [head_sums[0] + head_sums[1], up_sums[0] + up_sums[1]]
        )
        bases = next_bases
        ups = next_ups

    both = to_features(turned + finals)
    grads, outputs = both[:mine], both[mine:]

    wide_both = jnp.stack(wide_sums).reshape(2, 6, cols, width)
    wide_here = lax.dynamic_index_in_dim(wide_both, col, 2, keepdims=False)
    for j in range(1, cols):
        wide_here = wide_here + xor_step(
            lax.dynamic_index_in_dim(wide_both, col ^ j, 2, keepdims=False), "col", j
        )
    small_sums = jnp.concatenate([wide_here.reshape(2, -1), jnp.stack(narrow_sums)], axis=1)
    small_own = lax.dynamic_index_in_dim(small_sums, section, 0, keepdims=False)
    small_own = small_own + swap_section(
        lax.dynamic_index_in_dim(small_sums, 1 - section, 0, keepdims=False)
    )
    step = 1
    while step < lax.axis_size("row"):
        small_own = small_own + xor_step(small_own, "row", step)
        step *= 2
    small_out = small_own[: 6 * width].reshape(6, width)
    head_out = unalign_heads(
        small_own[6 * width : 6 * width + 2 * wide].reshape(2, wide), width, col
    )
    up_bias_grad = small_own[6 * width + 2 * wide :]

    def settle(first_half, second_half):
        got = swap_section(jnp.where(is_first, second_half, first_half))
        keep = jnp.where(is_first, first_half, second_half)
        low = jnp.where(is_first, keep, got)
        high = jnp.where(is_first, got, keep)
        return jnp.concatenate([low, high], axis=0)

    wide_out = settle(reduced[0][0], reduced[1][0])
    down_out = wide_out[:, : wide_out.shape[1] // 2].astype(F32)
    up_out = wide_out[:, wide_out.shape[1] // 2 :].astype(F32)
    heads_out = settle(reduced[0][2], reduced[1][2])
    heads_out = unalign_heads(
        jnp.stack([heads_out[:, i * wide : (i + 1) * wide] for i in range(4)]), width, col
    ).astype(F32)

    got = swap_section(jnp.where(is_first, outputs, grads))
    keep = jnp.where(is_first, grads, outputs)
    boundary = jnp.concatenate(
        [jnp.where(is_first, keep, got), jnp.where(is_first, got, keep)], axis=0
    ).astype(F32)

    return (
        boundary[None],
        small_out[0][None],
        small_out[1][None],
        heads_out[0][None],
        heads_out[1][None],
        heads_out[2][None],
        head_out[0][None],
        head_out[1][None],
        heads_out[3].T[None],
        small_out[2][None],
        small_out[3][None],
        small_out[4][None],
        up_out[None],
        up_bias_grad[None],
        down_out[None],
        small_out[5][None],
    )


def solution(mesh):
    vector = P("section", "col")
    matrix = P("section", "row", "col")
    turned = P("section", "col", "row")
    plane = P(None, "col", "row")
    in_specs = (
        plane, plane, P(), vector, vector, matrix, matrix, matrix, vector, vector,
        turned, vector, vector, vector, matrix, vector, matrix, vector,
    )
    out_specs = (
        P("section", None, "col", "row"), vector, vector, matrix, matrix, matrix, vector, vector,
        turned, vector, vector, vector, matrix, vector, matrix, vector,
    )
    return jax.shard_map(
        on_device, mesh=mesh, in_specs=in_specs, out_specs=out_specs, check_vma=False
    )
```

time: 1100 us -> 863 us (0.78)
  Pallas kernels: 57.3 us -> 324 us
  matrix products: 218 us -> 0 us
  other arithmetic: 137 us -> 29.8 us
  local copies, waits for them, and re-layouts: 216 us -> 117 us
  waiting for transfers between devices: 290 us -> 239 us
  starting transfers between devices: 151 us -> 130 us
    pallas_call x8 -> x41, Pallas kernels: 57.3 us -> 324 us  [call(): pl.pallas_call(kernel, out_shape=tuple(outs), in_specs=[pl.BlockSpec(memo...]
    dot_general x40 -> x0, matrix products: 218 us -> none  [contract(): lax.dot_general(left, right, (((left_dim,), (right_dim,)), ((), ())), pre...]
    ppermute x106 -> x105, waiting for transfers between devices: 270 us -> 189 us  [xor_step(): return lax.ppermute(value, axis, [(i, i ^ step) for i in range(count)])]
    reduce_sum x18 -> x2, other arithmetic: 31.8 us -> 0.11 us  [on_device(): base_sum = sum((jnp.sum(base, axis=0, keepdims=True) for base in bases))]
    another operation x11 -> x2, other arithmetic: 27.3 us -> 1.47 us  [the longest x1 1.37 us: to_features(): jnp.stack([item.reshape(cols, width, own) for item in pair], axis=1)]
    convert_element_type x10 -> x0, local copies, waits for them, and re-layouts: 24.4 us -> none  [the longest x2 9.35 us: on_device(): inputs_one = norm(inputs[batch].astype(F32), gain_one, bias_one)]
    another operation x39 -> x5, local copies, waits for them, and re-layouts: 23.4 us -> 0.16 us  [the longest x2 0.15 us: on_device(): wide_both = jnp.stack(wide_sums).reshape(2, 6, cols, width)]
    reduce_scatter x2, waiting for transfers between devices: 0.04 us -> 23.2 us  [scatter_rows(): lax.psum_scatter(grad, ('row', 'section'), scatter_dimension=0, tiled=True)]
  transfers between devices with their start and end apart: 121 -> 119, of which waited for: 50 -> 41; matrix products, arithmetic and copies ran while one was open for 49% -> 4% of each run, Pallas kernels for 5% -> 38%
where the time goes in v2:
time: 863 us; the launch traced here: 856 us
  Pallas kernels  324 us (38%)
  waiting for transfers between devices  239 us (28%)
  starting transfers between devices  130 us (15%)
  local copies, waits for them, and re-layouts  117 us (14%)
  other arithmetic  29.8 us (3%)
  between operations  16.3 us (2%)
    pallas_call x41, Pallas kernels, call(): pl.pallas_call(kernel, out_shape=tuple(outs), in_specs=[pl.BlockSpec(memo...  324 us
    ppermute x105, waiting for transfers between devices, xor_step(): return lax.ppermute(value, axis, [(i, i ^ step) for i in range(count)])  189 us
    ppermute x105, starting transfers between devices, xor_step(): return lax.ppermute(value, axis, [(i, i ^ step) for i in range(count)])  115 us
    unnamed x466, local copies, waits for them, and re-layouts  97.8 us
    reduce_scatter x2, waiting for transfers between devices, scatter_rows(): lax.psum_scatter(grad, ('row', 'section'), scatter_dimension=0, tiled=True)  23.2 us
  transfers between devices with their start and end apart: 119, of which 41 were waited for; matrix products, arithmetic and copies ran while one was open for 4% of the time, Pallas kernels for 38%

profile of v2, /device:TPU:0, one launch (start us, length us, event | category | flops | bytes accessed | tf_op | source)
XLA Modules:
  0.0 855.6 jit_solution(2558385511394328135)
XLA Ops:
  11.8 13.2 %collective-permute-done.11 = bf16[4,400,64]{2,1,0:T(8,128)(2,1)} collective-permute-done((bf16[4,400,64]{2,1,0:T(8,128)(2,1)}, bf16[4,400,64]{2,1,0:T(8,128)(2,1)}, u32[]{:S(2)}, u32[]{:S(2)}) %collective-permute-start.11) | collective-permute-done | bytes 204832 | tf_op jit(solution)/shard_map/ppermute | solution.py:68
  25.0 3.0 fusion.8
  38.8 8.8 %collective-permute-done.5.refs_1_ = bf16[400,512]{1,0:T(8,128)(2,1)S(1)} collective-permute-done((bf16[400,512]{1,0:T(8,128)(2,1)S(1)}, bf16[400,512]{1,0:T(8,128)(2,1)S(1)}, u32[]{:S(2)}, u32[]{:S(2)}) %collective-permute-start.5) | collective-permute-done | bytes 409632 | tf_op jit(solution)/shard_map/ppermute | solution.py:25
  47.6 9.8 %collective-permute-done.6.refs_2_ = bf16[400,512]{1,0:T(8,128)(2,1)S(1)} collective-permute-done((bf16[400,512]{1,0:T(8,128)(2,1)S(1)}, bf16[400,512]{1,0:T(8,128)(2,1)S(1)}, u32[]{:S(2)}, u32[]{:S(2)}) %collective-permute-start.6) | collective-permute-done | bytes 409632 | tf_op jit(solution)/shard_map/ppermute | solution.py:25
  59.3 3.1 collective-permute-done.13
  89.8 4.7 all-gather.5.cloned.1.call-done.refs_1_.refs_2_.refs_4_.refs_5_
  95.9 12.7 %shard_map.298 = (bf16[512,1344]{1,0:T(8,128)(2,1)S(1)}, bf16[512,448]{1,0:T(8,128)(2,1)S(1)}, f32[7,512]{1,0:T(8,128)S(1)}, bf16[128,1600]{1,0:T(8,128)(2,1)S(1...) custom-call(bf16[512,1600]{1,0:T(8,128)(2,1)S(1)} %copy-done.102, ...), custom_call_target="tpu_custom_call" | custom-call | flops 19260243968 | tf_op jit(solution)/shard_map/pallas_call | solution.py:117
  109.2 3.6 collective-permute-done.10
  112.8 25.7 %collective-permute-done.8 = bf16[3,400,512]{2,1,0:T(8,128)(2,1)} collective-permute-done((bf16[3,400,512]{2,1,0:T(8,128)(2,1)}, bf16[3,400,512]{2,1,0:T(8,128)(2,1)}, u32[]{:S(2)}, u32[]{:S(2)}) %collective-permute-start.8) | collective-permute-done | bytes 1228832 | tf_op jit(solution)/shard_map/ppermute | solution.py:25
  152.5 13.8 %shard_map.308 = (bf16[512,1344]{1,0:T(8,128)(2,1)S(1)}, bf16[512,448]{1,0:T(8,128)(2,1)S(1)}, f32[7,512]{1,0:T(8,128)S(1)}, bf16[128,1600]{1,0:T(8,128)(2,1)S(1...) custom-call(bf16[512,1600]{1,0:T(8,128)(2,1)S(1)} %get-tuple-element.210.refs_0_.refs, ...), custom_call_target="tpu_custom_call" | custom-call | flops 19260243968 | tf_op jit(solution)/shard_map/pallas_call | solution.py:117
  175.7 5.9 collective-permute-done.32.refs_1_
  183.3 9.0 %collective-permute-done.33.refs_2_ = bf16[128,1600]{1,0:T(8,128)(2,1)S(1)} collective-permute-done((bf16[128,1600]{1,0:T(8,128)(2,1)S(1)}, bf16[128,1600]{1,0:T(8,128)(2,1)S(1)}, u32[]{:S(2)}, u32[]{:S(2)}) %collective-permute-start.33) | collective-permute-done | bytes 409632 | tf_op jit(solution)/shard_map/ppermute | solution.py:25
  195.4 4.5 collective-permute-done.17.refs_1_.refs_11_
  202.4 8.2 collective-permute-done.18.refs_2_.refs_12_
  216.2 12.1 %shard_map.301 = (bf16[512,1600]{1,0:T(8,128)(2,1)S(1)}, bf16[512,1600]{1,0:T(8,128)(2,1)S(1)}, bf16[128,1600]{1,0:T(8,128)(2,1)S(1)}, bf16[128,1600]{1,0:T(8,12...) custom-call(bf16[128,1600]{1,0:T(8,128)(2,1)S(1)} %copy-done.112, ...), custom_call_target="tpu_custom_call" | custom-call | flops 20971520000 | tf_op jit(solution)/shard_map/pallas_call | solution.py:117
  234.3 14.8 %shard_map.310 = (bf16[512,1600]{1,0:T(8,128)(2,1)S(1)}, bf16[512,1600]{1,0:T(8,128)(2,1)S(1)}, bf16[128,1600]{1,0:T(8,128)(2,1)S(1)}, bf16[128,1600]{1,0:T(8,12...) custom-call(bf16[128,1600]{1,0:T(8,128)(2,1)} %get-tuple-element.216.refs_0_.refs_14_, ...), custom_call_target="tpu_custom_call" | custom-call | flops 20971520000 | tf_op jit(solution)/shard_map/pallas_call | solution.py:117
  259.1 5.2 collective-permute-done.38.refs_1_
  266.3 8.2 collective-permute-done.39.refs_2_
  283.8 8.9 %collective-permute-done.24.refs_2_ = bf16[128,1600]{1,0:T(8,128)(2,1)} collective-permute-done((bf16[128,1600]{1,0:T(8,128)(2,1)}, bf16[128,1600]{1,0:T(8,128)(2,1)}, u32[]{:S(2)}, u32[]{:S(2)}) %collective-permute-start.24) | collective-permute-done | bytes 409632 | tf_op jit(solution)/shard_map/ppermute | solution.py:25
  293.9 14.4 %shard_map.303 = (bf16[512,1344]{1,0:T(8,128)(2,1)S(1)}, bf16[512,448]{1,0:T(8,128)(2,1)S(1)}, f32[7,512]{1,0:T(8,128)S(1)}, bf16[128,1600]{1,0:T(8,128)(2,1)S(1...) custom-call(bf16[128,1600]{1,0:T(8,128)(2,1)} %get-tuple-element.200.refs_0_, ...), custom_call_target="tpu_custom_call" | custom-call | flops 19260243968 | tf_op jit(solution)/shard_map/pallas_call | solution.py:117
  313.7 14.2 %shard_map.312 = (bf16[512,1344]{1,0:T(8,128)(2,1)S(1)}, bf16[512,448]{1,0:T(8,128)(2,1)S(1)}, f32[7,512]{1,0:T(8,128)S(1)}, bf16[128,1600]{1,0:T(8,128)(2,1)S(1...) custom-call(bf16[128,1600]{1,0:T(8,128)(2,1)} %get-tuple-element.222.refs_0_.refs_4_,, ...), custom_call_target="tpu_custom_call" | custom-call | flops 19260243968 | tf_op jit(solution)/shard_map/pallas_call | solution.py:117
  337.7 5.0 collective-permute-done.44.refs_1_
  349.6 3.0 collective-permute-done.45.refs_2_
  357.3 3.7 collective-permute-done.29.refs_1_
  363.1 5.0 collective-permute-done.30.refs_2_
  370.4 13.3 %shard_map.305 = (bf16[512,1600]{1,0:T(8,128)(2,1)S(1)}, bf16[512,1600]{1,0:T(8,128)(2,1)S(1)}, bf16[128,1600]{1,0:T(8,128)(2,1)S(1)}, bf16[128,1600]{1,0:T(8,12...) custom-call(bf16[128,1600]{1,0:T(8,128)(2,1)} %get-tuple-element.206.refs_0_, ...), custom_call_target="tpu_custom_call" | custom-call | flops 20971520000 | tf_op jit(solution)/shard_map/pallas_call | solution.py:117
  388.5 13.8 %shard_map.314 = (bf16[512,1600]{1,0:T(8,128)(2,1)S(1)}, bf16[512,1600]{1,0:T(8,128)(2,1)S(1)}, bf16[128,1600]{1,0:T(8,128)(2,1)S(1)}, bf16[128,1600]{1,0:T(8,12...) custom-call(bf16[128,1600]{1,0:T(8,128)(2,1)} %get-tuple-element.228.refs_0_.refs_4_, ...), custom_call_target="tpu_custom_call" | custom-call | flops 20971520000 | tf_op jit(solution)/shard_map/pallas_call | solution.py:117
  406.7 8.5 shard_map.315
  424.6 11.9 %shard_map.316 = (bf16[512,1600]{1,0:T(8,128)(2,1)S(1)}, f32[1,1600]{1,0:T(1,128)S(1)}, bf16[128,1600]{1,0:T(8,128)(2,1)S(1)}, bf16[128,1600]{1,0:T(8,128)(2,1)}...) custom-call(bf16[512,1600]{1,0:T(8,128)(2,1)S(1)} %copy-done.110, ...), custom_call_target="tpu_custom_call" | custom-call | flops 20971520000 | tf_op jit(solution)/shard_map/pallas_call | solution.py:117
  437.2 9.1 %collective-permute-done.54.refs_2_ = bf16[128,1600]{1,0:T(8,128)(2,1)S(1)} collective-permute-done((bf16[128,1600]{1,0:T(8,128)(2,1)}, bf16[128,1600]{1,0:T(8,128)(2,1)S(1)}, u32[]{:S(2)}, u32[]{:S(2)}) %collective-permute-start.54) | collective-permute-done | bytes 409632 | tf_op jit(solution)/shard_map/ppermute | solution.py:25
  449.8 3.3 collective-permute-done.57.refs_2_
  453.2 11.3 %shard_map.317 = (bf16[512,1600]{1,0:T(8,128)(2,1)S(1)}, f32[1,1600]{1,0:T(1,128)S(1)}, bf16[128,1600]{1,0:T(8,128)(2,1)S(1)}, bf16[128,1600]{1,0:T(8,128)(2,1)S...) custom-call(bf16[512,1600]{1,0:T(8,128)(2,1)S(1)} %copy-done.107, ...), custom_call_target="tpu_custom_call" | custom-call | flops 20971520000 | tf_op jit(solution)/shard_map/pallas_call | solution.py:117
  468.2 10.8 %shard_map.318 = bf16[1600,1600]{1,0:T(8,128)(2,1)} custom-call(bf16[128,1600]{1,0:T(8,128)(2,1)} %get-tuple-element.206.refs_0_, bf16[128,1600]{1,0:T(8,128)(2,1)S(1)} %copy-done.125, bf16[128,1600]{1,0:T(8,128)(2,1)} %collective-permute-done.30.refs_2_, bf16[128,1600]{1,0:T(8,128)(2,1)} %collective-permute-done.31.refs_3_, ...), custom_call_target="tpu_custom_call" | custom-call | flops 20971520000 | tf_op jit(solution)/shard_map/pallas_call | solution.py:117
  484.7 2.9 shard_map.319
  493.6 4.9 collective-permute-done.66.refs_2_
  508.1 8.2 collective-permute-done.61.refs_3_.refs_13_
  516.4 17.0 %shard_map.320 = (bf16[512,1344]{1,0:T(8,128)(2,1)S(1)}, f32[2,448]{1,0:T(2,128)S(1)}, bf16[128,1600]{1,0:T(8,128)(2,1)S(1)}, bf16[128,1600]{1,0:T(8,128)(2,1)},...) custom-call(bf16[128,1600]{1,0:T(8,128)(2,1)} %get-tuple-element.251.refs_0_.refs_10_, ...), custom_call_target="tpu_custom_call" | custom-call | flops 30534533120 | tf_op jit(solution)/shard_map/pallas_call | solution.py:117
  533.5 3.4 collective-permute-start.64
  536.9 14.7 %shard_map.322 = (bf16[512,1344]{1,0:T(8,128)(2,1)S(1)}, f32[2,448]{1,0:T(2,128)S(1)}, bf16[128,1600]{1,0:T(8,128)(2,1)S(1)}, bf16[128,1600]{1,0:T(8,128)(2,1)S(...) custom-call(bf16[128,1600]{1,0:T(8,128)(2,1)S(1)} %get-tuple-element.266.refs_0_.refs_14_, ...), custom_call_target="tpu_custom_call" | custom-call | flops 30534533120 | tf_op jit(solution)/shard_map/pallas_call | solution.py:117
  555.8 12.9 %shard_map.323 = bf16[1600,1792]{1,0:T(8,128)(2,1)} custom-call(bf16[128,1600]{1,0:T(8,128)(2,1)} %get-tuple-element.200.refs_0_, bf16[128,1600]{1,0:T(8,128)(2,1)} %collective-permute-done.23.refs_1_, bf16[128,1600]{1,0:T(8,128)(2,1)} %collective-permute-done.24.refs_2_, bf16[128,1600]{1,0:T(8,128)(2,1)} %collective-permute-done.25.refs_3_, ...), custom_call_target="tpu_custom_call" | custom-call | flops 23488102400 | tf_op jit(solution)/shard_map/pallas_call | solution.py:117
  569.4 2.9 collective-permute-start.82
  574.4 2.9 shard_map.324
  579.0 2.9 collective-permute-start.73
  584.4 2.9 shard_map.327
  593.2 12.4 %shard_map.325 = (bf16[512,1600]{1,0:T(8,128)(2,1)S(1)}, f32[1,1600]{1,0:T(1,128)S(1)}, bf16[128,1600]{1,0:T(8,128)(2,1)S(1)}, bf16[128,1600]{1,0:T(8,128)(2,1)S...) custom-call(bf16[128,1600]{1,0:T(8,128)(2,1)} %get-tuple-element.274.refs_0_, ...), custom_call_target="tpu_custom_call" | custom-call | flops 20971520000 | tf_op jit(solution)/shard_map/pallas_call | solution.py:117
  610.5 13.1 %shard_map.328 = (bf16[512,1600]{1,0:T(8,128)(2,1)S(1)}, f32[1,1600]{1,0:T(1,128)S(1)}, bf16[128,1600]{1,0:T(8,128)(2,1)S(1)}, bf16[128,1600]{1,0:T(8,128)(2,1)S...) custom-call(bf16[128,1600]{1,0:T(8,128)(2,1)} %get-tuple-element.290.refs_0_.refs_4_, ...), custom_call_target="tpu_custom_call" | custom-call | flops 20971520000 | tf_op jit(solution)/shard_map/pallas_call | solution.py:117
  627.9 19.4 %shard_map.329 = bf16[1600,3200]{1,0:T(8,128)(2,1)} custom-call(bf16[128,1600]{1,0:T(8,128)(2,1)} %get-tuple-element.274.refs_0_, bf16[128,1600]{1,0:T(8,128)(2,1)} %collective-permute-done.71.refs_1_, bf16[128,1600]{1,0:T(8,128)(2,1)} %collective-permute-done.72.refs_2_, bf16[128,1600]{1,0:T(8,128)(2,1)} %collective-permute-done.73.refs_3_, ...), custom_call_target="tpu_custom_call" | custom-call | flops 41943040000 | tf_op jit(solution)/shard_map/pallas_call | solution.py:117
  653.3 7.3 collective-permute-done.74.refs_1_
  662.2 7.0 collective-permute-done.75.refs_2_
  676.0 6.1 collective-permute-done.91.refs_3_
  693.2 2.9 collective-permute-done.78.refs_2_.refs_6_
  699.8 17.3 %shard_map.330 = (bf16[512,1344]{1,0:T(8,128)(2,1)S(1)}, f32[2,448]{1,0:T(2,128)S(1)}, bf16[128,1600]{1,0:T(8,128)(2,1)S(1)}, bf16[128,1600]{1,0:T(8,128)(2,1)S(...) custom-call(bf16[128,1600]{1,0:T(8,128)(2,1)} %get-tuple-element.282.refs_0_.refs_4_, ...), custom_call_target="tpu_custom_call" | custom-call | flops 30534533120 | tf_op jit(solution)/shard_map/pallas_call | solution.py:117
  720.8 16.9 %shard_map.332 = (bf16[512,1344]{1,0:T(8,128)(2,1)S(1)}, f32[2,448]{1,0:T(2,128)S(1)}, bf16[128,1600]{1,0:T(8,128)(2,1)S(1)}, bf16[128,1600]{1,0:T(8,128)(2,1)},...) custom-call(bf16[128,1600]{1,0:T(8,128)(2,1)} %get-tuple-element.308.refs_0_.refs_8_, ...), custom_call_target="tpu_custom_call" | custom-call | flops 30534533120 | tf_op jit(solution)/shard_map/pallas_call | solution.py:117
  744.5 11.6 %shard_map.333 = bf16[1600,1792]{1,0:T(8,128)(2,1)} custom-call(bf16[512,1600]{1,0:T(8,128)(2,1)S(1)} %copy-done.103, bf16[512,1600]{1,0:T(8,128)(2,1)} %copy-done.104, bf16[512,1344]{1,0:T(8,128)(2,1)S(1)} %get-tuple-element.302.refs_2_, bf16[512,1344]{1,0:T(8,128)(2,1)S(1)} %get-tuple-element.312.refs_3_, ...), custom_call_target="tpu_custom_call" | custom-call | flops 23488102400 | tf_op jit(solution)/shard_map/pallas_call | solution.py:117
  756.2 3.1 shard_map.334
  760.1 3.0 shard_map.335
  778.0 3.6 all-to-all-start
  783.3 4.5 collective-permute-done.103
  787.8 5.5 collective-permute-done.104
  793.6 4.1 collective-permute-start.107
  805.1 23.2 %reduce-scatter.14.cloned.1.call-done = bf16[200,1792]{1,0:T(8,128)(2,1)} async-done(((bf16[1600,1792]{1,0:T(8,128)(2,1)}), bf16[200,1792]{1,0:T(8,128)(2,1)}) %reduce-scatter.14.cloned.1.call-update) | async-done | bytes 716816 | tf_op jit(solution)/shard_map/reduce_scatter | solution.py:735
  831.8 3.4 collective-permute-start.106
  835.2 2.9 fusion.13
  838.1 6.4 collective-permute-done.106
  (816 shorter events, 287.7 us)
Async XLA Ops:
  7.2 87.2 %all-gather.5.cloned.1.call-start = ((), (), s32[]{:S(2)}) async-start(), calls=%async_computation.6 | async-start | bytes 6451200 | tf_op jit(solution)/shard_map/all_gather | solution.py:602
  32.7 179.5 %all-gather.9.cloned.1.call-start = ((), (), s32[]{:S(2)}) async-start(), calls=%async_computation.8 | async-start | bytes 11980800 | tf_op jit(solution)/shard_map/all_gather | solution.py:602
  64.3 219.5 %all-gather.11.cloned.1.call-start = ((), (), s32[]{:S(2)}) async-start(), calls=%async_computation.9 | async-start | bytes 6451200 | tf_op jit(solution)/shard_map/all_gather | solution.py:602
  65.0 298.0 %all-gather.7.cloned.1.call-start = ((), (), s32[]{:S(2)}) async-start(), calls=%async_computation.7 | async-start | bytes 11980800 | tf_op jit(solution)/shard_map/all_gather | solution.py:602
  65.6 524.8 %reduce-scatter.16.cloned.1.call-start = ((), (), s32[]{:S(2)}) async-start(), calls=%async_computation.12 | async-start | bytes 5990400
  81.7 31.1 %collective-permute-start.10 = (bf16[3,400,512]{2,1,0:T(8,128)(2,1)}, bf16[3,400,512]{2,1,0:T(8,128)(2,1)}, u32[]{:S(2)}, u32[]{:S(2)}) collective-permute-start(bf16[3,400,512]{2,1,0:T(8,128)(2,1)} %pad_maximum_fusion.3), channel_id=1, source_target_pairs={{0,3},{1,2},{2,1},{3,0},{4,7},{5,6},{6,5},{7,4},{8,11},{9,10},{10,... | collective-permute-start | bytes 3686408 | tf_op jit(solution)/shard_map/ppermute | solution.py:25
  83.5 55.0 %collective-permute-start.8 = (bf16[3,400,512]{2,1,0:T(8,128)(2,1)}, bf16[3,400,512]{2,1,0:T(8,128)(2,1)}, u32[]{:S(2)}, u32[]{:S(2)}) collective-permute-start(bf16[3,400,512]{2,1,0:T(8,128)(2,1)} %pad_maximum_fusion.3), channel_id=1, source_target_pairs={{0,1},{1,0},{2,3},{3,2},{4,5},{5,4},{6,7},{7,6},{8,9},{9,8},{10,11... | collective-permute-start | bytes 3686408 | tf_op jit(solution)/shard_map/ppermute | solution.py:25
  84.4 54.3 %collective-permute-start.9 = (bf16[3,400,512]{2,1,0:T(8,128)(2,1)}, bf16[3,400,512]{2,1,0:T(8,128)(2,1)}, u32[]{:S(2)}, u32[]{:S(2)}) collective-permute-start(bf16[3,400,512]{2,1,0:T(8,128)(2,1)} %pad_maximum_fusion.3), channel_id=1, source_target_pairs={{0,2},{1,3},{2,0},{3,1},{4,6},{5,7},{6,4},{7,5},{8,10},{9,11},{10,... | collective-permute-start | bytes 3686408 | tf_op jit(solution)/shard_map/ppermute | solution.py:25
  138.7 32.5 %collective-permute-start.14 = (bf16[128,1600]{1,0:T(8,128)(2,1)S(1)}, bf16[128,1600]{1,0:T(8,128)(2,1)S(1)}, u32[]{:S(2)}, u32[]{:S(2)}) collective-permute-start(bf16[128,1600]{1,0:T(8,128)(2,1)S(1)} %get-tuple-element.190), channel_id=1, source_target_pairs={{0,1},{1,0},{2,3},{3,2},{4,5},{5,4},{6,7},{7,6},{8,9},{9,8},{10,11... | collective-permute-start | bytes 1228808 | tf_op jit(solution)/shard_map/ppermute | solution.py:25
  140.2 32.2 %collective-permute-start.15 = (bf16[128,1600]{1,0:T(8,128)(2,1)S(1)}, bf16[128,1600]{1,0:T(8,128)(2,1)S(1)}, u32[]{:S(2)}, u32[]{:S(2)}) collective-permute-start(bf16[128,1600]{1,0:T(8,128)(2,1)S(1)} %get-tuple-element.191), channel_id=1, source_target_pairs={{0,2},{1,3},{2,0},{3,1},{4,6},{5,7},{6,4},{7,5},{8,10},{9,11},{10,... | collective-permute-start | bytes 1228808 | tf_op jit(solution)/shard_map/ppermute | solution.py:25
  141.3 31.2 %collective-permute-start.16 = (bf16[128,1600]{1,0:T(8,128)(2,1)S(1)}, bf16[128,1600]{1,0:T(8,128)(2,1)S(1)}, u32[]{:S(2)}, u32[]{:S(2)}) collective-permute-start(bf16[128,1600]{1,0:T(8,128)(2,1)S(1)} %get-tuple-element.192), channel_id=1, source_target_pairs={{0,3},{1,2},{2,1},{3,0},{4,7},{5,6},{6,5},{7,4},{8,11},{9,10},{10,... | collective-permute-start | bytes 1228808 | tf_op jit(solution)/shard_map/ppermute | solution.py:25
  173.3 26.6 %collective-permute-start.17 = (bf16[128,1600]{1,0:T(8,128)(2,1)S(1)}, bf16[128,1600]{1,0:T(8,128)(2,1)S(1)}, u32[]{:S(2)}, u32[]{:S(2)}) collective-permute-start(bf16[128,1600]{1,0:T(8,128)(2,1)S(1)} %get-tuple-element.194.refs_0_.refs_10_), channel_id=1, source_target_pairs={{0,1},{1,0},{2,3},{3,2},{4,5},{5,4},{6,7},{7,6},{8,9},{9,8},{10,11... | collective-permute-start | bytes 1228808 | tf_op jit(solution)/shard_map/ppermute | solution.py:25
  174.9 35.7 %collective-permute-start.18 = (bf16[128,1600]{1,0:T(8,128)(2,1)S(1)}, bf16[128,1600]{1,0:T(8,128)(2,1)S(1)}, u32[]{:S(2)}, u32[]{:S(2)}) collective-permute-start(bf16[128,1600]{1,0:T(8,128)(2,1)S(1)} %get-tuple-element.194.refs_0_.refs_10_), channel_id=1, source_target_pairs={{0,2},{1,3},{2,0},{3,1},{4,6},{5,7},{6,4},{7,5},{8,10},{9,11},{10,... | collective-permute-start | bytes 1228808 | tf_op jit(solution)/shard_map/ppermute | solution.py:25
  181.6 29.8 %collective-permute-start.19 = (bf16[128,1600]{1,0:T(8,128)(2,1)S(1)}, bf16[128,1600]{1,0:T(8,128)(2,1)S(1)}, u32[]{:S(2)}, u32[]{:S(2)}) collective-permute-start(bf16[128,1600]{1,0:T(8,128)(2,1)S(1)} %get-tuple-element.194.refs_0_.refs_10_), channel_id=1, source_target_pairs={{0,3},{1,2},{2,1},{3,0},{4,7},{5,6},{6,5},{7,4},{8,11},{9,10},{10,... | collective-permute-start | bytes 1228808 | tf_op jit(solution)/shard_map/ppermute | solution.py:25
  193.7 38.7 %collective-permute-start.35 = (bf16[128,1600]{1,0:T(8,128)(2,1)}, bf16[128,1600]{1,0:T(8,128)(2,1)}, u32[]{:S(2)}, u32[]{:S(2)}) collective-permute-start(bf16[128,1600]{1,0:T(8,128)(2,1)} %get-tuple-element.216.refs_0_.refs_14_), channel_id=1, source_target_pairs={{0,1},{1,0},{2,3},{3,2},{4,5},{5,4},{6,7},{7,6},{8,9},{9,8},{10,11... | collective-permute-start | bytes 1228808 | tf_op jit(solution)/shard_map/ppermute | solution.py:25
  194.2 40.0 %collective-permute-start.36 = (bf16[128,1600]{1,0:T(8,128)(2,1)}, bf16[128,1600]{1,0:T(8,128)(2,1)}, u32[]{:S(2)}, u32[]{:S(2)}) collective-permute-start(bf16[128,1600]{1,0:T(8,128)(2,1)} %get-tuple-element.216.refs_0_.refs_14_), channel_id=1, source_target_pairs={{0,2},{1,3},{2,0},{3,1},{4,6},{5,7},{6,4},{7,5},{8,10},{9,11},{10,... | collective-permute-start | bytes 1228808 | tf_op jit(solution)/shard_map/ppermute | solution.py:25
  200.6 33.6 %collective-permute-start.37 = (bf16[128,1600]{1,0:T(8,128)(2,1)}, bf16[128,1600]{1,0:T(8,128)(2,1)}, u32[]{:S(2)}, u32[]{:S(2)}) collective-permute-start(bf16[128,1600]{1,0:T(8,128)(2,1)} %get-tuple-element.216.refs_0_.refs_14_), channel_id=1, source_target_pairs={{0,3},{1,2},{2,1},{3,0},{4,7},{5,6},{6,5},{7,4},{8,11},{9,10},{10,... | collective-permute-start | bytes 1228808 | tf_op jit(solution)/shard_map/ppermute | solution.py:25
  230.7 22.6 %collective-permute-start.20 = (bf16[128,1600]{1,0:T(8,128)(2,1)S(1)}, bf16[128,1600]{1,0:T(8,128)(2,1)S(1)}, u32[]{:S(2)}, u32[]{:S(2)}) collective-permute-start(bf16[128,1600]{1,0:T(8,128)(2,1)S(1)} %get-tuple-element.196), channel_id=1, source_target_pairs={{0,1},{1,0},{2,3},{3,2},{4,5},{5,4},{6,7},{7,6},{8,9},{9,8},{10,11... | collective-permute-start | bytes 1228808 | tf_op jit(solution)/shard_map/ppermute | solution.py:25
  231.2 24.0 %collective-permute-start.21 = (bf16[128,1600]{1,0:T(8,128)(2,1)S(1)}, bf16[128,1600]{1,0:T(8,128)(2,1)S(1)}, u32[]{:S(2)}, u32[]{:S(2)}) collective-permute-start(bf16[128,1600]{1,0:T(8,128)(2,1)S(1)} %get-tuple-element.197), channel_id=1, source_target_pairs={{0,2},{1,3},{2,0},{3,1},{4,6},{5,7},{6,4},{7,5},{8,10},{9,11},{10,... | collective-permute-start | bytes 1228808 | tf_op jit(solution)/shard_map/ppermute | solution.py:25
  232.4 22.8 %collective-permute-start.22 = (bf16[128,1600]{1,0:T(8,128)(2,1)S(1)}, bf16[128,1600]{1,0:T(8,128)(2,1)S(1)}, u32[]{:S(2)}, u32[]{:S(2)}) collective-permute-start(bf16[128,1600]{1,0:T(8,128)(2,1)S(1)} %get-tuple-element.198), channel_id=1, source_target_pairs={{0,3},{1,2},{2,1},{3,0},{4,7},{5,6},{6,5},{7,4},{8,11},{9,10},{10,... | collective-permute-start | bytes 1228808 | tf_op jit(solution)/shard_map/ppermute | solution.py:25
  257.5 25.2 %collective-permute-start.23 = (bf16[128,1600]{1,0:T(8,128)(2,1)}, bf16[128,1600]{1,0:T(8,128)(2,1)}, u32[]{:S(2)}, u32[]{:S(2)}) collective-permute-start(bf16[128,1600]{1,0:T(8,128)(2,1)} %get-tuple-element.200.refs_0_), channel_id=1, source_target_pairs={{0,1},{1,0},{2,3},{3,2},{4,5},{5,4},{6,7},{7,6},{8,9},{9,8},{10,11... | collective-permute-start | bytes 1228808 | tf_op jit(solution)/shard_map/ppermute | solution.py:25
  258.0 34.6 %collective-permute-start.24 = (bf16[128,1600]{1,0:T(8,128)(2,1)}, bf16[128,1600]{1,0:T(8,128)(2,1)}, u32[]{:S(2)}, u32[]{:S(2)}) collective-permute-start(bf16[128,1600]{1,0:T(8,128)(2,1)} %get-tuple-element.200.refs_0_), channel_id=1, source_target_pairs={{0,2},{1,3},{2,0},{3,1},{4,6},{5,7},{6,4},{7,5},{8,10},{9,11},{10,... | collective-permute-start | bytes 1228808 | tf_op jit(solution)/shard_map/ppermute | solution.py:25
  265.1 27.5 %collective-permute-start.25 = (bf16[128,1600]{1,0:T(8,128)(2,1)}, bf16[128,1600]{1,0:T(8,128)(2,1)}, u32[]{:S(2)}, u32[]{:S(2)}) collective-permute-start(bf16[128,1600]{1,0:T(8,128)(2,1)} %get-tuple-element.200.refs_0_), channel_id=1, source_target_pairs={{0,3},{1,2},{2,1},{3,0},{4,7},{5,6},{6,5},{7,4},{8,11},{9,10},{10,... | collective-permute-start | bytes 1228808 | tf_op jit(solution)/shard_map/ppermute | solution.py:25
  279.9 32.2 %collective-permute-start.41 = (bf16[128,1600]{1,0:T(8,128)(2,1)}, bf16[128,1600]{1,0:T(8,128)(2,1)}, u32[]{:S(2)}, u32[]{:S(2)}) collective-permute-start(bf16[128,1600]{1,0:T(8,128)(2,1)} %get-tuple-element.222.refs_0_.refs_4_), channel_id=1, source_target_pairs={{0,1},{1,0},{2,3},{3,2},{4,5},{5,4},{6,7},{7,6},{8,9},{9,8},{10,11... | collective-permute-start | bytes 1228808 | tf_op jit(solution)/shard_map/ppermute | solution.py:25
  281.4 32.3 %collective-permute-start.42 = (bf16[128,1600]{1,0:T(8,128)(2,1)}, bf16[128,1600]{1,0:T(8,128)(2,1)}, u32[]{:S(2)}, u32[]{:S(2)}) collective-permute-start(bf16[128,1600]{1,0:T(8,128)(2,1)} %get-tuple-element.222.refs_0_.refs_4_), channel_id=1, source_target_pairs={{0,2},{1,3},{2,0},{3,1},{4,6},{5,7},{6,4},{7,5},{8,10},{9,11},{10,... | collective-permute-start | bytes 1228808 | tf_op jit(solution)/shard_map/ppermute | solution.py:25
  282.7 31.0 %collective-permute-start.43 = (bf16[128,1600]{1,0:T(8,128)(2,1)}, bf16[128,1600]{1,0:T(8,128)(2,1)}, u32[]{:S(2)}, u32[]{:S(2)}) collective-permute-start(bf16[128,1600]{1,0:T(8,128)(2,1)} %get-tuple-element.222.refs_0_.refs_4_), channel_id=1, source_target_pairs={{0,3},{1,2},{2,1},{3,0},{4,7},{5,6},{6,5},{7,4},{8,11},{9,10},{10,... | collective-permute-start | bytes 1228808 | tf_op jit(solution)/shard_map/ppermute | solution.py:25
  310.9 22.6 %collective-permute-start.27 = (bf16[128,1600]{1,0:T(8,128)(2,1)S(1)}, bf16[128,1600]{1,0:T(8,128)(2,1)S(1)}, u32[]{:S(2)}, u32[]{:S(2)}) collective-permute-start(bf16[128,1600]{1,0:T(8,128)(2,1)S(1)} %get-tuple-element.203), channel_id=1, source_target_pairs={{0,2},{1,3},{2,0},{3,1},{4,6},{5,7},{6,4},{7,5},{8,10},{9,11},{10,... | collective-permute-start | bytes 1228808 | tf_op jit(solution)/shard_map/ppermute | solution.py:25
  335.8 25.1 %collective-permute-start.29 = (bf16[128,1600]{1,0:T(8,128)(2,1)}, bf16[128,1600]{1,0:T(8,128)(2,1)S(1)}, u32[]{:S(2)}, u32[]{:S(2)}) collective-permute-start(bf16[128,1600]{1,0:T(8,128)(2,1)} %get-tuple-element.206.refs_0_), channel_id=1, source_target_pairs={{0,1},{1,0},{2,3},{3,2},{4,5},{5,4},{6,7},{7,6},{8,9},{9,8},{10,11... | collective-permute-start | bytes 1228808 | tf_op jit(solution)/shard_map/ppermute | solution.py:25
  336.6 31.5 %collective-permute-start.30 = (bf16[128,1600]{1,0:T(8,128)(2,1)}, bf16[128,1600]{1,0:T(8,128)(2,1)}, u32[]{:S(2)}, u32[]{:S(2)}) collective-permute-start(bf16[128,1600]{1,0:T(8,128)(2,1)} %get-tuple-element.206.refs_0_), channel_id=1, source_target_pairs={{0,2},{1,3},{2,0},{3,1},{4,6},{5,7},{6,4},{7,5},{8,10},{9,11},{10,... | collective-permute-start | bytes 1228808 | tf_op jit(solution)/shard_map/ppermute | solution.py:25
  342.7 26.7 %collective-permute-start.31 = (bf16[128,1600]{1,0:T(8,128)(2,1)}, bf16[128,1600]{1,0:T(8,128)(2,1)}, u32[]{:S(2)}, u32[]{:S(2)}) collective-permute-start(bf16[128,1600]{1,0:T(8,128)(2,1)} %get-tuple-element.206.refs_0_), channel_id=1, source_target_pairs={{0,3},{1,2},{2,1},{3,0},{4,7},{5,6},{6,5},{7,4},{8,11},{9,10},{10,... | collective-permute-start | bytes 1228808 | tf_op jit(solution)/shard_map/ppermute | solution.py:25
  354.9 33.6 %collective-permute-start.47 = (bf16[128,1600]{1,0:T(8,128)(2,1)}, bf16[128,1600]{1,0:T(8,128)(2,1)}, u32[]{:S(2)}, u32[]{:S(2)}) collective-permute-start(bf16[128,1600]{1,0:T(8,128)(2,1)} %get-tuple-element.228.refs_0_.refs_4_), channel_id=1, source_target_pairs={{0,1},{1,0},{2,3},{3,2},{4,5},{5,4},{6,7},{7,6},{8,9},{9,8},{10,11... | collective-permute-start | bytes 1228808 | tf_op jit(solution)/shard_map/ppermute | solution.py:25
  356.2 32.3 %collective-permute-start.48 = (bf16[128,1600]{1,0:T(8,128)(2,1)}, bf16[128,1600]{1,0:T(8,128)(2,1)}, u32[]{:S(2)}, u32[]{:S(2)}) collective-permute-start(bf16[128,1600]{1,0:T(8,128)(2,1)} %get-tuple-element.228.refs_0_.refs_4_), channel_id=1, source_target_pairs={{0,2},{1,3},{2,0},{3,1},{4,6},{5,7},{6,4},{7,5},{8,10},{9,11},{10,... | collective-permute-start | bytes 1228808 | tf_op jit(solution)/shard_map/ppermute | solution.py:25
  361.8 26.8 %collective-permute-start.49 = (bf16[128,1600]{1,0:T(8,128)(2,1)}, bf16[128,1600]{1,0:T(8,128)(2,1)}, u32[]{:S(2)}, u32[]{:S(2)}) collective-permute-start(bf16[128,1600]{1,0:T(8,128)(2,1)} %get-tuple-element.228.refs_0_.refs_4_), channel_id=1, source_target_pairs={{0,3},{1,2},{2,1},{3,0},{4,7},{5,6},{6,5},{7,4},{8,11},{9,10},{10,... | collective-permute-start | bytes 1228808 | tf_op jit(solution)/shard_map/ppermute | solution.py:25
  387.2 32.9 %collective-permute-start.53 = (bf16[128,1600]{1,0:T(8,128)(2,1)}, bf16[128,1600]{1,0:T(8,128)(2,1)S(1)}, u32[]{:S(2)}, u32[]{:S(2)}) collective-permute-start(bf16[128,1600]{1,0:T(8,128)(2,1)} %get-tuple-element.240), channel_id=1, source_target_pairs={{0,1},{1,0},{2,3},{3,2},{4,5},{5,4},{6,7},{7,6},{8,9},{9,8},{10,11... | collective-permute-start | bytes 1228808 | tf_op jit(solution)/shard_map/ppermute | solution.py:25
  415.2 175.3 %reduce-scatter.18.cloned.1.call-start = ((), (), s32[]{:S(2)}) async-start(), calls=%async_computation.13 | async-start | bytes 5990400
  415.4 30.9 %collective-permute-start.54 = (bf16[128,1600]{1,0:T(8,128)(2,1)}, bf16[128,1600]{1,0:T(8,128)(2,1)S(1)}, u32[]{:S(2)}, u32[]{:S(2)}) collective-permute-start(bf16[128,1600]{1,0:T(8,128)(2,1)} %copy-done.147), channel_id=1, source_target_pairs={{0,2},{1,3},{2,0},{3,1},{4,6},{5,7},{6,4},{7,5},{8,10},{9,11},{10,... | collective-permute-start | bytes 1228808 | tf_op jit(solution)/shard_map/ppermute | solution.py:25
  416.6 30.4 %collective-permute-start.55 = (bf16[128,1600]{1,0:T(8,128)(2,1)}, bf16[128,1600]{1,0:T(8,128)(2,1)S(1)}, u32[]{:S(2)}, u32[]{:S(2)}) collective-permute-start(bf16[128,1600]{1,0:T(8,128)(2,1)} %copy-done.143), channel_id=1, source_target_pairs={{0,3},{1,2},{2,1},{3,0},{4,7},{5,6},{6,5},{7,4},{8,11},{9,10},{10,... | collective-permute-start | bytes 1228808 | tf_op jit(solution)/shard_map/ppermute | solution.py:25
  418.0 29.6 %collective-permute-start.56 = (bf16[128,1600]{1,0:T(8,128)(2,1)}, bf16[128,1600]{1,0:T(8,128)(2,1)S(1)}, u32[]{:S(2)}, u32[]{:S(2)}) collective-permute-start(bf16[128,1600]{1,0:T(8,128)(2,1)} %copy-done.148), channel_id=1, source_target_pairs={{0,1},{1,0},{2,3},{3,2},{4,5},{5,4},{6,7},{7,6},{8,9},{9,8},{10,11... | collective-permute-start | bytes 1228808 | tf_op jit(solution)/shard_map/ppermute | solution.py:25
  419.0 34.2 %collective-permute-start.57 = (bf16[128,1600]{1,0:T(8,128)(2,1)}, bf16[128,1600]{1,0:T(8,128)(2,1)S(1)}, u32[]{:S(2)}, u32[]{:S(2)}) collective-permute-start(bf16[128,1600]{1,0:T(8,128)(2,1)} %copy-done.145), channel_id=1, source_target_pairs={{0,2},{1,3},{2,0},{3,1},{4,6},{5,7},{6,4},{7,5},{8,10},{9,11},{10,... | collective-permute-start | bytes 1228808 | tf_op jit(solution)/shard_map/ppermute | solution.py:25
  420.1 33.1 %collective-permute-start.58 = (bf16[128,1600]{1,0:T(8,128)(2,1)S(1)}, bf16[128,1600]{1,0:T(8,128)(2,1)S(1)}, u32[]{:S(2)}, u32[]{:S(2)}) collective-permute-start(bf16[128,1600]{1,0:T(8,128)(2,1)S(1)} %copy-done.142), channel_id=1, source_target_pairs={{0,3},{1,2},{2,1},{3,0},{4,7},{5,6},{6,5},{7,4},{8,11},{9,10},{10,... | collective-permute-start | bytes 1228808 | tf_op jit(solution)/shard_map/ppermute | solution.py:25
  446.3 34.8 %collective-permute-start.50 = (bf16[128,1600]{1,0:T(8,128)(2,1)}, bf16[128,1600]{1,0:T(8,128)(2,1)}, u32[]{:S(2)}, u32[]{:S(2)}) collective-permute-start(bf16[128,1600]{1,0:T(8,128)(2,1)} %get-tuple-element.232), channel_id=1, source_target_pairs={{0,1},{1,0},{2,3},{3,2},{4,5},{5,4},{6,7},{7,6},{8,9},{9,8},{10,11... | collective-permute-start | bytes 1228808 | tf_op jit(solution)/shard_map/ppermute | solution.py:25
  447.0 35.5 %collective-permute-start.51 = (bf16[128,1600]{1,0:T(8,128)(2,1)}, bf16[128,1600]{1,0:T(8,128)(2,1)}, u32[]{:S(2)}, u32[]{:S(2)}) collective-permute-start(bf16[128,1600]{1,0:T(8,128)(2,1)} %get-tuple-element.233), channel_id=1, source_target_pairs={{0,2},{1,3},{2,0},{3,1},{4,6},{5,7},{6,4},{7,5},{8,10},{9,11},{10,... | collective-permute-start | bytes 1228808 | tf_op jit(solution)/shard_map/ppermute | solution.py:25
  447.6 34.9 %collective-permute-start.52 = (bf16[128,1600]{1,0:T(8,128)(2,1)}, bf16[128,1600]{1,0:T(8,128)(2,1)}, u32[]{:S(2)}, u32[]{:S(2)}) collective-permute-start(bf16[128,1600]{1,0:T(8,128)(2,1)} %get-tuple-element.234), channel_id=1, source_target_pairs={{0,3},{1,2},{2,1},{3,0},{4,7},{5,6},{6,5},{7,4},{8,11},{9,10},{10,... | collective-permute-start | bytes 1228808 | tf_op jit(solution)/shard_map/ppermute | solution.py:25
  490.6 197.1 %reduce-scatter.12.cloned.1.call-start = ((), (), s32[]{:S(2)}) async-start(), calls=%async_computation.10 | async-start | bytes 6451200 | tf_op jit(solution)/shard_map/reduce_scatter | solution.py:735
  492.1 24.3 %collective-permute-start.61 = (bf16[128,1600]{1,0:T(8,128)(2,1)}, bf16[128,1600]{1,0:T(8,128)(2,1)S(1)}, u32[]{:S(2)}, u32[]{:S(2)}) collective-permute-start(bf16[128,1600]{1,0:T(8,128)(2,1)} %get-tuple-element.251.refs_0_.refs_10_), channel_id=1, source_target_pairs={{0,3},{1,2},{2,1},{3,0},{4,7},{5,6},{6,5},{7,4},{8,11},{9,10},{10,... | collective-permute-start | bytes 1228808 | tf_op jit(solution)/shard_map/ppermute | solution.py:25
  504.5 29.0 %collective-permute-start.68 = (bf16[128,1600]{1,0:T(8,128)(2,1)S(1)}, bf16[128,1600]{1,0:T(8,128)(2,1)S(1)}, u32[]{:S(2)}, u32[]{:S(2)}) collective-permute-start(bf16[128,1600]{1,0:T(8,128)(2,1)S(1)} %get-tuple-element.266.refs_0_.refs_14_), channel_id=1, source_target_pairs={{0,1},{1,0},{2,3},{3,2},{4,5},{5,4},{6,7},{7,6},{8,9},{9,8},{10,11... | collective-permute-start | bytes 1228808 | tf_op jit(solution)/shard_map/ppermute | solution.py:25
  505.4 31.5 %collective-permute-start.69 = (bf16[128,1600]{1,0:T(8,128)(2,1)S(1)}, bf16[128,1600]{1,0:T(8,128)(2,1)S(1)}, u32[]{:S(2)}, u32[]{:S(2)}) collective-permute-start(bf16[128,1600]{1,0:T(8,128)(2,1)S(1)} %get-tuple-element.266.refs_0_.refs_14_), channel_id=1, source_target_pairs={{0,2},{1,3},{2,0},{3,1},{4,6},{5,7},{6,4},{7,5},{8,10},{9,11},{10,... | collective-permute-start | bytes 1228808 | tf_op jit(solution)/shard_map/ppermute | solution.py:25
  506.9 30.0 %collective-permute-start.70 = (bf16[128,1600]{1,0:T(8,128)(2,1)S(1)}, bf16[128,1600]{1,0:T(8,128)(2,1)S(1)}, u32[]{:S(2)}, u32[]{:S(2)}) collective-permute-start(bf16[128,1600]{1,0:T(8,128)(2,1)S(1)} %get-tuple-element.266.refs_0_.refs_14_), channel_id=1, source_target_pairs={{0,3},{1,2},{2,1},{3,0},{4,7},{5,6},{6,5},{7,4},{8,11},{9,10},{10,... | collective-permute-start | bytes 1228808 | tf_op jit(solution)/shard_map/ppermute | solution.py:25
  533.3 36.0 %collective-permute-start.62 = (bf16[128,1600]{1,0:T(8,128)(2,1)}, bf16[128,1600]{1,0:T(8,128)(2,1)}, u32[]{:S(2)}, u32[]{:S(2)}) collective-permute-start(bf16[128,1600]{1,0:T(8,128)(2,1)} %get-tuple-element.255), channel_id=1, source_target_pairs={{0,1},{1,0},{2,3},{3,2},{4,5},{5,4},{6,7},{7,6},{8,9},{9,8},{10,11... | collective-permute-start | bytes 1228808 | tf_op jit(solution)/shard_map/ppermute | solution.py:25
  533.4 38.8 %collective-permute-start.63 = (bf16[128,1600]{1,0:T(8,128)(2,1)}, bf16[128,1600]{1,0:T(8,128)(2,1)}, u32[]{:S(2)}, u32[]{:S(2)}) collective-permute-start(bf16[128,1600]{1,0:T(8,128)(2,1)} %get-tuple-element.256), channel_id=1, source_target_pairs={{0,2},{1,3},{2,0},{3,1},{4,6},{5,7},{6,4},{7,5},{8,10},{9,11},{10,... | collective-permute-start | bytes 1228808 | tf_op jit(solution)/shard_map/ppermute | solution.py:25
  533.5 38.7 %collective-permute-start.64 = (bf16[128,1600]{1,0:T(8,128)(2,1)}, bf16[128,1600]{1,0:T(8,128)(2,1)}, u32[]{:S(2)}, u32[]{:S(2)}) collective-permute-start(bf16[128,1600]{1,0:T(8,128)(2,1)} %get-tuple-element.257), channel_id=1, source_target_pairs={{0,3},{1,2},{2,1},{3,0},{4,7},{5,6},{6,5},{7,4},{8,11},{9,10},{10,... | collective-permute-start | bytes 1228808 | tf_op jit(solution)/shard_map/ppermute | solution.py:25
  578.9 185.6 %reduce-scatter.20.cloned.1.call-start = ((), (), s32[]{:S(2)}) async-start(), calls=%async_computation.14 | async-start | bytes 11520000
  647.4 180.9 %reduce-scatter.14.cloned.1.call-start = ((), (), s32[]{:S(2)}) async-start(), calls=%async_computation.11 | async-start | bytes 6451200 | tf_op jit(solution)/shard_map/reduce_scatter | solution.py:735
  651.2 23.3 %collective-permute-start.89 = (bf16[128,1600]{1,0:T(8,128)(2,1)}, bf16[128,1600]{1,0:T(8,128)(2,1)S(1)}, u32[]{:S(2)}, u32[]{:S(2)}) collective-permute-start(bf16[128,1600]{1,0:T(8,128)(2,1)} %copy-done.131), channel_id=1, source_target_pairs={{0,1},{1,0},{2,3},{3,2},{4,5},{5,4},{6,7},{7,6},{8,9},{9,8},{10,11... | collective-permute-start | bytes 1228808 | tf_op jit(solution)/shard_map/ppermute | solution.py:25
  653.1 22.9 %collective-permute-start.90 = (bf16[128,1600]{1,0:T(8,128)(2,1)}, bf16[128,1600]{1,0:T(8,128)(2,1)S(1)}, u32[]{:S(2)}, u32[]{:S(2)}) collective-permute-start(bf16[128,1600]{1,0:T(8,128)(2,1)} %copy-done.130), channel_id=1, source_target_pairs={{0,2},{1,3},{2,0},{3,1},{4,6},{5,7},{6,4},{7,5},{8,10},{9,11},{10,... | collective-permute-start | bytes 1228808 | tf_op jit(solution)/shard_map/ppermute | solution.py:25
  673.4 22.7 %collective-permute-start.78 = (bf16[128,1600]{1,0:T(8,128)(2,1)}, bf16[128,1600]{1,0:T(8,128)(2,1)}, u32[]{:S(2)}, u32[]{:S(2)}) collective-permute-start(bf16[128,1600]{1,0:T(8,128)(2,1)} %get-tuple-element.282.refs_0_.refs_4_), channel_id=1, source_target_pairs={{0,2},{1,3},{2,0},{3,1},{4,6},{5,7},{6,4},{7,5},{8,10},{9,11},{10,... | collective-permute-start | bytes 1228808 | tf_op jit(solution)/shard_map/ppermute | solution.py:25
  674.5 23.0 %collective-permute-start.79 = (bf16[128,1600]{1,0:T(8,128)(2,1)}, bf16[128,1600]{1,0:T(8,128)(2,1)}, u32[]{:S(2)}, u32[]{:S(2)}) collective-permute-start(bf16[128,1600]{1,0:T(8,128)(2,1)} %get-tuple-element.282.refs_0_.refs_4_), channel_id=1, source_target_pairs={{0,3},{1,2},{2,1},{3,0},{4,7},{5,6},{6,5},{7,4},{8,11},{9,10},{10,... | collective-permute-start | bytes 1228808 | tf_op jit(solution)/shard_map/ppermute | solution.py:25
  685.3 34.5 %collective-permute-start.92 = (bf16[128,1600]{1,0:T(8,128)(2,1)}, bf16[128,1600]{1,0:T(8,128)(2,1)S(1)}, u32[]{:S(2)}, u32[]{:S(2)}) collective-permute-start(bf16[128,1600]{1,0:T(8,128)(2,1)} %get-tuple-element.308.refs_0_.refs_8_), channel_id=1, source_target_pairs={{0,1},{1,0},{2,3},{3,2},{4,5},{5,4},{6,7},{7,6},{8,9},{9,8},{10,11... | collective-permute-start | bytes 1228808 | tf_op jit(solution)/shard_map/ppermute | solution.py:25
  686.4 34.3 %collective-permute-start.93 = (bf16[128,1600]{1,0:T(8,128)(2,1)}, bf16[128,1600]{1,0:T(8,128)(2,1)}, u32[]{:S(2)}, u32[]{:S(2)}) collective-permute-start(bf16[128,1600]{1,0:T(8,128)(2,1)} %get-tuple-element.308.refs_0_.refs_8_), channel_id=1, source_target_pairs={{0,2},{1,3},{2,0},{3,1},{4,6},{5,7},{6,4},{7,5},{8,10},{9,11},{10,... | collective-permute-start | bytes 1228808 | tf_op jit(solution)/shard_map/ppermute | solution.py:25
  691.0 29.7 %collective-permute-start.94 = (bf16[128,1600]{1,0:T(8,128)(2,1)}, bf16[128,1600]{1,0:T(8,128)(2,1)S(1)}, u32[]{:S(2)}, u32[]{:S(2)}) collective-permute-start(bf16[128,1600]{1,0:T(8,128)(2,1)} %get-tuple-element.308.refs_0_.refs_8_), channel_id=1, source_target_pairs={{0,3},{1,2},{2,1},{3,0},{4,7},{5,6},{6,5},{7,4},{8,11},{9,10},{10,... | collective-permute-start | bytes 1228808 | tf_op jit(solution)/shard_map/ppermute | solution.py:25
  717.2 24.8 %collective-permute-start.86 = (bf16[128,1600]{1,0:T(8,128)(2,1)S(1)}, bf16[128,1600]{1,0:T(8,128)(2,1)S(1)}, u32[]{:S(2)}, u32[]{:S(2)}) collective-permute-start(bf16[128,1600]{1,0:T(8,128)(2,1)S(1)} %get-tuple-element.299), channel_id=1, source_target_pairs={{0,1},{1,0},{2,3},{3,2},{4,5},{5,4},{6,7},{7,6},{8,9},{9,8},{10,11... | collective-permute-start | bytes 1228808 | tf_op jit(solution)/shard_map/ppermute | solution.py:25
  718.5 37.6 %collective-permute-start.87 = (bf16[128,1600]{1,0:T(8,128)(2,1)}, bf16[128,1600]{1,0:T(8,128)(2,1)}, u32[]{:S(2)}, u32[]{:S(2)}) collective-permute-start(bf16[128,1600]{1,0:T(8,128)(2,1)} %get-tuple-element.300), channel_id=1, source_target_pairs={{0,2},{1,3},{2,0},{3,1},{4,6},{5,7},{6,4},{7,5},{8,10},{9,11},{10,... | collective-permute-start | bytes 1228808 | tf_op jit(solution)/shard_map/ppermute | solution.py:25
  719.8 36.3 %collective-permute-start.88 = (bf16[128,1600]{1,0:T(8,128)(2,1)}, bf16[128,1600]{1,0:T(8,128)(2,1)}, u32[]{:S(2)}, u32[]{:S(2)}) collective-permute-start(bf16[128,1600]{1,0:T(8,128)(2,1)} %get-tuple-element.301), channel_id=1, source_target_pairs={{0,3},{1,2},{2,1},{3,0},{4,7},{5,6},{6,5},{7,4},{8,11},{9,10},{10,... | collective-permute-start | bytes 1228808 | tf_op jit(solution)/shard_map/ppermute | solution.py:25
  802.3 26.1 %collective-permute-start.108 = (bf16[200,3200]{1,0:T(8,128)(2,1)}, bf16[200,3200]{1,0:T(8,128)(2,1)}, u32[]{:S(2)}, u32[]{:S(2)}) collective-permute-start(bf16[200,3200]{1,0:T(8,128)(2,1)} %broadcast_select_fusion.6), channel_id=1, source_target_pairs={{0,16},{16,0},{1,17},{17,1},{2,18},{18,2},{3,19},{19,3},{4,20},{20... | collective-permute-start | bytes 3840008 | tf_op jit(solution)/shard_map/ppermute | solution.py:25
  (287 other events, 2519.2 us)
Sparse Core Ops, SparseCore 0:
  32.8 61.5 all-gather.4
  96.6 99.4 all-gather.8
  198.3 58.5 all-gather.10
  259.0 99.4 all-gather.6
  415.3 61.1 reduce-scatter.15
  490.7 62.9 reduce-scatter.17
  579.0 63.5 reduce-scatter.11
  647.5 106.9 reduce-scatter.19
  764.6 63.5 reduce-scatter.13

commit v3 on v2

--- a/solution.py
+++ b/solution.py
@@ -61,14 +61,26 @@
     return jnp.where(col_index == 0, 0, HD - (HD // count) * col_index)
 
 
-def align_heads(columns, col_index):
+def next_column(value):
     count = lax.axis_size("col")
+    return lax.ppermute(value, "col", [(i + 1, i) for i in range(count - 1)])
+
+
+def next_column_across(value):
+    count = lax.axis_size("col")
+    pairs = [
+        ((1 - s) * count + i + 1, s * count + i) for s in range(2) for i in range(count - 1)
+    ]
+    return lax.ppermute(value, ("section", "col"), pairs)
+
+
+def join_heads(columns, following, col_index):
     per, wide = head_share()
     lead = columns.shape[:-1]
-    after = lax.ppermute(columns[..., :HD], "col", [(i + 1, i) for i in range(count - 1)])
-    own = columns.shape[-1]
-    pad = max(0, wide + HD - own - HD)
-    extended = jnp.concatenate([columns, after, jnp.zeros(lead + (pad,), columns.dtype)], axis=-1)
+    pad = max(0, wide - columns.shape[-1])
+    extended = jnp.concatenate(
+        [columns, following, jnp.zeros(lead + (pad,), columns.dtype)], axis=-1
+    )
     moved = lax.dynamic_slice_in_dim(
         extended, head_shift(col_index), wide, axis=extended.ndim - 1
     )
@@ -76,34 +88,39 @@
     return jnp.where(jnp.arange(wide) < limit, moved, jnp.zeros((), moved.dtype))
 
 
-def unalign_heads(columns, width, col_index):
-    count = lax.axis_size("col")
-    per, wide = head_share()
-    shift = head_shift(col_index)
-    begin = width - shift
+def align_heads(columns, col_index):
+    return join_heads(columns, next_column(columns[..., :HD]), col_index)
+
+
+def tail_columns(columns, width, col_index):
+    begin = width - head_shift(col_index)
     padded = jnp.concatenate(
         [columns, jnp.zeros(columns.shape[:-1] + (HD,), columns.dtype)], axis=-1
     )
-    tail = lax.dynamic_slice_in_dim(padded, begin, HD, axis=columns.ndim - 1)
-    before = lax.ppermute(tail, "col", [(i, i + 1) for i in range(count - 1)])
-    joined = jnp.concatenate([before, columns], axis=-1)
-    rest = lax.dynamic_slice_in_dim(
-        jnp.concatenate(
-            [joined, jnp.zeros(columns.shape[:-1] + (HD,), columns.dtype)], axis=-1
-        ),
-        HD - shift,
-        width,
-        axis=columns.ndim - 1,
-    )
-    front = lax.dynamic_slice_in_dim(
-        jnp.concatenate(
-            [before, jnp.zeros(columns.shape[:-1] + (width - HD,), columns.dtype)], axis=-1
-        ),
-        0,
-        width,
-        axis=columns.ndim - 1,
-    )
+    return lax.dynamic_slice_in_dim(padded, begin, HD, axis=columns.ndim - 1)
+
+
+def split_heads(columns, before, width, col_index):
+    shift = head_shift(col_index)
+    pad = jnp.zeros(columns.shape[:-1] + (HD,), columns.dtype)
+    joined = jnp.concatenate([before, columns, pad], axis=-1)
+    rest = lax.dynamic_slice_in_dim(joined, HD - shift, width, axis=columns.ndim - 1)
+    fill = jnp.zeros(columns.shape[:-1] + (width - HD,), columns.dtype)
+    front = jnp.concatenate([before, fill], axis=-1)
     return jnp.where(jnp.arange(width) < shift, front, rest)
+
+
+def previous_column(value):
+    count = lax.axis_size("col")
+    return lax.ppermute(value, "col", [(i, i + 1) for i in range(count - 1)])
+
+
+def previous_column_across(value):
+    count = lax.axis_size("col")
+    pairs = [
+        ((1 - s) * count + i, s * count + i + 1) for s in range(2) for i in range(count - 1)
+    ]
+    return lax.ppermute(value, ("section", "col"), pairs)
 
 
 def contract(left, right, left_dim, right_dim):
@@ -133,26 +150,23 @@
 
 
 class Matrix:
-    def __init__(self, array, first, stride, block, count):
-        self.array, self.first, self.stride = array, first, stride
-        self.block, self.count = block, count
+    def __init__(self, array, runs):
+        self.array, self.runs = array, runs
 
     @property
     def dims(self):
-        return (self.block * self.count, self.array.shape[1])
+        return (sum(run[2] for run in self.runs), self.array.shape[1])
 
     def copies(self, source, target, sems):
         return [
             pltpu.make_async_copy(
-                source.at[pl.ds(self.first + self.stride * i, self.block), :],
-                target.at[pl.ds(self.block * i, self.block), :],
-                sems.at[i],
+                source.at[pl.ds(begin, size), :], target.at[pl.ds(to, size), :], sems.at[i]
             )
-            for i in range(self.count)
+            for i, (begin, to, size) in enumerate(self.runs)
         ]
 
     def scratch(self):
-        return [pltpu.VMEM(self.dims, BF), pltpu.SemaphoreType.DMA((self.count,))]
+        return [pltpu.VMEM(self.dims, BF), pltpu.SemaphoreType.DMA((len(self.runs),))]
 
 
 def fetch(matrices, sources, held):
@@ -246,7 +260,7 @@
     return result[0], result[1], result[2], result[3:]
 
 
-def heads_backward(pieces, first, second, qkv, lse, mask, heads, parts):
+def heads_backward(pieces, first, second, qkv, lse, mask, heads, parts, weight):
     rows = mask.shape[0]
     features = pieces[0].shape[1]
     wide = heads * HD
@@ -308,7 +322,7 @@
         [pltpu.VMEM((rows, features), BF), pltpu.VMEM((rows, wide), BF)]
         + first.scratch()
         + second.scratch(),
-        flops=8 * rows * features * wide + 40 * rows * rows * wide,
+        flops=8 * rows * features * wide + 40 * rows * rows * wide + weight,
         exps=rows * rows * heads,
         anywhere=(count, count + 1),
     )
@@ -323,6 +337,57 @@
         1.0 + 3.0 * cubic_weight * inputs * inputs
     )
     return value.astype(BF), slope.astype(BF)
+
+
+def feed_up(pieces, up, bias):
+    rows = sum(piece.shape[0] for piece in pieces)
+    features = pieces[0].shape[1]
+    hidden = up.dims[1]
+    count = len(pieces)
+
+    def kernel(*refs):
+        piece_refs, refs = refs[:count], refs[count:]
+        up_hbm, bias_ref, hidden_ref, slope_ref, whole, up_ref, up_sem = refs
+        (wait,) = fetch((up,), (up_hbm,), ((up_ref, up_sem),))
+        stack_pieces(piece_refs, whole)
+        finish(wait)
+        for begin in range(0, rows, CHUNK):
+            some = slice(begin, begin + CHUNK)
+            value, slope = gelu_both(contract(whole[some, :], up_ref[...], 1, 0) + bias_ref[...])
+            hidden_ref[some, :] = value
+            slope_ref[some, :] = slope
+
+    return call(
+        kernel,
+        [shape((rows, hidden), BF)] * 2,
+        list(pieces) + [up.array, bias],
+        [pltpu.VMEM((rows, features), BF)] + up.scratch(),
+        flops=2 * rows * features * hidden,
+        anywhere=(count,),
+    )
+
+
+def feed_down(hidden, down, parts):
+    rows, units = hidden.shape
+    features = down.dims[0]
+
+    def kernel(*refs):
+        hidden_ref, down_hbm = refs[:2]
+        part_refs, (down_ref, down_sem) = refs[2 : 2 + parts], refs[2 + parts :]
+        (wait,) = fetch((down,), (down_hbm,), ((down_ref, down_sem),))
+        finish(wait)
+        for begin in range(0, rows, CHUNK):
+            some = slice(begin, begin + CHUNK)
+            store_parts(part_refs, begin, contract(hidden_ref[some, :], down_ref[...], 1, 1))
+
+    return call(
+        kernel,
+        [shape((rows // parts, features), BF)] * parts,
+        [hidden, down.array],
+        down.scratch(),
+        flops=2 * rows * features * units,
+        anywhere=(1,),
+    )
 
 
 def feed_forward(pieces, up, down, bias, parts):
@@ -593,32 +658,38 @@
     features = width * cols
     is_first = section == 0
 
-    def pairs(one, two):
-        keep = jnp.where(is_first, one, two)
-        got = swap_section(jnp.where(is_first, two, one))
-        return jnp.where(is_first, keep, got), jnp.where(is_first, got, keep)
+    def gather_block(own_part):
+        full = lax.all_gather(own_part, ("row", "section"), axis=0, tiled=True)
+        return full, own_part.shape[0], full.shape[0] // (2 * own_part.shape[0])
 
     def gather_pair(own_part):
-        full = lax.all_gather(own_part, ("row", "section"), axis=0, tiled=True)
-        block = own_part.shape[0]
-        count = full.shape[0] // (2 * block)
+        full, block, count = gather_block(own_part)
         if block % 16 == 0:
-            return (
-                Matrix(full, 0, 2 * block, block, count),
-                Matrix(full, block, 2 * block, block, count),
+            return tuple(
+                Matrix(full, [((2 * i + k) * block, i * block, block) for i in range(count)])
+                for k in range(2)
             )
         full = full.reshape(count, 2, block, -1)
-        one = full[:, 0].reshape(count * block, -1)
-        two = full[:, 1].reshape(count * block, -1)
-        return Matrix(one, 0, 0, count * block, 1), Matrix(two, 0, 0, count * block, 1)
-
-    heads_pack = align_heads(
-        jnp.stack([query_weight[0], key_weight[0], value_weight[0], out_weight[0].T]), col
-    )
-    heads_parts = pairs(
-        jnp.concatenate([heads_pack[0], heads_pack[1]], axis=1),
-        jnp.concatenate([heads_pack[2], heads_pack[3]], axis=1),
-    )
+        both = [full[:, k].reshape(count * block, -1) for k in range(2)]
+        return tuple(Matrix(one, [(0, 0, count * block)]) for one in both)
+
+    pair_one = jnp.stack([query_weight[0], key_weight[0]])
+    pair_two = jnp.stack([value_weight[0], out_weight[0].T])
+    keep = jnp.where(is_first, pair_one, pair_two)
+    send = jnp.where(is_first, pair_two, pair_one)
+    got = swap_section(send)
+    keep_after = next_column(keep[..., :HD])
+    got_after = next_column_across(send[..., :HD])
+    keep = join_heads(keep, keep_after, col)
+    got = join_heads(got, got_after, col)
+    heads_parts = [
+        jnp.concatenate([item[0], item[1]], axis=1)
+        for item in (jnp.where(is_first, keep, got), jnp.where(is_first, got, keep))
+    ]
+    def exchange_wide(up_own, down_own):
+        keep = jnp.where(is_first, up_own, down_own)
+        got = swap_section(jnp.where(is_first, down_own, up_own))
+        return jnp.where(is_first, keep, got), jnp.where(is_first, got, keep)
 
     small_wide = jnp.stack(
         [first_gain[0], first_bias[0], out_bias[0], second_gain[0], second_bias[0], down_bias[0]]
@@ -649,11 +720,11 @@
     link = Link()
     input_own = lax.dynamic_slice_in_dim(block_input, section * mine, mine, 0)
     cotangent_own = lax.dynamic_slice_in_dim(out_cotangent, section * mine, mine, 0)
-    early = link.spread(input_own[0])
-    late_own = jnp.concatenate([input_own[1:], cotangent_own], axis=0)
-    late = link.spread(after(late_own, small_layers, early))
-
-    wide_parts = pairs(*after((up_weight[0], down_weight[0]), early))
+    early = link.spread(input_own)
+    late = link.spread(after(cotangent_own, early))
+    wide_first, wide_second = exchange_wide(
+        *after((up_weight[0], down_weight[0]), heads_parts, early, small_layers)
+    )
 
     blocks = group_order.shape[0]
     group_rows = L // blocks
@@ -670,12 +741,15 @@
     mask = jnp.where(allowed, 0.0, -jnp.inf).astype(F32)
 
     everyone = range(mine)
-    weights = [gather_pair(heads_parts[0]) + gather_pair(wide_parts[0])]
-    weights.append(gather_pair(heads_parts[1]) + gather_pair(wide_parts[1]))
+    weights = [gather_pair(heads_parts[0]) + gather_pair(wide_first)]
+    weights.append(gather_pair(heads_parts[1]) + gather_pair(wide_second))
     saved = [[None] * mine, [None] * mine]
-    turned_input = turn_blocks(early, smalls[0][0][0], smalls[0][0][1])
-    streams = [turned_input[1]]
-    pieces = [[turned_input[0]]]
+    turned_inputs = [
+        turn_blocks([item[i] for item in early], smalls[0][0][0], smalls[0][0][1])
+        for i in range(mine)
+    ]
+    streams = [item[1] for item in turned_inputs]
+    pieces = [[item[0]] for item in turned_inputs]
     for layer in range(2):
         vectors, qkv_shift, up_shift = smalls[layer]
         gain_one, bias_one, out_shift, gain_two, bias_two, down_shift = vectors
@@ -687,16 +761,9 @@
             )
             begun.append((qkv, attended, lse, link.exchange(parts)))
             if layer == 0 and batch == 0:
-                late = after(late, lse)
-                for i in range(1, mine):
-                    turned_input = turn_blocks(
-                        [item[i - 1] for item in late], smalls[0][0][0], smalls[0][0][1]
-                    )
-                    streams.append(turned_input[1])
-                    pieces.append([turned_input[0]])
+                streams = after(streams, late)
                 cotangents = [
-                    turn_blocks([item[mine - 1 + i] for item in late], None, None)
-                    for i in range(mine)
+                    turn_blocks([item[i] for item in late], None, None) for i in range(mine)
                 ]
         middles = []
         for batch in everyone:
@@ -707,11 +774,14 @@
         terms = []
         for batch in everyone:
             middle, twos = middles[batch]
-            hidden, slope, parts = feed_forward(twos, up, down, up_shift, cols)
+            if layer == 0:
+                hidden, slope, parts = feed_forward(twos, up, down, up_shift, cols)
+                terms.append(link.exchange(parts))
+            else:
+                hidden, slope = feed_up(twos, up, up_shift)
             saved[layer][batch] = (
                 streams[batch], pieces[batch], *begun[batch][:3], middle, twos, hidden, slope,
             )
-            terms.append(link.exchange(parts))
         if layer == 0:
             streams, pieces = [], []
             for batch in everyone:
@@ -720,11 +790,6 @@
                 )
                 streams.append(stream)
                 pieces.append(link.spread(normed))
-        else:
-            last_terms = terms
-            finals = [
-                add_and_turn(terms[batch], middles[batch][0], down_shift) for batch in everyone
-            ]
 
     def to_features(pair):
         blocks_out = jnp.stack([item.reshape(cols, width, own) for item in pair], axis=1)
@@ -762,8 +827,6 @@
         for batch in everyone:
             slope = saved[layer][batch][8]
             slope = after(slope, down_grad if layer == 1 else first_sum)
-            if layer == 1 and batch == mine - 1:
-                slope = after(slope, last_terms)
             hidden_grad, hidden_sum, parts = feed_backward(ups[batch], up, down, slope, cols)
             hidden_grads.append(hidden_grad)
             up_sums.append(hidden_sum[0])
@@ -782,7 +845,8 @@
             if layer == 1:
                 middle = after(middle, up_grad)
             middle_grad, half, second_sums = norm_backward(
-                terms[batch], middle, bases[batch], gain_two, False, layer * 15000000000
+                terms[batch], middle, bases[batch], gain_two, False,
+                layer * 15000000000 + (1 - layer) * 15000000000,
             )
             middle_grads.append(middle_grad)
             seconds.append(second_sums)
@@ -793,7 +857,8 @@
             if layer == 0:
                 lse = after(lse, wide_grad, reduced[1][2])
             qkv_grad, head_sum, parts = heads_backward(
-                mids[batch], first, second, qkv, lse, mask, heads, cols
+                mids[batch], first, second, qkv, lse, mask, heads, cols,
+                (1 - layer) * 15000000000,
             )
             qkv_grads.append(qkv_grad)
             head_sums.append(head_sum.reshape(-1))
@@ -834,9 +899,16 @@
         bases = next_bases
         ups = next_ups
 
-    both = to_features(turned + finals)
-    grads, outputs = both[:mine], both[mine:]
-
+
+    last_parts = [
+        feed_down(after(saved[1][batch][7], turned), weights[1][3], cols) for batch in everyone
+    ]
+    finals = []
+    for batch in everyone:
+        terms = link.exchange(last_parts[batch])
+        finals.append(add_and_turn(terms, saved[1][batch][5], smalls[1][0][5]))
+
+    wide_sums = after(wide_sums, last_parts)
     wide_both = jnp.stack(wide_sums).reshape(2, 6, cols, width)
     wide_here = lax.dynamic_index_in_dim(wide_both, col, 2, keepdims=False)
     for j in range(1, cols):
@@ -853,8 +925,9 @@
         small_own = small_own + xor_step(small_own, "row", step)
         step *= 2
     small_out = small_own[: 6 * width].reshape(6, width)
-    head_out = unalign_heads(
-        small_own[6 * width : 6 * width + 2 * wide].reshape(2, wide), width, col
+    head_out = small_own[6 * width : 6 * width + 2 * wide].reshape(2, wide)
+    head_out = split_heads(
+        head_out, previous_column(tail_columns(head_out, width, col)), width, col
     )
     up_bias_grad = small_own[6 * width + 2 * wide :]
 
@@ -868,11 +941,23 @@
     wide_out = settle(reduced[0][0], reduced[1][0])
     down_out = wide_out[:, : wide_out.shape[1] // 2].astype(F32)
     up_out = wide_out[:, wide_out.shape[1] // 2 :].astype(F32)
-    heads_out = settle(reduced[0][2], reduced[1][2])
-    heads_out = unalign_heads(
-        jnp.stack([heads_out[:, i * wide : (i + 1) * wide] for i in range(4)]), width, col
+
+    def by_matrix(flat):
+        return jnp.stack([flat[:, i * wide : (i + 1) * wide] for i in range(4)])
+
+    keep = by_matrix(jnp.where(is_first, reduced[0][2], reduced[1][2]))
+    send = by_matrix(jnp.where(is_first, reduced[1][2], reduced[0][2]))
+    got = swap_section(send)
+    keep_before = previous_column(tail_columns(keep, width, col))
+    got_before = previous_column_across(tail_columns(send, width, col))
+    keep = split_heads(keep, keep_before, width, col)
+    got = split_heads(got, got_before, width, col)
+    heads_out = jnp.concatenate(
+        [jnp.where(is_first, keep, got), jnp.where(is_first, got, keep)], axis=1
     ).astype(F32)
 
+    both = to_features(turned + finals)
+    grads, outputs = both[:mine], both[mine:]
     got = swap_section(jnp.where(is_first, outputs, grads))
     keep = jnp.where(is_first, grads, outputs)
     boundary = jnp.concatenate(

time: 863 us -> 866 us (level)
  waiting for transfers between devices: 239 us -> 217 us
  starting transfers between devices: 130 us -> 147 us
    reduce_scatter x2, waiting for transfers between devices: 23.2 us -> 0.02 us  [scatter_rows(): lax.psum_scatter(grad, ('row', 'section'), scatter_dimension=0, tiled=True)]
    ppermute x105, starting transfers between devices: 115 us -> 127 us  [xor_step(): return lax.ppermute(value, axis, [(i, i ^ step) for i in range(count)])]
    unnamed x466 -> x357, local copies, waits for them, and re-layouts: 97.8 us -> 88.9 us
    ppermute x4 -> x6, waiting for transfers between devices: 20.7 us -> 12.3 us  [the longest x2 6.1 us: next_column(): return lax.ppermute(value, 'col', [(i + 1, i) for i in range(count - 1)])]
    pallas_call x41 -> x43, Pallas kernels: 324 us -> 331 us  [call(): pl.pallas_call(kernel, out_shape=tuple(outs), in_specs=[pl.BlockSpec(memo...]
  transfers between devices with their start and end apart: 119 -> 121, of which waited for: 41 -> 40; matrix products, arithmetic and copies ran while one was open for 4% -> 5% of each run, Pallas kernels for 38% -> 37%
where the time goes in v3:
time: 866 us; the launch traced here: 853 us
  Pallas kernels  331 us (38%)
  waiting for transfers between devices  217 us (25%)
  starting transfers between devices  147 us (17%)
  local copies, waits for them, and re-layouts  115 us (13%)
  other arithmetic  27.9 us (3%)
  between operations  15.9 us (2%)
    pallas_call x43, Pallas kernels, call(): pl.pallas_call(kernel, out_shape=tuple(outs), in_specs=[pl.BlockSpec(memo...  331 us
    ppermute x105, waiting for transfers between devices, xor_step(): return lax.ppermute(value, axis, [(i, i ^ step) for i in range(count)])  185 us
    ppermute x105, starting transfers between devices, xor_step(): return lax.ppermute(value, axis, [(i, i ^ step) for i in range(count)])  127 us
    unnamed x357, local copies, waits for them, and re-layouts  88.9 us
  transfers between devices with their start and end apart: 121, of which 40 were waited for; matrix products, arithmetic and copies ran while one was open for 5% of the time, Pallas kernels for 37%

profile of v3, /device:TPU:0, one launch (start us, length us, event | category | flops | bytes accessed | tf_op | source)
XLA Modules:
  0.0 853.4 jit_solution(16728082748733884644)
XLA Ops:
  17.4 6.1 collective-permute-done.6
  23.5 4.0 collective-permute-done.8
  27.5 4.2 broadcast_select_fusion.12
  41.3 4.0 collective-permute-start.2
  50.9 13.8 %collective-permute-done.2 = bf16[2,400,512]{2,1,0:T(8,128)(2,1)} collective-permute-done((bf16[2,400,512]{2,1,0:T(8,128)(2,1)}, bf16[2,400,512]{2,1,0:T(8,128)(2,1)}, u32[]{:S(2)}, u32[]{:S(2)}) %collective-permute-start.2) | collective-permute-done | bytes 819232 | tf_op jit(solution)/shard_map/ppermute | solution.py:25
  64.7 15.8 %collective-permute-done.1 = bf16[2,400,512]{2,1,0:T(8,128)(2,1)} collective-permute-done((bf16[2,400,512]{2,1,0:T(8,128)(2,1)}, bf16[2,400,512]{2,1,0:T(8,128)(2,1)}, u32[]{:S(2)}, u32[]{:S(2)}) %collective-permute-start.1) | collective-permute-done | bytes 819232 | tf_op jit(solution)/shard_map/ppermute | solution.py:25
  82.2 3.0 collective-permute-done.14
  108.7 13.1 %shard_map.299 = (bf16[512,1344]{1,0:T(8,128)(2,1)S(1)}, bf16[512,448]{1,0:T(8,128)(2,1)S(1)}, f32[7,512]{1,0:T(8,128)S(1)}, bf16[128,1600]{1,0:T(8,128)(2,1)S(1...) custom-call(bf16[512,1600]{1,0:T(8,128)(2,1)S(1)} %copy-done.68, ...), custom_call_target="tpu_custom_call" | custom-call | flops 19260243968 | tf_op jit(solution)/shard_map/pallas_call | solution.py:134
  127.2 12.8 %shard_map.308 = (bf16[512,1344]{1,0:T(8,128)(2,1)S(1)}, bf16[512,448]{1,0:T(8,128)(2,1)S(1)}, f32[7,512]{1,0:T(8,128)S(1)}, bf16[128,1600]{1,0:T(8,128)(2,1)S(1...) custom-call(bf16[512,1600]{1,0:T(8,128)(2,1)S(1)} %copy-done.71, ...), custom_call_target="tpu_custom_call" | custom-call | flops 19260243968 | tf_op jit(solution)/shard_map/pallas_call | solution.py:134
  144.8 6.5 collective-permute-done.17.refs_3_
  155.6 4.3 collective-permute-done.33.refs_1_
  161.8 7.8 collective-permute-done.35.refs_3_
  175.2 3.5 collective-permute-done.20.refs_3_.refs_13_
  180.8 6.9 collective-permute-done.19.refs_2_.refs_12_
  189.3 7.3 all-gather.9.cloned.1.call-done.refs_4_.refs_5_
  200.6 12.2 %shard_map.302 = (bf16[512,1600]{1,0:T(8,128)(2,1)S(1)}, bf16[512,1600]{1,0:T(8,128)(2,1)S(1)}, bf16[128,1600]{1,0:T(8,128)(2,1)S(1)}, bf16[128,1600]{1,0:T(8,12...) custom-call(bf16[128,1600]{1,0:T(8,128)(2,1)S(1)} %copy-done.79, ...), custom_call_target="tpu_custom_call" | custom-call | flops 20971520000 | tf_op jit(solution)/shard_map/pallas_call | solution.py:134
  218.7 14.6 %shard_map.310 = (bf16[512,1600]{1,0:T(8,128)(2,1)S(1)}, bf16[512,1600]{1,0:T(8,128)(2,1)S(1)}, bf16[128,1600]{1,0:T(8,128)(2,1)S(1)}, bf16[128,1600]{1,0:T(8,12...) custom-call(bf16[128,1600]{1,0:T(8,128)(2,1)} %get-tuple-element.214.refs_0_.refs_14_, ...), custom_call_target="tpu_custom_call" | custom-call | flops 20971520000 | tf_op jit(solution)/shard_map/pallas_call | solution.py:134
  244.4 4.1 collective-permute-done.39.refs_1_
  250.7 17.8 %collective-permute-done.40.refs_2_ = bf16[128,1600]{1,0:T(8,128)(2,1)} collective-permute-done((bf16[128,1600]{1,0:T(8,128)(2,1)}, bf16[128,1600]{1,0:T(8,128)(2,1)}, u32[]{:S(2)}, u32[]{:S(2)}) %collective-permute-start.40) | collective-permute-done | bytes 409632 | tf_op jit(solution)/shard_map/ppermute | solution.py:25
  278.6 5.8 collective-permute-done.25.refs_2_
  284.4 14.5 %shard_map.304 = (bf16[512,1344]{1,0:T(8,128)(2,1)S(1)}, bf16[512,448]{1,0:T(8,128)(2,1)S(1)}, f32[7,512]{1,0:T(8,128)S(1)}, bf16[128,1600]{1,0:T(8,128)(2,1)S(1...) custom-call(bf16[128,1600]{1,0:T(8,128)(2,1)} %get-tuple-element.198.refs_0_, ...), custom_call_target="tpu_custom_call" | custom-call | flops 19260243968 | tf_op jit(solution)/shard_map/pallas_call | solution.py:134
  304.3 14.1 %shard_map.312 = (bf16[512,1344]{1,0:T(8,128)(2,1)S(1)}, bf16[512,448]{1,0:T(8,128)(2,1)S(1)}, f32[7,512]{1,0:T(8,128)S(1)}, bf16[128,1600]{1,0:T(8,128)(2,1)S(1...) custom-call(bf16[128,1600]{1,0:T(8,128)(2,1)} %get-tuple-element.220.refs_0_.refs_4_,, ...), custom_call_target="tpu_custom_call" | custom-call | flops 19260243968 | tf_op jit(solution)/shard_map/pallas_call | solution.py:134
  327.7 4.4 collective-permute-done.45.refs_1_
  342.0 9.6 %collective-permute-done.46.refs_2_ = bf16[128,1600]{1,0:T(8,128)(2,1)S(1)} collective-permute-done((bf16[128,1600]{1,0:T(8,128)(2,1)S(1)}, bf16[128,1600]{1,0:T(8,128)(2,1)S(1)}, u32[]{:S(2)}, u32[]{:S(2)}) %collective-permute-start.46) | collective-permute-done | bytes 409632 | tf_op jit(solution)/shard_map/ppermute | solution.py:25
  358.9 6.3 collective-permute-done.31.refs_2_
  366.2 8.7 %shard_map.306 = (bf16[512,1600]{1,0:T(8,128)(2,1)S(1)}, bf16[512,1600]{1,0:T(8,128)(2,1)S(1)}) custom-call(bf16[128,1600]{1,0:T(8,128)(2,1)} %get-tuple-element.204.refs_0_, bf16[128,1600]{1,0:T(8,128)(2,1)} %collective-permute-done.30.refs_1_, bf16[128,1600]{1,0:T(8,128)(2,1)} %collective-permute-done.31.refs_2_, bf16[128,1600]{1,0:T(8,128)(2,1)S(1)} %copy-done.91, ...), custom_call_target="tpu_custom_call" | custom-call | flops 10485760000 | tf_op jit(solution)/shard_map/pallas_call | solution.py:134
  376.1 9.6 %shard_map.314 = (bf16[512,1600]{1,0:T(8,128)(2,1)S(1)}, bf16[512,1600]{1,0:T(8,128)(2,1)S(1)}) custom-call(bf16[128,1600]{1,0:T(8,128)(2,1)} %get-tuple-element.226.refs_0_.refs_4_, bf16[128,1600]{1,0:T(8,128)(2,1)} %collective-permute-done.48.refs_1_.refs_5_, bf16[128,1600]{1,0:T(8,128)(2,1)} %collective-permute-done.49.refs_2_.refs_6_, ...), custom_call_target="tpu_custom_call" | custom-call | flops 10485760000 | tf_op jit(solution)/shard_map/pallas_call | solution.py:134
  387.0 8.7 %shard_map.315 = bf16[1600,1600]{1,0:T(8,128)(2,1)} custom-call(bf16[512,1600]{1,0:T(8,128)(2,1)S(1)} %copy-done.73, bf16[512,1600]{1,0:T(8,128)(2,1)S(1)} %copy-done.76, bf16[512,1600]{1,0:T(8,128)(2,1)S(1)} %get-tuple-element.315.refs_2_.refs_0_, bf16[512,1600]{1,0:T(8,128)(2,1)S(1)} %get-tuple-element.320.refs_3_.refs_0_), custom_call_target="tpu_custom_call" | custom-call | flops 20971520000 | tf_op jit(solution)/shard_map/pallas_call | solution.py:134
  399.8 12.1 %shard_map.317 = (bf16[512,1600]{1,0:T(8,128)(2,1)S(1)}, f32[1,1600]{1,0:T(1,128)S(1)}, bf16[128,1600]{1,0:T(8,128)(2,1)S(1)}, bf16[128,1600]{1,0:T(8,128)(2,1)}...) custom-call(bf16[512,1600]{1,0:T(8,128)(2,1)S(1)} %copy-done.77, ...), custom_call_target="tpu_custom_call" | custom-call | flops 20971520000 | tf_op jit(solution)/shard_map/pallas_call | solution.py:134
  416.2 10.9 %shard_map.316 = (bf16[512,1600]{1,0:T(8,128)(2,1)S(1)}, f32[1,1600]{1,0:T(1,128)S(1)}, bf16[128,1600]{1,0:T(8,128)(2,1)S(1)}, bf16[128,1600]{1,0:T(8,128)(2,1)S...) custom-call(bf16[512,1600]{1,0:T(8,128)(2,1)S(1)} %copy-done.74, ...), custom_call_target="tpu_custom_call" | custom-call | flops 20971520000 | tf_op jit(solution)/shard_map/pallas_call | solution.py:134
  430.2 10.8 %shard_map.318 = bf16[1600,1600]{1,0:T(8,128)(2,1)} custom-call(bf16[128,1600]{1,0:T(8,128)(2,1)} %get-tuple-element.204.refs_0_, bf16[128,1600]{1,0:T(8,128)(2,1)} %collective-permute-done.30.refs_1_, bf16[128,1600]{1,0:T(8,128)(2,1)} %collective-permute-done.31.refs_2_, bf16[128,1600]{1,0:T(8,128)(2,1)S(1)} %copy-done.92, ...), custom_call_target="tpu_custom_call" | custom-call | flops 20971520000 | tf_op jit(solution)/shard_map/pallas_call | solution.py:134
  455.2 16.7 %collective-permute-done.52.refs_2_ = bf16[128,1600]{1,0:T(8,128)(2,1)S(1)} collective-permute-done((bf16[128,1600]{1,0:T(8,128)(2,1)}, bf16[128,1600]{1,0:T(8,128)(2,1)S(1)}, u32[]{:S(2)}, u32[]{:S(2)}) %collective-permute-start.52) | collective-permute-done | bytes 409632 | tf_op jit(solution)/shard_map/ppermute | solution.py:25
  473.8 3.3 collective-permute-start.56
  478.2 8.2 collective-permute-done.64.refs_2_.refs_16_
  486.4 15.7 %shard_map.322 = (bf16[512,1344]{1,0:T(8,128)(2,1)S(1)}, f32[2,448]{1,0:T(2,128)S(1)}, bf16[128,1600]{1,0:T(8,128)(2,1)S(1)}, bf16[128,1600]{1,0:T(8,128)(2,1)},...) custom-call(bf16[128,1600]{1,0:T(8,128)(2,1)S(1)} %get-tuple-element.255.refs_0_.refs_14_, ...), custom_call_target="tpu_custom_call" | custom-call | flops 30534533120 | tf_op jit(solution)/shard_map/pallas_call | solution.py:134
  508.8 14.6 %shard_map.320 = (bf16[512,1344]{1,0:T(8,128)(2,1)S(1)}, f32[2,448]{1,0:T(2,128)S(1)}, bf16[128,1600]{1,0:T(8,128)(2,1)S(1)}, bf16[128,1600]{1,0:T(8,128)(2,1)S(...) custom-call(bf16[128,1600]{1,0:T(8,128)(2,1)S(1)} %get-tuple-element.240.refs_0_.refs_10_, ...), custom_call_target="tpu_custom_call" | custom-call | flops 30534533120 | tf_op jit(solution)/shard_map/pallas_call | solution.py:134
  526.5 12.3 %shard_map.323 = bf16[1600,1792]{1,0:T(8,128)(2,1)} custom-call(bf16[128,1600]{1,0:T(8,128)(2,1)} %get-tuple-element.198.refs_0_, bf16[128,1600]{1,0:T(8,128)(2,1)} %collective-permute-done.24.refs_1_, bf16[128,1600]{1,0:T(8,128)(2,1)} %collective-permute-done.25.refs_2_, bf16[128,1600]{1,0:T(8,128)(2,1)} %collective-permute-done.26.refs_3_, ...), custom_call_target="tpu_custom_call" | custom-call | flops 23488102400 | tf_op jit(solution)/shard_map/pallas_call | solution.py:134
  545.8 3.1 shard_map.327
  553.3 12.6 %collective-permute-done.58.refs_2_ = bf16[128,1600]{1,0:T(8,128)(2,1)S(1)} collective-permute-done((bf16[128,1600]{1,0:T(8,128)(2,1)}, bf16[128,1600]{1,0:T(8,128)(2,1)S(1)}, u32[]{:S(2)}, u32[]{:S(2)}) %collective-permute-start.58) | collective-permute-done | bytes 409632 | tf_op jit(solution)/shard_map/ppermute | solution.py:25
  572.9 4.0 collective-permute-done.79.refs_2_.refs_6_
  579.6 13.0 %shard_map.328 = (bf16[512,1600]{1,0:T(8,128)(2,1)S(1)}, f32[1,1600]{1,0:T(1,128)S(1)}, bf16[128,1600]{1,0:T(8,128)(2,1)S(1)}, bf16[128,1600]{1,0:T(8,128)(2,1)}...) custom-call(bf16[128,1600]{1,0:T(8,128)(2,1)} %get-tuple-element.280.refs_0_.refs_4_, ...), custom_call_target="tpu_custom_call" | custom-call | flops 20971520000 | tf_op jit(solution)/shard_map/pallas_call | solution.py:134
  597.2 13.2 %shard_map.325 = (bf16[512,1600]{1,0:T(8,128)(2,1)S(1)}, f32[1,1600]{1,0:T(1,128)S(1)}, bf16[128,1600]{1,0:T(8,128)(2,1)S(1)}, bf16[128,1600]{1,0:T(8,128)(2,1)}...) custom-call(bf16[128,1600]{1,0:T(8,128)(2,1)} %get-tuple-element.263.refs_0_, ...), custom_call_target="tpu_custom_call" | custom-call | flops 20971520000 | tf_op jit(solution)/shard_map/pallas_call | solution.py:134
  616.5 19.4 %shard_map.329 = bf16[1600,3200]{1,0:T(8,128)(2,1)} custom-call(bf16[128,1600]{1,0:T(8,128)(2,1)} %get-tuple-element.263.refs_0_, bf16[128,1600]{1,0:T(8,128)(2,1)S(1)} %collective-permute-done.66.refs_1_, bf16[128,1600]{1,0:T(8,128)(2,1)} %collective-permute-done.67.refs_2_, bf16[128,1600]{1,0:T(8,128)(2,1)} %collective-permute-done.68.refs_3_, ...), custom_call_target="tpu_custom_call" | custom-call | flops 41943040000 | tf_op jit(solution)/shard_map/pallas_call | solution.py:134
  641.5 3.1 shard_map.326
  650.2 2.8 shard_map.331
  659.7 8.9 %collective-permute-done.73.refs_2_.refs_6_ = bf16[128,1600]{1,0:T(8,128)(2,1)} collective-permute-done((bf16[128,1600]{1,0:T(8,128)(2,1)}, bf16[128,1600]{1,0:T(8,128)(2,1)}, u32[]{:S(2)}, u32[]{:S(2)}) %collective-permute-start.73) | collective-permute-done | bytes 409632 | tf_op jit(solution)/shard_map/ppermute | solution.py:25
  670.0 17.3 %shard_map.330 = (bf16[512,1344]{1,0:T(8,128)(2,1)S(1)}, f32[2,448]{1,0:T(2,128)S(1)}, bf16[128,1600]{1,0:T(8,128)(2,1)S(1)}, bf16[128,1600]{1,0:T(8,128)(2,1)S(...) custom-call(bf16[128,1600]{1,0:T(8,128)(2,1)} %get-tuple-element.271.refs_0_.refs_4_, ...), custom_call_target="tpu_custom_call" | custom-call | flops 90534535168 | tf_op jit(solution)/shard_map/pallas_call | solution.py:134
  688.9 2.7 collective-permute-start.83
  691.7 16.9 %shard_map.332 = (bf16[512,1344]{1,0:T(8,128)(2,1)S(1)}, f32[2,448]{1,0:T(2,128)S(1)}, bf16[128,1600]{1,0:T(8,128)(2,1)S(1)}, bf16[128,1600]{1,0:T(8,128)(2,1)},...) custom-call(bf16[128,1600]{1,0:T(8,128)(2,1)} %get-tuple-element.298.refs_0_.refs_8_, ...), custom_call_target="tpu_custom_call" | custom-call | flops 90534535168 | tf_op jit(solution)/shard_map/pallas_call | solution.py:134
  711.5 2.8 collective-permute-start.92
  714.3 12.3 %shard_map.333 = bf16[1600,1792]{1,0:T(8,128)(2,1)} custom-call(bf16[512,1600]{1,0:T(8,128)(2,1)S(1)} %copy-done.69, bf16[512,1600]{1,0:T(8,128)(2,1)} %copy-done.70, bf16[512,1344]{1,0:T(8,128)(2,1)S(1)} %get-tuple-element.292.refs_2_, bf16[512,1344]{1,0:T(8,128)(2,1)S(1)} %get-tuple-element.302.refs_3_, ...), custom_call_target="tpu_custom_call" | custom-call | flops 23488102400 | tf_op jit(solution)/shard_map/pallas_call | solution.py:134
  726.7 3.1 shard_map.334
  731.2 3.1 shard_map.335
  735.6 5.8 reduce-scatter.20.cloned.1.call-done
  746.1 7.6 shard_map.336
  757.3 7.2 shard_map.338
  778.6 6.2 collective-permute-done.96.refs_1_
  787.0 5.2 collective-permute-done.97.refs_2_
  795.0 3.7 all-to-all-start
  810.1 4.5 all-to-all-done
  817.0 3.3 collective-permute-start.109
  827.8 3.9 collective-permute-start.106
  832.0 4.2 collective-permute-start.107
  836.1 2.9 fusion.4
  (721 shorter events, 296.5 us)
Async XLA Ops:
  7.2 100.0 %all-gather.7.cloned.1.call-start = ((), (), s32[]{:S(2)}) async-start(), calls=%async_computation.7 | async-start | bytes 6451200 | tf_op jit(solution)/shard_map/all_gather | solution.py:662
  33.7 162.9 %all-gather.9.cloned.1.call-start = ((), (), s32[]{:S(2)}) async-start(), calls=%async_computation.8 | async-start | bytes 11980800 | tf_op jit(solution)/shard_map/all_gather | solution.py:662
  45.3 35.2 %collective-permute-start.1 = (bf16[2,400,512]{2,1,0:T(8,128)(2,1)}, bf16[2,400,512]{2,1,0:T(8,128)(2,1)}, u32[]{:S(2)}, u32[]{:S(2)}) collective-permute-start(bf16[2,400,512]{2,1,0:T(8,128)(2,1)} %constant_dynamic-slice_fusion.10), channel_id=1, source_target_pairs={{0,2},{1,3},{2,0},{3,1},{4,6},{5,7},{6,4},{7,5},{8,10},{9,11},{10,... | collective-permute-start | bytes 2457608 | tf_op jit(solution)/shard_map/ppermute | solution.py:25
  45.8 36.2 %collective-permute-start = (bf16[2,400,512]{2,1,0:T(8,128)(2,1)}, bf16[2,400,512]{2,1,0:T(8,128)(2,1)}, u32[]{:S(2)}, u32[]{:S(2)}) collective-permute-start(bf16[2,400,512]{2,1,0:T(8,128)(2,1)} %constant_dynamic-slice_fusion.10), channel_id=1, source_target_pairs={{0,1},{1,0},{2,3},{3,2},{4,5},{5,4},{6,7},{7,6},{8,9},{9,8},{10,11... | collective-permute-start | bytes 2457608 | tf_op jit(solution)/shard_map/ppermute | solution.py:25
  87.2 191.4 %all-gather.11.cloned.1.call-start = ((), (), s32[]{:S(2)}) async-start(), calls=%async_computation.9 | async-start | bytes 6451200 | tf_op jit(solution)/shard_map/all_gather | solution.py:662
  87.9 271.0 %all-gather.5.cloned.1.call-start = ((), (), s32[]{:S(2)}) async-start(), calls=%async_computation.6 | async-start | bytes 11980800 | tf_op jit(solution)/shard_map/all_gather | solution.py:662
  88.5 482.9 %reduce-scatter.16.cloned.1.call-start = ((), (), s32[]{:S(2)}) async-start(), calls=%async_computation.12 | async-start | bytes 5990400
  93.1 33.6 %collective-permute-start.5 = (bf16[2,400,512]{2,1,0:T(8,128)(2,1)}, bf16[2,400,512]{2,1,0:T(8,128)(2,1)}, u32[]{:S(2)}, u32[]{:S(2)}) collective-permute-start(bf16[2,400,512]{2,1,0:T(8,128)(2,1)} %constant_dynamic-slice_fusion.11), channel_id=1, source_target_pairs={{0,3},{1,2},{2,1},{3,0},{4,7},{5,6},{6,5},{7,4},{8,11},{9,10},{10,... | collective-permute-start | bytes 2457608 | tf_op jit(solution)/shard_map/ppermute | solution.py:25
  95.5 45.7 %collective-permute-start.4 = (bf16[2,400,512]{2,1,0:T(8,128)(2,1)}, bf16[2,400,512]{2,1,0:T(8,128)(2,1)}, u32[]{:S(2)}, u32[]{:S(2)}) collective-permute-start(bf16[2,400,512]{2,1,0:T(8,128)(2,1)} %constant_dynamic-slice_fusion.11), channel_id=1, source_target_pairs={{0,2},{1,3},{2,0},{3,1},{4,6},{5,7},{6,4},{7,5},{8,10},{9,11},{10,... | collective-permute-start | bytes 2457608 | tf_op jit(solution)/shard_map/ppermute | solution.py:25
  96.0 46.6 %collective-permute-start.3 = (bf16[2,400,512]{2,1,0:T(8,128)(2,1)}, bf16[2,400,512]{2,1,0:T(8,128)(2,1)}, u32[]{:S(2)}, u32[]{:S(2)}) collective-permute-start(bf16[2,400,512]{2,1,0:T(8,128)(2,1)} %constant_dynamic-slice_fusion.11), channel_id=1, source_target_pairs={{0,1},{1,0},{2,3},{3,2},{4,5},{5,4},{6,7},{7,6},{8,9},{9,8},{10,11... | collective-permute-start | bytes 2457608 | tf_op jit(solution)/shard_map/ppermute | solution.py:25
  126.6 24.6 %collective-permute-start.17 = (bf16[128,1600]{1,0:T(8,128)(2,1)S(1)}, bf16[128,1600]{1,0:T(8,128)(2,1)S(1)}, u32[]{:S(2)}, u32[]{:S(2)}) collective-permute-start(bf16[128,1600]{1,0:T(8,128)(2,1)S(1)} %get-tuple-element.188), channel_id=1, source_target_pairs={{0,3},{1,2},{2,1},{3,0},{4,7},{5,6},{6,5},{7,4},{8,11},{9,10},{10,... | collective-permute-start | bytes 1228808 | tf_op jit(solution)/shard_map/ppermute | solution.py:25
  144.2 25.3 %collective-permute-start.35 = (bf16[128,1600]{1,0:T(8,128)(2,1)S(1)}, bf16[128,1600]{1,0:T(8,128)(2,1)S(1)}, u32[]{:S(2)}, u32[]{:S(2)}) collective-permute-start(bf16[128,1600]{1,0:T(8,128)(2,1)S(1)} %get-tuple-element.212), channel_id=1, source_target_pairs={{0,3},{1,2},{2,1},{3,0},{4,7},{5,6},{6,5},{7,4},{8,11},{9,10},{10,... | collective-permute-start | bytes 1228808 | tf_op jit(solution)/shard_map/ppermute | solution.py:25
  152.7 25.9 %collective-permute-start.20 = (bf16[128,1600]{1,0:T(8,128)(2,1)S(1)}, bf16[128,1600]{1,0:T(8,128)(2,1)S(1)}, u32[]{:S(2)}, u32[]{:S(2)}) collective-permute-start(bf16[128,1600]{1,0:T(8,128)(2,1)S(1)} %get-tuple-element.192.refs_0_.refs_10_), channel_id=1, source_target_pairs={{0,3},{1,2},{2,1},{3,0},{4,7},{5,6},{6,5},{7,4},{8,11},{9,10},{10,... | collective-permute-start | bytes 1228808 | tf_op jit(solution)/shard_map/ppermute | solution.py:25
  155.1 32.7 %collective-permute-start.19 = (bf16[128,1600]{1,0:T(8,128)(2,1)S(1)}, bf16[128,1600]{1,0:T(8,128)(2,1)S(1)}, u32[]{:S(2)}, u32[]{:S(2)}) collective-permute-start(bf16[128,1600]{1,0:T(8,128)(2,1)S(1)} %get-tuple-element.192.refs_0_.refs_10_), channel_id=1, source_target_pairs={{0,2},{1,3},{2,0},{3,1},{4,6},{5,7},{6,4},{7,5},{8,10},{9,11},{10,... | collective-permute-start | bytes 1228808 | tf_op jit(solution)/shard_map/ppermute | solution.py:25
  159.9 28.7 %collective-permute-start.18 = (bf16[128,1600]{1,0:T(8,128)(2,1)S(1)}, bf16[128,1600]{1,0:T(8,128)(2,1)S(1)}, u32[]{:S(2)}, u32[]{:S(2)}) collective-permute-start(bf16[128,1600]{1,0:T(8,128)(2,1)S(1)} %get-tuple-element.192.refs_0_.refs_10_), channel_id=1, source_target_pairs={{0,1},{1,0},{2,3},{3,2},{4,5},{5,4},{6,7},{7,6},{8,9},{9,8},{10,11... | collective-permute-start | bytes 1228808 | tf_op jit(solution)/shard_map/ppermute | solution.py:25
  172.3 45.8 %collective-permute-start.38 = (bf16[128,1600]{1,0:T(8,128)(2,1)}, bf16[128,1600]{1,0:T(8,128)(2,1)}, u32[]{:S(2)}, u32[]{:S(2)}) collective-permute-start(bf16[128,1600]{1,0:T(8,128)(2,1)} %get-tuple-element.214.refs_0_.refs_14_), channel_id=1, source_target_pairs={{0,3},{1,2},{2,1},{3,0},{4,7},{5,6},{6,5},{7,4},{8,11},{9,10},{10,... | collective-permute-start | bytes 1228808 | tf_op jit(solution)/shard_map/ppermute | solution.py:25
  174.6 44.1 %collective-permute-start.37 = (bf16[128,1600]{1,0:T(8,128)(2,1)}, bf16[128,1600]{1,0:T(8,128)(2,1)}, u32[]{:S(2)}, u32[]{:S(2)}) collective-permute-start(bf16[128,1600]{1,0:T(8,128)(2,1)} %get-tuple-element.214.refs_0_.refs_14_), channel_id=1, source_target_pairs={{0,2},{1,3},{2,0},{3,1},{4,6},{5,7},{6,4},{7,5},{8,10},{9,11},{10,... | collective-permute-start | bytes 1228808 | tf_op jit(solution)/shard_map/ppermute | solution.py:25
  179.4 39.3 %collective-permute-start.36 = (bf16[128,1600]{1,0:T(8,128)(2,1)}, bf16[128,1600]{1,0:T(8,128)(2,1)}, u32[]{:S(2)}, u32[]{:S(2)}) collective-permute-start(bf16[128,1600]{1,0:T(8,128)(2,1)} %get-tuple-element.214.refs_0_.refs_14_), channel_id=1, source_target_pairs={{0,1},{1,0},{2,3},{3,2},{4,5},{5,4},{6,7},{7,6},{8,9},{9,8},{10,11... | collective-permute-start | bytes 1228808 | tf_op jit(solution)/shard_map/ppermute | solution.py:25
  237.1 31.4 %collective-permute-start.40 = (bf16[128,1600]{1,0:T(8,128)(2,1)}, bf16[128,1600]{1,0:T(8,128)(2,1)}, u32[]{:S(2)}, u32[]{:S(2)}) collective-permute-start(bf16[128,1600]{1,0:T(8,128)(2,1)} %get-tuple-element.217), channel_id=1, source_target_pairs={{0,2},{1,3},{2,0},{3,1},{4,6},{5,7},{6,4},{7,5},{8,10},{9,11},{10,... | collective-permute-start | bytes 1228808 | tf_op jit(solution)/shard_map/ppermute | solution.py:25
  238.6 29.9 %collective-permute-start.41 = (bf16[128,1600]{1,0:T(8,128)(2,1)}, bf16[128,1600]{1,0:T(8,128)(2,1)}, u32[]{:S(2)}, u32[]{:S(2)}) collective-permute-start(bf16[128,1600]{1,0:T(8,128)(2,1)} %get-tuple-element.218), channel_id=1, source_target_pairs={{0,3},{1,2},{2,1},{3,0},{4,7},{5,6},{6,5},{7,4},{8,11},{9,10},{10,... | collective-permute-start | bytes 1228808 | tf_op jit(solution)/shard_map/ppermute | solution.py:25
  241.6 35.9 %collective-permute-start.26 = (bf16[128,1600]{1,0:T(8,128)(2,1)}, bf16[128,1600]{1,0:T(8,128)(2,1)}, u32[]{:S(2)}, u32[]{:S(2)}) collective-permute-start(bf16[128,1600]{1,0:T(8,128)(2,1)} %get-tuple-element.198.refs_0_), channel_id=1, source_target_pairs={{0,3},{1,2},{2,1},{3,0},{4,7},{5,6},{6,5},{7,4},{8,11},{9,10},{10,... | collective-permute-start | bytes 1228808 | tf_op jit(solution)/shard_map/ppermute | solution.py:25
  243.8 40.6 %collective-permute-start.25 = (bf16[128,1600]{1,0:T(8,128)(2,1)}, bf16[128,1600]{1,0:T(8,128)(2,1)}, u32[]{:S(2)}, u32[]{:S(2)}) collective-permute-start(bf16[128,1600]{1,0:T(8,128)(2,1)} %get-tuple-element.198.refs_0_), channel_id=1, source_target_pairs={{0,2},{1,3},{2,0},{3,1},{4,6},{5,7},{6,4},{7,5},{8,10},{9,11},{10,... | collective-permute-start | bytes 1228808 | tf_op jit(solution)/shard_map/ppermute | solution.py:25
  249.2 35.2 %collective-permute-start.24 = (bf16[128,1600]{1,0:T(8,128)(2,1)}, bf16[128,1600]{1,0:T(8,128)(2,1)}, u32[]{:S(2)}, u32[]{:S(2)}) collective-permute-start(bf16[128,1600]{1,0:T(8,128)(2,1)} %get-tuple-element.198.refs_0_), channel_id=1, source_target_pairs={{0,1},{1,0},{2,3},{3,2},{4,5},{5,4},{6,7},{7,6},{8,9},{9,8},{10,11... | collective-permute-start | bytes 1228808 | tf_op jit(solution)/shard_map/ppermute | solution.py:25
  275.1 27.6 %collective-permute-start.44 = (bf16[128,1600]{1,0:T(8,128)(2,1)}, bf16[128,1600]{1,0:T(8,128)(2,1)}, u32[]{:S(2)}, u32[]{:S(2)}) collective-permute-start(bf16[128,1600]{1,0:T(8,128)(2,1)} %get-tuple-element.220.refs_0_.refs_4_), channel_id=1, source_target_pairs={{0,3},{1,2},{2,1},{3,0},{4,7},{5,6},{6,5},{7,4},{8,11},{9,10},{10,... | collective-permute-start | bytes 1228808 | tf_op jit(solution)/shard_map/ppermute | solution.py:25
  276.7 27.7 %collective-permute-start.43 = (bf16[128,1600]{1,0:T(8,128)(2,1)}, bf16[128,1600]{1,0:T(8,128)(2,1)}, u32[]{:S(2)}, u32[]{:S(2)}) collective-permute-start(bf16[128,1600]{1,0:T(8,128)(2,1)} %get-tuple-element.220.refs_0_.refs_4_), channel_id=1, source_target_pairs={{0,2},{1,3},{2,0},{3,1},{4,6},{5,7},{6,4},{7,5},{8,10},{9,11},{10,... | collective-permute-start | bytes 1228808 | tf_op jit(solution)/shard_map/ppermute | solution.py:25
  277.4 26.9 %collective-permute-start.42 = (bf16[128,1600]{1,0:T(8,128)(2,1)}, bf16[128,1600]{1,0:T(8,128)(2,1)}, u32[]{:S(2)}, u32[]{:S(2)}) collective-permute-start(bf16[128,1600]{1,0:T(8,128)(2,1)} %get-tuple-element.220.refs_0_.refs_4_), channel_id=1, source_target_pairs={{0,1},{1,0},{2,3},{3,2},{4,5},{5,4},{6,7},{7,6},{8,9},{9,8},{10,11... | collective-permute-start | bytes 1228808 | tf_op jit(solution)/shard_map/ppermute | solution.py:25
  321.3 30.3 %collective-permute-start.46 = (bf16[128,1600]{1,0:T(8,128)(2,1)S(1)}, bf16[128,1600]{1,0:T(8,128)(2,1)S(1)}, u32[]{:S(2)}, u32[]{:S(2)}) collective-permute-start(bf16[128,1600]{1,0:T(8,128)(2,1)S(1)} %get-tuple-element.223), channel_id=1, source_target_pairs={{0,2},{1,3},{2,0},{3,1},{4,6},{5,7},{6,4},{7,5},{8,10},{9,11},{10,... | collective-permute-start | bytes 1228808 | tf_op jit(solution)/shard_map/ppermute | solution.py:25
  322.8 28.8 %collective-permute-start.47 = (bf16[128,1600]{1,0:T(8,128)(2,1)S(1)}, bf16[128,1600]{1,0:T(8,128)(2,1)S(1)}, u32[]{:S(2)}, u32[]{:S(2)}) collective-permute-start(bf16[128,1600]{1,0:T(8,128)(2,1)S(1)} %get-tuple-element.224), channel_id=1, source_target_pairs={{0,3},{1,2},{2,1},{3,0},{4,7},{5,6},{6,5},{7,4},{8,11},{9,10},{10,... | collective-permute-start | bytes 1228808 | tf_op jit(solution)/shard_map/ppermute | solution.py:25
  325.5 30.7 %collective-permute-start.32 = (bf16[128,1600]{1,0:T(8,128)(2,1)}, bf16[128,1600]{1,0:T(8,128)(2,1)S(1)}, u32[]{:S(2)}, u32[]{:S(2)}) collective-permute-start(bf16[128,1600]{1,0:T(8,128)(2,1)} %get-tuple-element.204.refs_0_), channel_id=1, source_target_pairs={{0,3},{1,2},{2,1},{3,0},{4,7},{5,6},{6,5},{7,4},{8,11},{9,10},{10,... | collective-permute-start | bytes 1228808 | tf_op jit(solution)/shard_map/ppermute | solution.py:25
  327.1 38.1 %collective-permute-start.31 = (bf16[128,1600]{1,0:T(8,128)(2,1)}, bf16[128,1600]{1,0:T(8,128)(2,1)}, u32[]{:S(2)}, u32[]{:S(2)}) collective-permute-start(bf16[128,1600]{1,0:T(8,128)(2,1)} %get-tuple-element.204.refs_0_), channel_id=1, source_target_pairs={{0,2},{1,3},{2,0},{3,1},{4,6},{5,7},{6,4},{7,5},{8,10},{9,11},{10,... | collective-permute-start | bytes 1228808 | tf_op jit(solution)/shard_map/ppermute | solution.py:25
  332.1 33.1 %collective-permute-start.30 = (bf16[128,1600]{1,0:T(8,128)(2,1)}, bf16[128,1600]{1,0:T(8,128)(2,1)}, u32[]{:S(2)}, u32[]{:S(2)}) collective-permute-start(bf16[128,1600]{1,0:T(8,128)(2,1)} %get-tuple-element.204.refs_0_), channel_id=1, source_target_pairs={{0,1},{1,0},{2,3},{3,2},{4,5},{5,4},{6,7},{7,6},{8,9},{9,8},{10,11... | collective-permute-start | bytes 1228808 | tf_op jit(solution)/shard_map/ppermute | solution.py:25
  396.9 174.5 %reduce-scatter.18.cloned.1.call-start = ((), (), s32[]{:S(2)}) async-start(), calls=%async_computation.13 | async-start | bytes 5990400
  412.7 30.8 %collective-permute-start.60 = (bf16[128,1600]{1,0:T(8,128)(2,1)}, bf16[128,1600]{1,0:T(8,128)(2,1)}, u32[]{:S(2)}, u32[]{:S(2)}) collective-permute-start(bf16[128,1600]{1,0:T(8,128)(2,1)} %get-tuple-element.249), channel_id=1, source_target_pairs={{0,1},{1,0},{2,3},{3,2},{4,5},{5,4},{6,7},{7,6},{8,9},{9,8},{10,11... | collective-permute-start | bytes 1228808 | tf_op jit(solution)/shard_map/ppermute | solution.py:25
  413.8 30.8 %collective-permute-start.61 = (bf16[128,1600]{1,0:T(8,128)(2,1)}, bf16[128,1600]{1,0:T(8,128)(2,1)}, u32[]{:S(2)}, u32[]{:S(2)}) collective-permute-start(bf16[128,1600]{1,0:T(8,128)(2,1)} %get-tuple-element.250), channel_id=1, source_target_pairs={{0,2},{1,3},{2,0},{3,1},{4,6},{5,7},{6,4},{7,5},{8,10},{9,11},{10,... | collective-permute-start | bytes 1228808 | tf_op jit(solution)/shard_map/ppermute | solution.py:25
  415.1 29.5 %collective-permute-start.62 = (bf16[128,1600]{1,0:T(8,128)(2,1)}, bf16[128,1600]{1,0:T(8,128)(2,1)}, u32[]{:S(2)}, u32[]{:S(2)}) collective-permute-start(bf16[128,1600]{1,0:T(8,128)(2,1)} %get-tuple-element.251), channel_id=1, source_target_pairs={{0,3},{1,2},{2,1},{3,0},{4,7},{5,6},{6,5},{7,4},{8,11},{9,10},{10,... | collective-permute-start | bytes 1228808 | tf_op jit(solution)/shard_map/ppermute | solution.py:25
  441.0 216.5 %reduce-scatter.12.cloned.1.call-start = ((), (), s32[]{:S(2)}) async-start(), calls=%async_computation.10 | async-start | bytes 6451200 | tf_op jit(solution)/shard_map/reduce_scatter | solution.py:800
  442.2 29.7 %collective-permute-start.52 = (bf16[128,1600]{1,0:T(8,128)(2,1)}, bf16[128,1600]{1,0:T(8,128)(2,1)S(1)}, u32[]{:S(2)}, u32[]{:S(2)}) collective-permute-start(bf16[128,1600]{1,0:T(8,128)(2,1)} %copy-done.98), channel_id=1, source_target_pairs={{0,2},{1,3},{2,0},{3,1},{4,6},{5,7},{6,4},{7,5},{8,10},{9,11},{10,... | collective-permute-start | bytes 1228808 | tf_op jit(solution)/shard_map/ppermute | solution.py:25
  443.5 28.4 %collective-permute-start.53 = (bf16[128,1600]{1,0:T(8,128)(2,1)}, bf16[128,1600]{1,0:T(8,128)(2,1)S(1)}, u32[]{:S(2)}, u32[]{:S(2)}) collective-permute-start(bf16[128,1600]{1,0:T(8,128)(2,1)} %copy-done.97), channel_id=1, source_target_pairs={{0,3},{1,2},{2,1},{3,0},{4,7},{5,6},{6,5},{7,4},{8,11},{9,10},{10,... | collective-permute-start | bytes 1228808 | tf_op jit(solution)/shard_map/ppermute | solution.py:25
  450.3 26.9 %collective-permute-start.65 = (bf16[128,1600]{1,0:T(8,128)(2,1)S(1)}, bf16[128,1600]{1,0:T(8,128)(2,1)S(1)}, u32[]{:S(2)}, u32[]{:S(2)}) collective-permute-start(bf16[128,1600]{1,0:T(8,128)(2,1)S(1)} %get-tuple-element.255.refs_0_.refs_14_), channel_id=1, source_target_pairs={{0,3},{1,2},{2,1},{3,0},{4,7},{5,6},{6,5},{7,4},{8,11},{9,10},{10,... | collective-permute-start | bytes 1228808 | tf_op jit(solution)/shard_map/ppermute | solution.py:25
  452.2 34.2 %collective-permute-start.64 = (bf16[128,1600]{1,0:T(8,128)(2,1)S(1)}, bf16[128,1600]{1,0:T(8,128)(2,1)S(1)}, u32[]{:S(2)}, u32[]{:S(2)}) collective-permute-start(bf16[128,1600]{1,0:T(8,128)(2,1)S(1)} %get-tuple-element.255.refs_0_.refs_14_), channel_id=1, source_target_pairs={{0,2},{1,3},{2,0},{3,1},{4,6},{5,7},{6,4},{7,5},{8,10},{9,11},{10,... | collective-permute-start | bytes 1228808 | tf_op jit(solution)/shard_map/ppermute | solution.py:25
  454.1 32.3 %collective-permute-start.63 = (bf16[128,1600]{1,0:T(8,128)(2,1)S(1)}, bf16[128,1600]{1,0:T(8,128)(2,1)S(1)}, u32[]{:S(2)}, u32[]{:S(2)}) collective-permute-start(bf16[128,1600]{1,0:T(8,128)(2,1)S(1)} %get-tuple-element.255.refs_0_.refs_14_), channel_id=1, source_target_pairs={{0,1},{1,0},{2,3},{3,2},{4,5},{5,4},{6,7},{7,6},{8,9},{9,8},{10,11... | collective-permute-start | bytes 1228808 | tf_op jit(solution)/shard_map/ppermute | solution.py:25
  473.8 34.7 %collective-permute-start.56 = (bf16[128,1600]{1,0:T(8,128)(2,1)S(1)}, bf16[128,1600]{1,0:T(8,128)(2,1)S(1)}, u32[]{:S(2)}, u32[]{:S(2)}) collective-permute-start(bf16[128,1600]{1,0:T(8,128)(2,1)S(1)} %get-tuple-element.240.refs_0_.refs_10_), channel_id=1, source_target_pairs={{0,3},{1,2},{2,1},{3,0},{4,7},{5,6},{6,5},{7,4},{8,11},{9,10},{10,... | collective-permute-start | bytes 1228808 | tf_op jit(solution)/shard_map/ppermute | solution.py:25
  477.2 31.6 %collective-permute-start.55 = (bf16[128,1600]{1,0:T(8,128)(2,1)S(1)}, bf16[128,1600]{1,0:T(8,128)(2,1)S(1)}, u32[]{:S(2)}, u32[]{:S(2)}) collective-permute-start(bf16[128,1600]{1,0:T(8,128)(2,1)S(1)} %get-tuple-element.240.refs_0_.refs_10_), channel_id=1, source_target_pairs={{0,2},{1,3},{2,0},{3,1},{4,6},{5,7},{6,4},{7,5},{8,10},{9,11},{10,... | collective-permute-start | bytes 1228808 | tf_op jit(solution)/shard_map/ppermute | solution.py:25
  477.2 31.6 %collective-permute-start.54 = (bf16[128,1600]{1,0:T(8,128)(2,1)S(1)}, bf16[128,1600]{1,0:T(8,128)(2,1)S(1)}, u32[]{:S(2)}, u32[]{:S(2)}) collective-permute-start(bf16[128,1600]{1,0:T(8,128)(2,1)S(1)} %get-tuple-element.240.refs_0_.refs_10_), channel_id=1, source_target_pairs={{0,1},{1,0},{2,3},{3,2},{4,5},{5,4},{6,7},{7,6},{8,9},{9,8},{10,11... | collective-permute-start | bytes 1228808 | tf_op jit(solution)/shard_map/ppermute | solution.py:25
  504.6 37.6 %collective-permute-start.75 = (bf16[128,1600]{1,0:T(8,128)(2,1)}, bf16[128,1600]{1,0:T(8,128)(2,1)}, u32[]{:S(2)}, u32[]{:S(2)}) collective-permute-start(bf16[128,1600]{1,0:T(8,128)(2,1)} %get-tuple-element.275), channel_id=1, source_target_pairs={{0,1},{1,0},{2,3},{3,2},{4,5},{5,4},{6,7},{7,6},{8,9},{9,8},{10,11... | collective-permute-start | bytes 1228808 | tf_op jit(solution)/shard_map/ppermute | solution.py:25
  506.1 36.3 %collective-permute-start.76 = (bf16[128,1600]{1,0:T(8,128)(2,1)}, bf16[128,1600]{1,0:T(8,128)(2,1)}, u32[]{:S(2)}, u32[]{:S(2)}) collective-permute-start(bf16[128,1600]{1,0:T(8,128)(2,1)} %get-tuple-element.276), channel_id=1, source_target_pairs={{0,2},{1,3},{2,0},{3,1},{4,6},{5,7},{6,4},{7,5},{8,10},{9,11},{10,... | collective-permute-start | bytes 1228808 | tf_op jit(solution)/shard_map/ppermute | solution.py:25
  508.6 33.8 %collective-permute-start.77 = (bf16[128,1600]{1,0:T(8,128)(2,1)}, bf16[128,1600]{1,0:T(8,128)(2,1)}, u32[]{:S(2)}, u32[]{:S(2)}) collective-permute-start(bf16[128,1600]{1,0:T(8,128)(2,1)} %get-tuple-element.277), channel_id=1, source_target_pairs={{0,3},{1,2},{2,1},{3,0},{4,7},{5,6},{6,5},{7,4},{8,11},{9,10},{10,... | collective-permute-start | bytes 1228808 | tf_op jit(solution)/shard_map/ppermute | solution.py:25
  538.8 202.6 %reduce-scatter.20.cloned.1.call-start = ((), (), s32[]{:S(2)}) async-start(), calls=%async_computation.14 | async-start | bytes 11520000
  540.2 25.7 %collective-permute-start.58 = (bf16[128,1600]{1,0:T(8,128)(2,1)}, bf16[128,1600]{1,0:T(8,128)(2,1)S(1)}, u32[]{:S(2)}, u32[]{:S(2)}) collective-permute-start(bf16[128,1600]{1,0:T(8,128)(2,1)} %copy-done.95), channel_id=1, source_target_pairs={{0,2},{1,3},{2,0},{3,1},{4,6},{5,7},{6,4},{7,5},{8,10},{9,11},{10,... | collective-permute-start | bytes 1228808 | tf_op jit(solution)/shard_map/ppermute | solution.py:25
  552.5 25.6 %collective-permute-start.78 = (bf16[128,1600]{1,0:T(8,128)(2,1)}, bf16[128,1600]{1,0:T(8,128)(2,1)}, u32[]{:S(2)}, u32[]{:S(2)}) collective-permute-start(bf16[128,1600]{1,0:T(8,128)(2,1)} %get-tuple-element.280.refs_0_.refs_4_), channel_id=1, source_target_pairs={{0,1},{1,0},{2,3},{3,2},{4,5},{5,4},{6,7},{7,6},{8,9},{9,8},{10,11... | collective-permute-start | bytes 1228808 | tf_op jit(solution)/shard_map/ppermute | solution.py:25
  568.5 28.7 %collective-permute-start.68 = (bf16[128,1600]{1,0:T(8,128)(2,1)}, bf16[128,1600]{1,0:T(8,128)(2,1)}, u32[]{:S(2)}, u32[]{:S(2)}) collective-permute-start(bf16[128,1600]{1,0:T(8,128)(2,1)} %get-tuple-element.263.refs_0_), channel_id=1, source_target_pairs={{0,3},{1,2},{2,1},{3,0},{4,7},{5,6},{6,5},{7,4},{8,11},{9,10},{10,... | collective-permute-start | bytes 1228808 | tf_op jit(solution)/shard_map/ppermute | solution.py:25
  569.8 27.4 %collective-permute-start.67 = (bf16[128,1600]{1,0:T(8,128)(2,1)}, bf16[128,1600]{1,0:T(8,128)(2,1)}, u32[]{:S(2)}, u32[]{:S(2)}) collective-permute-start(bf16[128,1600]{1,0:T(8,128)(2,1)} %get-tuple-element.263.refs_0_), channel_id=1, source_target_pairs={{0,2},{1,3},{2,0},{3,1},{4,6},{5,7},{6,4},{7,5},{8,10},{9,11},{10,... | collective-permute-start | bytes 1228808 | tf_op jit(solution)/shard_map/ppermute | solution.py:25
  571.7 25.4 %collective-permute-start.66 = (bf16[128,1600]{1,0:T(8,128)(2,1)}, bf16[128,1600]{1,0:T(8,128)(2,1)S(1)}, u32[]{:S(2)}, u32[]{:S(2)}) collective-permute-start(bf16[128,1600]{1,0:T(8,128)(2,1)} %get-tuple-element.263.refs_0_), channel_id=1, source_target_pairs={{0,1},{1,0},{2,3},{3,2},{4,5},{5,4},{6,7},{7,6},{8,9},{9,8},{10,11... | collective-permute-start | bytes 1228808 | tf_op jit(solution)/shard_map/ppermute | solution.py:25
  594.6 53.5 %collective-permute-start.84 = (bf16[128,1600]{1,0:T(8,128)(2,1)}, bf16[128,1600]{1,0:T(8,128)(2,1)}, u32[]{:S(2)}, u32[]{:S(2)}) collective-permute-start(bf16[128,1600]{1,0:T(8,128)(2,1)} %get-tuple-element.294), channel_id=1, source_target_pairs={{0,1},{1,0},{2,3},{3,2},{4,5},{5,4},{6,7},{7,6},{8,9},{9,8},{10,11... | collective-permute-start | bytes 1228808 | tf_op jit(solution)/shard_map/ppermute | solution.py:25
  595.2 54.5 %collective-permute-start.85 = (bf16[128,1600]{1,0:T(8,128)(2,1)}, bf16[128,1600]{1,0:T(8,128)(2,1)}, u32[]{:S(2)}, u32[]{:S(2)}) collective-permute-start(bf16[128,1600]{1,0:T(8,128)(2,1)} %get-tuple-element.295), channel_id=1, source_target_pairs={{0,2},{1,3},{2,0},{3,1},{4,6},{5,7},{6,4},{7,5},{8,10},{9,11},{10,... | collective-permute-start | bytes 1228808 | tf_op jit(solution)/shard_map/ppermute | solution.py:25
  635.9 189.3 %reduce-scatter.14.cloned.1.call-start = ((), (), s32[]{:S(2)}) async-start(), calls=%async_computation.11 | async-start | bytes 6451200 | tf_op jit(solution)/shard_map/reduce_scatter | solution.py:800
  654.5 34.4 %collective-permute-start.89 = (bf16[128,1600]{1,0:T(8,128)(2,1)}, bf16[128,1600]{1,0:T(8,128)(2,1)}, u32[]{:S(2)}, u32[]{:S(2)}) collective-permute-start(bf16[128,1600]{1,0:T(8,128)(2,1)} %get-tuple-element.298.refs_0_.refs_8_), channel_id=1, source_target_pairs={{0,3},{1,2},{2,1},{3,0},{4,7},{5,6},{6,5},{7,4},{8,11},{9,10},{10,... | collective-permute-start | bytes 1228808 | tf_op jit(solution)/shard_map/ppermute | solution.py:25
  656.2 35.5 %collective-permute-start.88 = (bf16[128,1600]{1,0:T(8,128)(2,1)}, bf16[128,1600]{1,0:T(8,128)(2,1)}, u32[]{:S(2)}, u32[]{:S(2)}) collective-permute-start(bf16[128,1600]{1,0:T(8,128)(2,1)} %get-tuple-element.298.refs_0_.refs_8_), channel_id=1, source_target_pairs={{0,2},{1,3},{2,0},{3,1},{4,6},{5,7},{6,4},{7,5},{8,10},{9,11},{10,... | collective-permute-start | bytes 1228808 | tf_op jit(solution)/shard_map/ppermute | solution.py:25
  658.2 33.4 %collective-permute-start.87 = (bf16[128,1600]{1,0:T(8,128)(2,1)}, bf16[128,1600]{1,0:T(8,128)(2,1)S(1)}, u32[]{:S(2)}, u32[]{:S(2)}) collective-permute-start(bf16[128,1600]{1,0:T(8,128)(2,1)} %get-tuple-element.298.refs_0_.refs_8_), channel_id=1, source_target_pairs={{0,1},{1,0},{2,3},{3,2},{4,5},{5,4},{6,7},{7,6},{8,9},{9,8},{10,11... | collective-permute-start | bytes 1228808 | tf_op jit(solution)/shard_map/ppermute | solution.py:25
  688.7 38.0 %collective-permute-start.82 = (bf16[128,1600]{1,0:T(8,128)(2,1)}, bf16[128,1600]{1,0:T(8,128)(2,1)}, u32[]{:S(2)}, u32[]{:S(2)}) collective-permute-start(bf16[128,1600]{1,0:T(8,128)(2,1)} %get-tuple-element.290), channel_id=1, source_target_pairs={{0,2},{1,3},{2,0},{3,1},{4,6},{5,7},{6,4},{7,5},{8,10},{9,11},{10,... | collective-permute-start | bytes 1228808 | tf_op jit(solution)/shard_map/ppermute | solution.py:25
  688.9 37.8 %collective-permute-start.83 = (bf16[128,1600]{1,0:T(8,128)(2,1)}, bf16[128,1600]{1,0:T(8,128)(2,1)}, u32[]{:S(2)}, u32[]{:S(2)}) collective-permute-start(bf16[128,1600]{1,0:T(8,128)(2,1)} %get-tuple-element.291), channel_id=1, source_target_pairs={{0,3},{1,2},{2,1},{3,0},{4,7},{5,6},{6,5},{7,4},{8,11},{9,10},{10,... | collective-permute-start | bytes 1228808 | tf_op jit(solution)/shard_map/ppermute | solution.py:25
  765.9 26.3 %collective-permute-start.97 = (bf16[128,1600]{1,0:T(8,128)(2,1)}, bf16[128,1600]{1,0:T(8,128)(2,1)S(1)}, u32[]{:S(2)}, u32[]{:S(2)}) collective-permute-start(bf16[128,1600]{1,0:T(8,128)(2,1)} %get-tuple-element.323), channel_id=1, source_target_pairs={{0,2},{1,3},{2,0},{3,1},{4,6},{5,7},{6,4},{7,5},{8,10},{9,11},{10,... | collective-permute-start | bytes 1228808 | tf_op jit(solution)/shard_map/ppermute | solution.py:25
  767.4 24.9 %collective-permute-start.98 = (bf16[128,1600]{1,0:T(8,128)(2,1)}, bf16[128,1600]{1,0:T(8,128)(2,1)}, u32[]{:S(2)}, u32[]{:S(2)}) collective-permute-start(bf16[128,1600]{1,0:T(8,128)(2,1)} %get-tuple-element.324), channel_id=1, source_target_pairs={{0,3},{1,2},{2,1},{3,0},{4,7},{5,6},{6,5},{7,4},{8,11},{9,10},{10,... | collective-permute-start | bytes 1228808 | tf_op jit(solution)/shard_map/ppermute | solution.py:25
  774.1 24.6 %collective-permute-start.100 = (f32[2,6,400]{2,0,1:T(2,128)}, f32[2,6,400]{2,0,1:T(2,128)S(1)}, u32[]{:S(2)}, u32[]{:S(2)}) collective-permute-start(f32[2,6,400]{2,0,1:T(2,128)} %get-tuple-element.476), channel_id=1, source_target_pairs={{0,1},{1,0},{2,3},{3,2},{4,5},{5,4},{6,7},{7,6},{8,9},{9,8},{10,11... | collective-permute-start | bytes 57608 | tf_op jit(solution)/shard_map/ppermute | solution.py:25
  (235 other events, 2146.0 us)
Sparse Core Ops, SparseCore 0:
  33.9 61.5 all-gather.6
  97.1 99.4 all-gather.8
  198.8 58.5 all-gather.10
  259.4 99.4 all-gather.4
  397.0 58.4 reduce-scatter.15
  457.7 60.0 reduce-scatter.17
  538.9 63.5 reduce-scatter.11
  636.1 105.3 reduce-scatter.19
  743.7 63.1 reduce-scatter.13

commit v4 on v3

--- a/solution.py
+++ b/solution.py
@@ -29,8 +29,15 @@
     def move(self, parts):
         return [xor_step(part, "col", j + 1) for j, part in enumerate(parts)]
 
-    def spread(self, rows):
-        return [rows] + self.move([rows] * (lax.axis_size("col") - 1))
+    def spread(self, rows, axis=0):
+        count = lax.axis_size("col")
+        if count != 4:
+            return [rows] + self.move([rows] * (count - 1))
+        half = rows.shape[axis] // 2
+        one, two = xor_step(rows, "col", 1), xor_step(rows, "col", 2)
+        low = xor_step(lax.slice_in_dim(two, 0, half, axis=axis), "col", 1)
+        high = xor_step(lax.slice_in_dim(one, half, 2 * half, axis=axis), "col", 2)
+        return [rows, one, two, low, high]
 
     def exchange(self, parts):
         return [parts[0]] + self.move(list(parts[1:]))
@@ -367,27 +374,47 @@
     )
 
 
-def feed_down(hidden, down, parts):
-    rows, units = hidden.shape
-    features = down.dims[0]
+def feed_last(hiddens, middles, shift, down):
+    rows, units = hiddens[0].shape
+    own, features = middles[0].shape
+    cols = rows // own
+    width = features // cols
+    count = len(hiddens)
 
     def kernel(*refs):
-        hidden_ref, down_hbm = refs[:2]
-        part_refs, (down_ref, down_sem) = refs[2 : 2 + parts], refs[2 + parts :]
+        hidden_refs, refs = refs[:count], refs[count:]
+        middle_refs, refs = refs[:count], refs[count:]
+        shift_ref, down_hbm = refs[:2]
+        part_refs, refs = refs[2 : 2 + count * cols], refs[2 + count * cols :]
+        ordered, whole, down_ref, down_sem = refs
         (wait,) = fetch((down,), (down_hbm,), ((down_ref, down_sem),))
+        here = lax.axis_index("col")
         finish(wait)
-        for begin in range(0, rows, CHUNK):
-            some = slice(begin, begin + CHUNK)
-            store_parts(part_refs, begin, contract(hidden_ref[some, :], down_ref[...], 1, 1))
-
-    return call(
+        for i in range(count):
+            for t in range(cols):
+                start = pl.multiple_of((here ^ t) * own, own)
+                ordered[t * own : (t + 1) * own, :] = hidden_refs[i][pl.ds(start, own), :]
+            base = (middle_refs[i][...] + shift_ref[...]).T
+            for begin in range(0, features, width):
+                some = slice(begin, begin + width)
+                value = contract(down_ref[some, :], ordered[...], 1, 1)
+                for t in range(cols):
+                    tokens = slice(t * own, (t + 1) * own)
+                    extra = jnp.where(here == t, base[some, :], 0.0)
+                    whole[some, tokens] = value[:, tokens] + extra
+            for j in range(cols):
+                start = pl.multiple_of((here ^ j) * width, 8)
+                part_refs[i * cols + j][...] = whole[pl.ds(start, width), :].astype(BF)
+
+    result = call(
         kernel,
-        [shape((rows // parts, features), BF)] * parts,
-        [hidden, down.array],
-        down.scratch(),
-        flops=2 * rows * features * units,
-        anywhere=(1,),
-    )
+        [shape((width, rows), BF)] * (count * cols),
+        list(hiddens) + list(middles) + [shift, down.array],
+        [pltpu.VMEM((rows, units), BF), pltpu.VMEM((features, rows), F32)] + down.scratch(),
+        flops=2 * count * rows * features * units,
+        anywhere=(2 * count + 1,),
+    )
+    return [result[i * cols : (i + 1) * cols] for i in range(count)]
 
 
 def feed_forward(pieces, up, down, bias, parts):
@@ -532,20 +559,24 @@
 
 
 def turn_blocks(blocks, gain, offset):
-    cols = len(blocks)
+    count = len(blocks)
     width, rows = blocks[0].shape
+    cols = lax.axis_size("col")
     own = rows // cols
     normed = gain is not None
     vectors = [gain, offset] if normed else []
 
     def kernel(*refs):
-        block_refs, refs = refs[:cols], refs[cols:]
+        block_refs, refs = refs[:count], refs[count:]
         vector_refs, refs = refs[: len(vectors)], refs[len(vectors) :]
         out_ref, own_ref, held = refs[0], refs[1], refs[-1]
         whole = refs[2] if normed else out_ref
         here = lax.axis_index("col")
-        for j in range(cols):
-            held[j] = block_refs[j][...]
+        at = 0
+        for block_ref in block_refs:
+            columns = block_ref.shape[1]
+            held[at // rows, :, at % rows : at % rows + columns] = block_ref[...]
+            at += columns
         for t in range(cols):
             plane = held[here ^ t].T
             for i in range(cols):
@@ -584,17 +615,6 @@
         [shape(stream.shape, F32), shape(stream.shape, BF)],
         list(terms) + [stream, shift, gain, offset],
     )
-
-
-def add_and_turn(terms, stream, shift):
-    count = len(terms)
-
-    def kernel(*refs):
-        stream_ref, shift_ref, out_ref = refs[count:]
-        value = stream_ref[...] + sum_refs(refs[:count]) + shift_ref[...]
-        out_ref[...] = value.T.astype(BF)
-
-    return call(kernel, [shape(stream.shape[::-1], BF)], list(terms) + [stream, shift])[0]
 
 
 def norm_backward(terms, stream, base, gain, turn, weight):
@@ -673,6 +693,18 @@
         both = [full[:, k].reshape(count * block, -1) for k in range(2)]
         return tuple(Matrix(one, [(0, 0, count * block)]) for one in both)
 
+    def gather_halves(own_part, block):
+        full, low, count = gather_block(own_part)
+        high = block - low
+        if low % 16 == 0 and high % 16 == 0:
+            runs = []
+            for i in range(count):
+                runs.append((2 * i * low, i * block, low))
+                runs.append(((2 * i + 1) * low, i * block + low, high))
+            return Matrix(full, runs)
+        full = full.reshape(count, 2 * low, -1)[:, :block].reshape(count * block, -1)
+        return Matrix(full, [(0, 0, count * block)])
+
     pair_one = jnp.stack([query_weight[0], key_weight[0]])
     pair_two = jnp.stack([value_weight[0], out_weight[0].T])
     keep = jnp.where(is_first, pair_one, pair_two)
@@ -686,10 +718,20 @@
         jnp.concatenate([item[0], item[1]], axis=1)
         for item in (jnp.where(is_first, keep, got), jnp.where(is_first, got, keep))
     ]
+    block = up_weight.shape[1]
+    low = block // 2
+    low += -low % 16 if block % 16 == 0 else 0
+
     def exchange_wide(up_own, down_own):
-        keep = jnp.where(is_first, up_own, down_own)
-        got = swap_section(jnp.where(is_first, down_own, up_own))
-        return jnp.where(is_first, keep, got), jnp.where(is_first, got, keep)
+        fill = jnp.zeros((2 * low - block, up_own.shape[1]), BF)
+        lows = jnp.concatenate([up_own[:low], down_own[:low]])
+        got = swap_section(jnp.where(is_first, jnp.concatenate([down_own, fill]), lows))
+        first_layer = jnp.where(is_first, up_own, got[:block])
+        seconds = [
+            jnp.where(is_first, got[begin : begin + low], jnp.concatenate([item[low:], fill]))
+            for begin, item in ((0, up_own), (low, down_own))
+        ]
+        return first_layer, seconds
 
     small_wide = jnp.stack(
         [first_gain[0], first_bias[0], out_bias[0], second_gain[0], second_bias[0], down_bias[0]]
@@ -720,8 +762,8 @@
     link = Link()
     input_own = lax.dynamic_slice_in_dim(block_input, section * mine, mine, 0)
     cotangent_own = lax.dynamic_slice_in_dim(out_cotangent, section * mine, mine, 0)
-    early = link.spread(input_own)
-    late = link.spread(after(cotangent_own, early))
+    early = link.spread(input_own, 2)
+    late = link.spread(after(cotangent_own, early), 2)
     wide_first, wide_second = exchange_wide(
         *after((up_weight[0], down_weight[0]), heads_parts, early, small_layers)
     )
@@ -742,7 +784,10 @@
 
     everyone = range(mine)
     weights = [gather_pair(heads_parts[0]) + gather_pair(wide_first)]
-    weights.append(gather_pair(heads_parts[1]) + gather_pair(wide_second))
+    weights.append(
+        gather_pair(heads_parts[1])
+        + tuple(gather_halves(item, block) for item in wide_second)
+    )
     saved = [[None] * mine, [None] * mine]
     turned_inputs = [
         turn_blocks([item[i] for item in early], smalls[0][0][0], smalls[0][0][1])
@@ -799,6 +844,14 @@
     def scatter_rows(grad):
         return lax.psum_scatter(grad, ("row", "section"), scatter_dimension=0, tiled=True)
 
+    def all_heads_grad(qkv_grads):
+        return weight_grad(
+            [
+                (saved[layer][0][1] + saved[layer][1][1], qkv_grads),
+                (mids[0] + mids[1], [saved[layer][batch][3] for batch in everyone]),
+            ]
+        )
+
     reduced = [None, None]
     wide_sums = [None, None]
     narrow_sums = [None, None]
@@ -826,24 +879,18 @@
         terms = []
         for batch in everyone:
             slope = saved[layer][batch][8]
-            slope = after(slope, down_grad if layer == 1 else first_sum)
+            slope = after(slope, down_grad if layer == 1 else (first_sum, heads_grad))
             hidden_grad, hidden_sum, parts = feed_backward(ups[batch], up, down, slope, cols)
             hidden_grads.append(hidden_grad)
             up_sums.append(hidden_sum[0])
             terms.append(link.exchange(parts))
-        up_job = (saved[layer][0][6] + saved[layer][1][6], hidden_grads)
-        if layer == 1:
-            up_grad = weight_grad([up_job])
-            up_sum = scatter_rows(up_grad)
-        else:
-            wide_grad = weight_grad([down_job, up_job])
-            wide_sum = scatter_rows(wide_grad)
+        if layer == 0:
+            down_grad = weight_grad([(after(down_job[0], hidden_grads), down_job[1])])
+            down_sum = scatter_rows(down_grad)
         middle_grads = []
         seconds = []
         for batch in everyone:
             middle = saved[layer][batch][5]
-            if layer == 1:
-                middle = after(middle, up_grad)
             middle_grad, half, second_sums = norm_backward(
                 terms[batch], middle, bases[batch], gain_two, False,
                 layer * 15000000000 + (1 - layer) * 15000000000,
@@ -851,11 +898,14 @@
             middle_grads.append(middle_grad)
             seconds.append(second_sums)
             mids.append(link.spread(half))
+            if batch == 0:
+                up_job = (saved[layer][0][6] + saved[layer][1][6], after(hidden_grads, half))
+                up_grad = weight_grad([up_job])
+                up_sum = scatter_rows(up_grad)
         terms = []
         for batch in everyone:
             qkv, lse = saved[layer][batch][2], saved[layer][batch][4]
-            if layer == 0:
-                lse = after(lse, wide_grad, reduced[1][2])
+            lse = after(lse, up_grad, reduced[1][2] if layer == 0 else ())
             qkv_grad, head_sum, parts = heads_backward(
                 mids[batch], first, second, qkv, lse, mask, heads, cols,
                 (1 - layer) * 15000000000,
@@ -863,14 +913,12 @@
             qkv_grads.append(qkv_grad)
             head_sums.append(head_sum.reshape(-1))
             terms.append(link.exchange(parts))
-        heads_grad = weight_grad(
-            [
-                (saved[layer][0][1] + saved[layer][1][1], qkv_grads),
-                (mids[0] + mids[1], [saved[layer][batch][3] for batch in everyone]),
-            ]
-        )
+        if layer == 0:
+            heads_grad = all_heads_grad(qkv_grads)
         for batch in everyone:
-            stream = after(saved[layer][batch][0], heads_grad)
+            stream = saved[layer][batch][0]
+            if layer == 0:
+                stream = after(stream, heads_grad)
             stream_grad, half, first_sums = norm_backward(
                 terms[batch], stream, middle_grads[batch], gain_one, layer == 0, layer * 15000000000
             )
@@ -878,14 +926,15 @@
             next_bases.append(stream_grad)
             if layer == 1:
                 next_ups.append(link.spread(half))
+                if batch == 0:
+                    heads_grad = all_heads_grad(after(qkv_grads, half))
             else:
                 turned.append(half)
             sums.append((first_sums, second_sums))
-        if layer == 1:
-            wide_sum = jnp.concatenate([down_sum, up_sum], axis=1)
+        wide_sum = jnp.concatenate([down_sum, up_sum], axis=1)
         first_sum = (down_sum, up_sum) if layer == 1 else None
         if layer == 0:
-            heads_grad = after(heads_grad, wide_sum, turned)
+            heads_grad = after(heads_grad, down_sum, up_sum, turned)
         reduced[layer] = (wide_sum, up_sum, scatter_rows(heads_grad))
         first_sums = sums[0][0] + sums[1][0]
         second_sums = sums[0][1] + sums[1][1]
@@ -900,13 +949,17 @@
         ups = next_ups
 
 
-    last_parts = [
-        feed_down(after(saved[1][batch][7], turned), weights[1][3], cols) for batch in everyone
-    ]
-    finals = []
+    last_parts = feed_last(
+        after([saved[1][batch][7] for batch in everyone], turned),
+        [saved[1][batch][5] for batch in everyone],
+        smalls[1][0][5],
+        weights[1][3],
+    )
+    outputs = []
     for batch in everyone:
         terms = link.exchange(last_parts[batch])
-        finals.append(add_and_turn(terms, saved[1][batch][5], smalls[1][0][5]))
+        outputs.append(sum([term.astype(F32) for term in terms[1:]], terms[0].astype(F32)))
+    outputs = jnp.stack(outputs).astype(BF)
 
     wide_sums = after(wide_sums, last_parts)
     wide_both = jnp.stack(wide_sums).reshape(2, 6, cols, width)
@@ -956,8 +1009,7 @@
         [jnp.where(is_first, keep, got), jnp.where(is_first, got, keep)], axis=1
     ).astype(F32)
 
-    both = to_features(turned + finals)
-    grads, outputs = both[:mine], both[mine:]
+    grads = to_features(turned)
     got = swap_section(jnp.where(is_first, outputs, grads))
     keep = jnp.where(is_first, grads, outputs)
     boundary = jnp.concatenate(

time: 866 us -> 858 us (level)
  waiting for transfers between devices: 217 us -> 179 us
  local copies, waits for them, and re-layouts: 115 us -> 152 us
    slice x0 -> x32, local copies, waits for them, and re-layouts: none -> 30.5 us  [the longest x14 14.6 us: spread(): high = xor_step(lax.slice_in_dim(one, half, 2 * half, axis=axis), 'col', 2)]
    ppermute x105 -> x119, waiting for transfers between devices: 185 us -> 159 us  [xor_step(): return lax.ppermute(value, axis, [(i, i ^ step) for i in range(count)])]
    unnamed x357 -> x431, local copies, waits for them, and re-layouts: 88.9 us -> 98.1 us
    pallas_call x43 -> x41, Pallas kernels: 331 us -> 323 us  [call(): pl.pallas_call(kernel, out_shape=tuple(outs), in_specs=[pl.BlockSpec(memo...]
    ppermute x105 -> x119, starting transfers between devices: 127 us -> 127 us  [xor_step(): return lax.ppermute(value, axis, [(i, i ^ step) for i in range(count)])]
  transfers between devices with their start and end apart: 121 -> 137, of which waited for: 40 -> 41; matrix products, arithmetic and copies ran while one was open for 5% -> 8% of each run, Pallas kernels for 37% -> 38%
where the time goes in v4:
time: 858 us; the launch traced here: 848 us
  Pallas kernels  323 us (38%)
  waiting for transfers between devices  179 us (21%)
  local copies, waits for them, and re-layouts  152 us (18%)
  starting transfers between devices  146 us (17%)
  other arithmetic  31.4 us (4%)
  between operations  17.2 us (2%)
    pallas_call x41, Pallas kernels, call(): pl.pallas_call(kernel, out_shape=tuple(outs), in_specs=[pl.BlockSpec(memo...  323 us
    ppermute x119, waiting for transfers between devices, xor_step(): return lax.ppermute(value, axis, [(i, i ^ step) for i in range(count)])  159 us
    ppermute x119, starting transfers between devices, xor_step(): return lax.ppermute(value, axis, [(i, i ^ step) for i in range(count)])  127 us
    unnamed x431, local copies, waits for them, and re-layouts  98.1 us
  transfers between devices with their start and end apart: 137, of which 41 were waited for; matrix products, arithmetic and copies ran while one was open for 8% of the time, Pallas kernels for 38%

profile of v4, /device:TPU:0, one launch (start us, length us, event | category | flops | bytes accessed | tf_op | source)
XLA Modules:
  0.0 848.2 jit_solution(7756693479896337072)
XLA Ops:
  17.4 6.1 collective-permute-done.8
  23.5 4.0 collective-permute-done.10
  27.5 4.2 broadcast_select_fusion.8
  41.3 4.1 collective-permute-start.1
  46.8 16.4 %collective-permute-done.1 = bf16[2,400,512]{2,1,0:T(8,128)(2,1)} collective-permute-done((bf16[2,400,512]{2,1,0:T(8,128)(2,1)}, bf16[2,400,512]{2,1,0:T(8,128)(2,1)}, u32[]{:S(2)}, u32[]{:S(2)}) %collective-permute-start.1) | collective-permute-done | bytes 819232 | tf_op jit(solution)/shard_map/ppermute | solution.py:25
  71.0 4.1 collective-permute-done.2
  77.7 3.1 collective-permute-done.16
  107.3 4.6 collective-permute-done.5
  119.8 13.3 %shard_map.299 = (bf16[512,1344]{1,0:T(8,128)(2,1)S(1)}, bf16[512,448]{1,0:T(8,128)(2,1)S(1)}, f32[7,512]{1,0:T(8,128)S(1)}, bf16[128,1600]{1,0:T(8,128)(2,1)S(1...) custom-call(bf16[512,1600]{1,0:T(8,128)(2,1)S(1)} %copy-done.85, ...), custom_call_target="tpu_custom_call" | custom-call | flops 19260243968 | tf_op jit(solution)/shard_map/pallas_call | solution.py:141
  138.5 12.9 %shard_map.308 = (bf16[512,1344]{1,0:T(8,128)(2,1)S(1)}, bf16[512,448]{1,0:T(8,128)(2,1)S(1)}, f32[7,512]{1,0:T(8,128)S(1)}, bf16[128,1600]{1,0:T(8,128)(2,1)S(1...) custom-call(bf16[512,1600]{1,0:T(8,128)(2,1)S(1)} %copy-done.88, ...), custom_call_target="tpu_custom_call" | custom-call | flops 19260243968 | tf_op jit(solution)/shard_map/pallas_call | solution.py:141
  158.7 7.3 collective-permute-done.38.refs_1_
  166.0 9.5 %collective-permute-done.39.refs_2_ = bf16[128,1600]{1,0:T(8,128)(2,1)S(1)} collective-permute-done((bf16[128,1600]{1,0:T(8,128)(2,1)S(1)}, bf16[128,1600]{1,0:T(8,128)(2,1)S(1)}, u32[]{:S(2)}, u32[]{:S(2)}) %collective-permute-start.39) | collective-permute-done | bytes 409632 | tf_op jit(solution)/shard_map/ppermute | solution.py:25
  179.3 5.4 collective-permute-done.21.refs_2_
  188.7 4.9 collective-permute-done.42.refs_2_.refs_7_
  205.1 13.5 %shard_map.302 = (bf16[512,1600]{1,0:T(8,128)(2,1)S(1)}, bf16[512,1600]{1,0:T(8,128)(2,1)S(1)}, bf16[128,1600]{1,0:T(8,128)(2,1)S(1)}, bf16[128,1600]{1,0:T(8,12...) custom-call(bf16[128,1600]{1,0:T(8,128)(2,1)S(1)} %copy-done.102, bf16[128,1600]{1,0:T(8,128)(2,1)S(1)} %copy-done.42, ...), custom_call_target="tpu_custom_call" | custom-call | flops 20971520000 | tf_op jit(solution)/shard_map/pallas_call | solution.py:141
  225.3 14.4 %shard_map.310 = (bf16[512,1600]{1,0:T(8,128)(2,1)S(1)}, bf16[512,1600]{1,0:T(8,128)(2,1)S(1)}, bf16[128,1600]{1,0:T(8,128)(2,1)S(1)}, bf16[128,1600]{1,0:T(8,12...) custom-call(bf16[128,1600]{1,0:T(8,128)(2,1)S(1)} %copy-done.105, bf16[128,1600]{1,0:T(8,128)(2,1)S(1)} %copy-done.48, ...), custom_call_target="tpu_custom_call" | custom-call | flops 20971520000 | tf_op jit(solution)/shard_map/pallas_call | solution.py:141
  249.4 2.5 shard_map.303
  256.0 7.3 collective-permute-done.46.refs_2_
  263.3 2.9 collective-permute-done.47.refs_3_
  266.1 2.9 shard_map.311
  278.3 3.7 collective-permute-done.49.refs_2_.refs_7_
  288.7 14.0 %shard_map.304 = (bf16[512,1344]{1,0:T(8,128)(2,1)S(1)}, bf16[512,448]{1,0:T(8,128)(2,1)S(1)}, f32[7,512]{1,0:T(8,128)S(1)}, bf16[128,1600]{1,0:T(8,128)(2,1)S(1...) custom-call(bf16[128,1600]{1,0:T(8,128)(2,1)} %get-tuple-element.212.refs_0_, ...), custom_call_target="tpu_custom_call" | custom-call | flops 19260243968 | tf_op jit(solution)/shard_map/pallas_call | solution.py:141
  308.1 14.4 %shard_map.312 = (bf16[512,1344]{1,0:T(8,128)(2,1)S(1)}, bf16[512,448]{1,0:T(8,128)(2,1)S(1)}, f32[7,512]{1,0:T(8,128)S(1)}, bf16[128,1600]{1,0:T(8,128)(2,1)S(1...) custom-call(bf16[128,1600]{1,0:T(8,128)(2,1)} %get-tuple-element.234.refs_0_.refs_5_,, ...), custom_call_target="tpu_custom_call" | custom-call | flops 19260243968 | tf_op jit(solution)/shard_map/pallas_call | solution.py:141
  333.0 4.3 collective-permute-done.52.refs_1_
  337.3 5.0 collective-permute-done.53.refs_2_
  342.3 4.4 collective-permute-done.54.refs_3_
  371.4 8.6 %shard_map.306 = (bf16[512,1600]{1,0:T(8,128)(2,1)S(1)}, bf16[512,1600]{1,0:T(8,128)(2,1)S(1)}) custom-call(bf16[128,1600]{1,0:T(8,128)(2,1)S(1)} %copy-done.108, bf16[128,1600]{1,0:T(8,128)(2,1)S(1)} %copy-done.60, bf16[128,1600]{1,0:T(8,128)(2,1)S(1)} %copy-done.57, bf16[64,1600]{1,0:T(8,128)(2,1)} %collective-permute-done.36.refs_3_, ...), custom_call_target="tpu_custom_call" | custom-call | flops 10485760000 | tf_op jit(solution)/shard_map/pallas_call | solution.py:141
  381.3 9.2 %shard_map.314 = (bf16[512,1600]{1,0:T(8,128)(2,1)S(1)}, bf16[512,1600]{1,0:T(8,128)(2,1)S(1)}) custom-call(bf16[128,1600]{1,0:T(8,128)(2,1)S(1)} %copy-done.111, bf16[128,1600]{1,0:T(8,128)(2,1)S(1)} %copy-done.65, bf16[128,1600]{1,0:T(8,128)(2,1)S(1)} %copy-done.63, bf16[64,1600]{1,0:T(8,128)(2,1)S(1)} %collective-permute-done.57.refs_3_.refs_8_, ...), custom_call_target="tpu_custom_call" | custom-call | flops 10485760000 | tf_op jit(solution)/shard_map/pallas_call | solution.py:141
  391.7 8.7 %shard_map.315 = bf16[1600,1600]{1,0:T(8,128)(2,1)} custom-call(bf16[512,1600]{1,0:T(8,128)(2,1)S(1)} %copy-done.93, bf16[512,1600]{1,0:T(8,128)(2,1)S(1)} %copy-done.90, bf16[512,1600]{1,0:T(8,128)(2,1)S(1)} %get-tuple-element.331.refs_2_.refs_0_, bf16[512,1600]{1,0:T(8,128)(2,1)S(1)} %get-tuple-element.332.refs_3_.refs_1_), custom_call_target="tpu_custom_call" | custom-call | flops 20971520000 | tf_op jit(solution)/shard_map/pallas_call | solution.py:141
  404.8 11.3 %shard_map.316 = (bf16[512,1600]{1,0:T(8,128)(2,1)S(1)}, f32[1,1600]{1,0:T(1,128)S(1)}, bf16[128,1600]{1,0:T(8,128)(2,1)S(1)}, bf16[128,1600]{1,0:T(8,128)(2,1)S...) custom-call(bf16[512,1600]{1,0:T(8,128)(2,1)S(1)} %copy-done.94, ...), custom_call_target="tpu_custom_call" | custom-call | flops 20971520000 | tf_op jit(solution)/shard_map/pallas_call | solution.py:141
  419.7 11.2 %shard_map.318 = (bf16[512,1600]{1,0:T(8,128)(2,1)S(1)}, f32[1,1600]{1,0:T(1,128)S(1)}, bf16[128,1600]{1,0:T(8,128)(2,1)S(1)}, bf16[128,1600]{1,0:T(8,128)(2,1)S...) custom-call(bf16[512,1600]{1,0:T(8,128)(2,1)S(1)} %copy-done.91, ...), custom_call_target="tpu_custom_call" | custom-call | flops 20971520000 | tf_op jit(solution)/shard_map/pallas_call | solution.py:141
  439.4 4.4 collective-permute-done.73.refs_1_
  443.8 7.3 collective-permute-done.74.refs_2_
  451.2 2.6 collective-permute-done.75.refs_3_
  458.2 3.4 collective-permute-done.63.refs_2_.refs_14_
  465.2 10.1 %shard_map.319 = bf16[1600,1600]{1,0:T(8,128)(2,1)} custom-call(bf16[128,1600]{1,0:T(8,128)(2,1)S(1)} %copy-done.109, bf16[128,1600]{1,0:T(8,128)(2,1)S(1)} %copy-done.61, bf16[128,1600]{1,0:T(8,128)(2,1)S(1)} %copy-done.58, bf16[64,1600]{1,0:T(8,128)(2,1)} %collective-permute-done.36.refs_3_, bf16[64,1600]{1,0:T(8,128)(2,1)} %collective-permute-done.37.refs_4_, ...), custom_call_target="tpu_custom_call" | custom-call | flops 20971520000 | tf_op jit(solution)/shard_map/pallas_call | solution.py:141
  483.2 15.8 %shard_map.320 = (bf16[512,1344]{1,0:T(8,128)(2,1)S(1)}, f32[2,448]{1,0:T(2,128)S(1)}, bf16[128,1600]{1,0:T(8,128)(2,1)S(1)}, bf16[128,1600]{1,0:T(8,128)(2,1)S(...) custom-call(bf16[128,1600]{1,0:T(8,128)(2,1)S(1)} %copy-done.114, bf16[128,1600]{1,0:T(8,128)(2,1)S(1)} %copy-done.68, ...), custom_call_target="tpu_custom_call" | custom-call | flops 30534533120 | tf_op jit(solution)/shard_map/pallas_call | solution.py:141
  502.6 17.1 %shard_map.323 = (bf16[512,1344]{1,0:T(8,128)(2,1)S(1)}, f32[2,448]{1,0:T(2,128)S(1)}, bf16[128,1600]{1,0:T(8,128)(2,1)S(1)}, bf16[128,1600]{1,0:T(8,128)(2,1)},...) custom-call(bf16[128,1600]{1,0:T(8,128)(2,1)} %get-tuple-element.273.refs_0_.refs_17_, ...), custom_call_target="tpu_custom_call" | custom-call | flops 30534533120 | tf_op jit(solution)/shard_map/pallas_call | solution.py:141
  530.0 13.0 %shard_map.324 = bf16[1600,1792]{1,0:T(8,128)(2,1)} custom-call(bf16[128,1600]{1,0:T(8,128)(2,1)} %get-tuple-element.212.refs_0_, bf16[128,1600]{1,0:T(8,128)(2,1)S(1)} %copy-done.55, bf16[128,1600]{1,0:T(8,128)(2,1)S(1)} %copy-done.52, bf16[64,1600]{1,0:T(8,128)(2,1)} %collective-permute-done.29.refs_3_, bf16[64,1600]{1,0:T(8,128)(2,1)} %collective-permute-done.30.refs_4_, ...), custom_call_target="tpu_custom_call" | custom-call | flops 23488102400 | tf_op jit(solution)/shard_map/pallas_call | solution.py:141
  556.0 2.5 collective-permute-done.91.refs_2_.refs_7_
  564.5 13.2 %shard_map.325 = (bf16[512,1600]{1,0:T(8,128)(2,1)S(1)}, f32[1,1600]{1,0:T(1,128)S(1)}, bf16[128,1600]{1,0:T(8,128)(2,1)S(1)}, bf16[128,1600]{1,0:T(8,128)(2,1)}...) custom-call(bf16[128,1600]{1,0:T(8,128)(2,1)} %get-tuple-element.359.refs_0_, ...), custom_call_target="tpu_custom_call" | custom-call | flops 20971520000 | tf_op jit(solution)/shard_map/pallas_call | solution.py:141
  580.5 13.4 %shard_map.328 = (bf16[512,1600]{1,0:T(8,128)(2,1)S(1)}, f32[1,1600]{1,0:T(1,128)S(1)}, bf16[128,1600]{1,0:T(8,128)(2,1)S(1)}, bf16[128,1600]{1,0:T(8,128)(2,1)}...) custom-call(bf16[128,1600]{1,0:T(8,128)(2,1)S(1)} %copy-done.120, bf16[128,1600]{1,0:T(8,128)(2,1)S(1)} %copy-done.79, ...), custom_call_target="tpu_custom_call" | custom-call | flops 20971520000 | tf_op jit(solution)/shard_map/pallas_call | solution.py:141
  601.3 10.4 %shard_map.337 = bf16[1600,1600]{1,0:T(8,128)(2,1)} custom-call(bf16[128,1600]{1,0:T(8,128)(2,1)} %get-tuple-element.359.refs_0_, bf16[128,1600]{1,0:T(8,128)(2,1)} %collective-permute-done.69.refs_1_, bf16[128,1600]{1,0:T(8,128)(2,1)} %collective-permute-done.70.refs_2_, bf16[64,1600]{1,0:T(8,128)(2,1)} %collective-permute-done.71.refs_3_, ...), custom_call_target="tpu_custom_call" | custom-call | flops 20971520000 | tf_op jit(solution)/shard_map/pallas_call | solution.py:141
  611.7 4.8 collective-permute-done.97.refs_1_
  619.9 6.3 collective-permute-done.99.refs_3_
  634.7 3.0 shard_map.326
  646.8 9.8 %shard_map.329 = bf16[1600,1600]{1,0:T(8,128)(2,1)} custom-call(bf16[128,1600]{1,0:T(8,128)(2,1)S(1)} %copy-done.103, bf16[128,1600]{1,0:T(8,128)(2,1)S(1)} %copy-done.43, bf16[128,1600]{1,0:T(8,128)(2,1)S(1)} %copy-done.40, bf16[64,1600]{1,0:T(8,128)(2,1)S(1)} %copy-done.129, bf16[64,1600]{1,0:T(8,128)(2,1)S(1)} %copy-done.132, ...), custom_call_target="tpu_custom_call" | custom-call | flops 20971520000 | tf_op jit(solution)/shard_map/pallas_call | solution.py:141
  665.7 16.6 %shard_map.332 = (bf16[512,1344]{1,0:T(8,128)(2,1)S(1)}, f32[2,448]{1,0:T(2,128)S(1)}, bf16[128,1600]{1,0:T(8,128)(2,1)S(1)}, bf16[128,1600]{1,0:T(8,128)(2,1)S(...) custom-call(bf16[128,1600]{1,0:T(8,128)(2,1)S(1)} %copy-done.117, bf16[128,1600]{1,0:T(8,128)(2,1)S(1)} %copy-done.74, ...), custom_call_target="tpu_custom_call" | custom-call | flops 90534535168 | tf_op jit(solution)/shard_map/pallas_call | solution.py:141
  686.0 17.3 %shard_map.330 = (bf16[512,1344]{1,0:T(8,128)(2,1)S(1)}, f32[2,448]{1,0:T(2,128)S(1)}, bf16[128,1600]{1,0:T(8,128)(2,1)S(1)}, bf16[128,1600]{1,0:T(8,128)(2,1)},...) custom-call(bf16[128,1600]{1,0:T(8,128)(2,1)} %get-tuple-element.288.refs_0_.refs_4_, ...), custom_call_target="tpu_custom_call" | custom-call | flops 90534535168 | tf_op jit(solution)/shard_map/pallas_call | solution.py:141
  708.4 11.8 %shard_map.333 = bf16[1600,1792]{1,0:T(8,128)(2,1)} custom-call(bf16[512,1600]{1,0:T(8,128)(2,1)S(1)} %copy-done.86, bf16[512,1600]{1,0:T(8,128)(2,1)} %copy-done.87, bf16[512,1344]{1,0:T(8,128)(2,1)S(1)} %get-tuple-element.308.refs_2_, bf16[512,1344]{1,0:T(8,128)(2,1)S(1)} %get-tuple-element.318.refs_3_, ...), custom_call_target="tpu_custom_call" | custom-call | flops 23488102400 | tf_op jit(solution)/shard_map/pallas_call | solution.py:141
  721.3 3.1 shard_map.335
  725.2 3.1 shard_map.334
  728.3 4.4 reduce-scatter.25.cloned.1.call-done
  738.8 9.8 %shard_map.336 = (bf16[400,512]{1,0:T(8,128)(2,1)S(1)}, bf16[400,512]{1,0:T(8,128)(2,1)S(1)}, bf16[400,512]{1,0:T(8,128)(2,1)S(1)}, bf16[400,512]{1,0:T(8,128)(2...) custom-call(bf16[512,1600]{1,0:T(8,128)(2,1)S(1)} %copy-done.136, ...), custom_call_target="tpu_custom_call" | custom-call | flops 20971520000 | tf_op jit(solution)/shard_map/pallas_call | solution.py:141
  758.1 2.8 collective-permute-done.116
  763.8 4.5 collective-permute-done.118
  770.0 3.8 collective-permute-done.119
  774.4 2.4 collective-permute-start.112
  777.8 3.5 all-to-all-start
  784.6 20.4 %collective-permute-done.111 = bf16[400,512]{1,0:T(8,128)(2,1)} collective-permute-done((bf16[400,512]{1,0:T(8,128)(2,1)}, bf16[400,512]{1,0:T(8,128)(2,1)}, u32[]{:S(2)}, u32[]{:S(2)}) %collective-permute-start.111) | collective-permute-done | bytes 409632 | tf_op jit(solution)/shard_map/ppermute | solution.py:25
  812.0 2.4 collective-permute-start.123
  822.6 3.9 collective-permute-start.120
  826.7 4.1 collective-permute-start.121
  830.8 2.9 fusion.4
  (862 shorter events, 338.6 us)
Async XLA Ops:
  7.2 111.1 %all-gather.10.cloned.1.call-start = ((), (), s32[]{:S(2)}) async-start(), calls=%async_computation.9 | async-start | bytes 6451200 | tf_op jit(solution)/shard_map/all_gather | solution.py:682
  33.7 166.4 %all-gather.12.cloned.1.call-start = ((), (), s32[]{:S(2)}) async-start(), calls=%async_computation.10 | async-start | bytes 11980800 | tf_op jit(solution)/shard_map/all_gather | solution.py:682
  41.3 21.9 %collective-permute-start.1 = (bf16[2,400,512]{2,1,0:T(8,128)(2,1)}, bf16[2,400,512]{2,1,0:T(8,128)(2,1)}, u32[]{:S(2)}, u32[]{:S(2)}) collective-permute-start(bf16[2,400,512]{2,1,0:T(8,128)(2,1)} %constant_dynamic-slice_fusion.10), channel_id=1, source_target_pairs={{0,2},{1,3},{2,0},{3,1},{4,6},{5,7},{6,4},{7,5},{8,10},{9,11},{10,... | collective-permute-start | bytes 2457608 | tf_op jit(solution)/shard_map/ppermute | solution.py:25
  46.7 22.2 %collective-permute-start.15 = (f32[12096]{0:T(1024)S(1)}, f32[12096]{0:T(1024)S(1)}, u32[]{:S(2)}, u32[]{:S(2)}) collective-permute-start(f32[12096]{0:T(1024)S(1)} %pad_maximum_fusion.12), channel_id=1, source_target_pairs={{0,16},{16,0},{1,17},{17,1},{2,18},{18,2},{3,19},{19,3},{4,20},{20... | collective-permute-start | bytes 145160 | tf_op jit(solution)/shard_map/ppermute | solution.py:25
  83.2 204.3 %all-gather.14.cloned.1.call-start = ((), (), s32[]{:S(2)}) async-start(), calls=%async_computation.11 | async-start | bytes 6451200 | tf_op jit(solution)/shard_map/all_gather | solution.py:682
  83.9 284.1 %all-gather.6.cloned.1.call-start = ((), (), s32[]{:S(2)}) async-start(), calls=%async_computation.7 | async-start | bytes 6230016 | tf_op jit(solution)/shard_map/all_gather | solution.py:682
  91.2 20.7 %collective-permute-start.5 = (bf16[2,400,512]{2,1,0:T(8,128)(2,1)}, bf16[2,400,512]{2,1,0:T(8,128)(2,1)}, u32[]{:S(2)}, u32[]{:S(2)}) collective-permute-start(bf16[2,400,512]{2,1,0:T(8,128)(2,1)} %constant_dynamic-slice_fusion.11), channel_id=1, source_target_pairs={{0,2},{1,3},{2,0},{3,1},{4,6},{5,7},{6,4},{7,5},{8,10},{9,11},{10,... | collective-permute-start | bytes 2457608 | tf_op jit(solution)/shard_map/ppermute | solution.py:25
  92.4 22.6 %collective-permute-start.4 = (bf16[2,400,512]{2,1,0:T(8,128)(2,1)}, bf16[2,400,512]{2,1,0:T(8,128)(2,1)}, u32[]{:S(2)}, u32[]{:S(2)}) collective-permute-start(bf16[2,400,512]{2,1,0:T(8,128)(2,1)} %constant_dynamic-slice_fusion.11), channel_id=1, source_target_pairs={{0,1},{1,0},{2,3},{3,2},{4,5},{5,4},{6,7},{7,6},{8,9},{9,8},{10,11... | collective-permute-start | bytes 2457608 | tf_op jit(solution)/shard_map/ppermute | solution.py:25
  95.5 306.3 %all-gather.8.cloned.1.call-start = ((), (), s32[]{:S(2)}) async-start(), calls=%async_computation.8 | async-start | bytes 6230016 | tf_op jit(solution)/shard_map/all_gather | solution.py:682
  113.7 39.6 %collective-permute-start.6 = (bf16[2,400,256]{2,1,0:T(8,128)(2,1)}, bf16[2,400,256]{2,1,0:T(8,128)(2,1)}, u32[]{:S(2)}, u32[]{:S(2)}) collective-permute-start(bf16[2,400,256]{2,1,0:T(8,128)(2,1)} %slice.541), channel_id=1, source_target_pairs={{0,1},{1,0},{2,3},{3,2},{4,5},{5,4},{6,7},{7,6},{8,9},{9,8},{10,11... | collective-permute-start | bytes 1228808 | tf_op jit(solution)/shard_map/ppermute | solution.py:25
  116.9 36.8 %collective-permute-start.7 = (bf16[2,400,256]{2,1,0:T(8,128)(2,1)}, bf16[2,400,256]{2,1,0:T(8,128)(2,1)S(1)}, u32[]{:S(2)}, u32[]{:S(2)}) collective-permute-start(bf16[2,400,256]{2,1,0:T(8,128)(2,1)} %slice.543), channel_id=1, source_target_pairs={{0,2},{1,3},{2,0},{3,1},{4,6},{5,7},{6,4},{7,5},{8,10},{9,11},{10,... | collective-permute-start | bytes 1228808 | tf_op jit(solution)/shard_map/ppermute | solution.py:25
  135.4 21.4 %collective-permute-start.18 = (bf16[128,1600]{1,0:T(8,128)(2,1)S(1)}, bf16[128,1600]{1,0:T(8,128)(2,1)S(1)}, u32[]{:S(2)}, u32[]{:S(2)}) collective-permute-start(bf16[128,1600]{1,0:T(8,128)(2,1)S(1)} %get-tuple-element.201), channel_id=1, source_target_pairs={{0,2},{1,3},{2,0},{3,1},{4,6},{5,7},{6,4},{7,5},{8,10},{9,11},{10,... | collective-permute-start | bytes 1228808 | tf_op jit(solution)/shard_map/ppermute | solution.py:25
  136.3 20.5 %collective-permute-start.19 = (bf16[128,1600]{1,0:T(8,128)(2,1)S(1)}, bf16[128,1600]{1,0:T(8,128)(2,1)S(1)}, u32[]{:S(2)}, u32[]{:S(2)}) collective-permute-start(bf16[128,1600]{1,0:T(8,128)(2,1)S(1)} %get-tuple-element.202), channel_id=1, source_target_pairs={{0,3},{1,2},{2,1},{3,0},{4,7},{5,6},{6,5},{7,4},{8,11},{9,10},{10,... | collective-permute-start | bytes 1228808 | tf_op jit(solution)/shard_map/ppermute | solution.py:25
  153.7 21.9 %collective-permute-start.39 = (bf16[128,1600]{1,0:T(8,128)(2,1)S(1)}, bf16[128,1600]{1,0:T(8,128)(2,1)S(1)}, u32[]{:S(2)}, u32[]{:S(2)}) collective-permute-start(bf16[128,1600]{1,0:T(8,128)(2,1)S(1)} %get-tuple-element.225), channel_id=1, source_target_pairs={{0,2},{1,3},{2,0},{3,1},{4,6},{5,7},{6,4},{7,5},{8,10},{9,11},{10,... | collective-permute-start | bytes 1228808 | tf_op jit(solution)/shard_map/ppermute | solution.py:25
  154.5 21.1 %collective-permute-start.40 = (bf16[128,1600]{1,0:T(8,128)(2,1)S(1)}, bf16[128,1600]{1,0:T(8,128)(2,1)S(1)}, u32[]{:S(2)}, u32[]{:S(2)}) collective-permute-start(bf16[128,1600]{1,0:T(8,128)(2,1)S(1)} %get-tuple-element.226), channel_id=1, source_target_pairs={{0,3},{1,2},{2,1},{3,0},{4,7},{5,6},{6,5},{7,4},{8,11},{9,10},{10,... | collective-permute-start | bytes 1228808 | tf_op jit(solution)/shard_map/ppermute | solution.py:25
  157.5 27.2 %collective-permute-start.21 = (bf16[128,1600]{1,0:T(8,128)(2,1)S(1)}, bf16[128,1600]{1,0:T(8,128)(2,1)S(1)}, u32[]{:S(2)}, u32[]{:S(2)}) collective-permute-start(bf16[128,1600]{1,0:T(8,128)(2,1)S(1)} %get-tuple-element.206.refs_0_), channel_id=1, source_target_pairs={{0,2},{1,3},{2,0},{3,1},{4,6},{5,7},{6,4},{7,5},{8,10},{9,11},{10,... | collective-permute-start | bytes 1228808 | tf_op jit(solution)/shard_map/ppermute | solution.py:25
  158.1 29.1 %collective-permute-start.20 = (bf16[128,1600]{1,0:T(8,128)(2,1)S(1)}, bf16[128,1600]{1,0:T(8,128)(2,1)S(1)}, u32[]{:S(2)}, u32[]{:S(2)}) collective-permute-start(bf16[128,1600]{1,0:T(8,128)(2,1)S(1)} %get-tuple-element.206.refs_0_), channel_id=1, source_target_pairs={{0,1},{1,0},{2,3},{3,2},{4,5},{5,4},{6,7},{7,6},{8,9},{9,8},{10,11... | collective-permute-start | bytes 1228808 | tf_op jit(solution)/shard_map/ppermute | solution.py:25
  195.0 30.2 %collective-permute-start.43 = (bf16[64,1600]{1,0:T(8,128)(2,1)}, bf16[64,1600]{1,0:T(8,128)(2,1)}, u32[]{:S(2)}, u32[]{:S(2)}) collective-permute-start(bf16[64,1600]{1,0:T(8,128)(2,1)} %slice.589), channel_id=1, source_target_pairs={{0,1},{1,0},{2,3},{3,2},{4,5},{5,4},{6,7},{7,6},{8,9},{9,8},{10,11... | collective-permute-start | bytes 614408 | tf_op jit(solution)/shard_map/ppermute | solution.py:25
  198.3 27.0 %collective-permute-start.44 = (bf16[64,1600]{1,0:T(8,128)(2,1)}, bf16[64,1600]{1,0:T(8,128)(2,1)}, u32[]{:S(2)}, u32[]{:S(2)}) collective-permute-start(bf16[64,1600]{1,0:T(8,128)(2,1)} %slice.590), channel_id=1, source_target_pairs={{0,2},{1,3},{2,0},{3,1},{4,6},{5,7},{6,4},{7,5},{8,10},{9,11},{10,... | collective-permute-start | bytes 614408 | tf_op jit(solution)/shard_map/ppermute | solution.py:25
  221.8 23.3 %collective-permute-start.24 = (bf16[128,1600]{1,0:T(8,128)(2,1)S(1)}, bf16[128,1600]{1,0:T(8,128)(2,1)S(1)}, u32[]{:S(2)}, u32[]{:S(2)}) collective-permute-start(bf16[128,1600]{1,0:T(8,128)(2,1)S(1)} %get-tuple-element.208), channel_id=1, source_target_pairs={{0,1},{1,0},{2,3},{3,2},{4,5},{5,4},{6,7},{7,6},{8,9},{9,8},{10,11... | collective-permute-start | bytes 1228808 | tf_op jit(solution)/shard_map/ppermute | solution.py:25
  222.8 24.5 %collective-permute-start.25 = (bf16[128,1600]{1,0:T(8,128)(2,1)}, bf16[128,1600]{1,0:T(8,128)(2,1)}, u32[]{:S(2)}, u32[]{:S(2)}) collective-permute-start(bf16[128,1600]{1,0:T(8,128)(2,1)} %get-tuple-element.209), channel_id=1, source_target_pairs={{0,2},{1,3},{2,0},{3,1},{4,6},{5,7},{6,4},{7,5},{8,10},{9,11},{10,... | collective-permute-start | bytes 1228808 | tf_op jit(solution)/shard_map/ppermute | solution.py:25
  223.9 23.5 %collective-permute-start.26 = (bf16[128,1600]{1,0:T(8,128)(2,1)}, bf16[128,1600]{1,0:T(8,128)(2,1)}, u32[]{:S(2)}, u32[]{:S(2)}) collective-permute-start(bf16[128,1600]{1,0:T(8,128)(2,1)} %get-tuple-element.210), channel_id=1, source_target_pairs={{0,3},{1,2},{2,1},{3,0},{4,7},{5,6},{6,5},{7,4},{8,11},{9,10},{10,... | collective-permute-start | bytes 1228808 | tf_op jit(solution)/shard_map/ppermute | solution.py:25
  247.2 315.8 %reduce-scatter.19.cloned.1.call-start = ((), (), s32[]{:S(2)}) async-start(), calls=%async_computation.14 | async-start | bytes 5990400
  252.8 20.7 %collective-permute-start.28 = (bf16[128,1600]{1,0:T(8,128)(2,1)}, bf16[128,1600]{1,0:T(8,128)(2,1)S(1)}, u32[]{:S(2)}, u32[]{:S(2)}) collective-permute-start(bf16[128,1600]{1,0:T(8,128)(2,1)} %get-tuple-element.212.refs_0_), channel_id=1, source_target_pairs={{0,2},{1,3},{2,0},{3,1},{4,6},{5,7},{6,4},{7,5},{8,10},{9,11},{10,... | collective-permute-start | bytes 1228808 | tf_op jit(solution)/shard_map/ppermute | solution.py:25
  283.6 24.5 %collective-permute-start.50 = (bf16[64,1600]{1,0:T(8,128)(2,1)}, bf16[64,1600]{1,0:T(8,128)(2,1)}, u32[]{:S(2)}, u32[]{:S(2)}) collective-permute-start(bf16[64,1600]{1,0:T(8,128)(2,1)} %slice.591), channel_id=1, source_target_pairs={{0,1},{1,0},{2,3},{3,2},{4,5},{5,4},{6,7},{7,6},{8,9},{9,8},{10,11... | collective-permute-start | bytes 614408 | tf_op jit(solution)/shard_map/ppermute | solution.py:25
  286.3 21.8 %collective-permute-start.51 = (bf16[64,1600]{1,0:T(8,128)(2,1)}, bf16[64,1600]{1,0:T(8,128)(2,1)}, u32[]{:S(2)}, u32[]{:S(2)}) collective-permute-start(bf16[64,1600]{1,0:T(8,128)(2,1)} %slice.592), channel_id=1, source_target_pairs={{0,2},{1,3},{2,0},{3,1},{4,6},{5,7},{6,4},{7,5},{8,10},{9,11},{10,... | collective-permute-start | bytes 614408 | tf_op jit(solution)/shard_map/ppermute | solution.py:25
  304.7 21.7 %collective-permute-start.31 = (bf16[128,1600]{1,0:T(8,128)(2,1)S(1)}, bf16[128,1600]{1,0:T(8,128)(2,1)S(1)}, u32[]{:S(2)}, u32[]{:S(2)}) collective-permute-start(bf16[128,1600]{1,0:T(8,128)(2,1)S(1)} %get-tuple-element.214), channel_id=1, source_target_pairs={{0,1},{1,0},{2,3},{3,2},{4,5},{5,4},{6,7},{7,6},{8,9},{9,8},{10,11... | collective-permute-start | bytes 1228808 | tf_op jit(solution)/shard_map/ppermute | solution.py:25
  305.9 23.2 %collective-permute-start.32 = (bf16[128,1600]{1,0:T(8,128)(2,1)S(1)}, bf16[128,1600]{1,0:T(8,128)(2,1)S(1)}, u32[]{:S(2)}, u32[]{:S(2)}) collective-permute-start(bf16[128,1600]{1,0:T(8,128)(2,1)S(1)} %get-tuple-element.215), channel_id=1, source_target_pairs={{0,2},{1,3},{2,0},{3,1},{4,6},{5,7},{6,4},{7,5},{8,10},{9,11},{10,... | collective-permute-start | bytes 1228808 | tf_op jit(solution)/shard_map/ppermute | solution.py:25
  306.5 22.7 %collective-permute-start.33 = (bf16[128,1600]{1,0:T(8,128)(2,1)S(1)}, bf16[128,1600]{1,0:T(8,128)(2,1)S(1)}, u32[]{:S(2)}, u32[]{:S(2)}) collective-permute-start(bf16[128,1600]{1,0:T(8,128)(2,1)S(1)} %get-tuple-element.216), channel_id=1, source_target_pairs={{0,3},{1,2},{2,1},{3,0},{4,7},{5,6},{6,5},{7,4},{8,11},{9,10},{10,... | collective-permute-start | bytes 1228808 | tf_op jit(solution)/shard_map/ppermute | solution.py:25
  329.9 23.8 %collective-permute-start.35 = (bf16[128,1600]{1,0:T(8,128)(2,1)S(1)}, bf16[128,1600]{1,0:T(8,128)(2,1)S(1)}, u32[]{:S(2)}, u32[]{:S(2)}) collective-permute-start(bf16[128,1600]{1,0:T(8,128)(2,1)S(1)} %get-tuple-element.218.refs_0_), channel_id=1, source_target_pairs={{0,2},{1,3},{2,0},{3,1},{4,6},{5,7},{6,4},{7,5},{8,10},{9,11},{10,... | collective-permute-start | bytes 1228808 | tf_op jit(solution)/shard_map/ppermute | solution.py:25
  330.8 24.5 %collective-permute-start.34 = (bf16[128,1600]{1,0:T(8,128)(2,1)S(1)}, bf16[128,1600]{1,0:T(8,128)(2,1)S(1)}, u32[]{:S(2)}, u32[]{:S(2)}) collective-permute-start(bf16[128,1600]{1,0:T(8,128)(2,1)S(1)} %get-tuple-element.218.refs_0_), channel_id=1, source_target_pairs={{0,1},{1,0},{2,3},{3,2},{4,5},{5,4},{6,7},{7,6},{8,9},{9,8},{10,11... | collective-permute-start | bytes 1228808 | tf_op jit(solution)/shard_map/ppermute | solution.py:25
  401.7 161.3 %reduce-scatter.21.cloned.1.call-start = ((), (), s32[]{:S(2)}) async-start(), calls=%async_computation.15 | async-start | bytes 5990400
  433.0 20.8 %collective-permute-start.75 = (bf16[128,1600]{1,0:T(8,128)(2,1)S(1)}, bf16[128,1600]{1,0:T(8,128)(2,1)S(1)}, u32[]{:S(2)}, u32[]{:S(2)}) collective-permute-start(bf16[128,1600]{1,0:T(8,128)(2,1)S(1)} %get-tuple-element.270), channel_id=1, source_target_pairs={{0,3},{1,2},{2,1},{3,0},{4,7},{5,6},{6,5},{7,4},{8,11},{9,10},{10,... | collective-permute-start | bytes 1228808 | tf_op jit(solution)/shard_map/ppermute | solution.py:25
  437.7 23.9 %collective-permute-start.63 = (bf16[128,1600]{1,0:T(8,128)(2,1)S(1)}, bf16[128,1600]{1,0:T(8,128)(2,1)S(1)}, u32[]{:S(2)}, u32[]{:S(2)}) collective-permute-start(bf16[128,1600]{1,0:T(8,128)(2,1)S(1)} %get-tuple-element.249.refs_0_.refs_12_), channel_id=1, source_target_pairs={{0,2},{1,3},{2,0},{3,1},{4,6},{5,7},{6,4},{7,5},{8,10},{9,11},{10,... | collective-permute-start | bytes 1228808 | tf_op jit(solution)/shard_map/ppermute | solution.py:25
  438.3 25.0 %collective-permute-start.62 = (bf16[128,1600]{1,0:T(8,128)(2,1)S(1)}, bf16[128,1600]{1,0:T(8,128)(2,1)S(1)}, u32[]{:S(2)}, u32[]{:S(2)}) collective-permute-start(bf16[128,1600]{1,0:T(8,128)(2,1)S(1)} %get-tuple-element.249.refs_0_.refs_12_), channel_id=1, source_target_pairs={{0,1},{1,0},{2,3},{3,2},{4,5},{5,4},{6,7},{7,6},{8,9},{9,8},{10,11... | collective-permute-start | bytes 1228808 | tf_op jit(solution)/shard_map/ppermute | solution.py:25
  457.1 20.6 %collective-permute-start.76 = (bf16[128,1600]{1,0:T(8,128)(2,1)}, bf16[128,1600]{1,0:T(8,128)(2,1)}, u32[]{:S(2)}, u32[]{:S(2)}) collective-permute-start(bf16[128,1600]{1,0:T(8,128)(2,1)} %get-tuple-element.273.refs_0_.refs_17_), channel_id=1, source_target_pairs={{0,1},{1,0},{2,3},{3,2},{4,5},{5,4},{6,7},{7,6},{8,9},{9,8},{10,11... | collective-permute-start | bytes 1228808 | tf_op jit(solution)/shard_map/ppermute | solution.py:25
  475.4 186.0 %reduce-scatter.15.cloned.1.call-start = ((), (), s32[]{:S(2)}) async-start(), calls=%async_computation.12 | async-start | bytes 6451200 | tf_op jit(solution)/shard_map/reduce_scatter | solution.py:845
  476.8 25.7 %collective-permute-start.78 = (bf16[64,1600]{1,0:T(8,128)(2,1)S(1)}, bf16[64,1600]{1,0:T(8,128)(2,1)S(1)}, u32[]{:S(2)}, u32[]{:S(2)}) collective-permute-start(bf16[64,1600]{1,0:T(8,128)(2,1)S(1)} %slice.599), channel_id=1, source_target_pairs={{0,1},{1,0},{2,3},{3,2},{4,5},{5,4},{6,7},{7,6},{8,9},{9,8},{10,11... | collective-permute-start | bytes 614408 | tf_op jit(solution)/shard_map/ppermute | solution.py:25
  478.7 23.8 %collective-permute-start.79 = (bf16[64,1600]{1,0:T(8,128)(2,1)S(1)}, bf16[64,1600]{1,0:T(8,128)(2,1)S(1)}, u32[]{:S(2)}, u32[]{:S(2)}) collective-permute-start(bf16[64,1600]{1,0:T(8,128)(2,1)S(1)} %slice.600), channel_id=1, source_target_pairs={{0,2},{1,3},{2,0},{3,1},{4,6},{5,7},{6,4},{7,5},{8,10},{9,11},{10,... | collective-permute-start | bytes 614408 | tf_op jit(solution)/shard_map/ppermute | solution.py:25
  499.0 24.8 %collective-permute-start.66 = (bf16[128,1600]{1,0:T(8,128)(2,1)S(1)}, bf16[128,1600]{1,0:T(8,128)(2,1)S(1)}, u32[]{:S(2)}, u32[]{:S(2)}) collective-permute-start(bf16[128,1600]{1,0:T(8,128)(2,1)S(1)} %get-tuple-element.260), channel_id=1, source_target_pairs={{0,1},{1,0},{2,3},{3,2},{4,5},{5,4},{6,7},{7,6},{8,9},{9,8},{10,11... | collective-permute-start | bytes 1228808 | tf_op jit(solution)/shard_map/ppermute | solution.py:25
  500.1 25.0 %collective-permute-start.67 = (bf16[128,1600]{1,0:T(8,128)(2,1)S(1)}, bf16[128,1600]{1,0:T(8,128)(2,1)S(1)}, u32[]{:S(2)}, u32[]{:S(2)}) collective-permute-start(bf16[128,1600]{1,0:T(8,128)(2,1)S(1)} %get-tuple-element.261), channel_id=1, source_target_pairs={{0,2},{1,3},{2,0},{3,1},{4,6},{5,7},{6,4},{7,5},{8,10},{9,11},{10,... | collective-permute-start | bytes 1228808 | tf_op jit(solution)/shard_map/ppermute | solution.py:25
  501.2 23.9 %collective-permute-start.68 = (bf16[128,1600]{1,0:T(8,128)(2,1)S(1)}, bf16[128,1600]{1,0:T(8,128)(2,1)S(1)}, u32[]{:S(2)}, u32[]{:S(2)}) collective-permute-start(bf16[128,1600]{1,0:T(8,128)(2,1)S(1)} %get-tuple-element.262), channel_id=1, source_target_pairs={{0,3},{1,2},{2,1},{3,0},{4,7},{5,6},{6,5},{7,4},{8,11},{9,10},{10,... | collective-permute-start | bytes 1228808 | tf_op jit(solution)/shard_map/ppermute | solution.py:25
  521.6 21.5 %collective-permute-start.87 = (bf16[128,1600]{1,0:T(8,128)(2,1)}, bf16[128,1600]{1,0:T(8,128)(2,1)}, u32[]{:S(2)}, u32[]{:S(2)}) collective-permute-start(bf16[128,1600]{1,0:T(8,128)(2,1)} %get-tuple-element.293), channel_id=1, source_target_pairs={{0,1},{1,0},{2,3},{3,2},{4,5},{5,4},{6,7},{7,6},{8,9},{9,8},{10,11... | collective-permute-start | bytes 1228808 | tf_op jit(solution)/shard_map/ppermute | solution.py:25
  522.6 20.5 %collective-permute-start.88 = (bf16[128,1600]{1,0:T(8,128)(2,1)}, bf16[128,1600]{1,0:T(8,128)(2,1)}, u32[]{:S(2)}, u32[]{:S(2)}) collective-permute-start(bf16[128,1600]{1,0:T(8,128)(2,1)} %get-tuple-element.294), channel_id=1, source_target_pairs={{0,2},{1,3},{2,0},{3,1},{4,6},{5,7},{6,4},{7,5},{8,10},{9,11},{10,... | collective-permute-start | bytes 1228808 | tf_op jit(solution)/shard_map/ppermute | solution.py:25
  527.8 22.8 %collective-permute-start.70 = (bf16[128,1600]{1,0:T(8,128)(2,1)}, bf16[128,1600]{1,0:T(8,128)(2,1)}, u32[]{:S(2)}, u32[]{:S(2)}) collective-permute-start(bf16[128,1600]{1,0:T(8,128)(2,1)} %get-tuple-element.359.refs_0_), channel_id=1, source_target_pairs={{0,2},{1,3},{2,0},{3,1},{4,6},{5,7},{6,4},{7,5},{8,10},{9,11},{10,... | collective-permute-start | bytes 1228808 | tf_op jit(solution)/shard_map/ppermute | solution.py:25
  528.9 24.7 %collective-permute-start.69 = (bf16[128,1600]{1,0:T(8,128)(2,1)}, bf16[128,1600]{1,0:T(8,128)(2,1)}, u32[]{:S(2)}, u32[]{:S(2)}) collective-permute-start(bf16[128,1600]{1,0:T(8,128)(2,1)} %get-tuple-element.359.refs_0_), channel_id=1, source_target_pairs={{0,1},{1,0},{2,3},{3,2},{4,5},{5,4},{6,7},{7,6},{8,9},{9,8},{10,11... | collective-permute-start | bytes 1228808 | tf_op jit(solution)/shard_map/ppermute | solution.py:25
  543.0 185.3 %reduce-scatter.23.cloned.1.call-start = ((), (), s32[]{:S(2)}) async-start(), calls=%async_computation.16 | async-start | bytes 5990400
  595.9 38.7 %collective-permute-start.80 = (bf16[128,1600]{1,0:T(8,128)(2,1)}, bf16[128,1600]{1,0:T(8,128)(2,1)}, u32[]{:S(2)}, u32[]{:S(2)}) collective-permute-start(bf16[128,1600]{1,0:T(8,128)(2,1)} %get-tuple-element.284), channel_id=1, source_target_pairs={{0,1},{1,0},{2,3},{3,2},{4,5},{5,4},{6,7},{7,6},{8,9},{9,8},{10,11... | collective-permute-start | bytes 1228808 | tf_op jit(solution)/shard_map/ppermute | solution.py:25
  596.7 37.9 %collective-permute-start.81 = (bf16[128,1600]{1,0:T(8,128)(2,1)}, bf16[128,1600]{1,0:T(8,128)(2,1)}, u32[]{:S(2)}, u32[]{:S(2)}) collective-permute-start(bf16[128,1600]{1,0:T(8,128)(2,1)} %get-tuple-element.285), channel_id=1, source_target_pairs={{0,2},{1,3},{2,0},{3,1},{4,6},{5,7},{6,4},{7,5},{8,10},{9,11},{10,... | collective-permute-start | bytes 1228808 | tf_op jit(solution)/shard_map/ppermute | solution.py:25
  598.9 21.0 %collective-permute-start.98 = (bf16[128,1600]{1,0:T(8,128)(2,1)}, bf16[128,1600]{1,0:T(8,128)(2,1)}, u32[]{:S(2)}, u32[]{:S(2)}) collective-permute-start(bf16[128,1600]{1,0:T(8,128)(2,1)} %get-tuple-element.311), channel_id=1, source_target_pairs={{0,2},{1,3},{2,0},{3,1},{4,6},{5,7},{6,4},{7,5},{8,10},{9,11},{10,... | collective-permute-start | bytes 1228808 | tf_op jit(solution)/shard_map/ppermute | solution.py:25
  599.9 26.3 %collective-permute-start.99 = (bf16[128,1600]{1,0:T(8,128)(2,1)}, bf16[128,1600]{1,0:T(8,128)(2,1)}, u32[]{:S(2)}, u32[]{:S(2)}) collective-permute-start(bf16[128,1600]{1,0:T(8,128)(2,1)} %get-tuple-element.312), channel_id=1, source_target_pairs={{0,3},{1,2},{2,1},{3,0},{4,7},{5,6},{6,5},{7,4},{8,11},{9,10},{10,... | collective-permute-start | bytes 1228808 | tf_op jit(solution)/shard_map/ppermute | solution.py:25
  611.7 121.0 %reduce-scatter.25.cloned.1.call-start = ((), (), s32[]{:S(2)}) async-start(), calls=%async_computation.17 | async-start | bytes 5990400
  656.6 163.3 %reduce-scatter.17.cloned.1.call-start = ((), (), s32[]{:S(2)}) async-start(), calls=%async_computation.13 | async-start | bytes 6451200 | tf_op jit(solution)/shard_map/reduce_scatter | solution.py:845
  657.9 28.1 %collective-permute-start.85 = (bf16[64,1600]{1,0:T(8,128)(2,1)}, bf16[64,1600]{1,0:T(8,128)(2,1)}, u32[]{:S(2)}, u32[]{:S(2)}) collective-permute-start(bf16[64,1600]{1,0:T(8,128)(2,1)} %slice.601), channel_id=1, source_target_pairs={{0,1},{1,0},{2,3},{3,2},{4,5},{5,4},{6,7},{7,6},{8,9},{9,8},{10,11... | collective-permute-start | bytes 614408 | tf_op jit(solution)/shard_map/ppermute | solution.py:25
  660.6 25.4 %collective-permute-start.86 = (bf16[64,1600]{1,0:T(8,128)(2,1)}, bf16[64,1600]{1,0:T(8,128)(2,1)}, u32[]{:S(2)}, u32[]{:S(2)}) collective-permute-start(bf16[64,1600]{1,0:T(8,128)(2,1)} %slice.602), channel_id=1, source_target_pairs={{0,2},{1,3},{2,0},{3,1},{4,6},{5,7},{6,4},{7,5},{8,10},{9,11},{10,... | collective-permute-start | bytes 614408 | tf_op jit(solution)/shard_map/ppermute | solution.py:25
  682.4 24.0 %collective-permute-start.104 = (bf16[128,1600]{1,0:T(8,128)(2,1)S(1)}, bf16[128,1600]{1,0:T(8,128)(2,1)S(1)}, u32[]{:S(2)}, u32[]{:S(2)}) collective-permute-start(bf16[128,1600]{1,0:T(8,128)(2,1)S(1)} %get-tuple-element.325), channel_id=1, source_target_pairs={{0,1},{1,0},{2,3},{3,2},{4,5},{5,4},{6,7},{7,6},{8,9},{9,8},{10,11... | collective-permute-start | bytes 1228808 | tf_op jit(solution)/shard_map/ppermute | solution.py:25
  683.6 36.6 %collective-permute-start.105 = (bf16[128,1600]{1,0:T(8,128)(2,1)}, bf16[128,1600]{1,0:T(8,128)(2,1)}, u32[]{:S(2)}, u32[]{:S(2)}) collective-permute-start(bf16[128,1600]{1,0:T(8,128)(2,1)} %get-tuple-element.326), channel_id=1, source_target_pairs={{0,2},{1,3},{2,0},{3,1},{4,6},{5,7},{6,4},{7,5},{8,10},{9,11},{10,... | collective-permute-start | bytes 1228808 | tf_op jit(solution)/shard_map/ppermute | solution.py:25
  684.7 35.5 %collective-permute-start.106 = (bf16[128,1600]{1,0:T(8,128)(2,1)}, bf16[128,1600]{1,0:T(8,128)(2,1)}, u32[]{:S(2)}, u32[]{:S(2)}) collective-permute-start(bf16[128,1600]{1,0:T(8,128)(2,1)} %get-tuple-element.327), channel_id=1, source_target_pairs={{0,3},{1,2},{2,1},{3,0},{4,7},{5,6},{6,5},{7,4},{8,11},{9,10},{10,... | collective-permute-start | bytes 1228808 | tf_op jit(solution)/shard_map/ppermute | solution.py:25
  704.1 21.1 %collective-permute-start.94 = (bf16[128,1600]{1,0:T(8,128)(2,1)}, bf16[128,1600]{1,0:T(8,128)(2,1)}, u32[]{:S(2)}, u32[]{:S(2)}) collective-permute-start(bf16[128,1600]{1,0:T(8,128)(2,1)} %get-tuple-element.305), channel_id=1, source_target_pairs={{0,1},{1,0},{2,3},{3,2},{4,5},{5,4},{6,7},{7,6},{8,9},{9,8},{10,11... | collective-permute-start | bytes 1228808 | tf_op jit(solution)/shard_map/ppermute | solution.py:25
  761.6 21.4 %collective-permute-start.108 = (bf16[400,512]{1,0:T(8,128)(2,1)}, bf16[400,512]{1,0:T(8,128)(2,1)S(1)}, u32[]{:S(2)}, u32[]{:S(2)}) collective-permute-start(bf16[400,512]{1,0:T(8,128)(2,1)} %copy-done.125), channel_id=1, source_target_pairs={{0,2},{1,3},{2,0},{3,1},{4,6},{5,7},{6,4},{7,5},{8,10},{9,11},{10,... | collective-permute-start | bytes 1228808 | tf_op jit(solution)/shard_map/ppermute | solution.py:25
  762.2 20.9 %collective-permute-start.109 = (bf16[400,512]{1,0:T(8,128)(2,1)}, bf16[400,512]{1,0:T(8,128)(2,1)}, u32[]{:S(2)}, u32[]{:S(2)}) collective-permute-start(bf16[400,512]{1,0:T(8,128)(2,1)} %copy-done.124), channel_id=1, source_target_pairs={{0,3},{1,2},{2,1},{3,0},{4,7},{5,6},{6,5},{7,4},{8,11},{9,10},{10,... | collective-permute-start | bytes 1228808 | tf_op jit(solution)/shard_map/ppermute | solution.py:25
  773.8 31.2 %collective-permute-start.111 = (bf16[400,512]{1,0:T(8,128)(2,1)}, bf16[400,512]{1,0:T(8,128)(2,1)}, u32[]{:S(2)}, u32[]{:S(2)}) collective-permute-start(bf16[400,512]{1,0:T(8,128)(2,1)} %copy-done.122), channel_id=1, source_target_pairs={{0,2},{1,3},{2,0},{3,1},{4,6},{5,7},{6,4},{7,5},{8,10},{9,11},{10,... | collective-permute-start | bytes 1228808 | tf_op jit(solution)/shard_map/ppermute | solution.py:25
  774.4 30.6 %collective-permute-start.112 = (bf16[400,512]{1,0:T(8,128)(2,1)S(1)}, bf16[400,512]{1,0:T(8,128)(2,1)}, u32[]{:S(2)}, u32[]{:S(2)}) collective-permute-start(bf16[400,512]{1,0:T(8,128)(2,1)S(1)} %get-tuple-element.340), channel_id=1, source_target_pairs={{0,3},{1,2},{2,1},{3,0},{4,7},{5,6},{6,5},{7,4},{8,11},{9,10},{10,... | collective-permute-start | bytes 1228808 | tf_op jit(solution)/shard_map/ppermute | solution.py:25
  777.8 31.0 %all-to-all-start = ((bf16[4,2,400,128]{3,2,1,0:T(8,128)(2,1)}), bf16[4,2,400,128]{3,2,1,0:T(8,128)(2,1)S(1)}, u32[]{:S(2)}, u32[]{:S(2)}) async-start(bf16[4,2,400,128]{3,2,1,0:T(8,128)(2,1)} %pad_maximum_fusion.4), calls=%async_computation.1 | async-start | bytes 1638400 | tf_op jit(solution)/shard_map/all_to_all | solution.py:841
  (287 other events, 2834.4 us)
Sparse Core Ops, SparseCore 0:
  33.9 61.5 all-gather.9
  97.7 99.4 all-gather.11
  199.4 58.5 all-gather.13
  259.4 57.1 all-gather.5
  318.7 57.2 all-gather.7
  401.8 57.9 reduce-scatter.18
  475.5 58.2 reduce-scatter.20
  543.1 62.0 reduce-scatter.14
  611.8 58.5 reduce-scatter.22
  672.6 60.0 reduce-scatter.24
  735.0 64.6 reduce-scatter.16

commit v5 on v4

--- a/solution.py
+++ b/solution.py
@@ -956,12 +956,12 @@
         weights[1][3],
     )
     outputs = []
-    for batch in everyone:
-        terms = link.exchange(last_parts[batch])
+    last_terms = [link.exchange(last_parts[batch]) for batch in everyone]
+    for terms in last_terms:
         outputs.append(sum([term.astype(F32) for term in terms[1:]], terms[0].astype(F32)))
     outputs = jnp.stack(outputs).astype(BF)
 
-    wide_sums = after(wide_sums, last_parts)
+    wide_sums = after(wide_sums, last_terms[0])
     wide_both = jnp.stack(wide_sums).reshape(2, 6, cols, width)
     wide_here = lax.dynamic_index_in_dim(wide_both, col, 2, keepdims=False)
     for j in range(1, cols):
@@ -977,6 +977,7 @@
     while step < lax.axis_size("row"):
         small_own = small_own + xor_step(small_own, "row", step)
         step *= 2
+    small_own = after(small_own, reduced[0][2])
     small_out = small_own[: 6 * width].reshape(6, width)
     head_out = small_own[6 * width : 6 * width + 2 * wide].reshape(2, wide)
     head_out = split_heads(
@@ -1010,6 +1011,7 @@
     ).astype(F32)
 
     grads = to_features(turned)
+    outputs, grads = after((outputs, grads), reduced[0][2])
     got = swap_section(jnp.where(is_first, outputs, grads))
     keep = jnp.where(is_first, grads, outputs)
     boundary = jnp.concatenate(

time: 858 us -> 854 us (level)
  transfers between devices with their start and end apart: 137 -> 137, of which waited for: 41 -> 41; matrix products, arithmetic and copies ran while one was open for 8% -> 9% of each run, Pallas kernels for 38% -> 38%
where the time goes in v5:
time: 854 us; the launch traced here: 846 us
  Pallas kernels  324 us (38%)
  waiting for transfers between devices  173 us (20%)
  local copies, waits for them, and re-layouts  149 us (17%)
  starting transfers between devices  149 us (17%)
  other arithmetic  34.1 us (4%)
  between operations  16.8 us (2%)
    pallas_call x41, Pallas kernels, call(): pl.pallas_call(kernel, out_shape=tuple(outs), in_specs=[pl.BlockSpec(memo...  324 us
    ppermute x119, waiting for transfers between devices, xor_step(): return lax.ppermute(value, axis, [(i, i ^ step) for i in range(count)])  152 us
    ppermute x119, starting transfers between devices, xor_step(): return lax.ppermute(value, axis, [(i, i ^ step) for i in range(count)])  131 us
    unnamed x431, local copies, waits for them, and re-layouts  95.8 us
  transfers between devices with their start and end apart: 137, of which 41 were waited for; matrix products, arithmetic and copies ran while one was open for 9% of the time, Pallas kernels for 38%

profile of v5, /device:TPU:0, one launch (start us, length us, event | category | flops | bytes accessed | tf_op | source)
XLA Modules:
  0.0 845.6 jit_solution(11312969929244914871)
XLA Ops:
  17.4 6.1 collective-permute-done.9
  23.5 4.0 collective-permute-done.11
  27.5 4.2 broadcast_select_fusion.8
  41.3 4.1 collective-permute-start.1
  46.8 16.4 %collective-permute-done.1 = bf16[2,400,512]{2,1,0:T(8,128)(2,1)} collective-permute-done((bf16[2,400,512]{2,1,0:T(8,128)(2,1)}, bf16[2,400,512]{2,1,0:T(8,128)(2,1)}, u32[]{:S(2)}, u32[]{:S(2)}) %collective-permute-start.1) | collective-permute-done | bytes 819232 | tf_op jit(solution)/shard_map/ppermute | solution.py:25
  71.0 4.1 collective-permute-done.2
  77.8 3.1 collective-permute-done.23
  107.5 4.5 collective-permute-done.16
  119.9 13.3 %shard_map.298 = (bf16[512,1344]{1,0:T(8,128)(2,1)S(1)}, bf16[512,448]{1,0:T(8,128)(2,1)S(1)}, f32[7,512]{1,0:T(8,128)S(1)}, bf16[128,1600]{1,0:T(8,128)(2,1)S(1...) custom-call(bf16[512,1600]{1,0:T(8,128)(2,1)S(1)} %copy-done.90, ...), custom_call_target="tpu_custom_call" | custom-call | flops 19260243968 | tf_op jit(solution)/shard_map/pallas_call | solution.py:141
  138.6 12.8 %shard_map.306 = (bf16[512,1344]{1,0:T(8,128)(2,1)S(1)}, bf16[512,448]{1,0:T(8,128)(2,1)S(1)}, f32[7,512]{1,0:T(8,128)S(1)}, bf16[128,1600]{1,0:T(8,128)(2,1)S(1...) custom-call(bf16[512,1600]{1,0:T(8,128)(2,1)S(1)} %copy-done.88, ...), custom_call_target="tpu_custom_call" | custom-call | flops 19260243968 | tf_op jit(solution)/shard_map/pallas_call | solution.py:141
  158.8 7.4 collective-permute-done.38.refs_1_
  166.1 9.5 %collective-permute-done.39.refs_2_ = bf16[128,1600]{1,0:T(8,128)(2,1)S(1)} collective-permute-done((bf16[128,1600]{1,0:T(8,128)(2,1)S(1)}, bf16[128,1600]{1,0:T(8,128)(2,1)S(1)}, u32[]{:S(2)}, u32[]{:S(2)}) %collective-permute-start.39) | collective-permute-done | bytes 409632 | tf_op jit(solution)/shard_map/ppermute | solution.py:25
  179.4 5.4 collective-permute-done.20.refs_2_
  188.8 4.8 collective-permute-done.42.refs_2_.refs_7_
  205.2 13.5 %shard_map.301 = (bf16[512,1600]{1,0:T(8,128)(2,1)S(1)}, bf16[512,1600]{1,0:T(8,128)(2,1)S(1)}, bf16[128,1600]{1,0:T(8,128)(2,1)S(1)}, bf16[128,1600]{1,0:T(8,12...) custom-call(bf16[128,1600]{1,0:T(8,128)(2,1)S(1)} %copy-done.105, bf16[128,1600]{1,0:T(8,128)(2,1)S(1)} %copy-done.42, ...), custom_call_target="tpu_custom_call" | custom-call | flops 20971520000 | tf_op jit(solution)/shard_map/pallas_call | solution.py:141
  225.3 14.5 %shard_map.308 = (bf16[512,1600]{1,0:T(8,128)(2,1)S(1)}, bf16[512,1600]{1,0:T(8,128)(2,1)S(1)}, bf16[128,1600]{1,0:T(8,128)(2,1)S(1)}, bf16[128,1600]{1,0:T(8,12...) custom-call(bf16[128,1600]{1,0:T(8,128)(2,1)S(1)} %copy-done.108, bf16[128,1600]{1,0:T(8,128)(2,1)S(1)} %copy-done.48, ...), custom_call_target="tpu_custom_call" | custom-call | flops 20971520000 | tf_op jit(solution)/shard_map/pallas_call | solution.py:141
  249.5 2.5 shard_map.302
  256.0 7.4 collective-permute-done.46.refs_2_
  263.4 2.7 collective-permute-done.47.refs_3_
  266.2 2.9 shard_map.309
  278.5 3.6 collective-permute-done.49.refs_2_.refs_7_
  288.9 14.0 %shard_map.303 = (bf16[512,1344]{1,0:T(8,128)(2,1)S(1)}, bf16[512,448]{1,0:T(8,128)(2,1)S(1)}, f32[7,512]{1,0:T(8,128)S(1)}, bf16[128,1600]{1,0:T(8,128)(2,1)S(1...) custom-call(bf16[128,1600]{1,0:T(8,128)(2,1)} %get-tuple-element.214.refs_0_, ...), custom_call_target="tpu_custom_call" | custom-call | flops 19260243968 | tf_op jit(solution)/shard_map/pallas_call | solution.py:141
  308.3 14.4 %shard_map.310 = (bf16[512,1344]{1,0:T(8,128)(2,1)S(1)}, bf16[512,448]{1,0:T(8,128)(2,1)S(1)}, f32[7,512]{1,0:T(8,128)S(1)}, bf16[128,1600]{1,0:T(8,128)(2,1)S(1...) custom-call(bf16[128,1600]{1,0:T(8,128)(2,1)} %get-tuple-element.234.refs_0_.refs_5_,, ...), custom_call_target="tpu_custom_call" | custom-call | flops 19260243968 | tf_op jit(solution)/shard_map/pallas_call | solution.py:141
  333.1 4.3 collective-permute-done.52.refs_1_
  337.4 5.1 collective-permute-done.53.refs_2_
  342.4 4.3 collective-permute-done.54.refs_3_
  371.6 8.6 %shard_map.305 = (bf16[512,1600]{1,0:T(8,128)(2,1)S(1)}, bf16[512,1600]{1,0:T(8,128)(2,1)S(1)}) custom-call(bf16[128,1600]{1,0:T(8,128)(2,1)S(1)} %copy-done.111, bf16[128,1600]{1,0:T(8,128)(2,1)S(1)} %copy-done.60, bf16[128,1600]{1,0:T(8,128)(2,1)S(1)} %copy-done.57, bf16[64,1600]{1,0:T(8,128)(2,1)} %collective-permute-done.36.refs_3_, ...), custom_call_target="tpu_custom_call" | custom-call | flops 10485760000 | tf_op jit(solution)/shard_map/pallas_call | solution.py:141
  381.4 9.2 %shard_map.312 = (bf16[512,1600]{1,0:T(8,128)(2,1)S(1)}, bf16[512,1600]{1,0:T(8,128)(2,1)S(1)}) custom-call(bf16[128,1600]{1,0:T(8,128)(2,1)S(1)} %copy-done.114, bf16[128,1600]{1,0:T(8,128)(2,1)S(1)} %copy-done.66, bf16[128,1600]{1,0:T(8,128)(2,1)S(1)} %copy-done.63, bf16[64,1600]{1,0:T(8,128)(2,1)S(1)} %collective-permute-done.57.refs_3_.refs_8_, ...), custom_call_target="tpu_custom_call" | custom-call | flops 10485760000 | tf_op jit(solution)/shard_map/pallas_call | solution.py:141
  391.8 8.7 %shard_map.315 = bf16[1600,1600]{1,0:T(8,128)(2,1)} custom-call(bf16[512,1600]{1,0:T(8,128)(2,1)S(1)} %copy-done.96, bf16[512,1600]{1,0:T(8,128)(2,1)S(1)} %copy-done.93, bf16[512,1600]{1,0:T(8,128)(2,1)S(1)} %get-tuple-element.334.refs_2_.refs_0_, bf16[512,1600]{1,0:T(8,128)(2,1)S(1)} %get-tuple-element.335.refs_3_.refs_1_), custom_call_target="tpu_custom_call" | custom-call | flops 20971520000 | tf_op jit(solution)/shard_map/pallas_call | solution.py:141
  404.8 11.3 %shard_map.316 = (bf16[512,1600]{1,0:T(8,128)(2,1)S(1)}, f32[1,1600]{1,0:T(1,128)S(1)}, bf16[128,1600]{1,0:T(8,128)(2,1)S(1)}, bf16[128,1600]{1,0:T(8,128)(2,1)S...) custom-call(bf16[512,1600]{1,0:T(8,128)(2,1)S(1)} %copy-done.97, ...), custom_call_target="tpu_custom_call" | custom-call | flops 20971520000 | tf_op jit(solution)/shard_map/pallas_call | solution.py:141
  419.7 11.2 %shard_map.318 = (bf16[512,1600]{1,0:T(8,128)(2,1)S(1)}, f32[1,1600]{1,0:T(1,128)S(1)}, bf16[128,1600]{1,0:T(8,128)(2,1)S(1)}, bf16[128,1600]{1,0:T(8,128)(2,1)S...) custom-call(bf16[512,1600]{1,0:T(8,128)(2,1)S(1)} %copy-done.94, ...), custom_call_target="tpu_custom_call" | custom-call | flops 20971520000 | tf_op jit(solution)/shard_map/pallas_call | solution.py:141
  439.2 4.6 collective-permute-done.73.refs_1_
  443.8 7.7 collective-permute-done.74.refs_2_
  458.0 3.7 collective-permute-done.63.refs_2_.refs_14_
  466.8 9.9 %shard_map.319 = bf16[1600,1600]{1,0:T(8,128)(2,1)} custom-call(bf16[128,1600]{1,0:T(8,128)(2,1)S(1)} %copy-done.112, bf16[128,1600]{1,0:T(8,128)(2,1)S(1)} %copy-done.61, bf16[128,1600]{1,0:T(8,128)(2,1)S(1)} %copy-done.58, bf16[64,1600]{1,0:T(8,128)(2,1)} %collective-permute-done.36.refs_3_, bf16[64,1600]{1,0:T(8,128)(2,1)} %collective-permute-done.37.refs_4_, ...), custom_call_target="tpu_custom_call" | custom-call | flops 20971520000 | tf_op jit(solution)/shard_map/pallas_call | solution.py:141
  484.6 15.8 %shard_map.320 = (bf16[512,1344]{1,0:T(8,128)(2,1)S(1)}, f32[2,448]{1,0:T(2,128)S(1)}, bf16[128,1600]{1,0:T(8,128)(2,1)S(1)}, bf16[128,1600]{1,0:T(8,128)(2,1)S(...) custom-call(bf16[128,1600]{1,0:T(8,128)(2,1)S(1)} %copy-done.117, bf16[128,1600]{1,0:T(8,128)(2,1)S(1)} %copy-done.71, ...), custom_call_target="tpu_custom_call" | custom-call | flops 30534533120 | tf_op jit(solution)/shard_map/pallas_call | solution.py:141
  504.0 17.2 %shard_map.323 = (bf16[512,1344]{1,0:T(8,128)(2,1)S(1)}, f32[2,448]{1,0:T(2,128)S(1)}, bf16[128,1600]{1,0:T(8,128)(2,1)S(1)}, bf16[128,1600]{1,0:T(8,128)(2,1)},...) custom-call(bf16[128,1600]{1,0:T(8,128)(2,1)} %get-tuple-element.276.refs_0_.refs_17_, ...), custom_call_target="tpu_custom_call" | custom-call | flops 30534533120 | tf_op jit(solution)/shard_map/pallas_call | solution.py:141
  531.4 13.1 %shard_map.324 = bf16[1600,1792]{1,0:T(8,128)(2,1)} custom-call(bf16[128,1600]{1,0:T(8,128)(2,1)} %get-tuple-element.214.refs_0_, bf16[128,1600]{1,0:T(8,128)(2,1)S(1)} %copy-done.55, bf16[128,1600]{1,0:T(8,128)(2,1)S(1)} %copy-done.52, bf16[64,1600]{1,0:T(8,128)(2,1)} %collective-permute-done.29.refs_3_, bf16[64,1600]{1,0:T(8,128)(2,1)} %collective-permute-done.30.refs_4_, ...), custom_call_target="tpu_custom_call" | custom-call | flops 23488102400 | tf_op jit(solution)/shard_map/pallas_call | solution.py:141
  557.5 2.5 collective-permute-done.91.refs_2_.refs_7_
  566.0 13.2 %shard_map.325 = (bf16[512,1600]{1,0:T(8,128)(2,1)S(1)}, f32[1,1600]{1,0:T(1,128)S(1)}, bf16[128,1600]{1,0:T(8,128)(2,1)S(1)}, bf16[128,1600]{1,0:T(8,128)(2,1)}...) custom-call(bf16[128,1600]{1,0:T(8,128)(2,1)} %get-tuple-element.344.refs_0_, ...), custom_call_target="tpu_custom_call" | custom-call | flops 20971520000 | tf_op jit(solution)/shard_map/pallas_call | solution.py:141
  582.0 13.4 %shard_map.328 = (bf16[512,1600]{1,0:T(8,128)(2,1)S(1)}, f32[1,1600]{1,0:T(1,128)S(1)}, bf16[128,1600]{1,0:T(8,128)(2,1)S(1)}, bf16[128,1600]{1,0:T(8,128)(2,1)}...) custom-call(bf16[128,1600]{1,0:T(8,128)(2,1)S(1)} %copy-done.123, bf16[128,1600]{1,0:T(8,128)(2,1)S(1)} %copy-done.82, ...), custom_call_target="tpu_custom_call" | custom-call | flops 20971520000 | tf_op jit(solution)/shard_map/pallas_call | solution.py:141
  602.7 10.3 %shard_map.337 = bf16[1600,1600]{1,0:T(8,128)(2,1)} custom-call(bf16[128,1600]{1,0:T(8,128)(2,1)} %get-tuple-element.344.refs_0_, bf16[128,1600]{1,0:T(8,128)(2,1)} %collective-permute-done.69.refs_1_, bf16[128,1600]{1,0:T(8,128)(2,1)} %collective-permute-done.70.refs_2_, bf16[64,1600]{1,0:T(8,128)(2,1)} %collective-permute-done.71.refs_3_, ...), custom_call_target="tpu_custom_call" | custom-call | flops 20971520000 | tf_op jit(solution)/shard_map/pallas_call | solution.py:141
  613.1 5.0 collective-permute-done.97.refs_1_
  621.3 6.4 collective-permute-done.99.refs_3_
  636.2 2.9 shard_map.326
  648.2 9.8 %shard_map.329 = bf16[1600,1600]{1,0:T(8,128)(2,1)} custom-call(bf16[128,1600]{1,0:T(8,128)(2,1)S(1)} %copy-done.106, bf16[128,1600]{1,0:T(8,128)(2,1)S(1)} %copy-done.43, bf16[128,1600]{1,0:T(8,128)(2,1)S(1)} %copy-done.40, bf16[64,1600]{1,0:T(8,128)(2,1)S(1)} %copy-done.127, bf16[64,1600]{1,0:T(8,128)(2,1)S(1)} %copy-done.130, ...), custom_call_target="tpu_custom_call" | custom-call | flops 20971520000 | tf_op jit(solution)/shard_map/pallas_call | solution.py:141
  667.1 16.6 %shard_map.332 = (bf16[512,1344]{1,0:T(8,128)(2,1)S(1)}, f32[2,448]{1,0:T(2,128)S(1)}, bf16[128,1600]{1,0:T(8,128)(2,1)S(1)}, bf16[128,1600]{1,0:T(8,128)(2,1)S(...) custom-call(bf16[128,1600]{1,0:T(8,128)(2,1)S(1)} %copy-done.120, bf16[128,1600]{1,0:T(8,128)(2,1)S(1)} %copy-done.77, ...), custom_call_target="tpu_custom_call" | custom-call | flops 90534535168 | tf_op jit(solution)/shard_map/pallas_call | solution.py:141
  687.4 17.3 %shard_map.330 = (bf16[512,1344]{1,0:T(8,128)(2,1)S(1)}, f32[2,448]{1,0:T(2,128)S(1)}, bf16[128,1600]{1,0:T(8,128)(2,1)S(1)}, bf16[128,1600]{1,0:T(8,128)(2,1)},...) custom-call(bf16[128,1600]{1,0:T(8,128)(2,1)} %get-tuple-element.291.refs_0_.refs_4_, ...), custom_call_target="tpu_custom_call" | custom-call | flops 90534535168 | tf_op jit(solution)/shard_map/pallas_call | solution.py:141
  709.8 11.9 %shard_map.333 = bf16[1600,1792]{1,0:T(8,128)(2,1)} custom-call(bf16[512,1600]{1,0:T(8,128)(2,1)S(1)} %copy-done.91, bf16[512,1600]{1,0:T(8,128)(2,1)} %copy-done.87, bf16[512,1344]{1,0:T(8,128)(2,1)S(1)} %get-tuple-element.311.refs_2_, bf16[512,1344]{1,0:T(8,128)(2,1)S(1)} %get-tuple-element.321.refs_3_, ...), custom_call_target="tpu_custom_call" | custom-call | flops 23488102400 | tf_op jit(solution)/shard_map/pallas_call | solution.py:141
  722.7 3.1 shard_map.335
  726.5 3.1 shard_map.334
  729.7 4.5 reduce-scatter.25.cloned.1.call-done
  740.2 10.6 %shard_map.336 = (bf16[400,512]{1,0:T(8,128)(2,1)S(1)}, bf16[400,512]{1,0:T(8,128)(2,1)S(1)}, bf16[400,512]{1,0:T(8,128)(2,1)S(1)}, bf16[400,512]{1,0:T(8,128)(2...) custom-call(bf16[512,1600]{1,0:T(8,128)(2,1)S(1)} %copy-done.132, ...), custom_call_target="tpu_custom_call" | custom-call | flops 20971520000 | tf_op jit(solution)/shard_map/pallas_call | solution.py:141
  757.4 5.9 collective-permute-done.107
  763.3 10.3 %collective-permute-done.108 = bf16[400,512]{1,0:T(8,128)(2,1)S(1)} collective-permute-done((bf16[400,512]{1,0:T(8,128)(2,1)S(1)}, bf16[400,512]{1,0:T(8,128)(2,1)S(1)}, u32[]{:S(2)}, u32[]{:S(2)}) %collective-permute-start.108) | collective-permute-done | bytes 409632 | tf_op jit(solution)/shard_map/ppermute | solution.py:25
  779.6 3.5 all-to-all-start
  783.1 2.9 collective-permute-start.112
  786.0 3.2 collective-permute-done.115
  789.4 3.3 broadcast_select_fusion.2
  799.6 3.3 collective-permute-start.119
  804.8 2.9 broadcast_select_fusion
  807.7 2.9 fusion.4
  816.9 5.0 collective-permute-start.120
  827.3 3.7 collective-permute-done.121
  (864 shorter events, 341.4 us)
Async XLA Ops:
  7.2 111.2 %all-gather.6.cloned.1.call-start = ((), (), s32[]{:S(2)}) async-start(), calls=%async_computation.7 | async-start | bytes 6451200 | tf_op jit(solution)/shard_map/all_gather | solution.py:682
  33.7 166.5 %all-gather.8.cloned.1.call-start = ((), (), s32[]{:S(2)}) async-start(), calls=%async_computation.8 | async-start | bytes 11980800 | tf_op jit(solution)/shard_map/all_gather | solution.py:682
  41.3 21.9 %collective-permute-start.1 = (bf16[2,400,512]{2,1,0:T(8,128)(2,1)}, bf16[2,400,512]{2,1,0:T(8,128)(2,1)}, u32[]{:S(2)}, u32[]{:S(2)}) collective-permute-start(bf16[2,400,512]{2,1,0:T(8,128)(2,1)} %constant_dynamic-slice_fusion.11), channel_id=1, source_target_pairs={{0,2},{1,3},{2,0},{3,1},{4,6},{5,7},{6,4},{7,5},{8,10},{9,11},{10,... | collective-permute-start | bytes 2457608 | tf_op jit(solution)/shard_map/ppermute | solution.py:25
  46.7 22.2 %collective-permute-start.8 = (f32[12096]{0:T(1024)S(1)}, f32[12096]{0:T(1024)S(1)}, u32[]{:S(2)}, u32[]{:S(2)}) collective-permute-start(f32[12096]{0:T(1024)S(1)} %pad_maximum_fusion.12), channel_id=1, source_target_pairs={{0,16},{16,0},{1,17},{17,1},{2,18},{18,2},{3,19},{19,3},{4,20},{20... | collective-permute-start | bytes 145160 | tf_op jit(solution)/shard_map/ppermute | solution.py:25
  83.3 204.3 %all-gather.10.cloned.1.call-start = ((), (), s32[]{:S(2)}) async-start(), calls=%async_computation.9 | async-start | bytes 6451200 | tf_op jit(solution)/shard_map/all_gather | solution.py:682
  84.0 284.1 %all-gather.12.cloned.1.call-start = ((), (), s32[]{:S(2)}) async-start(), calls=%async_computation.10 | async-start | bytes 6230016 | tf_op jit(solution)/shard_map/all_gather | solution.py:682
  91.3 20.7 %collective-permute-start.16 = (bf16[2,400,512]{2,1,0:T(8,128)(2,1)}, bf16[2,400,512]{2,1,0:T(8,128)(2,1)}, u32[]{:S(2)}, u32[]{:S(2)}) collective-permute-start(bf16[2,400,512]{2,1,0:T(8,128)(2,1)} %constant_dynamic-slice_fusion.5), channel_id=1, source_target_pairs={{0,2},{1,3},{2,0},{3,1},{4,6},{5,7},{6,4},{7,5},{8,10},{9,11},{10,... | collective-permute-start | bytes 2457608 | tf_op jit(solution)/shard_map/ppermute | solution.py:25
  92.5 22.6 %collective-permute-start.15 = (bf16[2,400,512]{2,1,0:T(8,128)(2,1)}, bf16[2,400,512]{2,1,0:T(8,128)(2,1)}, u32[]{:S(2)}, u32[]{:S(2)}) collective-permute-start(bf16[2,400,512]{2,1,0:T(8,128)(2,1)} %constant_dynamic-slice_fusion.5), channel_id=1, source_target_pairs={{0,1},{1,0},{2,3},{3,2},{4,5},{5,4},{6,7},{7,6},{8,9},{9,8},{10,11... | collective-permute-start | bytes 2457608 | tf_op jit(solution)/shard_map/ppermute | solution.py:25
  95.6 306.1 %all-gather.14.cloned.1.call-start = ((), (), s32[]{:S(2)}) async-start(), calls=%async_computation.11 | async-start | bytes 6230016 | tf_op jit(solution)/shard_map/all_gather | solution.py:682
  113.8 39.6 %collective-permute-start.17 = (bf16[2,400,256]{2,1,0:T(8,128)(2,1)}, bf16[2,400,256]{2,1,0:T(8,128)(2,1)}, u32[]{:S(2)}, u32[]{:S(2)}) collective-permute-start(bf16[2,400,256]{2,1,0:T(8,128)(2,1)} %slice.555), channel_id=1, source_target_pairs={{0,1},{1,0},{2,3},{3,2},{4,5},{5,4},{6,7},{7,6},{8,9},{9,8},{10,11... | collective-permute-start | bytes 1228808 | tf_op jit(solution)/shard_map/ppermute | solution.py:25
  117.0 36.8 %collective-permute-start.18 = (bf16[2,400,256]{2,1,0:T(8,128)(2,1)}, bf16[2,400,256]{2,1,0:T(8,128)(2,1)S(1)}, u32[]{:S(2)}, u32[]{:S(2)}) collective-permute-start(bf16[2,400,256]{2,1,0:T(8,128)(2,1)} %slice.556), channel_id=1, source_target_pairs={{0,2},{1,3},{2,0},{3,1},{4,6},{5,7},{6,4},{7,5},{8,10},{9,11},{10,... | collective-permute-start | bytes 1228808 | tf_op jit(solution)/shard_map/ppermute | solution.py:25
  135.5 21.4 %collective-permute-start.13 = (bf16[128,1600]{1,0:T(8,128)(2,1)S(1)}, bf16[128,1600]{1,0:T(8,128)(2,1)S(1)}, u32[]{:S(2)}, u32[]{:S(2)}) collective-permute-start(bf16[128,1600]{1,0:T(8,128)(2,1)S(1)} %get-tuple-element.200), channel_id=1, source_target_pairs={{0,2},{1,3},{2,0},{3,1},{4,6},{5,7},{6,4},{7,5},{8,10},{9,11},{10,... | collective-permute-start | bytes 1228808 | tf_op jit(solution)/shard_map/ppermute | solution.py:25
  136.3 20.6 %collective-permute-start.14 = (bf16[128,1600]{1,0:T(8,128)(2,1)S(1)}, bf16[128,1600]{1,0:T(8,128)(2,1)S(1)}, u32[]{:S(2)}, u32[]{:S(2)}) collective-permute-start(bf16[128,1600]{1,0:T(8,128)(2,1)S(1)} %get-tuple-element.201), channel_id=1, source_target_pairs={{0,3},{1,2},{2,1},{3,0},{4,7},{5,6},{6,5},{7,4},{8,11},{9,10},{10,... | collective-permute-start | bytes 1228808 | tf_op jit(solution)/shard_map/ppermute | solution.py:25
  153.8 21.9 %collective-permute-start.39 = (bf16[128,1600]{1,0:T(8,128)(2,1)S(1)}, bf16[128,1600]{1,0:T(8,128)(2,1)S(1)}, u32[]{:S(2)}, u32[]{:S(2)}) collective-permute-start(bf16[128,1600]{1,0:T(8,128)(2,1)S(1)} %get-tuple-element.225), channel_id=1, source_target_pairs={{0,2},{1,3},{2,0},{3,1},{4,6},{5,7},{6,4},{7,5},{8,10},{9,11},{10,... | collective-permute-start | bytes 1228808 | tf_op jit(solution)/shard_map/ppermute | solution.py:25
  154.5 21.1 %collective-permute-start.40 = (bf16[128,1600]{1,0:T(8,128)(2,1)S(1)}, bf16[128,1600]{1,0:T(8,128)(2,1)S(1)}, u32[]{:S(2)}, u32[]{:S(2)}) collective-permute-start(bf16[128,1600]{1,0:T(8,128)(2,1)S(1)} %get-tuple-element.226), channel_id=1, source_target_pairs={{0,3},{1,2},{2,1},{3,0},{4,7},{5,6},{6,5},{7,4},{8,11},{9,10},{10,... | collective-permute-start | bytes 1228808 | tf_op jit(solution)/shard_map/ppermute | solution.py:25
  157.6 27.2 %collective-permute-start.20 = (bf16[128,1600]{1,0:T(8,128)(2,1)S(1)}, bf16[128,1600]{1,0:T(8,128)(2,1)S(1)}, u32[]{:S(2)}, u32[]{:S(2)}) collective-permute-start(bf16[128,1600]{1,0:T(8,128)(2,1)S(1)} %get-tuple-element.206.refs_0_), channel_id=1, source_target_pairs={{0,2},{1,3},{2,0},{3,1},{4,6},{5,7},{6,4},{7,5},{8,10},{9,11},{10,... | collective-permute-start | bytes 1228808 | tf_op jit(solution)/shard_map/ppermute | solution.py:25
  158.2 29.1 %collective-permute-start.19 = (bf16[128,1600]{1,0:T(8,128)(2,1)S(1)}, bf16[128,1600]{1,0:T(8,128)(2,1)S(1)}, u32[]{:S(2)}, u32[]{:S(2)}) collective-permute-start(bf16[128,1600]{1,0:T(8,128)(2,1)S(1)} %get-tuple-element.206.refs_0_), channel_id=1, source_target_pairs={{0,1},{1,0},{2,3},{3,2},{4,5},{5,4},{6,7},{7,6},{8,9},{9,8},{10,11... | collective-permute-start | bytes 1228808 | tf_op jit(solution)/shard_map/ppermute | solution.py:25
  195.1 30.2 %collective-permute-start.43 = (bf16[64,1600]{1,0:T(8,128)(2,1)}, bf16[64,1600]{1,0:T(8,128)(2,1)}, u32[]{:S(2)}, u32[]{:S(2)}) collective-permute-start(bf16[64,1600]{1,0:T(8,128)(2,1)} %slice.580), channel_id=1, source_target_pairs={{0,1},{1,0},{2,3},{3,2},{4,5},{5,4},{6,7},{7,6},{8,9},{9,8},{10,11... | collective-permute-start | bytes 614408 | tf_op jit(solution)/shard_map/ppermute | solution.py:25
  198.3 27.0 %collective-permute-start.44 = (bf16[64,1600]{1,0:T(8,128)(2,1)}, bf16[64,1600]{1,0:T(8,128)(2,1)}, u32[]{:S(2)}, u32[]{:S(2)}) collective-permute-start(bf16[64,1600]{1,0:T(8,128)(2,1)} %slice.581), channel_id=1, source_target_pairs={{0,2},{1,3},{2,0},{3,1},{4,6},{5,7},{6,4},{7,5},{8,10},{9,11},{10,... | collective-permute-start | bytes 614408 | tf_op jit(solution)/shard_map/ppermute | solution.py:25
  221.8 23.3 %collective-permute-start.24 = (bf16[128,1600]{1,0:T(8,128)(2,1)S(1)}, bf16[128,1600]{1,0:T(8,128)(2,1)S(1)}, u32[]{:S(2)}, u32[]{:S(2)}) collective-permute-start(bf16[128,1600]{1,0:T(8,128)(2,1)S(1)} %get-tuple-element.210), channel_id=1, source_target_pairs={{0,1},{1,0},{2,3},{3,2},{4,5},{5,4},{6,7},{7,6},{8,9},{9,8},{10,11... | collective-permute-start | bytes 1228808 | tf_op jit(solution)/shard_map/ppermute | solution.py:25
  222.8 24.6 %collective-permute-start.25 = (bf16[128,1600]{1,0:T(8,128)(2,1)}, bf16[128,1600]{1,0:T(8,128)(2,1)}, u32[]{:S(2)}, u32[]{:S(2)}) collective-permute-start(bf16[128,1600]{1,0:T(8,128)(2,1)} %get-tuple-element.211), channel_id=1, source_target_pairs={{0,2},{1,3},{2,0},{3,1},{4,6},{5,7},{6,4},{7,5},{8,10},{9,11},{10,... | collective-permute-start | bytes 1228808 | tf_op jit(solution)/shard_map/ppermute | solution.py:25
  223.9 23.5 %collective-permute-start.26 = (bf16[128,1600]{1,0:T(8,128)(2,1)}, bf16[128,1600]{1,0:T(8,128)(2,1)}, u32[]{:S(2)}, u32[]{:S(2)}) collective-permute-start(bf16[128,1600]{1,0:T(8,128)(2,1)} %get-tuple-element.212), channel_id=1, source_target_pairs={{0,3},{1,2},{2,1},{3,0},{4,7},{5,6},{6,5},{7,4},{8,11},{9,10},{10,... | collective-permute-start | bytes 1228808 | tf_op jit(solution)/shard_map/ppermute | solution.py:25
  247.2 317.2 %reduce-scatter.19.cloned.1.call-start = ((), (), s32[]{:S(2)}) async-start(), calls=%async_computation.14 | async-start | bytes 5990400
  252.9 20.8 %collective-permute-start.28 = (bf16[128,1600]{1,0:T(8,128)(2,1)}, bf16[128,1600]{1,0:T(8,128)(2,1)S(1)}, u32[]{:S(2)}, u32[]{:S(2)}) collective-permute-start(bf16[128,1600]{1,0:T(8,128)(2,1)} %get-tuple-element.214.refs_0_), channel_id=1, source_target_pairs={{0,2},{1,3},{2,0},{3,1},{4,6},{5,7},{6,4},{7,5},{8,10},{9,11},{10,... | collective-permute-start | bytes 1228808 | tf_op jit(solution)/shard_map/ppermute | solution.py:25
  283.7 24.6 %collective-permute-start.50 = (bf16[64,1600]{1,0:T(8,128)(2,1)}, bf16[64,1600]{1,0:T(8,128)(2,1)}, u32[]{:S(2)}, u32[]{:S(2)}) collective-permute-start(bf16[64,1600]{1,0:T(8,128)(2,1)} %slice.582), channel_id=1, source_target_pairs={{0,1},{1,0},{2,3},{3,2},{4,5},{5,4},{6,7},{7,6},{8,9},{9,8},{10,11... | collective-permute-start | bytes 614408 | tf_op jit(solution)/shard_map/ppermute | solution.py:25
  286.4 21.9 %collective-permute-start.51 = (bf16[64,1600]{1,0:T(8,128)(2,1)}, bf16[64,1600]{1,0:T(8,128)(2,1)}, u32[]{:S(2)}, u32[]{:S(2)}) collective-permute-start(bf16[64,1600]{1,0:T(8,128)(2,1)} %slice.583), channel_id=1, source_target_pairs={{0,2},{1,3},{2,0},{3,1},{4,6},{5,7},{6,4},{7,5},{8,10},{9,11},{10,... | collective-permute-start | bytes 614408 | tf_op jit(solution)/shard_map/ppermute | solution.py:25
  304.8 21.7 %collective-permute-start.31 = (bf16[128,1600]{1,0:T(8,128)(2,1)S(1)}, bf16[128,1600]{1,0:T(8,128)(2,1)S(1)}, u32[]{:S(2)}, u32[]{:S(2)}) collective-permute-start(bf16[128,1600]{1,0:T(8,128)(2,1)S(1)} %get-tuple-element.216), channel_id=1, source_target_pairs={{0,1},{1,0},{2,3},{3,2},{4,5},{5,4},{6,7},{7,6},{8,9},{9,8},{10,11... | collective-permute-start | bytes 1228808 | tf_op jit(solution)/shard_map/ppermute | solution.py:25
  306.1 23.2 %collective-permute-start.32 = (bf16[128,1600]{1,0:T(8,128)(2,1)S(1)}, bf16[128,1600]{1,0:T(8,128)(2,1)S(1)}, u32[]{:S(2)}, u32[]{:S(2)}) collective-permute-start(bf16[128,1600]{1,0:T(8,128)(2,1)S(1)} %get-tuple-element.217), channel_id=1, source_target_pairs={{0,2},{1,3},{2,0},{3,1},{4,6},{5,7},{6,4},{7,5},{8,10},{9,11},{10,... | collective-permute-start | bytes 1228808 | tf_op jit(solution)/shard_map/ppermute | solution.py:25
  306.6 22.7 %collective-permute-start.33 = (bf16[128,1600]{1,0:T(8,128)(2,1)S(1)}, bf16[128,1600]{1,0:T(8,128)(2,1)S(1)}, u32[]{:S(2)}, u32[]{:S(2)}) collective-permute-start(bf16[128,1600]{1,0:T(8,128)(2,1)S(1)} %get-tuple-element.218), channel_id=1, source_target_pairs={{0,3},{1,2},{2,1},{3,0},{4,7},{5,6},{6,5},{7,4},{8,11},{9,10},{10,... | collective-permute-start | bytes 1228808 | tf_op jit(solution)/shard_map/ppermute | solution.py:25
  330.0 23.8 %collective-permute-start.35 = (bf16[128,1600]{1,0:T(8,128)(2,1)S(1)}, bf16[128,1600]{1,0:T(8,128)(2,1)S(1)}, u32[]{:S(2)}, u32[]{:S(2)}) collective-permute-start(bf16[128,1600]{1,0:T(8,128)(2,1)S(1)} %get-tuple-element.220.refs_0_), channel_id=1, source_target_pairs={{0,2},{1,3},{2,0},{3,1},{4,6},{5,7},{6,4},{7,5},{8,10},{9,11},{10,... | collective-permute-start | bytes 1228808 | tf_op jit(solution)/shard_map/ppermute | solution.py:25
  330.9 24.5 %collective-permute-start.34 = (bf16[128,1600]{1,0:T(8,128)(2,1)S(1)}, bf16[128,1600]{1,0:T(8,128)(2,1)S(1)}, u32[]{:S(2)}, u32[]{:S(2)}) collective-permute-start(bf16[128,1600]{1,0:T(8,128)(2,1)S(1)} %get-tuple-element.220.refs_0_), channel_id=1, source_target_pairs={{0,1},{1,0},{2,3},{3,2},{4,5},{5,4},{6,7},{7,6},{8,9},{9,8},{10,11... | collective-permute-start | bytes 1228808 | tf_op jit(solution)/shard_map/ppermute | solution.py:25
  401.7 162.8 %reduce-scatter.21.cloned.1.call-start = ((), (), s32[]{:S(2)}) async-start(), calls=%async_computation.15 | async-start | bytes 5990400
  432.9 20.7 %collective-permute-start.75 = (bf16[128,1600]{1,0:T(8,128)(2,1)S(1)}, bf16[128,1600]{1,0:T(8,128)(2,1)S(1)}, u32[]{:S(2)}, u32[]{:S(2)}) collective-permute-start(bf16[128,1600]{1,0:T(8,128)(2,1)S(1)} %get-tuple-element.273), channel_id=1, source_target_pairs={{0,3},{1,2},{2,1},{3,0},{4,7},{5,6},{6,5},{7,4},{8,11},{9,10},{10,... | collective-permute-start | bytes 1228808 | tf_op jit(solution)/shard_map/ppermute | solution.py:25
  437.4 24.2 %collective-permute-start.63 = (bf16[128,1600]{1,0:T(8,128)(2,1)S(1)}, bf16[128,1600]{1,0:T(8,128)(2,1)S(1)}, u32[]{:S(2)}, u32[]{:S(2)}) collective-permute-start(bf16[128,1600]{1,0:T(8,128)(2,1)S(1)} %get-tuple-element.252.refs_0_.refs_12_), channel_id=1, source_target_pairs={{0,2},{1,3},{2,0},{3,1},{4,6},{5,7},{6,4},{7,5},{8,10},{9,11},{10,... | collective-permute-start | bytes 1228808 | tf_op jit(solution)/shard_map/ppermute | solution.py:25
  438.2 25.9 %collective-permute-start.62 = (bf16[128,1600]{1,0:T(8,128)(2,1)S(1)}, bf16[128,1600]{1,0:T(8,128)(2,1)S(1)}, u32[]{:S(2)}, u32[]{:S(2)}) collective-permute-start(bf16[128,1600]{1,0:T(8,128)(2,1)S(1)} %get-tuple-element.252.refs_0_.refs_12_), channel_id=1, source_target_pairs={{0,1},{1,0},{2,3},{3,2},{4,5},{5,4},{6,7},{7,6},{8,9},{9,8},{10,11... | collective-permute-start | bytes 1228808 | tf_op jit(solution)/shard_map/ppermute | solution.py:25
  456.3 21.0 %collective-permute-start.77 = (bf16[128,1600]{1,0:T(8,128)(2,1)}, bf16[128,1600]{1,0:T(8,128)(2,1)}, u32[]{:S(2)}, u32[]{:S(2)}) collective-permute-start(bf16[128,1600]{1,0:T(8,128)(2,1)} %get-tuple-element.276.refs_0_.refs_17_), channel_id=1, source_target_pairs={{0,2},{1,3},{2,0},{3,1},{4,6},{5,7},{6,4},{7,5},{8,10},{9,11},{10,... | collective-permute-start | bytes 1228808 | tf_op jit(solution)/shard_map/ppermute | solution.py:25
  457.0 22.0 %collective-permute-start.76 = (bf16[128,1600]{1,0:T(8,128)(2,1)}, bf16[128,1600]{1,0:T(8,128)(2,1)}, u32[]{:S(2)}, u32[]{:S(2)}) collective-permute-start(bf16[128,1600]{1,0:T(8,128)(2,1)} %get-tuple-element.276.refs_0_.refs_17_), channel_id=1, source_target_pairs={{0,1},{1,0},{2,3},{3,2},{4,5},{5,4},{6,7},{7,6},{8,9},{9,8},{10,11... | collective-permute-start | bytes 1228808 | tf_op jit(solution)/shard_map/ppermute | solution.py:25
  476.8 185.9 %reduce-scatter.15.cloned.1.call-start = ((), (), s32[]{:S(2)}) async-start(), calls=%async_computation.12 | async-start | bytes 6451200 | tf_op jit(solution)/shard_map/reduce_scatter | solution.py:845
  478.2 25.8 %collective-permute-start.78 = (bf16[64,1600]{1,0:T(8,128)(2,1)S(1)}, bf16[64,1600]{1,0:T(8,128)(2,1)S(1)}, u32[]{:S(2)}, u32[]{:S(2)}) collective-permute-start(bf16[64,1600]{1,0:T(8,128)(2,1)S(1)} %slice.599), channel_id=1, source_target_pairs={{0,1},{1,0},{2,3},{3,2},{4,5},{5,4},{6,7},{7,6},{8,9},{9,8},{10,11... | collective-permute-start | bytes 614408 | tf_op jit(solution)/shard_map/ppermute | solution.py:25
  480.0 23.9 %collective-permute-start.79 = (bf16[64,1600]{1,0:T(8,128)(2,1)S(1)}, bf16[64,1600]{1,0:T(8,128)(2,1)S(1)}, u32[]{:S(2)}, u32[]{:S(2)}) collective-permute-start(bf16[64,1600]{1,0:T(8,128)(2,1)S(1)} %slice.600), channel_id=1, source_target_pairs={{0,2},{1,3},{2,0},{3,1},{4,6},{5,7},{6,4},{7,5},{8,10},{9,11},{10,... | collective-permute-start | bytes 614408 | tf_op jit(solution)/shard_map/ppermute | solution.py:25
  500.4 24.8 %collective-permute-start.66 = (bf16[128,1600]{1,0:T(8,128)(2,1)S(1)}, bf16[128,1600]{1,0:T(8,128)(2,1)S(1)}, u32[]{:S(2)}, u32[]{:S(2)}) collective-permute-start(bf16[128,1600]{1,0:T(8,128)(2,1)S(1)} %get-tuple-element.263), channel_id=1, source_target_pairs={{0,1},{1,0},{2,3},{3,2},{4,5},{5,4},{6,7},{7,6},{8,9},{9,8},{10,11... | collective-permute-start | bytes 1228808 | tf_op jit(solution)/shard_map/ppermute | solution.py:25
  501.4 25.2 %collective-permute-start.67 = (bf16[128,1600]{1,0:T(8,128)(2,1)S(1)}, bf16[128,1600]{1,0:T(8,128)(2,1)S(1)}, u32[]{:S(2)}, u32[]{:S(2)}) collective-permute-start(bf16[128,1600]{1,0:T(8,128)(2,1)S(1)} %get-tuple-element.264), channel_id=1, source_target_pairs={{0,2},{1,3},{2,0},{3,1},{4,6},{5,7},{6,4},{7,5},{8,10},{9,11},{10,... | collective-permute-start | bytes 1228808 | tf_op jit(solution)/shard_map/ppermute | solution.py:25
  502.6 24.0 %collective-permute-start.68 = (bf16[128,1600]{1,0:T(8,128)(2,1)S(1)}, bf16[128,1600]{1,0:T(8,128)(2,1)S(1)}, u32[]{:S(2)}, u32[]{:S(2)}) collective-permute-start(bf16[128,1600]{1,0:T(8,128)(2,1)S(1)} %get-tuple-element.265), channel_id=1, source_target_pairs={{0,3},{1,2},{2,1},{3,0},{4,7},{5,6},{6,5},{7,4},{8,11},{9,10},{10,... | collective-permute-start | bytes 1228808 | tf_op jit(solution)/shard_map/ppermute | solution.py:25
  523.1 21.5 %collective-permute-start.87 = (bf16[128,1600]{1,0:T(8,128)(2,1)}, bf16[128,1600]{1,0:T(8,128)(2,1)}, u32[]{:S(2)}, u32[]{:S(2)}) collective-permute-start(bf16[128,1600]{1,0:T(8,128)(2,1)} %get-tuple-element.296), channel_id=1, source_target_pairs={{0,1},{1,0},{2,3},{3,2},{4,5},{5,4},{6,7},{7,6},{8,9},{9,8},{10,11... | collective-permute-start | bytes 1228808 | tf_op jit(solution)/shard_map/ppermute | solution.py:25
  524.0 20.6 %collective-permute-start.88 = (bf16[128,1600]{1,0:T(8,128)(2,1)}, bf16[128,1600]{1,0:T(8,128)(2,1)}, u32[]{:S(2)}, u32[]{:S(2)}) collective-permute-start(bf16[128,1600]{1,0:T(8,128)(2,1)} %get-tuple-element.297), channel_id=1, source_target_pairs={{0,2},{1,3},{2,0},{3,1},{4,6},{5,7},{6,4},{7,5},{8,10},{9,11},{10,... | collective-permute-start | bytes 1228808 | tf_op jit(solution)/shard_map/ppermute | solution.py:25
  529.3 22.9 %collective-permute-start.70 = (bf16[128,1600]{1,0:T(8,128)(2,1)}, bf16[128,1600]{1,0:T(8,128)(2,1)}, u32[]{:S(2)}, u32[]{:S(2)}) collective-permute-start(bf16[128,1600]{1,0:T(8,128)(2,1)} %get-tuple-element.344.refs_0_), channel_id=1, source_target_pairs={{0,2},{1,3},{2,0},{3,1},{4,6},{5,7},{6,4},{7,5},{8,10},{9,11},{10,... | collective-permute-start | bytes 1228808 | tf_op jit(solution)/shard_map/ppermute | solution.py:25
  530.2 24.7 %collective-permute-start.69 = (bf16[128,1600]{1,0:T(8,128)(2,1)}, bf16[128,1600]{1,0:T(8,128)(2,1)}, u32[]{:S(2)}, u32[]{:S(2)}) collective-permute-start(bf16[128,1600]{1,0:T(8,128)(2,1)} %get-tuple-element.344.refs_0_), channel_id=1, source_target_pairs={{0,1},{1,0},{2,3},{3,2},{4,5},{5,4},{6,7},{7,6},{8,9},{9,8},{10,11... | collective-permute-start | bytes 1228808 | tf_op jit(solution)/shard_map/ppermute | solution.py:25
  544.5 185.1 %reduce-scatter.23.cloned.1.call-start = ((), (), s32[]{:S(2)}) async-start(), calls=%async_computation.16 | async-start | bytes 5990400
  597.4 38.7 %collective-permute-start.80 = (bf16[128,1600]{1,0:T(8,128)(2,1)}, bf16[128,1600]{1,0:T(8,128)(2,1)}, u32[]{:S(2)}, u32[]{:S(2)}) collective-permute-start(bf16[128,1600]{1,0:T(8,128)(2,1)} %get-tuple-element.287), channel_id=1, source_target_pairs={{0,1},{1,0},{2,3},{3,2},{4,5},{5,4},{6,7},{7,6},{8,9},{9,8},{10,11... | collective-permute-start | bytes 1228808 | tf_op jit(solution)/shard_map/ppermute | solution.py:25
  598.1 37.9 %collective-permute-start.81 = (bf16[128,1600]{1,0:T(8,128)(2,1)}, bf16[128,1600]{1,0:T(8,128)(2,1)}, u32[]{:S(2)}, u32[]{:S(2)}) collective-permute-start(bf16[128,1600]{1,0:T(8,128)(2,1)} %get-tuple-element.288), channel_id=1, source_target_pairs={{0,2},{1,3},{2,0},{3,1},{4,6},{5,7},{6,4},{7,5},{8,10},{9,11},{10,... | collective-permute-start | bytes 1228808 | tf_op jit(solution)/shard_map/ppermute | solution.py:25
  600.4 20.8 %collective-permute-start.98 = (bf16[128,1600]{1,0:T(8,128)(2,1)}, bf16[128,1600]{1,0:T(8,128)(2,1)}, u32[]{:S(2)}, u32[]{:S(2)}) collective-permute-start(bf16[128,1600]{1,0:T(8,128)(2,1)} %get-tuple-element.314), channel_id=1, source_target_pairs={{0,2},{1,3},{2,0},{3,1},{4,6},{5,7},{6,4},{7,5},{8,10},{9,11},{10,... | collective-permute-start | bytes 1228808 | tf_op jit(solution)/shard_map/ppermute | solution.py:25
  601.4 26.2 %collective-permute-start.99 = (bf16[128,1600]{1,0:T(8,128)(2,1)}, bf16[128,1600]{1,0:T(8,128)(2,1)}, u32[]{:S(2)}, u32[]{:S(2)}) collective-permute-start(bf16[128,1600]{1,0:T(8,128)(2,1)} %get-tuple-element.315), channel_id=1, source_target_pairs={{0,3},{1,2},{2,1},{3,0},{4,7},{5,6},{6,5},{7,4},{8,11},{9,10},{10,... | collective-permute-start | bytes 1228808 | tf_op jit(solution)/shard_map/ppermute | solution.py:25
  613.0 121.1 %reduce-scatter.25.cloned.1.call-start = ((), (), s32[]{:S(2)}) async-start(), calls=%async_computation.17 | async-start | bytes 5990400
  658.1 152.6 %reduce-scatter.17.cloned.1.call-start = ((), (), s32[]{:S(2)}) async-start(), calls=%async_computation.13 | async-start | bytes 6451200 | tf_op jit(solution)/shard_map/reduce_scatter | solution.py:845
  659.3 28.1 %collective-permute-start.85 = (bf16[64,1600]{1,0:T(8,128)(2,1)}, bf16[64,1600]{1,0:T(8,128)(2,1)}, u32[]{:S(2)}, u32[]{:S(2)}) collective-permute-start(bf16[64,1600]{1,0:T(8,128)(2,1)} %slice.601), channel_id=1, source_target_pairs={{0,1},{1,0},{2,3},{3,2},{4,5},{5,4},{6,7},{7,6},{8,9},{9,8},{10,11... | collective-permute-start | bytes 614408 | tf_op jit(solution)/shard_map/ppermute | solution.py:25
  661.8 25.5 %collective-permute-start.86 = (bf16[64,1600]{1,0:T(8,128)(2,1)}, bf16[64,1600]{1,0:T(8,128)(2,1)}, u32[]{:S(2)}, u32[]{:S(2)}) collective-permute-start(bf16[64,1600]{1,0:T(8,128)(2,1)} %slice.602), channel_id=1, source_target_pairs={{0,2},{1,3},{2,0},{3,1},{4,6},{5,7},{6,4},{7,5},{8,10},{9,11},{10,... | collective-permute-start | bytes 614408 | tf_op jit(solution)/shard_map/ppermute | solution.py:25
  683.8 24.0 %collective-permute-start.104 = (bf16[128,1600]{1,0:T(8,128)(2,1)S(1)}, bf16[128,1600]{1,0:T(8,128)(2,1)S(1)}, u32[]{:S(2)}, u32[]{:S(2)}) collective-permute-start(bf16[128,1600]{1,0:T(8,128)(2,1)S(1)} %get-tuple-element.328), channel_id=1, source_target_pairs={{0,1},{1,0},{2,3},{3,2},{4,5},{5,4},{6,7},{7,6},{8,9},{9,8},{10,11... | collective-permute-start | bytes 1228808 | tf_op jit(solution)/shard_map/ppermute | solution.py:25
  685.1 36.6 %collective-permute-start.105 = (bf16[128,1600]{1,0:T(8,128)(2,1)}, bf16[128,1600]{1,0:T(8,128)(2,1)}, u32[]{:S(2)}, u32[]{:S(2)}) collective-permute-start(bf16[128,1600]{1,0:T(8,128)(2,1)} %get-tuple-element.329), channel_id=1, source_target_pairs={{0,2},{1,3},{2,0},{3,1},{4,6},{5,7},{6,4},{7,5},{8,10},{9,11},{10,... | collective-permute-start | bytes 1228808 | tf_op jit(solution)/shard_map/ppermute | solution.py:25
  686.1 35.5 %collective-permute-start.106 = (bf16[128,1600]{1,0:T(8,128)(2,1)}, bf16[128,1600]{1,0:T(8,128)(2,1)}, u32[]{:S(2)}, u32[]{:S(2)}) collective-permute-start(bf16[128,1600]{1,0:T(8,128)(2,1)} %get-tuple-element.330), channel_id=1, source_target_pairs={{0,3},{1,2},{2,1},{3,0},{4,7},{5,6},{6,5},{7,4},{8,11},{9,10},{10,... | collective-permute-start | bytes 1228808 | tf_op jit(solution)/shard_map/ppermute | solution.py:25
  705.5 21.1 %collective-permute-start.94 = (bf16[128,1600]{1,0:T(8,128)(2,1)}, bf16[128,1600]{1,0:T(8,128)(2,1)}, u32[]{:S(2)}, u32[]{:S(2)}) collective-permute-start(bf16[128,1600]{1,0:T(8,128)(2,1)} %get-tuple-element.308), channel_id=1, source_target_pairs={{0,1},{1,0},{2,3},{3,2},{4,5},{5,4},{6,7},{7,6},{8,9},{9,8},{10,11... | collective-permute-start | bytes 1228808 | tf_op jit(solution)/shard_map/ppermute | solution.py:25
  752.4 21.2 %collective-permute-start.108 = (bf16[400,512]{1,0:T(8,128)(2,1)S(1)}, bf16[400,512]{1,0:T(8,128)(2,1)S(1)}, u32[]{:S(2)}, u32[]{:S(2)}) collective-permute-start(bf16[400,512]{1,0:T(8,128)(2,1)S(1)} %get-tuple-element.338), channel_id=1, source_target_pairs={{0,2},{1,3},{2,0},{3,1},{4,6},{5,7},{6,4},{7,5},{8,10},{9,11},{10,... | collective-permute-start | bytes 1228808 | tf_op jit(solution)/shard_map/ppermute | solution.py:25
  754.4 41.4 %collective-permute-start.110 = (bf16[400,512]{1,0:T(8,128)(2,1)}, bf16[400,512]{1,0:T(8,128)(2,1)}, u32[]{:S(2)}, u32[]{:S(2)}) collective-permute-start(bf16[400,512]{1,0:T(8,128)(2,1)} %get-tuple-element.341), channel_id=1, source_target_pairs={{0,1},{1,0},{2,3},{3,2},{4,5},{5,4},{6,7},{7,6},{8,9},{9,8},{10,11... | collective-permute-start | bytes 1228808 | tf_op jit(solution)/shard_map/ppermute | solution.py:25
  755.9 39.9 %collective-permute-start.111 = (bf16[400,512]{1,0:T(8,128)(2,1)}, bf16[400,512]{1,0:T(8,128)(2,1)}, u32[]{:S(2)}, u32[]{:S(2)}) collective-permute-start(bf16[400,512]{1,0:T(8,128)(2,1)} %get-tuple-element.342), channel_id=1, source_target_pairs={{0,2},{1,3},{2,0},{3,1},{4,6},{5,7},{6,4},{7,5},{8,10},{9,11},{10,... | collective-permute-start | bytes 1228808 | tf_op jit(solution)/shard_map/ppermute | solution.py:25
  779.6 25.1 %all-to-all-start = ((bf16[4,2,400,128]{3,2,1,0:T(8,128)(2,1)}), bf16[4,2,400,128]{3,2,1,0:T(8,128)(2,1)S(1)}, u32[]{:S(2)}, u32[]{:S(2)}) async-start(bf16[4,2,400,128]{3,2,1,0:T(8,128)(2,1)} %pad_maximum_fusion.5), calls=%async_computation.1 | async-start | bytes 1638400 | tf_op jit(solution)/shard_map/all_to_all | solution.py:841
  (287 other events, 2914.1 us)
Sparse Core Ops, SparseCore 0:
  33.9 61.5 all-gather.5
  97.7 99.4 all-gather.7
  199.4 58.5 all-gather.9
  259.4 57.1 all-gather.11
  318.7 57.2 all-gather.13
  401.8 57.9 reduce-scatter.18
  476.9 58.2 reduce-scatter.20
  544.7 62.0 reduce-scatter.14
  613.2 58.6 reduce-scatter.22
  674.1 60.0 reduce-scatter.24
  736.5 64.1 reduce-scatter.16
